TPU v7x, 512 devices: a whole 4x8x8 slice. The times are simulated.
512 devices in a mesh: dp: 128 (over z, y, core), group: 4 (over x).
Axes of the slice: x: 4, y: 8, z: 8, core: 2. Of those that a mesh axis runs over, the one named last changes fastest.
Arguments:
- queries: bfloat16 [2048, 32, 128], P(('dp', 'group'))
- positives: bfloat16 [2048, 64, 128], P(('dp', 'group'))
- passage_pool: bfloat16 [4096, 64, 128], P('dp')
- negative_ids: int32 [2048, 7], P(('dp', 'group')), may hold values from 0 to 4095, as said below
- storage_row: int32 [4096], replicated, may hold values from 0 to 4095, as said below
Outputs:
- losses: float32 [2048], P(('dp', 'group'))
- query_grad: float32 [2048, 32, 128], P(('dp', 'group'))
- positive_grad: float32 [2048, 64, 128], P(('dp', 'group'))
- pool_grad: float32 [4096, 64, 128], P(('dp', 'group'))
Inputs may be any that keep to these rules, and one draw needn't show every extreme that they name: `storage_row`: each passage id appears exactly once. `negative_ids`: in each aligned block of 4 rows (the queries of one device), at most 2 of the 28 ids have storage_row[id] // 32 equal to any one value; in every block some value is reached exactly 2 times.
All inputs are finite; a program needn't handle non-finite values.
Results may differ from a plain program's by a relative error of at most 0.02.
Values may be sent and summed in bfloat16 or wider, within the bound.
No kernel may reach another device: no remote copies, remote signals or barrier semaphores. Data moves between devices by JAX's collectives and lax.ppermute only.
A program may use at most 128 MiB of HBM per device.

v0:
```python
import jax
import jax.numpy as jnp
from jax import lax
from jax.sharding import PartitionSpec as P

soft_temp = 0.1


def unit_rows(values):
    widened = values.astype(jnp.float32)
    return (widened / jnp.sqrt(jnp.sum(widened * widened, axis=-1, keepdims=True) + 1e-06)).astype(
        jnp.bfloat16
    )


def token_softmax(token_scores):
    exp_scores = jnp.exp(token_scores / soft_temp)
    token_total = jnp.sum(exp_scores, axis=-1)
    candidate_score = jnp.sum(soft_temp * jnp.log(token_total), axis=-1)
    return (candidate_score, exp_scores / token_total[..., None])


def candidate_loss(candidate_score, own_index):
    cand_count = candidate_score.shape[-1]
    own_hot = (jnp.arange(cand_count, dtype=jnp.int32) == own_index[..., None]).astype(jnp.float32)
    weights = jnp.exp(candidate_score)
    weight_sum = jnp.sum(weights, axis=-1)
    query_loss = jnp.log(weight_sum) - jnp.sum(candidate_score * own_hot, axis=-1)
    return (query_loss, weights / weight_sum[..., None] - own_hot)


def request_layout(negative_ids, storage_row, pool_rows, dp_count, capacity):
    home_rows = jnp.take(storage_row, negative_ids.reshape(-1), axis=0)
    owner_index = home_rows // pool_rows
    local_row = home_rows - owner_index * pool_rows
    positions = jnp.arange(home_rows.shape[0], dtype=jnp.int32)
    same_owner = (owner_index[:, None] == owner_index[None, :]) & (
        positions[None, :] < positions[:, None]
    )
    order_rank = jnp.sum(same_owner.astype(jnp.int32), axis=1)
    slot_index = owner_index * capacity + order_rank
    slot_source = jnp.full((dp_count * capacity,), -1, jnp.int32).at[slot_index].set(positions)
    filled = slot_source >= 0
    source = jnp.maximum(slot_source, 0)
    ask_rows = jnp.where(filled, jnp.take(local_row, source, axis=0), -1).reshape(
        dp_count, capacity
    )
    return (slot_index, filled, source, ask_rows)


def owner_sum(rows_in, terms, pool_rows):
    slot_rows = rows_in.reshape(-1)
    target = jnp.where(slot_rows >= 0, slot_rows, pool_rows)
    flat_terms = terms.reshape((slot_rows.shape[0],) + terms.shape[-2:])
    empty = jnp.zeros((pool_rows,) + terms.shape[-2:], jnp.float32)
    return empty.at[target].add(flat_terms, mode="drop")


def per_device(queries, positives, passage_pool, negative_ids, storage_row):
    dp_count = lax.axis_size("dp")
    local_queries = queries.shape[0]
    negatives_per = negative_ids.shape[1]
    pool_rows = passage_pool.shape[0]
    token_count = passage_pool.shape[1]
    features = passage_pool.shape[2]
    capacity = max(2, 9 * local_queries * negatives_per // (4 * dp_count))
    query_unit = unit_rows(queries)
    positive_unit = unit_rows(positives)
    pool_unit = unit_rows(passage_pool)
    slot_index, filled, source, ask_rows = request_layout(
        negative_ids, storage_row, pool_rows, dp_count, capacity
    )
    batch_width = lax.axis_size("group") * local_queries
    own_index = lax.axis_index("group") * local_queries + jnp.arange(local_queries, dtype=jnp.int32)
    gathered = lax.all_gather(positive_unit, "group", axis=0, tiled=True)
    rows_in = lax.all_to_all(ask_rows, "dp", split_axis=0, concat_axis=0, tiled=True)
    fetched = jnp.take(pool_unit, jnp.maximum(rows_in.reshape(-1), 0), axis=0)
    arrived = lax.all_to_all(
        fetched.reshape(dp_count, capacity, token_count, features),
        "dp",
        split_axis=0,
        concat_axis=0,
        tiled=True,
    )
    negatives = jnp.take(arrived.reshape(-1, token_count, features), slot_index, axis=0)
    negatives = negatives.reshape(local_queries, negatives_per, token_count, features)

    def score_one(running, inputs):
        query_vectors, query_own, query_negatives = inputs
        candidates = jnp.concatenate([gathered, query_negatives], axis=0)
        token_scores = jnp.einsum(
            "id,cjd->cij", query_vectors, candidates, preferred_element_type=jnp.float32
        )
        candidate_score, token_probs = token_softmax(token_scores)
        query_loss, score_grad = candidate_loss(candidate_score, query_own)
        weight_grad = (score_grad[:, None, None] * token_probs).astype(jnp.bfloat16)
        one_grad = jnp.einsum(
            "cij,cjd->id", weight_grad, candidates, preferred_element_type=jnp.float32
        )
        cand_grad = jnp.einsum(
            "cij,id->cjd", weight_grad, query_vectors, preferred_element_type=jnp.float32
        )
        return (running + cand_grad[:batch_width], (query_loss, one_grad, cand_grad[batch_width:]))

    start_grad = jnp.zeros((batch_width, token_count, features), jnp.float32)
    positive_sum, (losses, query_grad, negative_grad) = lax.scan(
        score_one, start_grad, (query_unit, own_index, negatives)
    )
    outgoing = jnp.where(
        filled[:, None, None],
        jnp.take(negative_grad.reshape(-1, token_count, features), source, axis=0),
        0.0,
    )
    grads_in = lax.all_to_all(
        outgoing.reshape(dp_count, capacity, token_count, features).astype(jnp.bfloat16),
        "dp",
        split_axis=0,
        concat_axis=0,
        tiled=True,
    ).astype(jnp.float32)
    pool_part = owner_sum(rows_in, grads_in, pool_rows)
    positive_grad, pool_grad = (
        lax.psum_scatter(
            positive_sum.astype(jnp.bfloat16), "group", scatter_dimension=0, tiled=True
        ).astype(jnp.float32),
        lax.psum_scatter(
            pool_part.astype(jnp.bfloat16), "group", scatter_dimension=0, tiled=True
        ).astype(jnp.float32),
    )
    return (losses, query_grad, positive_grad, pool_grad)


def solution(mesh):
    in_specs = (
        P(("dp", "group"), None, None),
        P(("dp", "group"), None, None),
        P("dp", None, None),
        P(("dp", "group"), None),
        P(),
    )
    out_specs = (
        P(("dp", "group")),
        P(("dp", "group"), None, None),
        P(("dp", "group"), None, None),
        P(("dp", "group"), None, None),
    )
    return jax.shard_map(
        per_device, mesh=mesh, in_specs=in_specs, out_specs=out_specs, check_vma=False
    )
```

profile of v0, /device:TPU:6, one launch (start us, length us, event | category | flops | bytes accessed | tf_op | source)
XLA Modules:
  0.0 394.5 jit_solution(849970238813822922)
XLA Ops:
  7.2 0.8 reshape.309
  7.9 0.8 reshape.310
  8.7 0.7 gather_fusion
  9.5 0.7 fusion.32
  10.2 0.7 fusion.33
  10.9 0.2 convert_reduce_fusion
  11.1 0.7 scatter_custom_fusion
  11.8 17.5 %fusion.26 = (s32[256]{0:T(256)S(1)}, pred[256]{0:T(512)(128)(4,1)S(1)}) fusion(s32[]{:T(128)} %bitcast.31, s32[]{:T(128)} %bitcast.4, s32[]{:T(128)} %bitcast.5, s32[]{:T(128)} %bitcast.6, s32[]{:T(128)} %bitcast.7, s32[]{:T(128)} %bitcast.8, s32[]{:T(128)} %bitcast.9, s32[]{:T(128)} %bitcast.10, s32[]{:T(128)} %bitcast.11, s32[]{:T(128)} %bitcast.12, ...), kind=kLoop, calls=%fused_computation.115 | loop fusion | flops 15104 | bytes 2416 | tf_op jit(solution)/shard_map/jit(_where)/select_n | solution.py:45
  29.3 0.8 all_to_all.12
  30.0 17.8 %all-to-all-start = ((s32[128,1,2]{2,1,0:T(1,128)}), s32[128,1,2]{2,1,0:T(1,128)S(1)}, u32[]{:S(2)}, u32[]{:S(2)}) async-start(s32[128,1,2]{2,1,0:T(1,128)} %bitcast.32), calls=%async_computation | async-start | bytes 131072 | tf_op jit(solution)/shard_map/all_to_all | solution.py:76
  47.9 1.4 fusion.14
  49.3 1.4 fusion.15
  50.7 8.3 %all-to-all-done = s32[128,1,2]{2,1,0:T(1,128)S(1)} async-done(((s32[128,1,2]{2,1,0:T(1,128)}), s32[128,1,2]{2,1,0:T(1,128)S(1)}, u32[]{:S(2)}, u32[]{:S(2)}) %all-to-all-start) | async-done | bytes 1056 | tf_op jit(solution)/shard_map/all_to_all | solution.py:76
  58.9 0.5 broadcast.557
  59.4 0.8 reduce.3
  60.5 0.2 copy.18
  60.6 3.1 gather_fusion.1
  63.7 3.8 broadcast_select_fusion
  67.5 7.5 %all-to-all-start.1 = ((bf16[128,2,64,128]{3,2,1,0:T(8,128)(2,1)}), bf16[128,2,64,128]{3,2,1,0:T(8,128)(2,1)}, u32[]{:S(2)}, u32[]{:S(2)}) async-start(bf16[128,2,64,128]{3,2,1,0:T(8,128)(2,1)} %broadcast_select_fusion), calls=%async_computation.1 | async-start | bytes 8388608 | tf_op jit(solution)/shard_map/all_to_all | solution.py:78
  75.2 0.2 broadcast_in_dim.111
  75.4 0.2 broadcast_in_dim.113
  75.8 12.6 %all_gather.3 = bf16[16,64,128]{2,1,0:T(8,128)(2,1)S(1)} all-gather(bf16[4,64,128]{2,1,0:T(8,128)(2,1)S(1)} %fusion.17), channel_id=1, replica_groups=mesh['dp'=128,'group'=4] {'group'}, dimensions={0}, use_global_device_ids=true | all-gather | bytes 327680 | tf_op jit(solution)/shard_map/all_gather | solution.py:75
  88.7 83.2 %all-to-all-done.1 = bf16[128,2,64,128]{3,2,1,0:T(8,128)(2,1)} async-done(((bf16[128,2,64,128]{3,2,1,0:T(8,128)(2,1)}), bf16[128,2,64,128]{3,2,1,0:T(8,128)(2,1)}, u32[]{:S(2)}, u32[]{:S(2)}) %all-to-all-start.1) | async-done | bytes 4194336 | tf_op jit(solution)/shard_map/all_to_all | solution.py:78
  171.8 2.8 gather_fusion.2
  174.8 28.7 %while.17 = (s32[]{:T(128)}, f32[16,64,128]{2,1,0:T(8,128)S(1)}, f32[4]{0:T(128)S(1)}, f32[4,32,128]{2,1,0:T(8,128)}, bf16[4,7,64,128]{3,2,1,0:T(8,128)(2,1)S(1)...) while((s32[]{:T(128)}, f32[16,64,128]{2,1,0:T(8,128)S(1)}, ...), condition=%wide.region_10.11_spmd.clone, body=%wide.region_5.10_spmd.clone.sunk | while | flops 37192576 | bytes 4348179 | solution.py:106
  174.8 0.6 fusion.41
  175.5 0.6 dynamic_slice.33
  176.1 1.3 fusion.42
  177.4 1.3 divide_subtract_fusion.2
  178.8 0.5 fusion.43
  179.3 0.2 slice_add_fusion.2
  179.5 1.0 fusion.44
  182.0 0.6 fusion.41
  182.7 0.6 dynamic_slice.33
  183.3 1.3 fusion.42
  184.6 1.3 divide_subtract_fusion.2
  185.9 0.5 fusion.43
  186.5 0.2 slice_add_fusion.2
  186.7 1.0 fusion.44
  189.2 0.6 fusion.41
  189.8 0.6 dynamic_slice.33
  190.4 1.3 fusion.42
  191.8 1.3 divide_subtract_fusion.2
  193.1 0.5 fusion.43
  193.6 0.2 slice_add_fusion.2
  193.9 1.0 fusion.44
  196.3 0.6 fusion.41
  197.0 0.6 dynamic_slice.33
  197.6 1.3 fusion.42
  198.9 1.3 divide_subtract_fusion.2
  200.3 0.5 fusion.43
  200.8 0.2 slice_add_fusion.2
  201.0 1.0 fusion.44
  203.5 3.1 gather_fusion.3
  206.6 4.3 %select_convert_fusion = bf16[128,2,64,128]{3,2,1,0:T(8,128)(2,1)} fusion(bf16[128,2,64,128]{3,2,1,0:T(8,128)(2,1)} %bitcast.91, pred[128,2]{1,0:T(8,128)(4,1)S(1)} %broadcast_in_dim.113, pred[128,2]{1,0:T(8,128)(4,1)S(1)} %broadcast_in_dim.111), kind=kLoop, calls=%fused_computation.32 | loop fusion | flops 4194304 | bytes 8389120 | tf_op jit(solution)/shard_map/convert_element_type | solution.py:115
  210.9 16.6 %all-to-all-start.2 = ((bf16[128,2,64,128]{3,2,1,0:T(8,128)(2,1)}), bf16[128,2,64,128]{3,2,1,0:T(8,128)(2,1)}, u32[]{:S(2)}, u32[]{:S(2)}) async-start(bf16[128,2,64,128]{3,2,1,0:T(8,128)(2,1)} %select_convert_fusion), calls=%async_computation.3 | async-start | bytes 8388608 | tf_op jit(solution)/shard_map/all_to_all | solution.py:114
  227.5 0.7 convert_element_type.54
  228.3 95.7 %all-to-all-done.2 = bf16[128,2,64,128]{3,2,1,0:T(8,128)(2,1)} async-done(((bf16[128,2,64,128]{3,2,1,0:T(8,128)(2,1)}), bf16[128,2,64,128]{3,2,1,0:T(8,128)(2,1)}, u32[]{:S(2)}, u32[]{:S(2)}) %all-to-all-start.2) | async-done | bytes 4194336 | tf_op jit(solution)/shard_map/all_to_all | solution.py:114
  324.0 6.5 %bitcast_convert_fusion = f32[256,64,128]{2,1,0:T(8,128)} fusion(bf16[128,2,64,128]{3,2,1,0:T(8,128)(2,1)} %all-to-all-done.2), kind=kLoop, calls=%fused_computation.33 | loop fusion | flops 2097152 | bytes 12582912 | tf_op jit(solution)/shard_map/reshape | solution.py:54
  330.5 26.3 %scatter_fusion = f32[32,64,128]{2,1,0:T(8,128)S(1)} fusion(f32[32,64,128]{2,1,0:T(8,128)S(1)} %broadcast_in_dim.110, s32[256]{0:T(256)S(1)} %bitcast.94, f32[256,64,128]{2,1,0:T(8,128)} %bitcast_convert_fusion), kind=kCustom, calls=%fused_computation.5 | custom fusion | flops 2097152 | bytes 25166848 | tf_op jit(solution)/shard_map/scatter-add | solution.py:56
  356.9 0.9 convert_element_type.57
  357.8 1.5 convert_element_type.55
  359.3 26.7 %reduce-scatter.5.cloned.1.call-done = bf16[8,64,128]{2,1,0:T(8,128)(2,1)} async-done(((bf16[32,64,128]{2,1,0:T(8,128)(2,1)}), bf16[8,64,128]{2,1,0:T(8,128)(2,1)}) %reduce-scatter.5.cloned.1.call-update) | async-done | bytes 131088 | tf_op jit(solution)/shard_map/reduce_scatter | solution.py:126
  386.0 1.6 convert_element_type.58
  (62 shorter events, 2.4 us)
Async XLA Ops:
  7.2 1.6 copy-start
  30.0 28.9 %all-to-all-start = ((s32[128,1,2]{2,1,0:T(1,128)}), s32[128,1,2]{2,1,0:T(1,128)S(1)}, u32[]{:S(2)}, u32[]{:S(2)}) async-start(s32[128,1,2]{2,1,0:T(1,128)} %bitcast.32), calls=%async_computation | async-start | bytes 131072 | tf_op jit(solution)/shard_map/all_to_all | solution.py:76
  67.5 8.0 %copy-start.1 = (bf16[4,64,128]{2,1,0:T(8,128)(2,1)S(1)}, bf16[4,64,128]{2,1,0:T(8,128)(2,1)}, u32[]{:S(2)}) copy-start(bf16[4,64,128]{2,1,0:T(8,128)(2,1)} %param.8) | copy-start | bytes 196612
  67.5 20.9 %copy-start.2 = (bf16[4,32,128]{2,1,0:T(8,128)(2,1)S(1)}, bf16[4,32,128]{2,1,0:T(8,128)(2,1)}, u32[]{:S(2)}) copy-start(bf16[4,32,128]{2,1,0:T(8,128)(2,1)} %param.7) | copy-start | bytes 98308
  67.5 21.0 %copy-start.3 = (s32[4,7]{1,0:T(4,128)S(1)}, s32[4,7]{1,0:T(4,128)}, u32[]{:S(2)}) copy-start(s32[4,7]{1,0:T(4,128)} %param.10) | copy-start | bytes 340
  67.5 104.3 %all-to-all-start.1 = ((bf16[128,2,64,128]{3,2,1,0:T(8,128)(2,1)}), bf16[128,2,64,128]{3,2,1,0:T(8,128)(2,1)}, u32[]{:S(2)}, u32[]{:S(2)}) async-start(bf16[128,2,64,128]{3,2,1,0:T(8,128)(2,1)} %broadcast_select_fusion), calls=%async_computation.1 | async-start | bytes 8388608 | tf_op jit(solution)/shard_map/all_to_all | solution.py:78
  203.5 3.1 copy-start.4
  210.9 113.1 %all-to-all-start.2 = ((bf16[128,2,64,128]{3,2,1,0:T(8,128)(2,1)}), bf16[128,2,64,128]{3,2,1,0:T(8,128)(2,1)}, u32[]{:S(2)}, u32[]{:S(2)}) async-start(bf16[128,2,64,128]{3,2,1,0:T(8,128)(2,1)} %select_convert_fusion), calls=%async_computation.3 | async-start | bytes 8388608 | tf_op jit(solution)/shard_map/all_to_all | solution.py:114
  227.4 130.4 %reduce-scatter.3.cloned.1.call-start = ((), (), s32[]{:S(2)}) async-start(), calls=%async_computation.5 | async-start | bytes 327680 | tf_op jit(solution)/shard_map/reduce_scatter | solution.py:123
  228.3 157.8 %reduce-scatter.5.cloned.1.call-start = ((), (), s32[]{:S(2)}) async-start(), calls=%async_computation.6 | async-start | bytes 655360 | tf_op jit(solution)/shard_map/reduce_scatter | solution.py:126
Sparse Core Ops, SparseCore 0:
  231.6 25.2 reduce-scatter.2
  357.9 28.0 reduce-scatter.4
where the time goes:
time: 398 us; the launch traced here: 394 us
  waiting for transfers between devices  214 us (54%)
  other arithmetic  79.4 us (20%)
  starting transfers between devices  42 us (11%)
  local copies, waits for them, and re-layouts  18.5 us (5%)
  between operations  14.3 us (4%)
  blocking collectives  12.6 us (3%)
  matrix products  8.18 us (2%)
  loops' own time  5.71 us (1%)
    all_to_all x1, waiting for transfers between devices, per_device(): lax.all_to_all(outgoing.reshape(dp_count, capacity, token_count, features...  95.7 us
    all_to_all x1, waiting for transfers between devices, per_device(): lax.all_to_all(fetched.reshape(dp_count, capacity, token_count, features)...  83.2 us
    reduce_scatter x1, waiting for transfers between devices, per_device(): lax.psum_scatter(pool_part.astype(jnp.bfloat16), 'group', scatter_dimensi...  26.7 us
    scatter-add x1, other arithmetic, owner_sum(): return empty.at[target].add(flat_terms, mode='drop')  26.3 us
    all_to_all x1, starting transfers between devices, per_device(): lax.all_to_all(ask_rows, 'dp', split_axis=0, concat_axis=0, tiled=True)  17.8 us
    select_n x1, other arithmetic, request_layout(): jnp.where(filled, jnp.take(local_row, source, axis=0), -1)  17.5 us
    all_to_all x1, starting transfers between devices, per_device(): lax.all_to_all(outgoing.reshape(dp_count, capacity, token_count, features...  16.6 us
    all_gather x1, blocking collectives, per_device(): gathered = lax.all_gather(positive_unit, 'group', axis=0, tiled=True)  12.6 us
  transfers between devices with their start and end apart: 5, of which 4 were waited for; matrix products, arithmetic and copies ran while one was open for 10% of the time, Pallas kernels for 0%

commit v1 on v0

v1 whole, which is shorter than its diff:
```python
import jax
import jax.numpy as jnp
from jax import lax
from jax.experimental import pallas as pl
from jax.experimental.pallas import tpu as pltpu
from jax.sharding import Mesh, PartitionSpec as P

LINE = ("c", "y", "z")
N_Z, N_Y, N_C = 8, 8, 2
N_LINE = N_Z * N_Y * N_C
HALF = N_LINE // 2
QD, QT, PT, D, NEG, ROWS, GROUP = 4, 32, 64, 128, 7, 32, 4
QROWS = QD * QT
SENT = QROWS + 16
BATCH = QD * GROUP
VMEM = 48 * 1024 * 1024
F32, BF16, I32 = jnp.float32, jnp.bfloat16, jnp.int32
EXACT = lax.Precision.HIGHEST


def call(body, out_shape, in_specs, out_specs, scratch=()):
    return pl.pallas_call(
        body,
        out_shape=out_shape,
        in_specs=in_specs,
        out_specs=out_specs,
        scratch_shapes=list(scratch),
        compiler_params=pltpu.CompilerParams(vmem_limit_bytes=VMEM),
    )


def vmem():
    return pl.BlockSpec(memory_space=pltpu.VMEM)


def smem():
    return pl.BlockSpec(memory_space=pltpu.SMEM)


def unit(values):
    wide = values.astype(F32)
    return (wide * lax.rsqrt(jnp.sum(wide * wide, axis=-1, keepdims=True) + 1e-06)).astype(BF16)


def iota(shape, dim):
    return lax.broadcasted_iota(I32, shape, dim)


def dot(a, b, dims, precision=None):
    return lax.dot_general(a, b, ((dims[0], dims[1]), ((), ())), precision=precision, preferred_element_type=F32)


def token_sum_matrix():
    return (iota((QROWS, QROWS), 0) // QT == iota((QROWS, QROWS), 1) // QT).astype(F32)


def prepare(ids, storage, queries, positives, sent, pos_unit, slots, count):
    sent[0:QROWS, :] = unit(queries[...]).reshape(QROWS, D)
    pos_unit[...] = unit(positives[...])
    lane = iota((16, N_LINE), 1)
    sub = iota((16, N_LINE), 0)
    homes = []
    for q in range(QD):
        for k in range(NEG):
            home = storage[ids[q, k]]
            owner = home // ROWS
            line = (owner % 2) * HALF + ((owner // 2) % N_Y) * N_Z + owner // (2 * N_Y)
            count[line] = 0
            homes.append((line, q * ROWS + home % ROWS + 1))
    codes = jnp.zeros((16, N_LINE), F32)
    for p, (line, code) in enumerate(homes):
        rank = count[line]
        count[line] = rank + 1
        slots[p] = line * 2 + jnp.minimum(rank, 1)
        codes = jnp.where((lane == line) & (sub == rank), code.astype(F32), codes)
    sent[QROWS:SENT, :] = codes.astype(BF16)


def positive_scores(q_unit, gathered):
    cands = gathered[...].reshape(BATCH * PT, D)
    exp_scores = jnp.exp(10.0 * dot(cands, q_unit, ((1,), (1,)))).reshape(BATCH, PT, QROWS)
    total = jnp.sum(exp_scores, axis=1)
    score = 0.1 * dot(jnp.log(total), token_sum_matrix(), ((1,), (0,)), EXACT)
    return cands, exp_scores, total, score


def request(codes, line, slot):
    code = codes[line, slot]
    spot = jnp.maximum(code - 1, 0)
    return code > 0, spot // ROWS, spot % ROWS


def four(step):
    return ((step, 0), (step, 1), (step + HALF, 0), (step + HALF, 1))


def spread(packed):
    block = iota((PT, QROWS), 1) // QT
    return jnp.concatenate([jnp.where(block == b, packed, 0.0).astype(BF16) for b in range(4)], axis=0)


def query_tile(sent, line, q):
    return sent[pl.ds(pl.multiple_of(line * SENT + q * QT, 16), QT), :]


def serve(me, codes, sent, pool, own_sent, gathered, back, probs, sums, rows, exps, totals, marks, factor):
    rows[...] = unit(pool[...])
    lane = iota((1, QROWS), 1)
    block = iota((PT, QROWS), 1) // QT

    def score(step, carry):
        q_tiles, c_tiles = [], []
        mark = jnp.full((1, QROWS), -1.0, F32)
        for b, (line, slot) in enumerate(four(step)):
            valid, q, row = request(codes, line, slot)
            q_tiles.append(query_tile(sent, line, q))
            c_tiles.append(rows[row])
            mark = jnp.where((lane // QT == b) & valid, q.astype(F32), mark)
        full = dot(jnp.concatenate(c_tiles, axis=0), jnp.concatenate(q_tiles, axis=0), ((1,), (1,)))
        packed = full[0:PT]
        for b in range(1, 4):
            packed = jnp.where(block == b, full[b * PT : (b + 1) * PT], packed)
        exp_scores = jnp.exp(10.0 * packed)
        exps[step] = exp_scores
        totals[pl.ds(step, 1), :] = jnp.sum(exp_scores, axis=0, keepdims=True)
        marks[pl.ds(step, 1), :] = mark
        return carry

    lax.fori_loop(0, HALF, score, 0, unroll=4)

    total = totals[...]
    mark = marks[...]
    weight = jnp.exp(0.1 * dot(jnp.log(total), token_sum_matrix(), ((1,), (0,)), EXACT))
    weight = jnp.where(mark >= 0.0, weight, 0.0)
    factor[...] = weight / total

    first = iota((QROWS, N_LINE), 0)
    last = iota((QROWS, N_LINE), 1)
    pick = ((first % QT == 0) & (first // (2 * QT) == last // HALF)).astype(F32)
    diag = iota((HALF, N_LINE), 1) % HALF == iota((HALF, N_LINE), 0)
    q_unit = own_sent[0:QROWS, :]
    _, _, _, pos_score = positive_scores(q_unit, gathered)
    pos_weight = jnp.sum(jnp.exp(pos_score), axis=0, keepdims=True)
    parts = []
    for q in range(QD):
        of_query = dot(jnp.where(mark == float(q), weight, 0.0), pick, ((1,), (0,)), EXACT)
        part = jnp.sum(jnp.where(diag, of_query, 0.0), axis=0, keepdims=True)
        own = jnp.sum(jnp.where(lane == q * QT, pos_weight, 0.0), axis=1, keepdims=True)
        parts.append(part + jnp.where(iota((1, N_LINE), 1) == me[0], own, 0.0))
    sums[...] = jnp.broadcast_to(jnp.concatenate(parts, axis=0)[None], (N_LINE, QD, N_LINE))

    def terms(step, carry):
        packed = (exps[step] * factor[pl.ds(step, 1), :]).astype(BF16)
        probs[step] = packed
        c_tiles = [rows[request(codes, line, slot)[2]] for line, slot in four(step)]
        grads = dot(spread(packed.astype(F32)), jnp.concatenate(c_tiles, axis=0), ((0,), (0,))).astype(BF16)
        back[step] = grads[0 : 2 * QT].reshape(2, QT, D)
        back[step + HALF] = grads[2 * QT :].reshape(2, QT, D)
        return carry

    lax.fori_loop(0, HALF, terms, 0, unroll=4)


def weigh(me, codes, weight_sum, weight_inv, sent, probs, own_sent, gathered, out, query_part, losses, acc):
    acc[...] = jnp.zeros_like(acc)

    def add(step, carry):
        spots = [(line,) + request(codes, line, slot) for line, slot in four(step)]
        q_tiles = [query_tile(sent, line, q) for line, _, q, _ in spots]
        grads = dot(spread(probs[step].astype(F32)), jnp.concatenate(q_tiles, axis=0), ((1,), (0,)))
        for b, (line, _, q, row) in enumerate(spots):
            acc[row] += grads[b * PT : (b + 1) * PT] * weight_inv[q, line]
        return carry

    lax.fori_loop(0, HALF, add, 0, unroll=4)

    q_unit = own_sent[0:QROWS, :]
    cands, exp_scores, total, score = positive_scores(q_unit, gathered)
    lane = iota((1, QROWS), 1)
    own_sum = jnp.zeros((1, QROWS), F32)
    for q in range(QD):
        own_sum = jnp.where(lane // QT == q, weight_sum[q, me[0]], own_sum)
    own = (iota((BATCH, QROWS), 0) == me[1] * QD + iota((BATCH, QROWS), 1) // QT).astype(F32)
    score_grad = jnp.exp(score) / own_sum - own
    losses[...] = jnp.log(own_sum) - jnp.sum(score * own, axis=0, keepdims=True)
    weight_grad = (exp_scores * (score_grad / total)[:, None, :]).astype(BF16).reshape(BATCH * PT, QROWS)
    query_part[...] = dot(weight_grad, cands, ((0,), (0,)))
    pos_part = dot(weight_grad, q_unit, ((1,), (0,))).astype(BF16).reshape(BATCH, PT, D)
    share = ROWS // GROUP
    for g in range(GROUP):
        out[g, 0:QD] = pos_part[g * QD : (g + 1) * QD]
        out[g, QD:] = acc[g * share : (g + 1) * share].astype(BF16)


def collect(slots, weight_inv, me, query_part, arrived, out, tiles, sems):
    copies = [
        pltpu.make_async_copy(arrived.at[slots[p] // 2, slots[p] % 2], tiles.at[p], sems.at[p])
        for p in range(QD * NEG)
    ]
    for copy in copies:
        copy.start()
    for copy in copies:
        copy.wait()
    for q in range(QD):
        total = jnp.sum(tiles[q * NEG : (q + 1) * NEG].astype(F32), axis=0)
        out[q] = query_part[q * QT : (q + 1) * QT, :] + total * weight_inv[q, me[0]]


def per_device(queries, positives, passage_pool, negative_ids, storage_row):
    struct = jax.ShapeDtypeStruct
    me = jnp.stack([lax.axis_index(LINE), lax.axis_index("x")]).astype(I32)
    own_sent, pos_unit, slots = call(
        prepare,
        (struct((SENT, D), BF16), struct((QD, PT, D), BF16), struct((QD * NEG,), I32)),
        [smem(), smem(), vmem(), vmem()],
        (vmem(), vmem(), smem()),
        [pltpu.SMEM((N_LINE,), I32)],
    )(negative_ids, storage_row, queries, positives)

    sent = own_sent[None]
    for axis in ("z", "y", "c"):
        sent = lax.all_gather(sent, axis, axis=0, tiled=True)
    gathered = lax.all_gather(pos_unit, "x", axis=0, tiled=True)
    codes = lax.dynamic_index_in_dim(sent[:, QROWS : QROWS + 2, :], me[0], axis=2, keepdims=False).astype(I32)
    sent = sent.reshape(N_LINE * SENT, D)

    back, probs, sums = call(
        serve,
        (
            struct((N_LINE, 2, QT, D), BF16),
            struct((HALF, PT, QROWS), BF16),
            struct((N_LINE, QD, N_LINE), F32),
        ),
        [smem(), smem(), vmem(), vmem(), vmem(), vmem()],
        (vmem(), vmem(), vmem()),
        [
            pltpu.VMEM((ROWS, PT, D), BF16),
            pltpu.VMEM((HALF, PT, QROWS), F32),
            pltpu.VMEM((HALF, QROWS), F32),
            pltpu.VMEM((HALF, QROWS), F32),
            pltpu.VMEM((HALF, QROWS), F32),
        ],
    )(me, codes, sent, passage_pool, own_sent, gathered)

    sums_in = lax.all_to_all(sums, LINE, split_axis=0, concat_axis=0, tiled=True)
    arrived = lax.all_to_all(back, LINE, split_axis=0, concat_axis=0, tiled=True)
    weight_sum = jnp.sum(sums_in, axis=0)
    weight_inv = 1.0 / weight_sum

    parts, query_part, losses = call(
        weigh,
        (
            struct((GROUP, QD + ROWS // GROUP, PT, D), BF16),
            struct((QROWS, D), F32),
            struct((1, QROWS), F32),
        ),
        [smem(), smem(), smem(), smem(), vmem(), vmem(), vmem(), vmem()],
        (vmem(), vmem(), vmem()),
        [pltpu.VMEM((ROWS, PT, D), F32)],
    )(me, codes, weight_sum, weight_inv, sent, probs, own_sent, gathered)

    parts_in = lax.all_to_all(parts, "x", split_axis=0, concat_axis=0, tiled=True)
    total = jnp.sum(parts_in.astype(F32), axis=0)

    query_grad = call(
        collect,
        struct((QD, QT, D), F32),
        [smem(), smem(), smem(), vmem(), pl.BlockSpec(memory_space=pl.ANY)],
        vmem(),
        [pltpu.VMEM((QD * NEG, QT, D), BF16), pltpu.SemaphoreType.DMA((QD * NEG,))],
    )(slots, weight_inv, me, query_part, arrived)
    return losses.reshape(QD, QT)[:, 0], query_grad, total[:QD], total[QD:]


def solution(mesh):
    fine = Mesh(mesh.devices.reshape(N_Z, N_Y, N_C, GROUP), ("z", "y", "c", "x"))
    every, line = ("z", "y", "c", "x"), ("z", "y", "c")
    in_specs = (P(every), P(every), P(line), P(every), P())
    out_specs = (P(every), P(every), P(every), P(every))
    return jax.shard_map(per_device, mesh=fine, in_specs=in_specs, out_specs=out_specs, check_vma=False)
```

time: 398 us -> 293 us (0.74)
  waiting for transfers between devices: 214 us -> 132 us
  other arithmetic: 79.4 us -> 1.03 us
  blocking collectives: 12.6 us -> 88.5 us
  starting transfers between devices: 42 us -> 6.29 us
  Pallas kernels: 0 us -> 24.9 us
  matrix products: 8.18 us -> 0 us
  loops' own time: 5.71 us -> 0 us
    all_to_all x3 -> x1, waiting for transfers between devices: 187 us -> 51.9 us  [per_device(): lax.all_to_all(back, LINE, split_axis=0, concat_axis=0, tiled=True)]
    all_gather x0 -> x2, waiting for transfers between devices: none -> 79.9 us  [per_device(): sent = lax.all_gather(sent, axis, axis=0, tiled=True)]
    all_to_all x0 -> x2, blocking collectives: none -> 45 us  [the longest x1 30.5 us: per_device(): lax.all_to_all(sums, LINE, split_axis=0, concat_axis=0, tiled=True)]
    all_to_all x3 -> x1, starting transfers between devices: 41.9 us -> 6.21 us  [per_device(): lax.all_to_all(back, LINE, split_axis=0, concat_axis=0, tiled=True)]
    all_gather x1 -> x2, blocking collectives: 12.6 us -> 43.5 us  [the longest x1 31.2 us: per_device(): sent = lax.all_gather(sent, axis, axis=0, tiled=True)]
    reduce_scatter x2 -> x0, waiting for transfers between devices: 26.7 us -> none  [the longest x1 26.7 us: per_device(): lax.psum_scatter(pool_part.astype(jnp.bfloat16), 'group', scatter_dimensi...]
    scatter-add x1 -> x0, other arithmetic: 26.3 us -> none  [owner_sum(): return empty.at[target].add(flat_terms, mode='drop')]
    pallas_call x0 -> x4, Pallas kernels: none -> 24.9 us  [the longest x1 13 us: per_device(): call(serve, (struct((N_LINE, 2, QT, D), BF16), struct((HALF, PT, QROWS),...]
  transfers between devices with their start and end apart: 5 -> 3, of which waited for: 4 -> 3; matrix products, arithmetic and copies ran while one was open for 10% -> 1% of each run, Pallas kernels for 0% -> 0%
where the time goes in v1:
time: 293 us; the launch traced here: 289 us
  waiting for transfers between devices  132 us (45%)
  blocking collectives  88.5 us (30%)
  Pallas kernels  24.9 us (8%)
  local copies, waits for them, and re-layouts  22.4 us (8%)
  between operations  14.1 us (5%)
  starting transfers between devices  6.29 us (2%)
    all_gather x2, waiting for transfers between devices, per_device(): sent = lax.all_gather(sent, axis, axis=0, tiled=True)  79.9 us
    all_to_all x1, waiting for transfers between devices, per_device(): lax.all_to_all(back, LINE, split_axis=0, concat_axis=0, tiled=True)  51.9 us
    all_gather x1, blocking collectives, per_device(): sent = lax.all_gather(sent, axis, axis=0, tiled=True)  31.2 us
    all_to_all x1, blocking collectives, per_device(): lax.all_to_all(sums, LINE, split_axis=0, concat_axis=0, tiled=True)  30.5 us
    all_to_all x1, blocking collectives, per_device(): lax.all_to_all(parts, 'x', split_axis=0, concat_axis=0, tiled=True)  14.5 us
    all_gather x2, local copies, waits for them, and re-layouts, per_device(): sent = lax.all_gather(sent, axis, axis=0, tiled=True)  13.2 us
    pallas_call x1, Pallas kernels, per_device(): call(serve, (struct((N_LINE, 2, QT, D), BF16), struct((HALF, PT, QROWS),...  13 us
    all_gather x1, blocking collectives, per_device(): gathered = lax.all_gather(pos_unit, 'x', axis=0, tiled=True)  12.3 us
  transfers between devices with their start and end apart: 3, of which 3 were waited for; matrix products, arithmetic and copies ran while one was open for 1% of the time, Pallas kernels for 0%

profile of v1, /device:TPU:6, one launch (start us, length us, event | category | flops | bytes accessed | tf_op | source)
XLA Modules:
  0.0 289.1 jit_solution(1529024649253965756)
XLA Ops:
  7.2 0.0 all-gather.4.cloned.1.call-start
  7.2 0.0 copy-start.2
  7.2 0.8 copy-done.2
  8.1 0.0 copy-start.3
  8.1 0.8 copy-done.3
  8.8 0.0 copy-start.4
  8.8 0.7 copy-done.4
  9.5 0.0 copy-start.5
  9.5 0.7 copy-done.5
  10.2 2.0 shard_map.84
  12.3 31.2 %all-gather = bf16[1152,128]{1,0:T(8,128)(2,1)S(1)} all-gather(bf16[144,128]{1,0:T(8,128)(2,1)S(1)} %get-tuple-element.13.own_sent), channel_id=2, replica_groups=mesh['z'=8,'y'=8,'c'=2,'x'=4] {'z'}, dimensions={0}, use_global_device_ids=true | all-gather | bytes 331776 | tf_op jit(solution)/shard_map/all_gather | solution.py:222
  43.5 1.2 copy.13
  44.7 0.0 all-gather.4.cloned.1.call-update
  44.7 0.0 all-gather.6.cloned.1.call-start
  44.7 63.2 %all-gather.4.cloned.1.call-done = bf16[64,144,128]{1,0,2:T(8,128)(2,1)} async-done(((bf16[8,144,128]{1,0,2:T(8,128)(2,1)}), bf16[64,144,128]{1,0,2:T(8,128)(2,1)}) %all-gather.4.cloned.1.call-update) | async-done | bytes 2359312 | tf_op jit(solution)/shard_map/all_gather | solution.py:222
  108.0 0.0 all-gather.6.cloned.1.call-update
  108.0 12.3 %all_gather.15.gathered = bf16[16,64,128]{2,1,0:T(8,128)(2,1)S(1)} all-gather(bf16[4,64,128]{2,1,0:T(8,128)(2,1)S(1)} %get-tuple-element.14), channel_id=1, replica_groups=mesh['z'=8,'y'=8,'c'=2,'x'=4] {'x'}, dimensions={0}, use_global_device_ids=true | all-gather | bytes 327680 | tf_op jit(solution)/shard_map/all_gather | solution.py:223
  120.2 0.1 pad_add_fusion.me
  120.3 16.7 %all-gather.6.cloned.1.call-done = bf16[128,144,128]{1,0,2:T(8,128)(2,1)} async-done(((bf16[64,144,128]{1,0,2:T(8,128)(2,1)}), bf16[128,144,128]{1,0,2:T(8,128)(2,1)}) %all-gather.6.cloned.1.call-update) | async-done | bytes 4718608 | tf_op jit(solution)/shard_map/all_gather | solution.py:222
  137.0 0.0 slice-start
  137.0 2.2 slice-done
  139.2 0.0 copy-start.1
  139.3 12.0 %copy.14 = bf16[128,144,128]{2,1,0:T(8,128)(2,1)} copy(bf16[128,144,128]{1,0,2:T(8,128)(2,1)} %all-gather.6.cloned.1.call-done) | data formatting | bytes 9437184 | tf_op jit(solution)/shard_map/all_gather | solution.py:222
  151.3 0.0 copy-done.1
  151.3 13.0 %shard_map.85 = (bf16[128,2,32,128]{3,2,1,0:T(8,128)(2,1)S(1)}, bf16[64,64,128]{2,1,0:T(8,128)(2,1)S(1)}, f32[128,4,128]{2,1,0:T(4,128)S(1)}) custom-call(s32[2]{0:T(128)S(1)} %pad_add_fusion.me, s32[128,2]{1,0:T(8,128)S(1)} %bitcast_convert_fusion.codes, bf16[18432,128]{1,0:T(8,128)(2,1)} %bitcast.7, bf16[32,64,128]{2,1,0:T(8,128)(2,1)S(1)} %copy-done.1, ...), custom_call_target="tpu_custom_call" | custom-call | tf_op jit(solution)/shard_map/pallas_call | solution.py:227
  164.3 0.0 copy-start
  164.3 1.3 copy-done
  165.6 30.5 %all_to_all.15 = f32[128,4,128]{2,1,0:T(4,128)S(1)} all-to-all(f32[128,4,128]{2,1,0:T(4,128)S(1)} %get-tuple-element.15), channel_id=1, replica_groups=mesh['z'=8,'y'=8,'c'=2,'x'=4] {'c','y','z'}, dimensions={0} | all-to-all | bytes 524288 | tf_op jit(solution)/shard_map/all_to_all | solution.py:245
  196.2 0.1 reduce_sum.18.weight_sum
  196.3 7.8 %shard_map.86 = (bf16[4,12,64,128]{3,2,1,0:T(8,128)(2,1)S(1)}, f32[128,128]{1,0:T(8,128)S(1)}, f32[1,128]{1,0:T(1,128)S(1)}) custom-call(s32[2]{0:T(128)S(1)} %pad_add_fusion.me, s32[128,2]{1,0:T(8,128)S(1)} %bitcast_convert_fusion.codes, f32[4,128]{1,0:T(4,128)S(1)} %reduce_sum.18.weight_sum, f32[4,128]{1,0:T(4,128)S(1)} %broadcast_divide_fusion.weight_inv, ...), custom_call_target="tpu_custom_call" | custom-call | tf_op jit(solution)/shard_map/pallas_call | solution.py:250
  204.1 14.5 %all_to_all.16 = bf16[4,12,64,128]{3,2,1,0:T(8,128)(2,1)S(1)} all-to-all(bf16[4,12,64,128]{3,2,1,0:T(8,128)(2,1)S(1)} %get-tuple-element.21), channel_id=1, replica_groups=mesh['z'=8,'y'=8,'c'=2,'x'=4] {'x'}, dimensions={0} | all-to-all | bytes 1572864 | tf_op jit(solution)/shard_map/all_to_all | solution.py:262
  218.6 6.2 %all-to-all-start.1 = ((bf16[128,2,32,128]{3,2,1,0:T(8,128)(2,1)}), bf16[128,2,32,128]{3,2,1,0:T(8,128)(2,1)S(1)}, u32[]{:S(2)}, u32[]{:S(2)}) async-start(bf16[128,2,32,128]{3,2,1,0:T(8,128)(2,1)} %copy-done), calls=%async_computation.1 | async-start | bytes 4194304 | tf_op jit(solution)/shard_map/all_to_all | solution.py:246
  224.8 0.5 broadcast.4
  225.3 0.7 reduce.5
  226.0 0.1 reshape.17
  226.1 0.6 slice_reduce_fusion
  226.7 0.1 convert_reduce_fusion
  226.8 0.7 slice.18
  227.5 0.7 slice.17
  228.2 51.9 %all-to-all-done.1.arrived = bf16[128,2,32,128]{3,2,1,0:T(8,128)(2,1)S(1)} async-done(((bf16[128,2,32,128]{3,2,1,0:T(8,128)(2,1)}), bf16[128,2,32,128]{3,2,1,0:T(8,128)(2,1)S(1)}, u32[]{:S(2)}, u32[]{:S(2)}) %all-to-all-start.1) | async-done | bytes 2097184 | tf_op jit(solution)/shard_map/all_to_all | solution.py:246
  280.1 2.1 shard_map.87
  (2 shorter events, 0.0 us)
Async XLA Ops:
  7.2 100.8 %all-gather.4.cloned.1.call-start = ((), (), s32[]{:S(2)}) async-start(), calls=%async_computation.3 | async-start | bytes 4718592 | tf_op jit(solution)/shard_map/all_gather | solution.py:222
  7.2 0.8 copy-start.2
  8.1 0.8 copy-start.3
  8.8 0.7 copy-start.4
  9.5 0.7 copy-start.5
  44.7 92.4 %all-gather.6.cloned.1.call-start = ((), (), s32[]{:S(2)}) async-start(), calls=%async_computation.4 | async-start | bytes 12582912 | tf_op jit(solution)/shard_map/all_gather | solution.py:222
  137.0 2.2 slice-start
  139.2 12.1 %copy-start.1 = (bf16[32,64,128]{2,1,0:T(8,128)(2,1)S(1)}, bf16[32,64,128]{2,1,0:T(8,128)(2,1)}, u32[]{:S(2)}) copy-start(bf16[32,64,128]{2,1,0:T(8,128)(2,1)} %pool.1) | copy-start | bytes 1572868
  164.3 1.3 copy-start
  218.6 61.5 %all-to-all-start.1 = ((bf16[128,2,32,128]{3,2,1,0:T(8,128)(2,1)}), bf16[128,2,32,128]{3,2,1,0:T(8,128)(2,1)S(1)}, u32[]{:S(2)}, u32[]{:S(2)}) async-start(bf16[128,2,32,128]{3,2,1,0:T(8,128)(2,1)} %copy-done), calls=%async_computation.1 | async-start | bytes 4194304 | tf_op jit(solution)/shard_map/all_to_all | solution.py:246
Sparse Core Ops, SparseCore 0:
  44.8 63.1 all-gather.3
  110.0 26.9 all-gather.5

commit v2 on v1

--- a/solution.py
+++ b/solution.py
@@ -11,7 +11,7 @@
 HALF = N_LINE // 2
 QD, QT, PT, D, NEG, ROWS, GROUP = 4, 32, 64, 128, 7, 32, 4
 QROWS = QD * QT
-SENT = QROWS + 16
+SENT = 2 * QT + 8
 BATCH = QD * GROUP
 VMEM = 48 * 1024 * 1024
 F32, BF16, I32 = jnp.float32, jnp.bfloat16, jnp.int32
@@ -54,11 +54,10 @@
     return (iota((QROWS, QROWS), 0) // QT == iota((QROWS, QROWS), 1) // QT).astype(F32)
 
 
-def prepare(ids, storage, queries, positives, sent, pos_unit, slots, count):
-    sent[0:QROWS, :] = unit(queries[...]).reshape(QROWS, D)
+def prepare(ids, storage, queries, positives, sent, q_unit, pos_unit, slots, count):
+    q_unit[...] = unit(queries[...])
     pos_unit[...] = unit(positives[...])
-    lane = iota((16, N_LINE), 1)
-    sub = iota((16, N_LINE), 0)
+    sent[...] = jnp.zeros_like(sent)
     homes = []
     for q in range(QD):
         for k in range(NEG):
@@ -66,14 +65,15 @@
             owner = home // ROWS
             line = (owner % 2) * HALF + ((owner // 2) % N_Y) * N_Z + owner // (2 * N_Y)
             count[line] = 0
-            homes.append((line, q * ROWS + home % ROWS + 1))
-    codes = jnp.zeros((16, N_LINE), F32)
-    for p, (line, code) in enumerate(homes):
-        rank = count[line]
+            homes.append((line, q, q * ROWS + home % ROWS + 1))
+    sub = iota((8, D), 0)
+    for p, (line, q, code) in enumerate(homes):
+        rank = jnp.minimum(count[line], 1)
         count[line] = rank + 1
-        slots[p] = line * 2 + jnp.minimum(rank, 1)
-        codes = jnp.where((lane == line) & (sub == rank), code.astype(F32), codes)
-    sent[QROWS:SENT, :] = codes.astype(BF16)
+        slots[p] = line * 2 + rank
+        sent[line, pl.ds(pl.multiple_of(rank * QT, QT), QT), :] = q_unit[q]
+        marks = sent[line, 2 * QT : SENT, :].astype(F32)
+        sent[line, 2 * QT : SENT, :] = jnp.where(sub == rank, code.astype(F32), marks).astype(BF16)
 
 
 def positive_scores(q_unit, gathered):
@@ -99,24 +99,23 @@
     return jnp.concatenate([jnp.where(block == b, packed, 0.0).astype(BF16) for b in range(4)], axis=0)
 
 
-def query_tile(sent, line, q):
-    return sent[pl.ds(pl.multiple_of(line * SENT + q * QT, 16), QT), :]
-
-
-def serve(me, codes, sent, pool, own_sent, gathered, back, probs, sums, rows, exps, totals, marks, factor):
+def query_tiles(sent, step):
+    return jnp.concatenate([sent[step, 0 : 2 * QT], sent[step + HALF, 0 : 2 * QT]], axis=0)
+
+
+def serve(me, codes, sent, pool, own_queries, gathered, back, probs, sums, rows, exps, totals, marks, factor):
     rows[...] = unit(pool[...])
     lane = iota((1, QROWS), 1)
     block = iota((PT, QROWS), 1) // QT
 
     def score(step, carry):
-        q_tiles, c_tiles = [], []
+        c_tiles = []
         mark = jnp.full((1, QROWS), -1.0, F32)
         for b, (line, slot) in enumerate(four(step)):
             valid, q, row = request(codes, line, slot)
-            q_tiles.append(query_tile(sent, line, q))
             c_tiles.append(rows[row])
             mark = jnp.where((lane // QT == b) & valid, q.astype(F32), mark)
-        full = dot(jnp.concatenate(c_tiles, axis=0), jnp.concatenate(q_tiles, axis=0), ((1,), (1,)))
+        full = dot(jnp.concatenate(c_tiles, axis=0), query_tiles(sent, step), ((1,), (1,)))
         packed = full[0:PT]
         for b in range(1, 4):
             packed = jnp.where(block == b, full[b * PT : (b + 1) * PT], packed)
@@ -138,7 +137,7 @@
     last = iota((QROWS, N_LINE), 1)
     pick = ((first % QT == 0) & (first // (2 * QT) == last // HALF)).astype(F32)
     diag = iota((HALF, N_LINE), 1) % HALF == iota((HALF, N_LINE), 0)
-    q_unit = own_sent[0:QROWS, :]
+    q_unit = own_queries[...].reshape(QROWS, D)
     _, _, _, pos_score = positive_scores(q_unit, gathered)
     pos_weight = jnp.sum(jnp.exp(pos_score), axis=0, keepdims=True)
     parts = []
@@ -147,7 +146,7 @@
         part = jnp.sum(jnp.where(diag, of_query, 0.0), axis=0, keepdims=True)
         own = jnp.sum(jnp.where(lane == q * QT, pos_weight, 0.0), axis=1, keepdims=True)
         parts.append(part + jnp.where(iota((1, N_LINE), 1) == me[0], own, 0.0))
-    sums[...] = jnp.broadcast_to(jnp.concatenate(parts, axis=0)[None], (N_LINE, QD, N_LINE))
+    sums[...] = jnp.concatenate(parts, axis=0)
 
     def terms(step, carry):
         packed = (exps[step] * factor[pl.ds(step, 1), :]).astype(BF16)
@@ -161,20 +160,19 @@
     lax.fori_loop(0, HALF, terms, 0, unroll=4)
 
 
-def weigh(me, codes, weight_sum, weight_inv, sent, probs, own_sent, gathered, out, query_part, losses, acc):
+def weigh(me, codes, weight_sum, weight_inv, sent, probs, own_queries, gathered, kept, off1, off2, off3, query_part, losses, acc, pos_acc):
     acc[...] = jnp.zeros_like(acc)
 
     def add(step, carry):
         spots = [(line,) + request(codes, line, slot) for line, slot in four(step)]
-        q_tiles = [query_tile(sent, line, q) for line, _, q, _ in spots]
-        grads = dot(spread(probs[step].astype(F32)), jnp.concatenate(q_tiles, axis=0), ((1,), (0,)))
+        grads = dot(spread(probs[step].astype(F32)), query_tiles(sent, step), ((1,), (0,)))
         for b, (line, _, q, row) in enumerate(spots):
             acc[row] += grads[b * PT : (b + 1) * PT] * weight_inv[q, line]
         return carry
 
     lax.fori_loop(0, HALF, add, 0, unroll=4)
 
-    q_unit = own_sent[0:QROWS, :]
+    q_unit = own_queries[...].reshape(QROWS, D)
     cands, exp_scores, total, score = positive_scores(q_unit, gathered)
     lane = iota((1, QROWS), 1)
     own_sum = jnp.zeros((1, QROWS), F32)
@@ -185,11 +183,12 @@
     losses[...] = jnp.log(own_sum) - jnp.sum(score * own, axis=0, keepdims=True)
     weight_grad = (exp_scores * (score_grad / total)[:, None, :]).astype(BF16).reshape(BATCH * PT, QROWS)
     query_part[...] = dot(weight_grad, cands, ((0,), (0,)))
-    pos_part = dot(weight_grad, q_unit, ((1,), (0,))).astype(BF16).reshape(BATCH, PT, D)
+    pos_acc[...] = dot(weight_grad, q_unit, ((1,), (0,))).reshape(BATCH, PT, D)
     share = ROWS // GROUP
-    for g in range(GROUP):
-        out[g, 0:QD] = pos_part[g * QD : (g + 1) * QD]
-        out[g, QD:] = acc[g * share : (g + 1) * share].astype(BF16)
+    for ahead, out in enumerate((kept, off1, off2, off3)):
+        g = (me[1] + ahead) % GROUP
+        out[0:QD] = pos_acc[pl.ds(g * QD, QD)].astype(out.dtype)
+        out[QD:] = acc[pl.ds(g * share, share)].astype(out.dtype)
 
 
 def collect(slots, weight_inv, me, query_part, arrived, out, tiles, sems):
@@ -209,27 +208,29 @@
 def per_device(queries, positives, passage_pool, negative_ids, storage_row):
     struct = jax.ShapeDtypeStruct
     me = jnp.stack([lax.axis_index(LINE), lax.axis_index("x")]).astype(I32)
-    own_sent, pos_unit, slots = call(
+    sent, q_unit, pos_unit, slots = call(
         prepare,
-        (struct((SENT, D), BF16), struct((QD, PT, D), BF16), struct((QD * NEG,), I32)),
+        (
+            struct((N_LINE, SENT, D), BF16),
+            struct((QD, QT, D), BF16),
+            struct((QD, PT, D), BF16),
+            struct((QD * NEG,), I32),
+        ),
         [smem(), smem(), vmem(), vmem()],
-        (vmem(), vmem(), smem()),
+        (vmem(), vmem(), vmem(), smem()),
         [pltpu.SMEM((N_LINE,), I32)],
     )(negative_ids, storage_row, queries, positives)
 
-    sent = own_sent[None]
-    for axis in ("z", "y", "c"):
-        sent = lax.all_gather(sent, axis, axis=0, tiled=True)
+    asked = lax.all_to_all(sent, LINE, split_axis=0, concat_axis=0, tiled=True)
     gathered = lax.all_gather(pos_unit, "x", axis=0, tiled=True)
-    codes = lax.dynamic_index_in_dim(sent[:, QROWS : QROWS + 2, :], me[0], axis=2, keepdims=False).astype(I32)
-    sent = sent.reshape(N_LINE * SENT, D)
+    codes = asked[:, 2 * QT : 2 * QT + 2, 0].astype(I32)
 
     back, probs, sums = call(
         serve,
         (
             struct((N_LINE, 2, QT, D), BF16),
             struct((HALF, PT, QROWS), BF16),
-            struct((N_LINE, QD, N_LINE), F32),
+            struct((QD, N_LINE), F32),
         ),
         [smem(), smem(), vmem(), vmem(), vmem(), vmem()],
         (vmem(), vmem(), vmem()),
@@ -240,27 +241,34 @@
             pltpu.VMEM((HALF, QROWS), F32),
             pltpu.VMEM((HALF, QROWS), F32),
         ],
-    )(me, codes, sent, passage_pool, own_sent, gathered)
-
-    sums_in = lax.all_to_all(sums, LINE, split_axis=0, concat_axis=0, tiled=True)
+    )(me, codes, asked, passage_pool, q_unit, gathered)
+
     arrived = lax.all_to_all(back, LINE, split_axis=0, concat_axis=0, tiled=True)
-    weight_sum = jnp.sum(sums_in, axis=0)
+    weight_sum = sums
+    for axis in ("z", "y", "c"):
+        weight_sum = jnp.sum(lax.all_gather(weight_sum, axis, axis=0), axis=0)
     weight_inv = 1.0 / weight_sum
 
-    parts, query_part, losses = call(
+    block = (QD + ROWS // GROUP, PT, D)
+    kept, off1, off2, off3, query_part, losses = call(
         weigh,
         (
-            struct((GROUP, QD + ROWS // GROUP, PT, D), BF16),
+            struct(block, F32),
+            struct(block, BF16),
+            struct(block, BF16),
+            struct(block, BF16),
             struct((QROWS, D), F32),
             struct((1, QROWS), F32),
         ),
         [smem(), smem(), smem(), smem(), vmem(), vmem(), vmem(), vmem()],
-        (vmem(), vmem(), vmem()),
-        [pltpu.VMEM((ROWS, PT, D), F32)],
-    )(me, codes, weight_sum, weight_inv, sent, probs, own_sent, gathered)
-
-    parts_in = lax.all_to_all(parts, "x", split_axis=0, concat_axis=0, tiled=True)
-    total = jnp.sum(parts_in.astype(F32), axis=0)
+        (vmem(),) * 6,
+        [pltpu.VMEM((ROWS, PT, D), F32), pltpu.VMEM((BATCH, PT, D), F32)],
+    )(me, codes, weight_sum, weight_inv, asked, probs, q_unit, gathered)
+
+    total = kept
+    for ahead, part in ((1, off1), (2, off2), (3, off3)):
+        moved = lax.ppermute(part, "x", [(g, (g + ahead) % GROUP) for g in range(GROUP)])
+        total = total + moved.astype(F32)
 
     query_grad = call(
         collect,

time: 293 us -> 242 us (0.83)
  waiting for transfers between devices: 132 us -> 57.8 us
  starting transfers between devices: 6.29 us -> 38.4 us
  blocking collectives: 88.5 us -> 106 us
  between operations: 14.1 us -> 0.77 us
  local copies, waits for them, and re-layouts: 22.4 us -> 11.8 us
    all_gather x2 -> x0, waiting for transfers between devices: 79.9 us -> none  [per_device(): sent = lax.all_gather(sent, axis, axis=0, tiled=True)]
    all_gather x1 -> x3, blocking collectives: 31.2 us -> 93.8 us  [per_device(): weight_sum = jnp.sum(lax.all_gather(weight_sum, axis, axis=0), axis=0)]
    all_to_all x1, waiting for transfers between devices: 51.9 us -> 0.01 us  [per_device(): lax.all_to_all(back, LINE, split_axis=0, concat_axis=0, tiled=True)]
    all_to_all x0 -> x1, waiting for transfers between devices: none -> 51.3 us  [per_device(): asked = lax.all_to_all(sent, LINE, split_axis=0, concat_axis=0, tiled=True)]
    all_to_all x2 -> x0, blocking collectives: 45 us -> none  [the longest x1 30.5 us: per_device(): lax.all_to_all(sums, LINE, split_axis=0, concat_axis=0, tiled=True)]
    all_to_all x0 -> x1, starting transfers between devices: none -> 17.9 us  [per_device(): asked = lax.all_to_all(sent, LINE, split_axis=0, concat_axis=0, tiled=True)]
    all_gather x2 -> x0, local copies, waits for them, and re-layouts: 13.2 us -> none  [per_device(): sent = lax.all_gather(sent, axis, axis=0, tiled=True)]
    ppermute x0 -> x3, starting transfers between devices: none -> 8.62 us  [per_device(): lax.ppermute(part, 'x', [(g, (g + ahead) % GROUP) for g in range(GROUP)])]
  transfers between devices with their start and end apart: 3 -> 5, of which waited for: 3 -> 3; matrix products, arithmetic and copies ran while one was open for 1% -> 1% of each run, Pallas kernels for 0% -> 3%
where the time goes in v2:
time: 242 us; the launch traced here: 240 us
  blocking collectives  106 us (44%)
  waiting for transfers between devices  57.8 us (24%)
  starting transfers between devices  38.4 us (16%)
  Pallas kernels  24 us (10%)
  local copies, waits for them, and re-layouts  11.8 us (5%)
    all_gather x3, blocking collectives, per_device(): weight_sum = jnp.sum(lax.all_gather(weight_sum, axis, axis=0), axis=0)  93.8 us
    all_to_all x1, waiting for transfers between devices, per_device(): asked = lax.all_to_all(sent, LINE, split_axis=0, concat_axis=0, tiled=True)  51.3 us
    all_to_all x1, starting transfers between devices, per_device(): asked = lax.all_to_all(sent, LINE, split_axis=0, concat_axis=0, tiled=True)  17.9 us
    all_gather x1, blocking collectives, per_device(): gathered = lax.all_gather(pos_unit, 'x', axis=0, tiled=True)  12.3 us
    all_to_all x1, starting transfers between devices, per_device(): lax.all_to_all(back, LINE, split_axis=0, concat_axis=0, tiled=True)  11.8 us
    pallas_call x1, Pallas kernels, per_device(): call(serve, (struct((N_LINE, 2, QT, D), BF16), struct((HALF, PT, QROWS),...  11.6 us
    unnamed x22, local copies, waits for them, and re-layouts  9.03 us
    ppermute x3, starting transfers between devices, per_device(): lax.ppermute(part, 'x', [(g, (g + ahead) % GROUP) for g in range(GROUP)])  8.62 us
  transfers between devices with their start and end apart: 5, of which 3 were waited for; matrix products, arithmetic and copies ran while one was open for 1% of the time, Pallas kernels for 3%

profile of v2, /device:TPU:6, one launch (start us, length us, event | category | flops | bytes accessed | tf_op | source)
XLA Modules:
  0.0 239.8 jit_solution(2310755711550711833)
XLA Ops:
  0.6 0.0 copy-start.7
  0.6 0.8 copy-done.7
  1.5 0.0 copy-start.8
  1.5 0.8 copy-done.8
  2.2 0.0 copy-start.9
  2.2 0.7 copy-done.9
  2.9 0.0 copy-start.10
  3.0 0.7 copy-done.10
  3.6 2.4 shard_map.84
  6.0 0.0 copy-start.2
  6.0 1.4 copy-done.2
  7.4 0.0 copy-start.6
  7.4 17.9 %all-to-all-start = ((bf16[128,72,128]{2,1,0:T(8,128)(2,1)}), bf16[128,72,128]{2,1,0:T(8,128)(2,1)S(1)}, u32[]{:S(2)}, u32[]{:S(2)}) async-start(bf16[128,72,128]{2,1,0:T(8,128)(2,1)} %copy-done.2), calls=%async_computation | async-start | bytes 4718592 | tf_op jit(solution)/shard_map/all_to_all | solution.py:224
  25.4 12.3 %all_gather.21.gathered = bf16[16,64,128]{2,1,0:T(8,128)(2,1)S(1)} all-gather(bf16[4,64,128]{2,1,0:T(8,128)(2,1)S(1)} %get-tuple-element.19), channel_id=1, replica_groups=mesh['z'=8,'y'=8,'c'=2,'x'=4] {'x'}, dimensions={0}, use_global_device_ids=true | all-gather | bytes 327680 | tf_op jit(solution)/shard_map/all_gather | solution.py:225
  37.7 0.1 pad_add_fusion.me
  37.8 51.3 %all-to-all-done.sent = bf16[128,72,128]{2,1,0:T(8,128)(2,1)S(1)} async-done(((bf16[128,72,128]{2,1,0:T(8,128)(2,1)}), bf16[128,72,128]{2,1,0:T(8,128)(2,1)S(1)}, u32[]{:S(2)}, u32[]{:S(2)}) %all-to-all-start) | async-done | bytes 2359328 | tf_op jit(solution)/shard_map/all_to_all | solution.py:224
  89.1 0.0 copy-start
  89.1 0.1 slice_convert_fusion
  89.2 0.1 copy.15
  89.2 0.1 copy.17.codes
  89.4 1.1 copy-done
  90.5 0.0 copy-done.6
  90.5 11.6 %shard_map.85 = (bf16[128,2,32,128]{3,2,1,0:T(8,128)(2,1)S(1)}, bf16[64,64,128]{2,1,0:T(8,128)(2,1)S(1)}, f32[4,128]{1,0:T(4,128)S(1)}) custom-call(s32[2]{0:T(128)S(1)} %pad_add_fusion.me, s32[128,2]{1,0:T(8,128)S(1)} %copy.17.codes, bf16[128,72,128]{2,1,0:T(8,128)(2,1)} %copy-done, bf16[32,64,128]{2,1,0:T(8,128)(2,1)S(1)} %copy-done.6, ...), custom_call_target="tpu_custom_call" | custom-call | tf_op jit(solution)/shard_map/pallas_call | solution.py:228
  102.1 0.0 copy-start.3
  102.2 1.3 copy-done.3
  103.4 0.0 copy-start.4
  103.4 1.0 copy-done.4
  104.4 0.0 copy-start.1
  104.4 11.8 %all-to-all-start.1 = ((bf16[128,2,32,128]{3,2,1,0:T(8,128)(2,1)}), bf16[128,2,32,128]{3,2,1,0:T(8,128)(2,1)}, u32[]{:S(2)}, u32[]{:S(2)}) async-start(bf16[128,2,32,128]{3,2,1,0:T(8,128)(2,1)} %copy-done.3), calls=%async_computation.1 | async-start | bytes 4194304 | tf_op jit(solution)/shard_map/all_to_all | solution.py:246
  116.3 65.3 %all-gather.3 = f32[8,4,128]{2,1,0:T(4,128)S(1)} all-gather(f32[1,4,128]{2,1,0:T(4,128)S(1)} %bitcast.6), channel_id=2, replica_groups=mesh['z'=8,'y'=8,'c'=2,'x'=4] {'z'}, dimensions={0}, use_global_device_ids=true | all-gather | bytes 18432 | tf_op jit(solution)/shard_map/all_gather | solution.py:249
  181.6 26.7 %all-gather.4 = f32[8,4,128]{2,1,0:T(4,128)S(1)} all-gather(f32[1,4,128]{2,1,0:T(4,128)S(1)} %bitcast.7), channel_id=3, replica_groups=mesh['z'=8,'y'=8,'c'=2,'x'=4] {'y'}, dimensions={0}, use_global_device_ids=true | all-gather | bytes 18432 | tf_op jit(solution)/shard_map/all_gather | solution.py:249
  208.3 1.8 all-gather.5
  210.1 0.0 copy-done.1
  210.1 0.0 copy-start.5
  210.1 1.2 copy-done.5
  211.3 7.5 %shard_map.86 = (f32[12,64,128]{2,1,0:T(8,128)S(1)}, bf16[12,64,128]{2,1,0:T(8,128)(2,1)}, bf16[12,64,128]{2,1,0:T(8,128)(2,1)}, bf16[12,64,128]{2,1,0:T(8,128)(...) custom-call(s32[2]{0:T(128)S(1)} %pad_add_fusion.me, s32[128,2]{1,0:T(8,128)S(1)} %copy.17.codes, ...), custom_call_target="tpu_custom_call" | custom-call | tf_op jit(solution)/shard_map/pallas_call | solution.py:253
  218.8 2.4 collective-permute-start
  221.2 4.3 %collective-permute-start.1 = (bf16[12,64,128]{2,1,0:T(8,128)(2,1)}, bf16[12,64,128]{2,1,0:T(8,128)(2,1)S(1)}, u32[]{:S(2)}, u32[]{:S(2)}) collective-permute-start(bf16[12,64,128]{2,1,0:T(8,128)(2,1)} %get-tuple-element.28), channel_id=1, source_target_pairs={{0,2},{1,3},{2,0},{3,1},{4,6},{5,7},{6,4},{7,5},{8,10},{9,11},{10,... | collective-permute-start | bytes 589832 | tf_op jit(solution)/shard_map/ppermute | solution.py:270
  225.5 1.9 collective-permute-start.2
  227.5 0.5 broadcast.4
  228.0 0.7 reduce.8
  228.7 0.1 reshape.13
  228.7 0.6 slice_reduce_fusion
  229.4 0.0 collective-permute-done
  229.4 2.8 %collective-permute-done.1 = bf16[12,64,128]{2,1,0:T(8,128)(2,1)S(1)} collective-permute-done((bf16[12,64,128]{2,1,0:T(8,128)(2,1)}, bf16[12,64,128]{2,1,0:T(8,128)(2,1)S(1)}, u32[]{:S(2)}, u32[]{:S(2)}) %collective-permute-start.1) | collective-permute-done | bytes 196640 | tf_op jit(solution)/shard_map/ppermute | solution.py:270
  232.1 3.7 %collective-permute-done.2 = bf16[12,64,128]{2,1,0:T(8,128)(2,1)S(1)} collective-permute-done((bf16[12,64,128]{2,1,0:T(8,128)(2,1)S(1)}, bf16[12,64,128]{2,1,0:T(8,128)(2,1)S(1)}, u32[]{:S(2)}, u32[]{:S(2)}) %collective-permute-start.2) | collective-permute-done | bytes 196640 | tf_op jit(solution)/shard_map/ppermute | solution.py:270
  235.8 0.1 convert_add_fusion
  235.9 0.7 slice.18
  236.6 0.7 slice.17
  237.3 0.0 all-to-all-done.1.arrived
  237.3 2.5 %shard_map.87 = f32[4,32,128]{2,1,0:T(8,128)} custom-call(s32[28]{0:T(128)S(1)} %get-tuple-element.23.slots, f32[4,128]{1,0:T(4,128)S(1)} %broadcast_divide_fusion.weight_inv, s32[2]{0:T(128)S(1)} %pad_add_fusion.me, f32[128,128]{1,0:T(8,128)S(1)} %get-tuple-element.24.query_part, bf16[128,2,32,128]{3,2,1,0:T(8,128)(2,1)} %all-to-all-done.1.arrived), custom_call_target="tpu_custom_call" | custom-call | tf_op jit(solution)/shard_map/pallas_call | solution.py:273
  (4 shorter events, 0.1 us)
Async XLA Ops:
  0.6 0.8 copy-start.7
  1.5 0.8 copy-start.8
  2.2 0.7 copy-start.9
  2.9 0.7 copy-start.10
  6.0 1.4 copy-start.2
  7.4 83.1 %copy-start.6 = (bf16[32,64,128]{2,1,0:T(8,128)(2,1)S(1)}, bf16[32,64,128]{2,1,0:T(8,128)(2,1)}, u32[]{:S(2)}) copy-start(bf16[32,64,128]{2,1,0:T(8,128)(2,1)} %pool.1) | copy-start | bytes 1572868
  7.4 81.7 %all-to-all-start = ((bf16[128,72,128]{2,1,0:T(8,128)(2,1)}), bf16[128,72,128]{2,1,0:T(8,128)(2,1)S(1)}, u32[]{:S(2)}, u32[]{:S(2)}) async-start(bf16[128,72,128]{2,1,0:T(8,128)(2,1)} %copy-done.2), calls=%async_computation | async-start | bytes 4718592 | tf_op jit(solution)/shard_map/all_to_all | solution.py:224
  89.1 1.4 copy-start
  102.1 1.3 copy-start.3
  103.4 1.0 copy-start.4
  104.4 105.7 %copy-start.1 = (bf16[128,72,128]{2,1,0:T(8,128)(2,1)S(1)}, bf16[128,72,128]{2,1,0:T(8,128)(2,1)}, u32[]{:S(2)}) copy-start(bf16[128,72,128]{2,1,0:T(8,128)(2,1)} %copy-done) | copy-start | bytes 7077892
  104.4 132.9 %all-to-all-start.1 = ((bf16[128,2,32,128]{3,2,1,0:T(8,128)(2,1)}), bf16[128,2,32,128]{3,2,1,0:T(8,128)(2,1)}, u32[]{:S(2)}, u32[]{:S(2)}) async-start(bf16[128,2,32,128]{3,2,1,0:T(8,128)(2,1)} %copy-done.3), calls=%async_computation.1 | async-start | bytes 4194304 | tf_op jit(solution)/shard_map/all_to_all | solution.py:246
  210.1 1.2 copy-start.5
  218.8 10.5 %collective-permute-start = (bf16[12,64,128]{2,1,0:T(8,128)(2,1)}, bf16[12,64,128]{2,1,0:T(8,128)(2,1)S(1)}, u32[]{:S(2)}, u32[]{:S(2)}) collective-permute-start(bf16[12,64,128]{2,1,0:T(8,128)(2,1)} %get-tuple-element.27), channel_id=1, source_target_pairs={{0,1},{1,2},{2,3},{3,0},{4,5},{5,6},{6,7},{7,4},{8,9},{9,10},{10,1... | collective-permute-start | bytes 589832 | tf_op jit(solution)/shard_map/ppermute | solution.py:270
  221.2 10.9 %collective-permute-start.1 = (bf16[12,64,128]{2,1,0:T(8,128)(2,1)}, bf16[12,64,128]{2,1,0:T(8,128)(2,1)S(1)}, u32[]{:S(2)}, u32[]{:S(2)}) collective-permute-start(bf16[12,64,128]{2,1,0:T(8,128)(2,1)} %get-tuple-element.28), channel_id=1, source_target_pairs={{0,2},{1,3},{2,0},{3,1},{4,6},{5,7},{6,4},{7,5},{8,10},{9,11},{10,... | collective-permute-start | bytes 589832 | tf_op jit(solution)/shard_map/ppermute | solution.py:270
  225.5 10.3 %collective-permute-start.2 = (bf16[12,64,128]{2,1,0:T(8,128)(2,1)S(1)}, bf16[12,64,128]{2,1,0:T(8,128)(2,1)S(1)}, u32[]{:S(2)}, u32[]{:S(2)}) collective-permute-start(bf16[12,64,128]{2,1,0:T(8,128)(2,1)S(1)} %get-tuple-element.29), channel_id=1, source_target_pairs={{0,3},{1,0},{2,1},{3,2},{4,7},{5,4},{6,5},{7,6},{8,11},{9,8},{10,9... | collective-permute-start | bytes 589832 | tf_op jit(solution)/shard_map/ppermute | solution.py:270

commit v3 on v2

v3 whole, which is shorter than its diff:
```python
import jax
import jax.numpy as jnp
from jax import lax
from jax.experimental import pallas as pl
from jax.experimental.pallas import tpu as pltpu
from jax.sharding import PartitionSpec as P

N_Z, N_Y, N_C, GROUP = 8, 8, 2, 4
N_DP = N_Z * N_Y * N_C
SPOTS = N_Z * N_Y
QD, QT, PT, D, NEG, ROWS = 4, 32, 64, 128, 7, 32
QROWS = QD * QT
SENT = QROWS + 8
BATCH = QD * GROUP
SLOTS = 4
VMEM = 48 * 1024 * 1024
F32, BF16, I32 = jnp.float32, jnp.bfloat16, jnp.int32
EXACT = lax.Precision.HIGHEST
EVERY = ("dp", "group")


def device(z, y, c, x):
    return ((z * N_Y + y) * N_C + c) * GROUP + x


def along(z_core):
    z_lines = [[device(z, y, z_core, x) for z in range(N_Z)] for y in range(N_Y) for x in range(GROUP)]
    y_lines = [[device(z, y, 1 - z_core, x) for y in range(N_Y)] for z in range(N_Z) for x in range(GROUP)]
    return z_lines + y_lines


def planes():
    first = [[device(z, y, 0, x) for z in range(N_Z) for y in range(N_Y)] for x in range(GROUP)]
    second = [[device(z, y, 1, x) for y in range(N_Y) for z in range(N_Z)] for x in range(GROUP)]
    return first + second


def exchange(blocks, groups):
    return lax.all_to_all(blocks, EVERY, split_axis=0, concat_axis=0, axis_index_groups=groups, tiled=True)


def call(body, out_shape, in_specs, out_specs, scratch=()):
    return pl.pallas_call(
        body,
        out_shape=out_shape,
        in_specs=in_specs,
        out_specs=out_specs,
        scratch_shapes=list(scratch),
        compiler_params=pltpu.CompilerParams(vmem_limit_bytes=VMEM),
    )


def vmem():
    return pl.BlockSpec(memory_space=pltpu.VMEM)


def smem():
    return pl.BlockSpec(memory_space=pltpu.SMEM)


def unit(values):
    wide = values.astype(F32)
    return (wide * lax.rsqrt(jnp.sum(wide * wide, axis=-1, keepdims=True) + 1e-06)).astype(BF16)


def iota(shape, dim):
    return lax.broadcasted_iota(I32, shape, dim)


def dot(a, b, dims, precision=None):
    return lax.dot_general(a, b, ((dims[0], dims[1]), ((), ())), precision=precision, preferred_element_type=F32)


def token_sum_matrix():
    return (iota((QROWS, QROWS), 0) // QT == iota((QROWS, QROWS), 1) // QT).astype(F32)


def prepare(ids, storage, queries, positives, sent, q_unit, pos_unit, count):
    tiles = unit(queries[...])
    q_unit[...] = tiles
    pos_unit[...] = unit(positives[...])
    homes = []
    for q in range(QD):
        for k in range(NEG):
            home = storage[ids[q, k]]
            owner = home // ROWS
            lane_of = (owner % N_C) * SPOTS + owner // N_C
            count[lane_of] = 0
            homes.append((lane_of, q * ROWS + home % ROWS + 1))
    lane = iota((8, N_DP), 1)
    sub = iota((8, N_DP), 0)
    codes = jnp.zeros((8, N_DP), F32)
    for lane_of, code in homes:
        rank = count[lane_of]
        count[lane_of] = rank + 1
        codes = jnp.where((lane == lane_of) & (sub == rank), code.astype(F32), codes)
    for copy in range(N_Y):
        sent[copy, 0:QROWS, :] = tiles.reshape(QROWS, D)
        sent[copy, QROWS:SENT, :] = codes.astype(BF16)


def normalize(values, out):
    out[...] = unit(values[...])


def positive_scores(q_unit, gathered):
    cands = gathered[...].reshape(BATCH * PT, D)
    exp_scores = jnp.exp(10.0 * dot(cands, q_unit, ((1,), (1,)))).reshape(BATCH, PT, QROWS)
    total = jnp.sum(exp_scores, axis=1)
    score = 0.1 * dot(jnp.log(total), token_sum_matrix(), ((1,), (0,)), EXACT)
    return cands, exp_scores, total, score


def positive_weight(q_tiles, gathered, out):
    score = positive_scores(q_tiles[...].reshape(QROWS, D), gathered)[3]
    out[...] = jnp.sum(jnp.exp(score), axis=0, keepdims=True)


def request(codes, source, slot):
    code = codes[source, slot]
    spot = jnp.maximum(code - 1, 0)
    return code > 0, spot // ROWS, spot % ROWS


def passages(codes, own_rows, other_rows, source):
    picked = [request(codes, source, slot)[2] for slot in range(SLOTS)]
    return jnp.concatenate([own_rows[picked[0]], own_rows[picked[1]], other_rows[picked[2]], other_rows[picked[3]]], axis=0)


def asking(codes, asked, source):
    picked = [request(codes, source, slot)[1] for slot in range(SLOTS)]
    return jnp.concatenate([asked[source, pl.ds(pl.multiple_of(q * QT, QT), QT), :] for q in picked], axis=0)


def spread(packed):
    block = iota((PT, QROWS), 1) // QT
    return jnp.concatenate([jnp.where(block == b, packed, 0.0).astype(BF16) for b in range(SLOTS)], axis=0)


def score(me, codes, asked, own_rows, other_rows, pos_weight, probs, sums, exps, totals, marks, factor):
    lane = iota((1, QROWS), 1)
    block = iota((PT, QROWS), 1) // QT

    def one(source, carry):
        mark = jnp.full((1, QROWS), -1.0, F32)
        for b in range(SLOTS):
            valid, q, _ = request(codes, source, b)
            mark = jnp.where((lane // QT == b) & valid, q.astype(F32), mark)
        full = dot(passages(codes, own_rows, other_rows, source), asking(codes, asked, source), ((1,), (1,)))
        packed = full[0:PT]
        for b in range(1, SLOTS):
            packed = jnp.where(block == b, full[b * PT : (b + 1) * PT], packed)
        exp_scores = jnp.exp(10.0 * packed)
        exps[source] = exp_scores
        totals[pl.ds(source, 1), :] = jnp.sum(exp_scores, axis=0, keepdims=True)
        marks[pl.ds(source, 1), :] = mark
        return carry

    lax.fori_loop(0, SPOTS, one, 0, unroll=4)

    total = totals[...]
    mark = marks[...]
    weight = jnp.exp(0.1 * dot(jnp.log(total), token_sum_matrix(), ((1,), (0,)), EXACT))
    weight = jnp.where(mark >= 0.0, weight, 0.0)
    factor[...] = weight / total
    first = iota((SPOTS, QROWS), 1) % QT == 0
    pad = jnp.zeros((QROWS - SPOTS, QROWS), F32)
    ones = jnp.ones((8, QROWS), F32)
    parts = []
    for q in range(QD):
        mine = jnp.where((mark == float(q)) & first, weight, 0.0)
        part = dot(ones, jnp.concatenate([mine, pad], axis=0), ((1,), (1,)), EXACT)[0:1]
        own = jnp.sum(jnp.where(lane == q * QT, pos_weight[...], 0.0), axis=1, keepdims=True)
        parts.append(part + jnp.where(lane == me[0], own, 0.0))
    sums[...] = jnp.broadcast_to(jnp.concatenate(parts, axis=0)[None], (SPOTS, QD, QROWS))

    def scale(source, carry):
        probs[source] = (exps[source] * factor[pl.ds(source, 1), :]).astype(BF16)
        return carry

    lax.fori_loop(0, SPOTS, scale, 0, unroll=4)


def terms(codes, own_rows, other_rows, probs, back):
    def one(source, carry):
        grads = dot(spread(probs[source].astype(F32)), passages(codes, own_rows, other_rows, source), ((0,), (0,)))
        picked = [request(codes, source, slot)[1] for slot in range(SLOTS)]
        for q in range(QD):
            total = jnp.zeros((QT, D), F32)
            for b in range(SLOTS):
                total += grads[b * QT : (b + 1) * QT] * (picked[b] == q).astype(F32)
            back[source, q * QT : (q + 1) * QT, :] = total.astype(BF16)
        return carry

    lax.fori_loop(0, SPOTS, one, 0, unroll=4)


def weigh(me, codes, weight_sum, weight_inv, asked, probs, q_tiles, gathered, own_grad, other_grad, pos_grad, query_part, losses, other_acc):
    own_grad[...] = jnp.zeros_like(own_grad)
    other_acc[...] = jnp.zeros_like(other_acc)

    def add(source, carry):
        grads = dot(spread(probs[source].astype(F32)), asking(codes, asked, source), ((1,), (0,)))
        for b in range(SLOTS):
            _, q, row = request(codes, source, b)
            acc = own_grad if b < 2 else other_acc
            acc[row] += grads[b * PT : (b + 1) * PT] * weight_inv[q, source]
        return carry

    lax.fori_loop(0, SPOTS, add, 0, unroll=4)
    other_grad[...] = other_acc[...].astype(BF16)

    q_unit = q_tiles[...].reshape(QROWS, D)
    cands, exp_scores, total, scores = positive_scores(q_unit, gathered)
    lane = iota((1, QROWS), 1)
    own_sum = jnp.zeros((1, QROWS), F32)
    for q in range(QD):
        own_sum = jnp.where(lane // QT == q, weight_sum[q, me[0]], own_sum)
    own = (iota((BATCH, QROWS), 0) == me[1] * QD + iota((BATCH, QROWS), 1) // QT).astype(F32)
    score_grad = jnp.exp(scores) / own_sum - own
    losses[...] = jnp.log(own_sum) - jnp.sum(scores * own, axis=0, keepdims=True)
    weight_grad = (exp_scores * (score_grad / total)[:, None, :]).astype(BF16).reshape(BATCH * PT, QROWS)
    query_part[...] = dot(weight_grad, cands, ((0,), (0,)))
    pos_grad[...] = dot(weight_grad, q_unit, ((1,), (0,))).reshape(BATCH, PT, D)


def split(me, own_grad, moved, pos_grad, kept, off1, off2, off3):
    share = ROWS // GROUP
    for ahead, out in enumerate((kept, off1, off2, off3)):
        g = (me[1] + ahead) % GROUP
        out[0:QD] = pos_grad[pl.ds(g * QD, QD)].astype(out.dtype)
        rows = pl.ds(g * share, share)
        out[QD:] = (own_grad[rows] + moved[rows].astype(F32)).astype(out.dtype)


def collect(weight_inv, me, query_part, arrived, out):
    def add(source, total):
        return total + arrived[source].astype(F32)

    total = lax.fori_loop(0, SPOTS, add, jnp.zeros((QROWS, D), F32), unroll=4)
    for q in range(QD):
        rows = slice(q * QT, (q + 1) * QT)
        out[q] = query_part[rows, :] + total[rows] * weight_inv[q, me[0]]


def per_device(queries, positives, passage_pool, negative_ids, storage_row):
    struct = jax.ShapeDtypeStruct
    holder = lax.axis_index("dp")
    z, y, core = holder // (N_Y * N_C), (holder // N_C) % N_Y, holder % N_C
    source = jnp.where(core == 0, z * N_Y + y, y * N_Z + z)
    me = jnp.stack([source, lax.axis_index("group")]).astype(I32)
    swap = [(h, h ^ 1) for h in range(N_DP)]
    tiles = struct((QD, QT, D), BF16)

    sent, q_unit, pos_unit = call(
        prepare,
        (struct((N_Y, SENT, D), BF16), tiles, struct((QD, PT, D), BF16)),
        [smem(), smem(), vmem(), vmem()],
        (vmem(), vmem(), vmem()),
        [pltpu.SMEM((N_DP,), I32)],
    )(negative_ids, storage_row, queries, positives)
    asked = exchange(sent, along(1))
    asked = exchange(jnp.broadcast_to(asked[None], (N_Z, N_Y, SENT, D)), along(0)).reshape(SPOTS, SENT, D)

    own_rows = call(normalize, struct((ROWS, PT, D), BF16), [vmem()], vmem())(passage_pool)
    other_rows = lax.ppermute(own_rows, "dp", swap)
    gathered = lax.all_gather(pos_unit, "group", axis=0, tiled=True)
    pos_weight = call(positive_weight, struct((1, QROWS), F32), [vmem(), vmem()], vmem())(q_unit, gathered)

    codes = asked[:, QROWS : QROWS + 2, :]
    codes = jnp.concatenate(
        [lax.dynamic_index_in_dim(codes, c * SPOTS + holder // N_C, 2, False) for c in (core, 1 - core)], axis=1
    ).astype(I32)

    probs, sums = call(
        score,
        (struct((SPOTS, PT, QROWS), BF16), struct((SPOTS, QD, QROWS), F32)),
        [smem(), smem(), vmem(), vmem(), vmem(), vmem()],
        (vmem(), vmem()),
        [
            pltpu.VMEM((SPOTS, PT, QROWS), F32),
            pltpu.VMEM((SPOTS, QROWS), F32),
            pltpu.VMEM((SPOTS, QROWS), F32),
            pltpu.VMEM((SPOTS, QROWS), F32),
        ],
    )(me, codes, asked, own_rows, other_rows, pos_weight)
    weight_sum = jnp.sum(exchange(sums, planes()), axis=0)
    weight_inv = 1.0 / weight_sum

    back = call(
        terms, struct((SPOTS, QROWS, D), BF16), [smem(), vmem(), vmem(), vmem()], vmem()
    )(codes, own_rows, other_rows, probs)
    arrived = exchange(back, planes())

    own_grad, other_grad, pos_grad, query_part, losses = call(
        weigh,
        (
            struct((ROWS, PT, D), F32),
            struct((ROWS, PT, D), BF16),
            struct((BATCH, PT, D), F32),
            struct((QROWS, D), F32),
            struct((1, QROWS), F32),
        ),
        [smem(), smem(), smem(), smem(), vmem(), vmem(), vmem(), vmem()],
        (vmem(),) * 5,
        [pltpu.VMEM((ROWS, PT, D), F32)],
    )(me, codes, weight_sum, weight_inv, asked, probs, q_unit, gathered)

    block = (QD + ROWS // GROUP, PT, D)
    kept, off1, off2, off3 = call(
        split,
        (struct(block, F32), struct(block, BF16), struct(block, BF16), struct(block, BF16)),
        [smem(), vmem(), vmem(), vmem()],
        (vmem(),) * 4,
    )(me, own_grad, lax.ppermute(other_grad, "dp", swap), pos_grad)
    total = kept
    for ahead, part in ((1, off1), (2, off2), (3, off3)):
        moved = lax.ppermute(part, "group", [(g, (g + ahead) % GROUP) for g in range(GROUP)])
        total = total + moved.astype(F32)

    query_grad = call(
        collect, struct((QD, QT, D), F32), [smem(), smem(), vmem(), vmem()], vmem()
    )(weight_inv, me, query_part, arrived)
    return losses.reshape(QD, QT)[:, 0], query_grad, total[:QD], total[QD:]


def solution(mesh):
    in_specs = (P(EVERY), P(EVERY), P("dp"), P(EVERY), P())
    out_specs = (P(EVERY), P(EVERY), P(EVERY), P(EVERY))
    return jax.shard_map(per_device, mesh=mesh, in_specs=in_specs, out_specs=out_specs, check_vma=False)
```

time: 242 us -> 164 us (0.68)
  the two profiles are of different devices: /device:TPU:6 before, /device:TPU:26 now
where the time goes in v3:
time: 164 us; the launch traced here: 162 us
  starting transfers between devices  45.9 us (28%)
  waiting for transfers between devices  42.3 us (26%)
  blocking collectives  27 us (16%)
  Pallas kernels  24 us (15%)
  local copies, waits for them, and re-layouts  19.1 us (12%)
  other arithmetic  3.21 us (2%)
    all_to_all x3, waiting for transfers between devices, exchange(): lax.all_to_all(blocks, EVERY, split_axis=0, concat_axis=0, axis_index_gro...  35.1 us
    all_to_all x3, starting transfers between devices, exchange(): lax.all_to_all(blocks, EVERY, split_axis=0, concat_axis=0, axis_index_gro...  30.5 us
    all_to_all x1, blocking collectives, exchange(): lax.all_to_all(blocks, EVERY, split_axis=0, concat_axis=0, axis_index_gro...  14.5 us
    all_gather x1, blocking collectives, per_device(): gathered = lax.all_gather(pos_unit, 'group', axis=0, tiled=True)  12.5 us
    unnamed x38, local copies, waits for them, and re-layouts  11 us
    ppermute x3, starting transfers between devices, per_device(): lax.ppermute(part, 'group', [(g, (g + ahead) % GROUP) for g in range(GROU...  10.5 us
    pallas_call x1, Pallas kernels, per_device(): call(score, (struct((SPOTS, PT, QROWS), BF16), struct((SPOTS, QD, QROWS),...  6.61 us
    pallas_call x1, Pallas kernels, per_device(): call(weigh, (struct((ROWS, PT, D), F32), struct((ROWS, PT, D), BF16), str...  6.26 us
  transfers between devices with their start and end apart: 8, of which 6 were waited for; matrix products, arithmetic and copies ran while one was open for 6% of the time, Pallas kernels for 8%

profile of v3, /device:TPU:26, one launch (start us, length us, event | category | flops | bytes accessed | tf_op | source)
XLA Modules:
  0.0 162.4 jit_solution(14547470721989463272)
XLA Ops:
  0.6 0.0 copy-start.15
  0.6 0.8 copy-done.15
  1.5 0.8 copy-done.16
  2.2 0.7 copy-done.17
  3.0 0.7 copy-done.18
  3.6 1.3 shard_map.84
  4.9 0.0 copy-start.8
  4.9 0.0 copy-start.12
  4.9 14.5 %all_to_all.20 = bf16[8,136,128]{2,1,0:T(8,128)(2,1)S(1)} all-to-all(bf16[8,136,128]{2,1,0:T(8,128)(2,1)S(1)} %get-tuple-element.18), channel_id=1, replica_groups={{4,68,132,196,260,324,388,452},{5,69,133,197,261,325,389,453},{6,70,134..., dimensions={0} | all-to-all | bytes 557056 | tf_op jit(solution)/shard_map/all_to_all | solution.py:39
  19.4 1.7 %broadcast_in_dim.2 = bf16[8,8,136,128]{3,2,1,0:T(8,128)(2,1)} broadcast(bf16[8,136,128]{2,1,0:T(8,128)(2,1)S(1)} %all_to_all.20), dimensions={1,2,3} | broadcast | bytes 2506752 | tf_op jit(solution)/shard_map/broadcast_in_dim | solution.py:263
  21.1 0.0 copy-done.8
  21.1 0.0 copy-done.12
  21.1 10.4 %all-to-all-start.1 = ((bf16[8,8,136,128]{3,2,1,0:T(8,128)(2,1)}), bf16[8,8,136,128]{3,2,1,0:T(8,128)(2,1)S(1)}, u32[]{:S(2)}, u32[]{:S(2)}) async-start(bf16[8,8,136,128]{3,2,1,0:T(8,128)(2,1)} %broadcast_in_dim.2), calls=%async_computation.1 | async-start | bytes 4456448 | tf_op jit(solution)/shard_map/all_to_all | solution.py:39
  31.6 0.4 shard_map.85.own_rows
  31.9 3.0 %collective-permute-start = (bf16[32,64,128]{2,1,0:T(8,128)(2,1)S(1)}, bf16[32,64,128]{2,1,0:T(8,128)(2,1)S(1)}, u32[]{:S(2)}, u32[]{:S(2)}) collective-permute-start(bf16[32,64,128]{2,1,0:T(8,128)(2,1)S(1)} %shard_map.85.own_rows), channel_id=1, source_target_pairs={{0,4},{4,0},{8,12},{12,8},{16,20},{20,16},{24,28},{28,24},{32,36},... | collective-permute-start | bytes 1572872 | tf_op jit(solution)/shard_map/ppermute | solution.py:266
  35.0 12.5 %all_gather.3.gathered = bf16[16,64,128]{2,1,0:T(8,128)(2,1)S(1)} all-gather(bf16[4,64,128]{2,1,0:T(8,128)(2,1)} %copy-done.12), channel_id=1, replica_groups=mesh['dp'=128,'group'=4] {'group'}, dimensions={0}, use_global_device_ids=true | all-gather | bytes 327680 | tf_op jit(solution)/shard_map/all_gather | solution.py:267
  47.6 0.8 copy-done.9
  48.3 0.5 shard_map.86.pos_weight
  48.8 0.1 pad_add_fusion.me
  48.9 14.3 %all-to-all-done.1 = bf16[8,8,136,128]{3,2,1,0:T(8,128)(2,1)S(1)} async-done(((bf16[8,8,136,128]{3,2,1,0:T(8,128)(2,1)}), bf16[8,8,136,128]{3,2,1,0:T(8,128)(2,1)S(1)}, u32[]{:S(2)}, u32[]{:S(2)}) %all-to-all-start.1) | async-done | bytes 2228256 | tf_op jit(solution)/shard_map/all_to_all | solution.py:39
  63.3 0.8 constant_dynamic-slice_fusion.1
  64.0 0.9 copy.17
  64.9 1.4 copy.18
  66.3 0.7 pad_maximum_fusion
  66.9 0.7 copy.19
  67.6 0.7 convert_element_type.12.codes
  68.4 0.0 collective-permute-done.other_rows
  68.4 6.6 %shard_map.87 = (bf16[64,64,128]{2,1,0:T(8,128)(2,1)S(1)}, f32[64,4,128]{2,1,0:T(4,128)S(1)}) custom-call(s32[2]{0:T(128)S(1)} %pad_add_fusion.me, s32[64,4]{1,0:T(8,128)S(1)} %convert_element_type.12.codes, bf16[64,136,128]{2,1,0:T(8,128)(2,1)S(1)} %bitcast.6, bf16[32,64,128]{2,1,0:T(8,128)(2,1)S(1)} %shard_map.85.own_rows, ...), custom_call_target="tpu_custom_call" | custom-call | tf_op jit(solution)/shard_map/pallas_call | solution.py:275
  75.0 0.0 copy-done.4
  75.0 0.0 copy-start.1
  75.0 1.0 copy-done.1
  76.0 0.7 copy-done.11
  76.6 8.1 %all-to-all-start.2 = ((f32[64,4,128]{2,1,0:T(4,128)}), f32[64,4,128]{2,1,0:T(4,128)}, u32[]{:S(2)}, u32[]{:S(2)}) async-start(f32[64,4,128]{2,1,0:T(4,128)} %copy-done.11), calls=%async_computation.2 | async-start | bytes 262144 | tf_op jit(solution)/shard_map/all_to_all | solution.py:39
  84.8 1.2 copy-done.2
  86.0 0.8 copy-done.5
  86.8 5.8 %shard_map.89 = bf16[64,128,128]{2,1,0:T(8,128)(2,1)S(1)} custom-call(s32[64,4]{1,0:T(8,128)S(1)} %copy-done.5, bf16[32,64,128]{2,1,0:T(8,128)(2,1)S(1)} %shard_map.85.own_rows, bf16[32,64,128]{2,1,0:T(8,128)(2,1)S(1)} %collective-permute-done.other_rows, bf16[64,64,128]{2,1,0:T(8,128)(2,1)S(1)} %copy-done.2), custom_call_target="tpu_custom_call" | custom-call | tf_op jit(solution)/shard_map/pallas_call | solution.py:290
  92.6 1.3 copy-done
  93.9 1.2 all-to-all-done.2
  95.1 11.9 %all-to-all-start.3 = ((bf16[64,128,128]{2,1,0:T(8,128)(2,1)}), bf16[64,128,128]{2,1,0:T(8,128)(2,1)}, u32[]{:S(2)}, u32[]{:S(2)}) async-start(bf16[64,128,128]{2,1,0:T(8,128)(2,1)} %copy-done), calls=%async_computation.3 | async-start | bytes 4194304 | tf_op jit(solution)/shard_map/all_to_all | solution.py:39
  107.0 1.0 reduce_sum.9.weight_sum
  108.0 0.0 copy-start.6
  108.0 0.7 copy-done.6
  108.8 0.8 copy-done.10
  109.5 6.3 %shard_map.88 = (f32[32,64,128]{2,1,0:T(8,128)S(1)}, bf16[32,64,128]{2,1,0:T(8,128)(2,1)S(1)}, f32[16,64,128]{2,1,0:T(8,128)S(1)}, f32[128,128]{1,0:T(8,128)S(1)}, f32[1,128]{1,0:T(1,128)S(1)}) custom-call(s32[2]{0:T(128)S(1)} %pad_add_fusion.me, s32[64,4]{1,0:T(8,128)S(1)} %copy-done.6, f32[4,128]{1,0:T(4,128)S(1)} %reduce_sum.9.weight_sum, ...), custom_call_target="tpu_custom_call" | custom-call | tf_op jit(solution)/shard_map/pallas_call | solution.py:295
  115.8 0.0 copy-start.13
  115.8 1.9 %collective-permute-start.1 = (bf16[32,64,128]{2,1,0:T(8,128)(2,1)S(1)}, bf16[32,64,128]{2,1,0:T(8,128)(2,1)S(1)}, u32[]{:S(2)}, u32[]{:S(2)}) collective-permute-start(bf16[32,64,128]{2,1,0:T(8,128)(2,1)S(1)} %get-tuple-element.26), channel_id=1, source_target_pairs={{0,4},{4,0},{8,12},{12,8},{16,20},{20,16},{24,28},{28,24},{32,36},... | collective-permute-start | bytes 1572872 | tf_op jit(solution)/shard_map/ppermute | solution.py:315
  117.7 1.9 %collective-permute-done.1.moved = bf16[32,64,128]{2,1,0:T(8,128)(2,1)S(1)} collective-permute-done((bf16[32,64,128]{2,1,0:T(8,128)(2,1)S(1)}, bf16[32,64,128]{2,1,0:T(8,128)(2,1)S(1)}, u32[]{:S(2)}, u32[]{:S(2)}) %collective-permute-start.1) | collective-permute-done | bytes 524320 | tf_op jit(solution)/shard_map/ppermute | solution.py:315
  119.6 0.7 shard_map.91
  120.3 3.4 %collective-permute-start.2 = (bf16[12,64,128]{2,1,0:T(8,128)(2,1)S(1)}, bf16[12,64,128]{2,1,0:T(8,128)(2,1)S(1)}, u32[]{:S(2)}, u32[]{:S(2)}) collective-permute-start(bf16[12,64,128]{2,1,0:T(8,128)(2,1)S(1)} %get-tuple-element.29), channel_id=1, source_target_pairs={{0,1},{1,2},{2,3},{3,0},{4,5},{5,6},{6,7},{7,4},{8,9},{9,10},{10,1... | collective-permute-start | bytes 589832 | tf_op jit(solution)/shard_map/ppermute | solution.py:318
  123.7 3.0 %collective-permute-start.3 = (bf16[12,64,128]{2,1,0:T(8,128)(2,1)S(1)}, bf16[12,64,128]{2,1,0:T(8,128)(2,1)S(1)}, u32[]{:S(2)}, u32[]{:S(2)}) collective-permute-start(bf16[12,64,128]{2,1,0:T(8,128)(2,1)S(1)} %get-tuple-element.30), channel_id=1, source_target_pairs={{0,2},{1,3},{2,0},{3,1},{4,6},{5,7},{6,4},{7,5},{8,10},{9,11},{10,... | collective-permute-start | bytes 589832 | tf_op jit(solution)/shard_map/ppermute | solution.py:318
  126.7 4.1 %collective-permute-start.4 = (bf16[12,64,128]{2,1,0:T(8,128)(2,1)S(1)}, bf16[12,64,128]{2,1,0:T(8,128)(2,1)S(1)}, u32[]{:S(2)}, u32[]{:S(2)}) collective-permute-start(bf16[12,64,128]{2,1,0:T(8,128)(2,1)S(1)} %get-tuple-element.31), channel_id=1, source_target_pairs={{0,3},{1,0},{2,1},{3,2},{4,7},{5,4},{6,5},{7,6},{8,11},{9,8},{10,9... | collective-permute-start | bytes 589832 | tf_op jit(solution)/shard_map/ppermute | solution.py:318
  130.8 0.5 broadcast.9
  131.3 0.7 reduce.5
  132.0 0.1 reshape.16
  132.1 0.6 slice_reduce_fusion
  132.7 0.0 collective-permute-done.2
  132.7 2.2 %collective-permute-done.3 = bf16[12,64,128]{2,1,0:T(8,128)(2,1)S(1)} collective-permute-done((bf16[12,64,128]{2,1,0:T(8,128)(2,1)S(1)}, bf16[12,64,128]{2,1,0:T(8,128)(2,1)S(1)}, u32[]{:S(2)}, u32[]{:S(2)}) %collective-permute-start.3) | collective-permute-done | bytes 196640 | tf_op jit(solution)/shard_map/ppermute | solution.py:318
  134.9 3.0 %collective-permute-done.4 = bf16[12,64,128]{2,1,0:T(8,128)(2,1)S(1)} collective-permute-done((bf16[12,64,128]{2,1,0:T(8,128)(2,1)S(1)}, bf16[12,64,128]{2,1,0:T(8,128)(2,1)S(1)}, u32[]{:S(2)}, u32[]{:S(2)}) %collective-permute-start.4) | collective-permute-done | bytes 196640 | tf_op jit(solution)/shard_map/ppermute | solution.py:318
  138.0 0.1 convert_add_fusion
  138.1 0.7 slice.18
  138.8 0.7 slice.17
  139.4 19.5 %all-to-all-done.3.arrived = bf16[64,128,128]{2,1,0:T(8,128)(2,1)} async-done(((bf16[64,128,128]{2,1,0:T(8,128)(2,1)}), bf16[64,128,128]{2,1,0:T(8,128)(2,1)}, u32[]{:S(2)}, u32[]{:S(2)}) %all-to-all-start.3) | async-done | bytes 2097184 | tf_op jit(solution)/shard_map/all_to_all | solution.py:39
  159.0 0.8 copy-done.14
  159.8 2.6 %shard_map.90 = f32[4,32,128]{2,1,0:T(8,128)} custom-call(f32[4,128]{1,0:T(4,128)S(1)} %broadcast_divide_fusion.weight_inv, s32[2]{0:T(128)S(1)} %pad_add_fusion.me, f32[128,128]{1,0:T(8,128)S(1)} %copy-done.14, bf16[64,128,128]{2,1,0:T(8,128)(2,1)} %all-to-all-done.3.arrived), custom_call_target="tpu_custom_call" | custom-call | tf_op jit(solution)/shard_map/pallas_call | solution.py:321
  (18 shorter events, 0.1 us)
Async XLA Ops:
  0.6 0.8 copy-start.15
  1.5 0.8 copy-start.16
  2.2 0.7 copy-start.17
  2.9 0.7 copy-start.18
  4.9 16.2 %copy-start.8 = (bf16[4,32,128]{2,1,0:T(8,128)(2,1)}, bf16[4,32,128]{2,1,0:T(8,128)(2,1)S(1)}, u32[]{:S(2)}) copy-start(bf16[4,32,128]{2,1,0:T(8,128)(2,1)S(1)} %get-tuple-element.19.q_tiles) | copy-start | bytes 98308
  4.9 16.2 %copy-start.12 = (bf16[4,64,128]{2,1,0:T(8,128)(2,1)}, bf16[4,64,128]{2,1,0:T(8,128)(2,1)S(1)}, u32[]{:S(2)}) copy-start(bf16[4,64,128]{2,1,0:T(8,128)(2,1)S(1)} %get-tuple-element.20) | copy-start | bytes 196612
  21.1 10.5 %copy-start.7 = (bf16[32,64,128]{2,1,0:T(8,128)(2,1)S(1)}, bf16[32,64,128]{2,1,0:T(8,128)(2,1)}, u32[]{:S(2)}) copy-start(bf16[32,64,128]{2,1,0:T(8,128)(2,1)} %values.1) | copy-start | bytes 1572868
  21.1 42.1 %all-to-all-start.1 = ((bf16[8,8,136,128]{3,2,1,0:T(8,128)(2,1)}), bf16[8,8,136,128]{3,2,1,0:T(8,128)(2,1)S(1)}, u32[]{:S(2)}, u32[]{:S(2)}) async-start(bf16[8,8,136,128]{3,2,1,0:T(8,128)(2,1)} %broadcast_in_dim.2), calls=%async_computation.1 | async-start | bytes 4456448 | tf_op jit(solution)/shard_map/all_to_all | solution.py:39
  31.9 36.4 %collective-permute-start = (bf16[32,64,128]{2,1,0:T(8,128)(2,1)S(1)}, bf16[32,64,128]{2,1,0:T(8,128)(2,1)S(1)}, u32[]{:S(2)}, u32[]{:S(2)}) collective-permute-start(bf16[32,64,128]{2,1,0:T(8,128)(2,1)S(1)} %shard_map.85.own_rows), channel_id=1, source_target_pairs={{0,4},{4,0},{8,12},{12,8},{16,20},{20,16},{24,28},{28,24},{32,36},... | collective-permute-start | bytes 1572872 | tf_op jit(solution)/shard_map/ppermute | solution.py:266
  47.6 0.8 copy-start.9
  68.4 6.6 %copy-start.4 = (s32[64,4]{1,0:T(8,128)}, s32[64,4]{1,0:T(8,128)S(1)}, u32[]{:S(2)}) copy-start(s32[64,4]{1,0:T(8,128)S(1)} %convert_element_type.12.codes) | copy-start | bytes 3076
  75.0 1.0 copy-start.1
  76.0 0.7 copy-start.11
  76.6 18.5 %all-to-all-start.2 = ((f32[64,4,128]{2,1,0:T(4,128)}), f32[64,4,128]{2,1,0:T(4,128)}, u32[]{:S(2)}, u32[]{:S(2)}) async-start(f32[64,4,128]{2,1,0:T(4,128)} %copy-done.11), calls=%async_computation.2 | async-start | bytes 262144 | tf_op jit(solution)/shard_map/all_to_all | solution.py:39
  84.8 1.2 copy-start.2
  86.0 0.8 copy-start.5
  92.6 1.3 copy-start
  93.9 14.1 %copy-start.3 = (bf16[64,64,128]{2,1,0:T(8,128)(2,1)S(1)}, bf16[64,64,128]{2,1,0:T(8,128)(2,1)}, u32[]{:S(2)}) copy-start(bf16[64,64,128]{2,1,0:T(8,128)(2,1)} %copy-done.1) | copy-start | bytes 3145732
  95.1 63.9 %all-to-all-start.3 = ((bf16[64,128,128]{2,1,0:T(8,128)(2,1)}), bf16[64,128,128]{2,1,0:T(8,128)(2,1)}, u32[]{:S(2)}, u32[]{:S(2)}) async-start(bf16[64,128,128]{2,1,0:T(8,128)(2,1)} %copy-done), calls=%async_computation.3 | async-start | bytes 4194304 | tf_op jit(solution)/shard_map/all_to_all | solution.py:39
  108.0 0.8 copy-start.6
  108.8 0.8 copy-start.10
  115.8 4.5 %copy-start.13 = (f32[128,128]{1,0:T(8,128)}, f32[128,128]{1,0:T(8,128)S(1)}, u32[]{:S(2)}) copy-start(f32[128,128]{1,0:T(8,128)S(1)} %get-tuple-element.24.query_part) | copy-start | bytes 196612
  115.8 3.8 %collective-permute-start.1 = (bf16[32,64,128]{2,1,0:T(8,128)(2,1)S(1)}, bf16[32,64,128]{2,1,0:T(8,128)(2,1)S(1)}, u32[]{:S(2)}, u32[]{:S(2)}) collective-permute-start(bf16[32,64,128]{2,1,0:T(8,128)(2,1)S(1)} %get-tuple-element.26), channel_id=1, source_target_pairs={{0,4},{4,0},{8,12},{12,8},{16,20},{20,16},{24,28},{28,24},{32,36},... | collective-permute-start | bytes 1572872 | tf_op jit(solution)/shard_map/ppermute | solution.py:315
  120.3 12.4 %collective-permute-start.2 = (bf16[12,64,128]{2,1,0:T(8,128)(2,1)S(1)}, bf16[12,64,128]{2,1,0:T(8,128)(2,1)S(1)}, u32[]{:S(2)}, u32[]{:S(2)}) collective-permute-start(bf16[12,64,128]{2,1,0:T(8,128)(2,1)S(1)} %get-tuple-element.29), channel_id=1, source_target_pairs={{0,1},{1,2},{2,3},{3,0},{4,5},{5,6},{6,7},{7,4},{8,9},{9,10},{10,1... | collective-permute-start | bytes 589832 | tf_op jit(solution)/shard_map/ppermute | solution.py:318
  123.7 11.2 %collective-permute-start.3 = (bf16[12,64,128]{2,1,0:T(8,128)(2,1)S(1)}, bf16[12,64,128]{2,1,0:T(8,128)(2,1)S(1)}, u32[]{:S(2)}, u32[]{:S(2)}) collective-permute-start(bf16[12,64,128]{2,1,0:T(8,128)(2,1)S(1)} %get-tuple-element.30), channel_id=1, source_target_pairs={{0,2},{1,3},{2,0},{3,1},{4,6},{5,7},{6,4},{7,5},{8,10},{9,11},{10,... | collective-permute-start | bytes 589832 | tf_op jit(solution)/shard_map/ppermute | solution.py:318
  126.7 11.2 %collective-permute-start.4 = (bf16[12,64,128]{2,1,0:T(8,128)(2,1)S(1)}, bf16[12,64,128]{2,1,0:T(8,128)(2,1)S(1)}, u32[]{:S(2)}, u32[]{:S(2)}) collective-permute-start(bf16[12,64,128]{2,1,0:T(8,128)(2,1)S(1)} %get-tuple-element.31), channel_id=1, source_target_pairs={{0,3},{1,0},{2,1},{3,2},{4,7},{5,4},{6,5},{7,6},{8,11},{9,8},{10,9... | collective-permute-start | bytes 589832 | tf_op jit(solution)/shard_map/ppermute | solution.py:318
  159.0 0.8 copy-start.14

commit v4 on v3

--- a/solution.py
+++ b/solution.py
@@ -117,7 +117,7 @@
 
 
 def request(codes, source, slot):
-    code = codes[source, slot]
+    code = codes[slot // 2, source * 8 + slot % 2]
     spot = jnp.maximum(code - 1, 0)
     return code > 0, spot // ROWS, spot % ROWS
 
@@ -137,7 +137,19 @@
     return jnp.concatenate([jnp.where(block == b, packed, 0.0).astype(BF16) for b in range(SLOTS)], axis=0)
 
 
-def score(me, codes, asked, own_rows, other_rows, pos_weight, probs, sums, exps, totals, marks, factor):
+def read_codes(me, asked, codes, table, sem):
+    rows = asked[:, QROWS:SENT, :].reshape(SPOTS * 8, N_DP)
+    which = iota((8, N_DP), 0)
+    spot = jnp.where(which == 0, me[2], me[3])
+    pick = ((iota((8, N_DP), 1) == spot) & (which < 2)).astype(F32).astype(BF16)
+    table[...] = dot(pick, rows, ((1,), (1,))).astype(I32)
+    copy = pltpu.make_async_copy(table, codes, sem)
+    copy.start()
+    copy.wait()
+
+
+def score(me, asked, own_rows, other_rows, pos_weight, probs, sums, codes, exps, totals, marks, factor, table, sem):
+    read_codes(me, asked, codes, table, sem)
     lane = iota((1, QROWS), 1)
     block = iota((PT, QROWS), 1) // QT
 
@@ -233,11 +245,12 @@
         out[QD:] = (own_grad[rows] + moved[rows].astype(F32)).astype(out.dtype)
 
 
+def add_blocks(arrived, out):
+    out[...] = jnp.sum(arrived[...].astype(F32), axis=0).astype(BF16)
+
+
 def collect(weight_inv, me, query_part, arrived, out):
-    def add(source, total):
-        return total + arrived[source].astype(F32)
-
-    total = lax.fori_loop(0, SPOTS, add, jnp.zeros((QROWS, D), F32), unroll=4)
+    total = jnp.sum(arrived[...].astype(F32), axis=0)
     for q in range(QD):
         rows = slice(q * QT, (q + 1) * QT)
         out[q] = query_part[rows, :] + total[rows] * weight_inv[q, me[0]]
@@ -248,7 +261,8 @@
     holder = lax.axis_index("dp")
     z, y, core = holder // (N_Y * N_C), (holder // N_C) % N_Y, holder % N_C
     source = jnp.where(core == 0, z * N_Y + y, y * N_Z + z)
-    me = jnp.stack([source, lax.axis_index("group")]).astype(I32)
+    spot = holder // N_C
+    me = jnp.stack([source, lax.axis_index("group"), core * SPOTS + spot, (1 - core) * SPOTS + spot]).astype(I32)
     swap = [(h, h ^ 1) for h in range(N_DP)]
     tiles = struct((QD, QT, D), BF16)
 
@@ -267,30 +281,29 @@
     gathered = lax.all_gather(pos_unit, "group", axis=0, tiled=True)
     pos_weight = call(positive_weight, struct((1, QROWS), F32), [vmem(), vmem()], vmem())(q_unit, gathered)
 
-    codes = asked[:, QROWS : QROWS + 2, :]
-    codes = jnp.concatenate(
-        [lax.dynamic_index_in_dim(codes, c * SPOTS + holder // N_C, 2, False) for c in (core, 1 - core)], axis=1
-    ).astype(I32)
-
-    probs, sums = call(
+    probs, sums, codes = call(
         score,
-        (struct((SPOTS, PT, QROWS), BF16), struct((SPOTS, QD, QROWS), F32)),
-        [smem(), smem(), vmem(), vmem(), vmem(), vmem()],
-        (vmem(), vmem()),
+        (struct((SPOTS, PT, QROWS), BF16), struct((SPOTS, QD, QROWS), F32), struct((8, SPOTS * 8), I32)),
+        [smem(), vmem(), vmem(), vmem(), vmem()],
+        (vmem(), vmem(), smem()),
         [
             pltpu.VMEM((SPOTS, PT, QROWS), F32),
             pltpu.VMEM((SPOTS, QROWS), F32),
             pltpu.VMEM((SPOTS, QROWS), F32),
             pltpu.VMEM((SPOTS, QROWS), F32),
+            pltpu.VMEM((8, SPOTS * 8), I32),
+            pltpu.SemaphoreType.DMA,
         ],
-    )(me, codes, asked, own_rows, other_rows, pos_weight)
+    )(me, asked, own_rows, other_rows, pos_weight)
     weight_sum = jnp.sum(exchange(sums, planes()), axis=0)
     weight_inv = 1.0 / weight_sum
 
     back = call(
         terms, struct((SPOTS, QROWS, D), BF16), [smem(), vmem(), vmem(), vmem()], vmem()
     )(codes, own_rows, other_rows, probs)
-    arrived = exchange(back, planes())
+    arrived = exchange(back.reshape(N_Z, N_Y, QROWS, D), along(0))
+    arrived = call(add_blocks, struct((N_Y, QROWS, D), BF16), [vmem()], vmem())(arrived)
+    arrived = exchange(arrived, along(1))
 
     own_grad, other_grad, pos_grad, query_part, losses = call(
         weigh,

time: 164 us -> 160 us (0.976)
  the two profiles are of different devices: /device:TPU:26 before, /device:TPU:6 now
where the time goes in v4:
time: 160 us; the launch traced here: 158 us
  starting transfers between devices  37.9 us (24%)
  waiting for transfers between devices  37.7 us (24%)
  blocking collectives  30 us (19%)
  Pallas kernels  27.6 us (17%)
  local copies, waits for them, and re-layouts  20.2 us (13%)
  other arithmetic  3.65 us (2%)
    all_to_all x4, waiting for transfers between devices, exchange(): lax.all_to_all(blocks, EVERY, split_axis=0, concat_axis=0, axis_index_gro...  32.8 us
    all_to_all x4, starting transfers between devices, exchange(): lax.all_to_all(blocks, EVERY, split_axis=0, concat_axis=0, axis_index_gro...  25.3 us
    all_to_all x1, blocking collectives, exchange(): lax.all_to_all(blocks, EVERY, split_axis=0, concat_axis=0, axis_index_gro...  17.6 us
    unnamed x60, local copies, waits for them, and re-layouts  15.9 us
    all_gather x1, blocking collectives, per_device(): gathered = lax.all_gather(pos_unit, 'group', axis=0, tiled=True)  12.5 us
    ppermute x3, starting transfers between devices, per_device(): lax.ppermute(part, 'group', [(g, (g + ahead) % GROUP) for g in range(GROU...  8.63 us
    pallas_call x1, Pallas kernels, per_device(): call(score, (struct((SPOTS, PT, QROWS), BF16), struct((SPOTS, QD, QROWS),...  8 us
    pallas_call x1, Pallas kernels, per_device(): call(weigh, (struct((ROWS, PT, D), F32), struct((ROWS, PT, D), BF16), str...  6.91 us
  transfers between devices with their start and end apart: 9, of which 5 were waited for; matrix products, arithmetic and copies ran while one was open for 4% of the time, Pallas kernels for 11%

profile of v4, /device:TPU:6, one launch (start us, length us, event | category | flops | bytes accessed | tf_op | source)
XLA Modules:
  0.0 158.1 jit_solution(13542730140563740397)
XLA Ops:
  0.6 0.8 copy-done.14
  1.5 0.8 copy-done.17
  2.2 0.7 copy-done.21
  3.0 0.7 copy-done.25
  3.6 1.3 shard_map.84
  4.9 0.0 copy-start.9
  4.9 0.0 copy-start.13
  4.9 17.6 %all_to_all.25 = bf16[8,136,128]{2,1,0:T(8,128)(2,1)S(1)} all-to-all(bf16[8,136,128]{2,1,0:T(8,128)(2,1)S(1)} %get-tuple-element.19), channel_id=1, replica_groups={{4,68,132,196,260,324,388,452},{5,69,133,197,261,325,389,453},{6,70,134..., dimensions={0} | all-to-all | bytes 557056 | tf_op jit(solution)/shard_map/all_to_all | solution.py:39
  22.5 1.7 %broadcast_in_dim.2 = bf16[8,8,136,128]{3,2,1,0:T(8,128)(2,1)} broadcast(bf16[8,136,128]{2,1,0:T(8,128)(2,1)S(1)} %all_to_all.25), dimensions={1,2,3} | broadcast | bytes 2506752 | tf_op jit(solution)/shard_map/broadcast_in_dim | solution.py:277
  24.2 10.4 %all-to-all-start.1 = ((bf16[8,8,136,128]{3,2,1,0:T(8,128)(2,1)}), bf16[8,8,136,128]{3,2,1,0:T(8,128)(2,1)S(1)}, u32[]{:S(2)}, u32[]{:S(2)}) async-start(bf16[8,8,136,128]{3,2,1,0:T(8,128)(2,1)} %broadcast_in_dim.2), calls=%async_computation.1 | async-start | bytes 4456448 | tf_op jit(solution)/shard_map/all_to_all | solution.py:39
  34.6 0.4 shard_map.85.own_rows
  35.0 1.9 %collective-permute-start = (bf16[32,64,128]{2,1,0:T(8,128)(2,1)S(1)}, bf16[32,64,128]{2,1,0:T(8,128)(2,1)S(1)}, u32[]{:S(2)}, u32[]{:S(2)}) collective-permute-start(bf16[32,64,128]{2,1,0:T(8,128)(2,1)S(1)} %shard_map.85.own_rows), channel_id=1, source_target_pairs={{0,4},{4,0},{8,12},{12,8},{16,20},{20,16},{24,28},{28,24},{32,36},... | collective-permute-start | bytes 1572872 | tf_op jit(solution)/shard_map/ppermute | solution.py:280
  37.0 12.5 %all_gather.3.gathered = bf16[16,64,128]{2,1,0:T(8,128)(2,1)S(1)} all-gather(bf16[4,64,128]{2,1,0:T(8,128)(2,1)} %copy-done.13), channel_id=1, replica_groups=mesh['dp'=128,'group'=4] {'group'}, dimensions={0}, use_global_device_ids=true | all-gather | bytes 327680 | tf_op jit(solution)/shard_map/all_gather | solution.py:281
  49.4 0.8 copy-done.10
  50.2 0.5 shard_map.86.pos_weight
  50.7 0.0 copy-start.26
  50.7 0.5 copy-done.26
  51.2 0.7 pad_add_fusion.me
  51.9 0.0 collective-permute-done.other_rows
  51.9 14.4 %all-to-all-done.1 = bf16[8,8,136,128]{3,2,1,0:T(8,128)(2,1)S(1)} async-done(((bf16[8,8,136,128]{3,2,1,0:T(8,128)(2,1)}), bf16[8,8,136,128]{3,2,1,0:T(8,128)(2,1)S(1)}, u32[]{:S(2)}, u32[]{:S(2)}) %all-to-all-start.1) | async-done | bytes 2228256 | tf_op jit(solution)/shard_map/all_to_all | solution.py:39
  66.3 0.7 copy-done.22
  67.0 0.6 copy-done.27
  67.6 8.0 %shard_map.87 = (bf16[64,64,128]{2,1,0:T(8,128)(2,1)S(1)}, f32[64,4,128]{2,1,0:T(4,128)S(1)}, s32[8,512]{1,0:T(8,128)S(1)}) custom-call(s32[4]{0:T(128)S(1)} %copy-done.22, bf16[64,136,128]{2,1,0:T(8,128)(2,1)S(1)} %bitcast.6, bf16[32,64,128]{2,1,0:T(8,128)(2,1)S(1)} %shard_map.85.own_rows, bf16[32,64,128]{2,1,0:T(8,128)(2,1)S(1)} %collective-permute-done.other_rows, ...), custom_call_target="tpu_custom_call" | custom-call | tf_op jit(solution)/shard_map/pallas_call | solution.py:284
  75.6 1.0 copy-done.1
  76.6 0.7 copy-done.12
  77.3 5.5 %all-to-all-start.2 = ((f32[64,4,128]{2,1,0:T(4,128)}), f32[64,4,128]{2,1,0:T(4,128)}, u32[]{:S(2)}, u32[]{:S(2)}) async-start(f32[64,4,128]{2,1,0:T(4,128)} %copy-done.12), calls=%async_computation.2 | async-start | bytes 262144 | tf_op jit(solution)/shard_map/all_to_all | solution.py:39
  82.8 1.2 copy-done.2
  84.0 5.6 %shard_map.89 = bf16[64,128,128]{2,1,0:T(8,128)(2,1)S(1)} custom-call(s32[8,512]{1,0:T(8,128)S(1)} %get-tuple-element.22.codes, bf16[32,64,128]{2,1,0:T(8,128)(2,1)S(1)} %shard_map.85.own_rows, bf16[32,64,128]{2,1,0:T(8,128)(2,1)S(1)} %collective-permute-done.other_rows, bf16[64,64,128]{2,1,0:T(8,128)(2,1)S(1)} %copy-done.2), custom_call_target="tpu_custom_call" | custom-call | tf_op jit(solution)/shard_map/pallas_call | solution.py:301
  89.5 1.3 copy-done
  90.9 4.4 %all-to-all-done.2 = f32[64,4,128]{2,1,0:T(4,128)} async-done(((f32[64,4,128]{2,1,0:T(4,128)}), f32[64,4,128]{2,1,0:T(4,128)}, u32[]{:S(2)}, u32[]{:S(2)}) %all-to-all-start.2) | async-done | bytes 131104 | tf_op jit(solution)/shard_map/all_to_all | solution.py:39
  95.3 4.3 %all-to-all-start.3 = ((bf16[8,8,128,128]{3,2,1,0:T(8,128)(2,1)}), bf16[8,8,128,128]{3,2,1,0:T(8,128)(2,1)}, u32[]{:S(2)}, u32[]{:S(2)}) async-start(bf16[8,8,128,128]{3,2,1,0:T(8,128)(2,1)} %bitcast.8), calls=%async_computation.3 | async-start | bytes 4194304 | tf_op jit(solution)/shard_map/all_to_all | solution.py:39
  99.6 1.6 reduce_sum.9.weight_sum
  101.2 0.7 broadcast_divide_fusion.weight_inv
  101.9 0.8 copy-done.11
  102.6 0.7 copy-done.20
  103.3 0.7 copy-done.23
  104.0 6.9 %shard_map.88 = (f32[32,64,128]{2,1,0:T(8,128)S(1)}, bf16[32,64,128]{2,1,0:T(8,128)(2,1)}, f32[16,64,128]{2,1,0:T(8,128)S(1)}, f32[128,128]{1,0:T(8,128)S(1)}, f32[1,128]{1,0:T(1,128)S(1)}) custom-call(s32[4]{0:T(128)S(1)} %copy-done.23, s32[8,512]{1,0:T(8,128)S(1)} %get-tuple-element.22.codes, f32[4,128]{1,0:T(4,128)S(1)} %copy-done.20, ...), custom_call_target="tpu_custom_call" | custom-call | tf_op jit(solution)/shard_map/pallas_call | solution.py:308
  110.9 1.0 copy-done.4
  111.9 0.8 copy-done.6
  112.8 0.6 copy-done.15
  113.4 0.5 copy-done.28
  113.9 2.0 %collective-permute-start.1 = (bf16[32,64,128]{2,1,0:T(8,128)(2,1)}, bf16[32,64,128]{2,1,0:T(8,128)(2,1)}, u32[]{:S(2)}, u32[]{:S(2)}) collective-permute-start(bf16[32,64,128]{2,1,0:T(8,128)(2,1)} %get-tuple-element.28), channel_id=1, source_target_pairs={{0,4},{4,0},{8,12},{12,8},{16,20},{20,16},{24,28},{28,24},{32,36},... | collective-permute-start | bytes 1572872 | tf_op jit(solution)/shard_map/ppermute | solution.py:328
  115.9 0.0 copy-start.29
  116.0 14.0 %all-to-all-done.3.arrived = bf16[8,8,128,128]{3,2,1,0:T(8,128)(2,1)} async-done(((bf16[8,8,128,128]{3,2,1,0:T(8,128)(2,1)}), bf16[8,8,128,128]{3,2,1,0:T(8,128)(2,1)}, u32[]{:S(2)}, u32[]{:S(2)}) %all-to-all-start.3) | async-done | bytes 2097184 | tf_op jit(solution)/shard_map/all_to_all | solution.py:39
  129.9 2.6 %shard_map.90 = bf16[8,128,128]{2,1,0:T(8,128)(2,1)} custom-call(bf16[8,8,128,128]{3,2,1,0:T(8,128)(2,1)} %all-to-all-done.3.arrived), custom_call_target="tpu_custom_call" | custom-call | tf_op jit(solution)/shard_map/pallas_call | solution.py:305
  132.5 5.1 %all-to-all-start.4 = ((bf16[8,128,128]{2,1,0:T(8,128)(2,1)}), bf16[8,128,128]{2,1,0:T(8,128)(2,1)S(1)}, u32[]{:S(2)}, u32[]{:S(2)}) async-start(bf16[8,128,128]{2,1,0:T(8,128)(2,1)} %shard_map.90), calls=%async_computation.4 | async-start | bytes 524288 | tf_op jit(solution)/shard_map/all_to_all | solution.py:39
  137.5 0.0 collective-permute-done.1.moved
  137.6 1.0 copy-done.7
  138.6 1.2 shard_map.92
  139.8 2.4 %collective-permute-start.2 = (bf16[12,64,128]{2,1,0:T(8,128)(2,1)S(1)}, bf16[12,64,128]{2,1,0:T(8,128)(2,1)S(1)}, u32[]{:S(2)}, u32[]{:S(2)}) collective-permute-start(bf16[12,64,128]{2,1,0:T(8,128)(2,1)S(1)} %get-tuple-element.31), channel_id=1, source_target_pairs={{0,1},{1,2},{2,3},{3,0},{4,5},{5,6},{6,7},{7,4},{8,9},{9,10},{10,1... | collective-permute-start | bytes 589832 | tf_op jit(solution)/shard_map/ppermute | solution.py:331
  142.2 4.3 %collective-permute-start.3 = (bf16[12,64,128]{2,1,0:T(8,128)(2,1)S(1)}, bf16[12,64,128]{2,1,0:T(8,128)(2,1)S(1)}, u32[]{:S(2)}, u32[]{:S(2)}) collective-permute-start(bf16[12,64,128]{2,1,0:T(8,128)(2,1)S(1)} %get-tuple-element.32), channel_id=1, source_target_pairs={{0,2},{1,3},{2,0},{3,1},{4,6},{5,7},{6,4},{7,5},{8,10},{9,11},{10,... | collective-permute-start | bytes 589832 | tf_op jit(solution)/shard_map/ppermute | solution.py:331
  146.6 1.9 %collective-permute-start.4 = (bf16[12,64,128]{2,1,0:T(8,128)(2,1)S(1)}, bf16[12,64,128]{2,1,0:T(8,128)(2,1)S(1)}, u32[]{:S(2)}, u32[]{:S(2)}) collective-permute-start(bf16[12,64,128]{2,1,0:T(8,128)(2,1)S(1)} %get-tuple-element.33), channel_id=1, source_target_pairs={{0,3},{1,0},{2,1},{3,2},{4,7},{5,4},{6,5},{7,6},{8,11},{9,8},{10,9... | collective-permute-start | bytes 589832 | tf_op jit(solution)/shard_map/ppermute | solution.py:331
  148.5 0.5 broadcast.9
  149.0 0.7 reduce.5
  149.7 0.1 reshape.19
  149.7 0.6 slice_reduce_fusion
  150.4 0.0 collective-permute-done.2
  150.4 0.9 collective-permute-done.3
  151.3 4.0 %collective-permute-done.4 = bf16[12,64,128]{2,1,0:T(8,128)(2,1)S(1)} collective-permute-done((bf16[12,64,128]{2,1,0:T(8,128)(2,1)S(1)}, bf16[12,64,128]{2,1,0:T(8,128)(2,1)S(1)}, u32[]{:S(2)}, u32[]{:S(2)}) %collective-permute-start.4) | collective-permute-done | bytes 196640 | tf_op jit(solution)/shard_map/ppermute | solution.py:331
  155.3 0.1 convert_add_fusion
  155.4 0.7 slice.13
  156.1 0.7 slice.12
  156.8 0.0 all-to-all-done.4.arrived
  156.8 1.2 shard_map.91
  (36 shorter events, 0.1 us)
Async XLA Ops:
  0.6 0.8 copy-start.14
  1.5 0.8 copy-start.17
  2.2 0.7 copy-start.21
  2.9 0.7 copy-start.25
  4.9 19.3 %copy-start.9 = (bf16[4,32,128]{2,1,0:T(8,128)(2,1)}, bf16[4,32,128]{2,1,0:T(8,128)(2,1)S(1)}, u32[]{:S(2)}) copy-start(bf16[4,32,128]{2,1,0:T(8,128)(2,1)S(1)} %get-tuple-element.20.q_tiles) | copy-start | bytes 98308
  4.9 19.3 %copy-start.13 = (bf16[4,64,128]{2,1,0:T(8,128)(2,1)}, bf16[4,64,128]{2,1,0:T(8,128)(2,1)S(1)}, u32[]{:S(2)}) copy-start(bf16[4,64,128]{2,1,0:T(8,128)(2,1)S(1)} %get-tuple-element.21) | copy-start | bytes 196612
  24.2 10.5 %copy-start.8 = (bf16[32,64,128]{2,1,0:T(8,128)(2,1)S(1)}, bf16[32,64,128]{2,1,0:T(8,128)(2,1)}, u32[]{:S(2)}) copy-start(bf16[32,64,128]{2,1,0:T(8,128)(2,1)} %values.1) | copy-start | bytes 1572868
  24.2 42.1 %all-to-all-start.1 = ((bf16[8,8,136,128]{3,2,1,0:T(8,128)(2,1)}), bf16[8,8,136,128]{3,2,1,0:T(8,128)(2,1)S(1)}, u32[]{:S(2)}, u32[]{:S(2)}) async-start(bf16[8,8,136,128]{3,2,1,0:T(8,128)(2,1)} %broadcast_in_dim.2), calls=%async_computation.1 | async-start | bytes 4456448 | tf_op jit(solution)/shard_map/all_to_all | solution.py:39
  35.0 16.9 %collective-permute-start = (bf16[32,64,128]{2,1,0:T(8,128)(2,1)S(1)}, bf16[32,64,128]{2,1,0:T(8,128)(2,1)S(1)}, u32[]{:S(2)}, u32[]{:S(2)}) collective-permute-start(bf16[32,64,128]{2,1,0:T(8,128)(2,1)S(1)} %shard_map.85.own_rows), channel_id=1, source_target_pairs={{0,4},{4,0},{8,12},{12,8},{16,20},{20,16},{24,28},{28,24},{32,36},... | collective-permute-start | bytes 1572872 | tf_op jit(solution)/shard_map/ppermute | solution.py:280
  49.4 0.8 copy-start.10
  50.7 0.5 copy-start.26
  66.3 0.7 copy-start.22
  67.0 0.6 copy-start.27
  75.6 1.0 copy-start.1
  76.6 0.7 copy-start.12
  77.3 18.0 %all-to-all-start.2 = ((f32[64,4,128]{2,1,0:T(4,128)}), f32[64,4,128]{2,1,0:T(4,128)}, u32[]{:S(2)}, u32[]{:S(2)}) async-start(f32[64,4,128]{2,1,0:T(4,128)} %copy-done.12), calls=%async_computation.2 | async-start | bytes 262144 | tf_op jit(solution)/shard_map/all_to_all | solution.py:39
  82.8 1.2 copy-start.2
  89.5 1.3 copy-start
  90.9 11.0 %copy-start.3 = (bf16[64,64,128]{2,1,0:T(8,128)(2,1)S(1)}, bf16[64,64,128]{2,1,0:T(8,128)(2,1)}, u32[]{:S(2)}) copy-start(bf16[64,64,128]{2,1,0:T(8,128)(2,1)} %copy-done.1) | copy-start | bytes 3145732
  95.3 34.6 %all-to-all-start.3 = ((bf16[8,8,128,128]{3,2,1,0:T(8,128)(2,1)}), bf16[8,8,128,128]{3,2,1,0:T(8,128)(2,1)}, u32[]{:S(2)}, u32[]{:S(2)}) async-start(bf16[8,8,128,128]{3,2,1,0:T(8,128)(2,1)} %bitcast.8), calls=%async_computation.3 | async-start | bytes 4194304 | tf_op jit(solution)/shard_map/all_to_all | solution.py:39
  101.9 0.8 copy-start.11
  102.6 0.7 copy-start.20
  103.3 0.7 copy-start.23
  104.0 6.9 %copy-start.18 = (f32[4,128]{1,0:T(4,128)}, f32[4,128]{1,0:T(4,128)S(1)}, u32[]{:S(2)}) copy-start(f32[4,128]{1,0:T(4,128)S(1)} %broadcast_divide_fusion.weight_inv) | copy-start | bytes 6148
  110.9 1.0 copy-start.4
  111.9 0.8 copy-start.6
  112.7 0.6 copy-start.15
  113.4 0.5 copy-start.28
  113.4 24.2 %copy-start.24 = (s32[4]{0:T(128)S(1)}, s32[4]{0:T(128)}, u32[]{:S(2)}) copy-start(s32[4]{0:T(128)} %pad_add_fusion.me) | copy-start | bytes 52
  113.9 23.7 %copy-start.5 = (f32[32,64,128]{2,1,0:T(8,128)S(1)}, f32[32,64,128]{2,1,0:T(8,128)}, u32[]{:S(2)}) copy-start(f32[32,64,128]{2,1,0:T(8,128)} %copy-done.4) | copy-start | bytes 3145732
  113.9 23.7 %collective-permute-start.1 = (bf16[32,64,128]{2,1,0:T(8,128)(2,1)}, bf16[32,64,128]{2,1,0:T(8,128)(2,1)}, u32[]{:S(2)}, u32[]{:S(2)}) collective-permute-start(bf16[32,64,128]{2,1,0:T(8,128)(2,1)} %get-tuple-element.28), channel_id=1, source_target_pairs={{0,4},{4,0},{8,12},{12,8},{16,20},{20,16},{24,28},{28,24},{32,36},... | collective-permute-start | bytes 1572872 | tf_op jit(solution)/shard_map/ppermute | solution.py:328
  115.9 33.1 %copy-start.29 = (f32[1,128]{1,0:T(1,128)S(1)}, f32[1,128]{1,0:T(1,128)}, u32[]{:S(2)}) copy-start(f32[1,128]{1,0:T(1,128)} %copy-done.28) | copy-start | bytes 1540
  132.5 24.3 %copy-start.16 = (f32[128,128]{1,0:T(8,128)S(1)}, f32[128,128]{1,0:T(8,128)}, u32[]{:S(2)}) copy-start(f32[128,128]{1,0:T(8,128)} %copy-done.15) | copy-start | bytes 196612
  132.5 24.3 %all-to-all-start.4 = ((bf16[8,128,128]{2,1,0:T(8,128)(2,1)}), bf16[8,128,128]{2,1,0:T(8,128)(2,1)S(1)}, u32[]{:S(2)}, u32[]{:S(2)}) async-start(bf16[8,128,128]{2,1,0:T(8,128)(2,1)} %shard_map.90), calls=%async_computation.4 | async-start | bytes 524288 | tf_op jit(solution)/shard_map/all_to_all | solution.py:39
  137.5 19.3 %copy-start.19 = (f32[4,128]{1,0:T(4,128)S(1)}, f32[4,128]{1,0:T(4,128)}, u32[]{:S(2)}) copy-start(f32[4,128]{1,0:T(4,128)} %copy-done.18) | copy-start | bytes 6148
  137.6 1.0 copy-start.7
  139.8 10.6 %collective-permute-start.2 = (bf16[12,64,128]{2,1,0:T(8,128)(2,1)S(1)}, bf16[12,64,128]{2,1,0:T(8,128)(2,1)S(1)}, u32[]{:S(2)}, u32[]{:S(2)}) collective-permute-start(bf16[12,64,128]{2,1,0:T(8,128)(2,1)S(1)} %get-tuple-element.31), channel_id=1, source_target_pairs={{0,1},{1,2},{2,3},{3,0},{4,5},{5,6},{6,7},{7,4},{8,9},{9,10},{10,1... | collective-permute-start | bytes 589832 | tf_op jit(solution)/shard_map/ppermute | solution.py:331
  142.2 9.1 %collective-permute-start.3 = (bf16[12,64,128]{2,1,0:T(8,128)(2,1)S(1)}, bf16[12,64,128]{2,1,0:T(8,128)(2,1)S(1)}, u32[]{:S(2)}, u32[]{:S(2)}) collective-permute-start(bf16[12,64,128]{2,1,0:T(8,128)(2,1)S(1)} %get-tuple-element.32), channel_id=1, source_target_pairs={{0,2},{1,3},{2,0},{3,1},{4,6},{5,7},{6,4},{7,5},{8,10},{9,11},{10,... | collective-permute-start | bytes 589832 | tf_op jit(solution)/shard_map/ppermute | solution.py:331
  146.6 8.8 %collective-permute-start.4 = (bf16[12,64,128]{2,1,0:T(8,128)(2,1)S(1)}, bf16[12,64,128]{2,1,0:T(8,128)(2,1)S(1)}, u32[]{:S(2)}, u32[]{:S(2)}) collective-permute-start(bf16[12,64,128]{2,1,0:T(8,128)(2,1)S(1)} %get-tuple-element.33), channel_id=1, source_target_pairs={{0,3},{1,0},{2,1},{3,2},{4,7},{5,4},{6,5},{7,6},{8,11},{9,8},{10,9... | collective-permute-start | bytes 589832 | tf_op jit(solution)/shard_map/ppermute | solution.py:331

commit v5 on v4

--- a/solution.py
+++ b/solution.py
@@ -13,6 +13,7 @@
 SENT = QROWS + 8
 BATCH = QD * GROUP
 SLOTS = 4
+CHUNKS = 8
 VMEM = 48 * 1024 * 1024
 F32, BF16, I32 = jnp.float32, jnp.bfloat16, jnp.int32
 EXACT = lax.Precision.HIGHEST
@@ -54,6 +55,10 @@
     return pl.BlockSpec(memory_space=pltpu.VMEM)
 
 
+def anywhere():
+    return pl.BlockSpec(memory_space=pl.ANY)
+
+
 def smem():
     return pl.BlockSpec(memory_space=pltpu.SMEM)
 
@@ -75,7 +80,17 @@
     return (iota((QROWS, QROWS), 0) // QT == iota((QROWS, QROWS), 1) // QT).astype(F32)
 
 
-def prepare(ids, storage, queries, positives, sent, q_unit, pos_unit, count):
+def fetch(pairs, sems):
+    copies = [pltpu.make_async_copy(src, dst, sems.at[i]) for i, (src, dst) in enumerate(pairs)]
+    for copy in copies:
+        copy.start()
+    return copies
+
+
+def prepare(ids_in, storage_in, queries_in, positives_in, sent, q_unit, pos_unit, ids, storage, queries, positives, sems, count):
+    pairs = [(storage_in, storage), (ids_in, ids), (queries_in, queries), (positives_in, positives)]
+    for copy in fetch(pairs, sems):
+        copy.wait()
     tiles = unit(queries[...])
     q_unit[...] = tiles
     pos_unit[...] = unit(positives[...])
@@ -148,8 +163,8 @@
     copy.wait()
 
 
-def score(me, asked, own_rows, other_rows, pos_weight, probs, sums, codes, exps, totals, marks, factor, table, sem):
-    read_codes(me, asked, codes, table, sem)
+def score(me, asked, own_rows, other_rows, pos_weight, exps_out, factor, sums, codes, exps, totals, marks, table, sems):
+    read_codes(me, asked, codes, table, sems.at[CHUNKS])
     lane = iota((1, QROWS), 1)
     block = iota((PT, QROWS), 1) // QT
 
@@ -168,7 +183,13 @@
         marks[pl.ds(source, 1), :] = mark
         return carry
 
-    lax.fori_loop(0, SPOTS, one, 0, unroll=4)
+    size = SPOTS // CHUNKS
+    copies = []
+    for chunk in range(CHUNKS):
+        lax.fori_loop(chunk * size, (chunk + 1) * size, one, 0, unroll=4)
+        part = pl.ds(chunk * size, size)
+        copies.append(pltpu.make_async_copy(exps.at[part], exps_out.at[part], sems.at[chunk]))
+        copies[-1].start()
 
     total = totals[...]
     mark = marks[...]
@@ -185,17 +206,15 @@
         own = jnp.sum(jnp.where(lane == q * QT, pos_weight[...], 0.0), axis=1, keepdims=True)
         parts.append(part + jnp.where(lane == me[0], own, 0.0))
     sums[...] = jnp.broadcast_to(jnp.concatenate(parts, axis=0)[None], (SPOTS, QD, QROWS))
-
-    def scale(source, carry):
-        probs[source] = (exps[source] * factor[pl.ds(source, 1), :]).astype(BF16)
-        return carry
-
-    lax.fori_loop(0, SPOTS, scale, 0, unroll=4)
-
-
-def terms(codes, own_rows, other_rows, probs, back):
+    for copy in copies:
+        copy.wait()
+
+
+def terms(codes, own_rows, other_rows, exps, factor, probs, back):
     def one(source, carry):
-        grads = dot(spread(probs[source].astype(F32)), passages(codes, own_rows, other_rows, source), ((0,), (0,)))
+        packed = exps[source] * factor[pl.ds(source, 1), :]
+        probs[source] = packed.astype(BF16)
+        grads = dot(spread(packed), passages(codes, own_rows, other_rows, source), ((0,), (0,)))
         picked = [request(codes, source, slot)[1] for slot in range(SLOTS)]
         for q in range(QD):
             total = jnp.zeros((QT, D), F32)
@@ -207,9 +226,19 @@
     lax.fori_loop(0, SPOTS, one, 0, unroll=4)
 
 
-def weigh(me, codes, weight_sum, weight_inv, asked, probs, q_tiles, gathered, own_grad, other_grad, pos_grad, query_part, losses, other_acc):
+def weigh(
+    me, codes, sums, asked, probs, q_in, gathered_in, own_grad, other_grad, pos_grad, query_part, losses, weight_inv,
+    other_acc, inverse, q_tiles, gathered, sems,
+):
+    later = fetch([(q_in, q_tiles), (gathered_in, gathered)], sems)
+    weight_sum = jnp.sum(sums[...], axis=0)
+    inverse[...] = jnp.zeros_like(inverse)
+    inverse[0:QD] = 1.0 / weight_sum
+    copy = pltpu.make_async_copy(inverse, weight_inv, sems.at[2])
+    copy.start()
     own_grad[...] = jnp.zeros_like(own_grad)
     other_acc[...] = jnp.zeros_like(other_acc)
+    copy.wait()
 
     def add(source, carry):
         grads = dot(spread(probs[source].astype(F32)), asking(codes, asked, source), ((1,), (0,)))
@@ -222,12 +251,15 @@
     lax.fori_loop(0, SPOTS, add, 0, unroll=4)
     other_grad[...] = other_acc[...].astype(BF16)
 
+    for copy in later:
+        copy.wait()
     q_unit = q_tiles[...].reshape(QROWS, D)
     cands, exp_scores, total, scores = positive_scores(q_unit, gathered)
     lane = iota((1, QROWS), 1)
+    mine = jnp.sum(jnp.where(lane == me[0], weight_sum, 0.0), axis=1, keepdims=True)
     own_sum = jnp.zeros((1, QROWS), F32)
     for q in range(QD):
-        own_sum = jnp.where(lane // QT == q, weight_sum[q, me[0]], own_sum)
+        own_sum = jnp.where(lane // QT == q, mine[q : q + 1], own_sum)
     own = (iota((BATCH, QROWS), 0) == me[1] * QD + iota((BATCH, QROWS), 1) // QT).astype(F32)
     score_grad = jnp.exp(scores) / own_sum - own
     losses[...] = jnp.log(own_sum) - jnp.sum(scores * own, axis=0, keepdims=True)
@@ -245,7 +277,8 @@
         out[QD:] = (own_grad[rows] + moved[rows].astype(F32)).astype(out.dtype)
 
 
-def add_blocks(arrived, out):
+def add_blocks(arrived, after, out):
+    del after
     out[...] = jnp.sum(arrived[...].astype(F32), axis=0).astype(BF16)
 
 
@@ -269,9 +302,16 @@
     sent, q_unit, pos_unit = call(
         prepare,
         (struct((N_Y, SENT, D), BF16), tiles, struct((QD, PT, D), BF16)),
-        [smem(), smem(), vmem(), vmem()],
+        [anywhere()] * 4,
         (vmem(), vmem(), vmem()),
-        [pltpu.SMEM((N_DP,), I32)],
+        [
+            pltpu.SMEM(negative_ids.shape, I32),
+            pltpu.SMEM(storage_row.shape, I32),
+            pltpu.VMEM((QD, QT, D), BF16),
+            pltpu.VMEM((QD, PT, D), BF16),
+            pltpu.SemaphoreType.DMA((4,)),
+            pltpu.SMEM((N_DP,), I32),
+        ],
     )(negative_ids, storage_row, queries, positives)
     asked = exchange(sent, along(1))
     asked = exchange(jnp.broadcast_to(asked[None], (N_Z, N_Y, SENT, D)), along(0)).reshape(SPOTS, SENT, D)
@@ -281,31 +321,35 @@
     gathered = lax.all_gather(pos_unit, "group", axis=0, tiled=True)
     pos_weight = call(positive_weight, struct((1, QROWS), F32), [vmem(), vmem()], vmem())(q_unit, gathered)
 
-    probs, sums, codes = call(
+    exps, factor, sums, codes = call(
         score,
-        (struct((SPOTS, PT, QROWS), BF16), struct((SPOTS, QD, QROWS), F32), struct((8, SPOTS * 8), I32)),
+        (
+            struct((SPOTS, PT, QROWS), F32),
+            struct((SPOTS, QROWS), F32),
+            struct((SPOTS, QD, QROWS), F32),
+            struct((8, SPOTS * 8), I32),
+        ),
         [smem(), vmem(), vmem(), vmem(), vmem()],
-        (vmem(), vmem(), smem()),
+        (anywhere(), vmem(), vmem(), smem()),
         [
             pltpu.VMEM((SPOTS, PT, QROWS), F32),
             pltpu.VMEM((SPOTS, QROWS), F32),
             pltpu.VMEM((SPOTS, QROWS), F32),
-            pltpu.VMEM((SPOTS, QROWS), F32),
             pltpu.VMEM((8, SPOTS * 8), I32),
-            pltpu.SemaphoreType.DMA,
+            pltpu.SemaphoreType.DMA((CHUNKS + 1,)),
         ],
     )(me, asked, own_rows, other_rows, pos_weight)
-    weight_sum = jnp.sum(exchange(sums, planes()), axis=0)
-    weight_inv = 1.0 / weight_sum
-
-    back = call(
-        terms, struct((SPOTS, QROWS, D), BF16), [smem(), vmem(), vmem(), vmem()], vmem()
-    )(codes, own_rows, other_rows, probs)
+    sums = exchange(sums, planes())
+
+    probs, back = call(
+        terms,
+        (struct((SPOTS, PT, QROWS), BF16), struct((SPOTS, QROWS, D), BF16)),
+        [smem()] + [vmem()] * 4,
+        (vmem(), vmem()),
+    )(codes, own_rows, other_rows, exps, factor)
     arrived = exchange(back.reshape(N_Z, N_Y, QROWS, D), along(0))
-    arrived = call(add_blocks, struct((N_Y, QROWS, D), BF16), [vmem()], vmem())(arrived)
-    arrived = exchange(arrived, along(1))
-
-    own_grad, other_grad, pos_grad, query_part, losses = call(
+
+    own_grad, other_grad, pos_grad, query_part, losses, weight_inv = call(
         weigh,
         (
             struct((ROWS, PT, D), F32),
@@ -313,11 +357,18 @@
             struct((BATCH, PT, D), F32),
             struct((QROWS, D), F32),
             struct((1, QROWS), F32),
+            struct((8, QROWS), F32),
         ),
-        [smem(), smem(), smem(), smem(), vmem(), vmem(), vmem(), vmem()],
-        (vmem(),) * 5,
-        [pltpu.VMEM((ROWS, PT, D), F32)],
-    )(me, codes, weight_sum, weight_inv, asked, probs, q_unit, gathered)
+        [smem(), smem(), vmem(), vmem(), vmem(), anywhere(), anywhere()],
+        (vmem(),) * 5 + (smem(),),
+        [
+            pltpu.VMEM((ROWS, PT, D), F32),
+            pltpu.VMEM((8, QROWS), F32),
+            pltpu.VMEM((QD, QT, D), BF16),
+            pltpu.VMEM((BATCH, PT, D), BF16),
+            pltpu.SemaphoreType.DMA((3,)),
+        ],
+    )(me, codes, sums, asked, probs, q_unit, gathered)
 
     block = (QD + ROWS // GROUP, PT, D)
     kept, off1, off2, off3 = call(
@@ -331,6 +382,8 @@
         moved = lax.ppermute(part, "group", [(g, (g + ahead) % GROUP) for g in range(GROUP)])
         total = total + moved.astype(F32)
 
+    arrived = call(add_blocks, struct((N_Y, QROWS, D), BF16), [vmem(), anywhere()], vmem())(arrived, total)
+    arrived = exchange(arrived, along(1))
     query_grad = call(
         collect, struct((QD, QT, D), F32), [smem(), smem(), vmem(), vmem()], vmem()
     )(weight_inv, me, query_part, arrived)

time: 160 us -> 155 us (0.969)
  the two profiles are of different devices: /device:TPU:6 before, /device:TPU:1 now
where the time goes in v5:
time: 155 us; the launch traced here: 154 us
  starting transfers between devices  43.6 us (28%)
  waiting for transfers between devices  32.1 us (21%)
  blocking collectives  31 us (20%)
  Pallas kernels  28.1 us (18%)
  local copies, waits for them, and re-layouts  16.7 us (11%)
    all_to_all x4, starting transfers between devices, exchange(): lax.all_to_all(blocks, EVERY, split_axis=0, concat_axis=0, axis_index_gro...  23.7 us
    all_to_all x4, waiting for transfers between devices, exchange(): lax.all_to_all(blocks, EVERY, split_axis=0, concat_axis=0, axis_index_gro...  21.2 us
    all_to_all x1, blocking collectives, exchange(): lax.all_to_all(blocks, EVERY, split_axis=0, concat_axis=0, axis_index_gro...  20.2 us
    unnamed x40, local copies, waits for them, and re-layouts  12.4 us
    all_gather x1, blocking collectives, per_device(): gathered = lax.all_gather(pos_unit, 'group', axis=0, tiled=True)  10.8 us
    ppermute x3, waiting for transfers between devices, per_device(): lax.ppermute(part, 'group', [(g, (g + ahead) % GROUP) for g in range(GROU...  9.35 us
    ppermute x3, starting transfers between devices, per_device(): lax.ppermute(part, 'group', [(g, (g + ahead) % GROUP) for g in range(GROU...  9.33 us
    pallas_call x1, Pallas kernels, per_device(): call(score, (struct((SPOTS, PT, QROWS), F32), struct((SPOTS, QROWS), F32)...  8.05 us
  transfers between devices with their start and end apart: 9, of which 7 were waited for; matrix products, arithmetic and copies ran while one was open for 3% of the time, Pallas kernels for 10%

profile of v5, /device:TPU:1, one launch (start us, length us, event | category | flops | bytes accessed | tf_op | source)
XLA Modules:
  0.0 153.7 jit_solution(12225452459176873408)
XLA Ops:
  0.6 0.0 copy-start.10
  0.6 0.8 copy-done.10
  1.5 0.8 copy-done.13
  2.2 0.7 copy-done.14
  3.0 0.7 copy-done.17
  3.6 1.3 shard_map.84
  5.0 0.0 copy-start.5
  5.0 0.0 copy-start.9
  5.0 20.2 %all_to_all.25 = bf16[8,136,128]{2,1,0:T(8,128)(2,1)S(1)} all-to-all(bf16[8,136,128]{2,1,0:T(8,128)(2,1)S(1)} %get-tuple-element.23), channel_id=1, replica_groups={{4,68,132,196,260,324,388,452},{5,69,133,197,261,325,389,453},{6,70,134..., dimensions={0} | all-to-all | bytes 557056 | tf_op jit(solution)/shard_map/all_to_all | solution.py:40
  25.2 1.7 %broadcast_in_dim.2 = bf16[8,8,136,128]{3,2,1,0:T(8,128)(2,1)} broadcast(bf16[8,136,128]{2,1,0:T(8,128)(2,1)S(1)} %all_to_all.25), dimensions={1,2,3} | broadcast | bytes 2506752 | tf_op jit(solution)/shard_map/broadcast_in_dim | solution.py:317
  26.8 0.0 copy-done.5
  26.8 0.0 copy-done.9
  26.8 7.0 %all-to-all-start.1 = ((bf16[8,8,136,128]{3,2,1,0:T(8,128)(2,1)}), bf16[8,8,136,128]{3,2,1,0:T(8,128)(2,1)S(1)}, u32[]{:S(2)}, u32[]{:S(2)}) async-start(bf16[8,8,136,128]{3,2,1,0:T(8,128)(2,1)} %broadcast_in_dim.2), calls=%async_computation.1 | async-start | bytes 4456448 | tf_op jit(solution)/shard_map/all_to_all | solution.py:40
  33.8 0.0 copy-done.4
  33.8 0.4 shard_map.85.own_rows
  34.2 4.3 %collective-permute-start = (bf16[32,64,128]{2,1,0:T(8,128)(2,1)S(1)}, bf16[32,64,128]{2,1,0:T(8,128)(2,1)S(1)}, u32[]{:S(2)}, u32[]{:S(2)}) collective-permute-start(bf16[32,64,128]{2,1,0:T(8,128)(2,1)S(1)} %shard_map.85.own_rows), channel_id=1, source_target_pairs={{0,4},{4,0},{8,12},{12,8},{16,20},{20,16},{24,28},{28,24},{32,36},... | collective-permute-start | bytes 1572872 | tf_op jit(solution)/shard_map/ppermute | solution.py:320
  38.5 10.8 %all_gather.3.gathered.gathered_in = bf16[16,64,128]{2,1,0:T(8,128)(2,1)S(1)} all-gather(bf16[4,64,128]{2,1,0:T(8,128)(2,1)} %copy-done.9), channel_id=1, replica_groups=mesh['dp'=128,'group'=4] {'group'}, dimensions={0}, use_global_device_ids=true | all-gather | bytes 327680 | tf_op jit(solution)/shard_map/all_gather | solution.py:321
  49.3 0.8 copy-done.6
  50.1 0.5 shard_map.86.pos_weight
  50.6 0.0 copy-start.18
  50.6 0.5 copy-done.18
  51.1 0.6 pad_add_fusion.me
  51.7 0.0 collective-permute-done.other_rows
  51.7 12.8 %all-to-all-done.1 = bf16[8,8,136,128]{3,2,1,0:T(8,128)(2,1)S(1)} async-done(((bf16[8,8,136,128]{3,2,1,0:T(8,128)(2,1)}), bf16[8,8,136,128]{3,2,1,0:T(8,128)(2,1)S(1)}, u32[]{:S(2)}, u32[]{:S(2)}) %all-to-all-start.1) | async-done | bytes 2228256 | tf_op jit(solution)/shard_map/all_to_all | solution.py:40
  64.5 0.6 copy-done.15
  65.2 0.6 copy-done.19
  65.8 8.1 %shard_map.87 = (f32[64,64,128]{2,1,0:T(8,128)S(1)}, f32[64,128]{1,0:T(8,128)S(1)}, f32[64,4,128]{2,1,0:T(4,128)S(1)}, s32[8,512]{1,0:T(8,128)S(1)}) custom-call(s32[4]{0:T(128)S(1)} %copy-done.15, bf16[64,136,128]{2,1,0:T(8,128)(2,1)S(1)} %bitcast.6, bf16[32,64,128]{2,1,0:T(8,128)(2,1)S(1)} %shard_map.85.own_rows, ...), custom_call_target="tpu_custom_call" | custom-call | tf_op jit(solution)/shard_map/pallas_call | solution.py:324
  73.8 0.0 copy-start
  73.8 1.4 copy-done
  75.2 0.7 copy-done.8
  75.8 0.6 copy-done.11
  76.5 5.5 %all-to-all-start.2 = ((f32[64,4,128]{2,1,0:T(4,128)}), f32[64,4,128]{2,1,0:T(4,128)}, u32[]{:S(2)}, u32[]{:S(2)}) async-start(f32[64,4,128]{2,1,0:T(4,128)} %copy-done.8), calls=%async_computation.2 | async-start | bytes 262144 | tf_op jit(solution)/shard_map/all_to_all | solution.py:40
  81.9 0.0 copy-start.12
  81.9 0.7 copy-done.12
  82.7 6.4 %shard_map.88 = (bf16[64,64,128]{2,1,0:T(8,128)(2,1)S(1)}, bf16[64,128,128]{2,1,0:T(8,128)(2,1)S(1)}) custom-call(s32[8,512]{1,0:T(8,128)S(1)} %get-tuple-element.26.codes, bf16[32,64,128]{2,1,0:T(8,128)(2,1)S(1)} %shard_map.85.own_rows, bf16[32,64,128]{2,1,0:T(8,128)(2,1)S(1)} %collective-permute-done.other_rows, f32[64,64,128]{2,1,0:T(8,128)} %copy-done, ...), custom_call_target="tpu_custom_call" | custom-call | tf_op jit(solution)/shard_map/pallas_call | solution.py:344
  89.1 0.0 copy-start.1
  89.1 1.3 copy-done.1
  90.4 1.0 copy-done.2
  91.4 2.0 %all-to-all-done.2.sums = f32[64,4,128]{2,1,0:T(4,128)} async-done(((f32[64,4,128]{2,1,0:T(4,128)}), f32[64,4,128]{2,1,0:T(4,128)}, u32[]{:S(2)}, u32[]{:S(2)}) %all-to-all-start.2) | async-done | bytes 131104 | tf_op jit(solution)/shard_map/all_to_all | solution.py:40
  93.4 4.5 %all-to-all-start.3 = ((bf16[8,8,128,128]{3,2,1,0:T(8,128)(2,1)}), bf16[8,8,128,128]{3,2,1,0:T(8,128)(2,1)}, u32[]{:S(2)}, u32[]{:S(2)}) async-start(bf16[8,8,128,128]{3,2,1,0:T(8,128)(2,1)} %bitcast.8), calls=%async_computation.3 | async-start | bytes 4194304 | tf_op jit(solution)/shard_map/all_to_all | solution.py:40
  97.9 0.0 copy-done.7
  97.9 1.2 copy-done.3
  99.1 7.0 %shard_map.89 = (f32[32,64,128]{2,1,0:T(8,128)S(1)}, bf16[32,64,128]{2,1,0:T(8,128)(2,1)S(1)}, f32[16,64,128]{2,1,0:T(8,128)S(1)}, f32[128,128]{1,0:T(8,128)S(1)...) custom-call(s32[4]{0:T(128)S(1)} %copy-done.16, s32[8,512]{1,0:T(8,128)S(1)} %get-tuple-element.26.codes, ...), custom_call_target="tpu_custom_call" | custom-call | tf_op jit(solution)/shard_map/pallas_call | solution.py:352
  106.1 6.3 %collective-permute-start.1 = (bf16[32,64,128]{2,1,0:T(8,128)(2,1)S(1)}, bf16[32,64,128]{2,1,0:T(8,128)(2,1)S(1)}, u32[]{:S(2)}, u32[]{:S(2)}) collective-permute-start(bf16[32,64,128]{2,1,0:T(8,128)(2,1)S(1)} %get-tuple-element.36), channel_id=1, source_target_pairs={{0,4},{4,0},{8,12},{12,8},{16,20},{20,16},{24,28},{28,24},{32,36},... | collective-permute-start | bytes 1572872 | tf_op jit(solution)/shard_map/ppermute | solution.py:379
  112.4 1.5 collective-permute-done.1.moved
  113.9 0.7 shard_map.90
  114.6 4.4 %collective-permute-start.4 = (bf16[12,64,128]{2,1,0:T(8,128)(2,1)S(1)}, bf16[12,64,128]{2,1,0:T(8,128)(2,1)S(1)}, u32[]{:S(2)}, u32[]{:S(2)}) collective-permute-start(bf16[12,64,128]{2,1,0:T(8,128)(2,1)S(1)} %get-tuple-element.41), channel_id=1, source_target_pairs={{0,3},{1,0},{2,1},{3,2},{4,7},{5,4},{6,5},{7,6},{8,11},{9,8},{10,9... | collective-permute-start | bytes 589832 | tf_op jit(solution)/shard_map/ppermute | solution.py:382
  119.0 2.4 %collective-permute-start.3 = (bf16[12,64,128]{2,1,0:T(8,128)(2,1)S(1)}, bf16[12,64,128]{2,1,0:T(8,128)(2,1)S(1)}, u32[]{:S(2)}, u32[]{:S(2)}) collective-permute-start(bf16[12,64,128]{2,1,0:T(8,128)(2,1)S(1)} %get-tuple-element.40), channel_id=1, source_target_pairs={{0,2},{1,3},{2,0},{3,1},{4,6},{5,7},{6,4},{7,5},{8,10},{9,11},{10,... | collective-permute-start | bytes 589832 | tf_op jit(solution)/shard_map/ppermute | solution.py:382
  121.4 2.5 %collective-permute-start.2 = (bf16[12,64,128]{2,1,0:T(8,128)(2,1)S(1)}, bf16[12,64,128]{2,1,0:T(8,128)(2,1)S(1)}, u32[]{:S(2)}, u32[]{:S(2)}) collective-permute-start(bf16[12,64,128]{2,1,0:T(8,128)(2,1)S(1)} %get-tuple-element.39), channel_id=1, source_target_pairs={{0,1},{1,2},{2,3},{3,0},{4,5},{5,6},{6,7},{7,4},{8,9},{9,10},{10,1... | collective-permute-start | bytes 589832 | tf_op jit(solution)/shard_map/ppermute | solution.py:382
  124.0 3.0 %collective-permute-done.4 = bf16[12,64,128]{2,1,0:T(8,128)(2,1)S(1)} collective-permute-done((bf16[12,64,128]{2,1,0:T(8,128)(2,1)S(1)}, bf16[12,64,128]{2,1,0:T(8,128)(2,1)S(1)}, u32[]{:S(2)}, u32[]{:S(2)}) %collective-permute-start.4) | collective-permute-done | bytes 196640 | tf_op jit(solution)/shard_map/ppermute | solution.py:382
  127.0 1.3 collective-permute-done.3
  128.3 5.0 %collective-permute-done.2 = bf16[12,64,128]{2,1,0:T(8,128)(2,1)S(1)} collective-permute-done((bf16[12,64,128]{2,1,0:T(8,128)(2,1)S(1)}, bf16[12,64,128]{2,1,0:T(8,128)(2,1)S(1)}, u32[]{:S(2)}, u32[]{:S(2)}) %collective-permute-start.2) | collective-permute-done | bytes 196640 | tf_op jit(solution)/shard_map/ppermute | solution.py:382
  133.3 0.1 convert_add_fusion.after
  133.4 0.0 all-to-all-done.3.arrived
  133.4 2.6 %shard_map.91 = bf16[8,128,128]{2,1,0:T(8,128)(2,1)} custom-call(bf16[8,8,128,128]{3,2,1,0:T(8,128)(2,1)} %all-to-all-done.3.arrived, f32[12,64,128]{2,1,0:T(8,128)S(1)} %convert_add_fusion.after), custom_call_target="tpu_custom_call" | custom-call | tf_op jit(solution)/shard_map/pallas_call | solution.py:385
  136.0 6.8 %all-to-all-start.4 = ((bf16[8,128,128]{2,1,0:T(8,128)(2,1)}), bf16[8,128,128]{2,1,0:T(8,128)(2,1)S(1)}, u32[]{:S(2)}, u32[]{:S(2)}) async-start(bf16[8,128,128]{2,1,0:T(8,128)(2,1)} %shard_map.91), calls=%async_computation.4 | async-start | bytes 524288 | tf_op jit(solution)/shard_map/all_to_all | solution.py:40
  142.8 0.5 broadcast.9
  143.3 0.7 reduce.5
  144.0 0.1 reshape.19
  144.1 0.6 slice_reduce_fusion
  144.7 0.7 slice.12
  145.3 0.7 slice.13
  146.1 6.4 %all-to-all-done.4.arrived = bf16[8,128,128]{2,1,0:T(8,128)(2,1)S(1)} async-done(((bf16[8,128,128]{2,1,0:T(8,128)(2,1)}), bf16[8,128,128]{2,1,0:T(8,128)(2,1)S(1)}, u32[]{:S(2)}, u32[]{:S(2)}) %all-to-all-start.4) | async-done | bytes 262176 | tf_op jit(solution)/shard_map/all_to_all | solution.py:40
  152.4 1.3 shard_map.92
  (14 shorter events, 0.0 us)
Async XLA Ops:
  0.6 0.8 copy-start.10
  1.5 0.8 copy-start.13
  2.2 0.7 copy-start.14
  2.9 0.7 copy-start.17
  5.0 21.9 %copy-start.5 = (bf16[4,32,128]{2,1,0:T(8,128)(2,1)}, bf16[4,32,128]{2,1,0:T(8,128)(2,1)S(1)}, u32[]{:S(2)}) copy-start(bf16[4,32,128]{2,1,0:T(8,128)(2,1)S(1)} %get-tuple-element.24.q_tiles.q_in) | copy-start | bytes 98308
  5.0 21.9 %copy-start.9 = (bf16[4,64,128]{2,1,0:T(8,128)(2,1)}, bf16[4,64,128]{2,1,0:T(8,128)(2,1)S(1)}, u32[]{:S(2)}) copy-start(bf16[4,64,128]{2,1,0:T(8,128)(2,1)S(1)} %get-tuple-element.25) | copy-start | bytes 196612
  26.8 7.0 %copy-start.4 = (bf16[32,64,128]{2,1,0:T(8,128)(2,1)S(1)}, bf16[32,64,128]{2,1,0:T(8,128)(2,1)}, u32[]{:S(2)}) copy-start(bf16[32,64,128]{2,1,0:T(8,128)(2,1)} %values.1) | copy-start | bytes 1572868
  26.8 37.7 %all-to-all-start.1 = ((bf16[8,8,136,128]{3,2,1,0:T(8,128)(2,1)}), bf16[8,8,136,128]{3,2,1,0:T(8,128)(2,1)S(1)}, u32[]{:S(2)}, u32[]{:S(2)}) async-start(bf16[8,8,136,128]{3,2,1,0:T(8,128)(2,1)} %broadcast_in_dim.2), calls=%async_computation.1 | async-start | bytes 4456448 | tf_op jit(solution)/shard_map/all_to_all | solution.py:40
  34.2 17.6 %collective-permute-start = (bf16[32,64,128]{2,1,0:T(8,128)(2,1)S(1)}, bf16[32,64,128]{2,1,0:T(8,128)(2,1)S(1)}, u32[]{:S(2)}, u32[]{:S(2)}) collective-permute-start(bf16[32,64,128]{2,1,0:T(8,128)(2,1)S(1)} %shard_map.85.own_rows), channel_id=1, source_target_pairs={{0,4},{4,0},{8,12},{12,8},{16,20},{20,16},{24,28},{28,24},{32,36},... | collective-permute-start | bytes 1572872 | tf_op jit(solution)/shard_map/ppermute | solution.py:320
  49.3 0.8 copy-start.6
  50.6 0.5 copy-start.18
  64.5 0.6 copy-start.15
  65.2 0.6 copy-start.19
  73.8 1.4 copy-start
  75.2 0.7 copy-start.8
  75.8 0.6 copy-start.11
  76.5 16.9 %all-to-all-start.2 = ((f32[64,4,128]{2,1,0:T(4,128)}), f32[64,4,128]{2,1,0:T(4,128)}, u32[]{:S(2)}, u32[]{:S(2)}) async-start(f32[64,4,128]{2,1,0:T(4,128)} %copy-done.8), calls=%async_computation.2 | async-start | bytes 262144 | tf_op jit(solution)/shard_map/all_to_all | solution.py:40
  81.9 0.8 copy-start.12
  89.1 1.3 copy-start.1
  90.4 1.0 copy-start.2
  93.4 4.5 %copy-start.7 = (bf16[4,32,128]{2,1,0:T(8,128)(2,1)S(1)}, bf16[4,32,128]{2,1,0:T(8,128)(2,1)}, u32[]{:S(2)}) copy-start(bf16[4,32,128]{2,1,0:T(8,128)(2,1)} %copy-done.5) | copy-start | bytes 98308
  93.4 4.5 %copy-start.16 = (s32[4]{0:T(128)S(1)}, s32[4]{0:T(128)}, u32[]{:S(2)}) copy-start(s32[4]{0:T(128)} %pad_add_fusion.me) | copy-start | bytes 52
  93.4 40.0 %all-to-all-start.3 = ((bf16[8,8,128,128]{3,2,1,0:T(8,128)(2,1)}), bf16[8,8,128,128]{3,2,1,0:T(8,128)(2,1)}, u32[]{:S(2)}, u32[]{:S(2)}) async-start(bf16[8,8,128,128]{3,2,1,0:T(8,128)(2,1)} %bitcast.8), calls=%async_computation.3 | async-start | bytes 4194304 | tf_op jit(solution)/shard_map/all_to_all | solution.py:40
  97.9 1.2 copy-start.3
  106.1 7.8 %collective-permute-start.1 = (bf16[32,64,128]{2,1,0:T(8,128)(2,1)S(1)}, bf16[32,64,128]{2,1,0:T(8,128)(2,1)S(1)}, u32[]{:S(2)}, u32[]{:S(2)}) collective-permute-start(bf16[32,64,128]{2,1,0:T(8,128)(2,1)S(1)} %get-tuple-element.36), channel_id=1, source_target_pairs={{0,4},{4,0},{8,12},{12,8},{16,20},{20,16},{24,28},{28,24},{32,36},... | collective-permute-start | bytes 1572872 | tf_op jit(solution)/shard_map/ppermute | solution.py:379
  114.6 12.4 %collective-permute-start.4 = (bf16[12,64,128]{2,1,0:T(8,128)(2,1)S(1)}, bf16[12,64,128]{2,1,0:T(8,128)(2,1)S(1)}, u32[]{:S(2)}, u32[]{:S(2)}) collective-permute-start(bf16[12,64,128]{2,1,0:T(8,128)(2,1)S(1)} %get-tuple-element.41), channel_id=1, source_target_pairs={{0,3},{1,0},{2,1},{3,2},{4,7},{5,4},{6,5},{7,6},{8,11},{9,8},{10,9... | collective-permute-start | bytes 589832 | tf_op jit(solution)/shard_map/ppermute | solution.py:382
  119.0 9.3 %collective-permute-start.3 = (bf16[12,64,128]{2,1,0:T(8,128)(2,1)S(1)}, bf16[12,64,128]{2,1,0:T(8,128)(2,1)S(1)}, u32[]{:S(2)}, u32[]{:S(2)}) collective-permute-start(bf16[12,64,128]{2,1,0:T(8,128)(2,1)S(1)} %get-tuple-element.40), channel_id=1, source_target_pairs={{0,2},{1,3},{2,0},{3,1},{4,6},{5,7},{6,4},{7,5},{8,10},{9,11},{10,... | collective-permute-start | bytes 589832 | tf_op jit(solution)/shard_map/ppermute | solution.py:382
  121.4 11.9 %collective-permute-start.2 = (bf16[12,64,128]{2,1,0:T(8,128)(2,1)S(1)}, bf16[12,64,128]{2,1,0:T(8,128)(2,1)S(1)}, u32[]{:S(2)}, u32[]{:S(2)}) collective-permute-start(bf16[12,64,128]{2,1,0:T(8,128)(2,1)S(1)} %get-tuple-element.39), channel_id=1, source_target_pairs={{0,1},{1,2},{2,3},{3,0},{4,5},{5,6},{6,7},{7,4},{8,9},{9,10},{10,1... | collective-permute-start | bytes 589832 | tf_op jit(solution)/shard_map/ppermute | solution.py:382
  136.0 16.4 %all-to-all-start.4 = ((bf16[8,128,128]{2,1,0:T(8,128)(2,1)}), bf16[8,128,128]{2,1,0:T(8,128)(2,1)S(1)}, u32[]{:S(2)}, u32[]{:S(2)}) async-start(bf16[8,128,128]{2,1,0:T(8,128)(2,1)} %shard_map.91), calls=%async_computation.4 | async-start | bytes 524288 | tf_op jit(solution)/shard_map/all_to_all | solution.py:40

commit v6 on v5

--- a/solution.py
+++ b/solution.py
@@ -13,8 +13,7 @@
 SENT = QROWS + 8
 BATCH = QD * GROUP
 SLOTS = 4
-CHUNKS = 8
-VMEM = 48 * 1024 * 1024
+VMEM = 16 * 1024 * 1024
 F32, BF16, I32 = jnp.float32, jnp.bfloat16, jnp.int32
 EXACT = lax.Precision.HIGHEST
 EVERY = ("dp", "group")
@@ -59,6 +58,10 @@
     return pl.BlockSpec(memory_space=pl.ANY)
 
 
+def hbm():
+    return pl.BlockSpec(memory_space=pltpu.HBM)
+
+
 def smem():
     return pl.BlockSpec(memory_space=pltpu.SMEM)
 
@@ -87,13 +90,12 @@
     return copies
 
 
-def prepare(ids_in, storage_in, queries_in, positives_in, sent, q_unit, pos_unit, ids, storage, queries, positives, sems, count):
-    pairs = [(storage_in, storage), (ids_in, ids), (queries_in, queries), (positives_in, positives)]
+def prepare(ids_in, storage_in, queries_in, sent, q_unit, ids, storage, queries, sems, count):
+    pairs = [(storage_in, storage), (ids_in, ids), (queries_in, queries)]
     for copy in fetch(pairs, sems):
         copy.wait()
     tiles = unit(queries[...])
     q_unit[...] = tiles
-    pos_unit[...] = unit(positives[...])
     homes = []
     for q in range(QD):
         for k in range(NEG):
@@ -126,7 +128,8 @@
     return cands, exp_scores, total, score
 
 
-def positive_weight(q_tiles, gathered, out):
+def positive_weight(q_tiles, positives, gathered, out):
+    gathered[...] = unit(positives[...])
     score = positive_scores(q_tiles[...].reshape(QROWS, D), gathered)[3]
     out[...] = jnp.sum(jnp.exp(score), axis=0, keepdims=True)
 
@@ -152,7 +155,7 @@
     return jnp.concatenate([jnp.where(block == b, packed, 0.0).astype(BF16) for b in range(SLOTS)], axis=0)
 
 
-def read_codes(me, asked, codes, table, sem):
+def read_codes(me, asked, table, codes, sem):
     rows = asked[:, QROWS:SENT, :].reshape(SPOTS * 8, N_DP)
     which = iota((8, N_DP), 0)
     spot = jnp.where(which == 0, me[2], me[3])
@@ -163,33 +166,32 @@
     copy.wait()
 
 
-def score(me, asked, own_rows, other_rows, pos_weight, exps_out, factor, sums, codes, exps, totals, marks, table, sems):
-    read_codes(me, asked, codes, table, sems.at[CHUNKS])
+def exponentials(codes, asked, own_rows, other_rows, source):
+    block = iota((PT, QROWS), 1) // QT
+    full = dot(passages(codes, own_rows, other_rows, source), asking(codes, asked, source), ((1,), (1,)))
+    packed = full[0:PT]
+    for b in range(1, SLOTS):
+        packed = jnp.where(block == b, full[b * PT : (b + 1) * PT], packed)
+    return jnp.exp(10.0 * packed)
+
+
+def score(me, asked, own_rows, other_rows, pos_weight, factor, sums, table, totals, marks, codes, sem):
+    read_codes(me, asked, table, codes, sem)
     lane = iota((1, QROWS), 1)
-    block = iota((PT, QROWS), 1) // QT
 
     def one(source, carry):
         mark = jnp.full((1, QROWS), -1.0, F32)
         for b in range(SLOTS):
             valid, q, _ = request(codes, source, b)
             mark = jnp.where((lane // QT == b) & valid, q.astype(F32), mark)
-        full = dot(passages(codes, own_rows, other_rows, source), asking(codes, asked, source), ((1,), (1,)))
-        packed = full[0:PT]
-        for b in range(1, SLOTS):
-            packed = jnp.where(block == b, full[b * PT : (b + 1) * PT], packed)
-        exp_scores = jnp.exp(10.0 * packed)
-        exps[source] = exp_scores
+        exp_scores = exponentials(codes, asked, own_rows, other_rows, source)
         totals[pl.ds(source, 1), :] = jnp.sum(exp_scores, axis=0, keepdims=True)
         marks[pl.ds(source, 1), :] = mark
         return carry
 
-    size = SPOTS // CHUNKS
-    copies = []
-    for chunk in range(CHUNKS):
-        lax.fori_loop(chunk * size, (chunk + 1) * size, one, 0, unroll=4)
-        part = pl.ds(chunk * size, size)
-        copies.append(pltpu.make_async_copy(exps.at[part], exps_out.at[part], sems.at[chunk]))
-        copies[-1].start()
+    size = 8
+    for chunk in range(SPOTS // size):
+        lax.fori_loop(chunk * size, (chunk + 1) * size, one, 0, unroll=size)
 
     total = totals[...]
     mark = marks[...]
@@ -206,13 +208,11 @@
         own = jnp.sum(jnp.where(lane == q * QT, pos_weight[...], 0.0), axis=1, keepdims=True)
         parts.append(part + jnp.where(lane == me[0], own, 0.0))
     sums[...] = jnp.broadcast_to(jnp.concatenate(parts, axis=0)[None], (SPOTS, QD, QROWS))
-    for copy in copies:
-        copy.wait()
-
-
-def terms(codes, own_rows, other_rows, exps, factor, probs, back):
+
+
+def terms(codes, asked, own_rows, other_rows, factor, probs, back):
     def one(source, carry):
-        packed = exps[source] * factor[pl.ds(source, 1), :]
+        packed = exponentials(codes, asked, own_rows, other_rows, source) * factor[pl.ds(source, 1), :]
         probs[source] = packed.astype(BF16)
         grads = dot(spread(packed), passages(codes, own_rows, other_rows, source), ((0,), (0,)))
         picked = [request(codes, source, slot)[1] for slot in range(SLOTS)]
@@ -223,7 +223,7 @@
             back[source, q * QT : (q + 1) * QT, :] = total.astype(BF16)
         return carry
 
-    lax.fori_loop(0, SPOTS, one, 0, unroll=4)
+    lax.fori_loop(0, SPOTS, one, 0, unroll=8)
 
 
 def weigh(
@@ -248,7 +248,7 @@
             acc[row] += grads[b * PT : (b + 1) * PT] * weight_inv[q, source]
         return carry
 
-    lax.fori_loop(0, SPOTS, add, 0, unroll=4)
+    lax.fori_loop(0, SPOTS, add, 0, unroll=8)
     other_grad[...] = other_acc[...].astype(BF16)
 
     for copy in later:
@@ -277,9 +277,13 @@
         out[QD:] = (own_grad[rows] + moved[rows].astype(F32)).astype(out.dtype)
 
 
-def add_blocks(arrived, after, out):
+def add_blocks(arrived, after, out, blocks, sems):
     del after
-    out[...] = jnp.sum(arrived[...].astype(F32), axis=0).astype(BF16)
+    pairs = [(arrived.at[:, pl.ds(2 * i, 2)], blocks.at[:, pl.ds(2 * i, 2)]) for i in range(N_Y // 2)]
+    for i, copy in enumerate(fetch(pairs, sems)):
+        copy.wait()
+        part = slice(2 * i, 2 * i + 2)
+        out[part] = jnp.sum(blocks[:, part].astype(F32), axis=0).astype(BF16)
 
 
 def collect(weight_inv, me, query_part, arrived, out):
@@ -299,44 +303,43 @@
     swap = [(h, h ^ 1) for h in range(N_DP)]
     tiles = struct((QD, QT, D), BF16)
 
-    sent, q_unit, pos_unit = call(
+    sent, q_unit = call(
         prepare,
-        (struct((N_Y, SENT, D), BF16), tiles, struct((QD, PT, D), BF16)),
-        [anywhere()] * 4,
-        (vmem(), vmem(), vmem()),
+        (struct((N_Y, SENT, D), BF16), tiles),
+        [hbm()] * 3,
+        (vmem(), vmem()),
         [
             pltpu.SMEM(negative_ids.shape, I32),
             pltpu.SMEM(storage_row.shape, I32),
             pltpu.VMEM((QD, QT, D), BF16),
-            pltpu.VMEM((QD, PT, D), BF16),
-            pltpu.SemaphoreType.DMA((4,)),
+            pltpu.SemaphoreType.DMA((3,)),
             pltpu.SMEM((N_DP,), I32),
         ],
-    )(negative_ids, storage_row, queries, positives)
+    )(negative_ids, storage_row, queries)
     asked = exchange(sent, along(1))
     asked = exchange(jnp.broadcast_to(asked[None], (N_Z, N_Y, SENT, D)), along(0)).reshape(SPOTS, SENT, D)
 
     own_rows = call(normalize, struct((ROWS, PT, D), BF16), [vmem()], vmem())(passage_pool)
     other_rows = lax.ppermute(own_rows, "dp", swap)
-    gathered = lax.all_gather(pos_unit, "group", axis=0, tiled=True)
-    pos_weight = call(positive_weight, struct((1, QROWS), F32), [vmem(), vmem()], vmem())(q_unit, gathered)
-
-    exps, factor, sums, codes = call(
+    gathered = lax.all_gather(positives, "group", axis=0, tiled=True)
+    gathered, pos_weight = call(
+        positive_weight, (struct((BATCH, PT, D), BF16), struct((1, QROWS), F32)), [vmem(), vmem()], (vmem(), vmem())
+    )(q_unit, gathered)
+
+    factor, sums, codes = call(
         score,
         (
-            struct((SPOTS, PT, QROWS), F32),
             struct((SPOTS, QROWS), F32),
             struct((SPOTS, QD, QROWS), F32),
             struct((8, SPOTS * 8), I32),
         ),
         [smem(), vmem(), vmem(), vmem(), vmem()],
-        (anywhere(), vmem(), vmem(), smem()),
+        (vmem(), vmem(), vmem()),
         [
-            pltpu.VMEM((SPOTS, PT, QROWS), F32),
             pltpu.VMEM((SPOTS, QROWS), F32),
             pltpu.VMEM((SPOTS, QROWS), F32),
-            pltpu.VMEM((8, SPOTS * 8), I32),
-            pltpu.SemaphoreType.DMA((CHUNKS + 1,)),
+            pltpu.SMEM((8, SPOTS * 8), I32),
+            pltpu.SemaphoreType.DMA,
         ],
     )(me, asked, own_rows, other_rows, pos_weight)
     sums = exchange(sums, planes())
@@ -346,7 +349,7 @@
         (struct((SPOTS, PT, QROWS), BF16), struct((SPOTS, QROWS, D), BF16)),
         [smem()] + [vmem()] * 4,
         (vmem(), vmem()),
-    )(codes, own_rows, other_rows, exps, factor)
+    )(codes, asked, own_rows, other_rows, factor)
     arrived = exchange(back.reshape(N_Z, N_Y, QROWS, D), along(0))
 
     own_grad, other_grad, pos_grad, query_part, losses, weight_inv = call(
@@ -359,7 +362,7 @@
             struct((1, QROWS), F32),
             struct((8, QROWS), F32),
         ),
-        [smem(), smem(), vmem(), vmem(), vmem(), anywhere(), anywhere()],
+        [smem(), smem(), vmem(), vmem(), vmem(), hbm(), hbm()],
         (vmem(),) * 5 + (smem(),),
         [
             pltpu.VMEM((ROWS, PT, D), F32),
@@ -382,7 +385,13 @@
         moved = lax.ppermute(part, "group", [(g, (g + ahead) % GROUP) for g in range(GROUP)])
         total = total + moved.astype(F32)
 
-    arrived = call(add_blocks, struct((N_Y, QROWS, D), BF16), [vmem(), anywhere()], vmem())(arrived, total)
+    arrived = call(
+        add_blocks,
+        struct((N_Y, QROWS, D), BF16),
+        [hbm(), anywhere()],
+        vmem(),
+        [pltpu.VMEM((N_Z, N_Y, QROWS, D), BF16), pltpu.SemaphoreType.DMA((N_Y // 2,))],
+    )(arrived, total)
     arrived = exchange(arrived, along(1))
     query_grad = call(
         collect, struct((QD, QT, D), F32), [smem(), smem(), vmem(), vmem()], vmem()

time: 155 us -> 144 us (0.929)
  the two profiles are of different devices: /device:TPU:1 before, /device:TPU:6 now
where the time goes in v6:
time: 144 us; the launch traced here: 143 us
  starting transfers between devices  38.5 us (27%)
  waiting for transfers between devices  37.2 us (26%)
  blocking collectives  29.8 us (21%)
  Pallas kernels  24.3 us (17%)
  local copies, waits for them, and re-layouts  11.3 us (8%)
    all_to_all x4, waiting for transfers between devices, exchange(): lax.all_to_all(blocks, EVERY, split_axis=0, concat_axis=0, axis_index_gro...  27.3 us
    all_to_all x4, starting transfers between devices, exchange(): lax.all_to_all(blocks, EVERY, split_axis=0, concat_axis=0, axis_index_gro...  26.1 us
    all_to_all x1, blocking collectives, exchange(): lax.all_to_all(blocks, EVERY, split_axis=0, concat_axis=0, axis_index_gro...  17.6 us
    all_gather x1, blocking collectives, per_device(): gathered = lax.all_gather(positives, 'group', axis=0, tiled=True)  12.3 us
    ppermute x3, starting transfers between devices, per_device(): lax.ppermute(part, 'group', [(g, (g + ahead) % GROUP) for g in range(GROU...  8.62 us
    ppermute x3, waiting for transfers between devices, per_device(): lax.ppermute(part, 'group', [(g, (g + ahead) % GROUP) for g in range(GROU...  8.02 us
    pallas_call x1, Pallas kernels, per_device(): call(terms, (struct((SPOTS, PT, QROWS), BF16), struct((SPOTS, QROWS, D),...  7.59 us
    unnamed x22, local copies, waits for them, and re-layouts  7.05 us
  transfers between devices with their start and end apart: 9, of which 8 were waited for; matrix products, arithmetic and copies ran while one was open for 2% of the time, Pallas kernels for 11%

profile of v6, /device:TPU:6, one launch (start us, length us, event | category | flops | bytes accessed | tf_op | source)
XLA Modules:
  0.0 142.9 jit_solution(3261153007663778726)
XLA Ops:
  0.6 0.0 copy-start.7
  0.6 0.7 copy-done.7
  1.4 0.0 copy-start.8
  1.4 0.7 copy-done.8
  2.1 0.0 copy-start.9
  2.1 0.7 copy-done.9
  2.8 1.3 shard_map.84
  4.1 17.6 %all_to_all.25 = bf16[8,136,128]{2,1,0:T(8,128)(2,1)S(1)} all-to-all(bf16[8,136,128]{2,1,0:T(8,128)(2,1)S(1)} %get-tuple-element.23), channel_id=1, replica_groups={{4,68,132,196,260,324,388,452},{5,69,133,197,261,325,389,453},{6,70,134..., dimensions={0} | all-to-all | bytes 557056 | tf_op jit(solution)/shard_map/all_to_all | solution.py:39
  21.7 1.7 %broadcast_in_dim.2 = bf16[8,8,136,128]{3,2,1,0:T(8,128)(2,1)} broadcast(bf16[8,136,128]{2,1,0:T(8,128)(2,1)S(1)} %all_to_all.25), dimensions={1,2,3} | broadcast | bytes 2506752 | tf_op jit(solution)/shard_map/broadcast_in_dim | solution.py:320
  23.3 0.0 copy-start.3
  23.4 0.0 copy-start.10
  23.4 10.4 %all-to-all-start.1 = ((bf16[8,8,136,128]{3,2,1,0:T(8,128)(2,1)}), bf16[8,8,136,128]{3,2,1,0:T(8,128)(2,1)S(1)}, u32[]{:S(2)}, u32[]{:S(2)}) async-start(bf16[8,8,136,128]{3,2,1,0:T(8,128)(2,1)} %broadcast_in_dim.2), calls=%async_computation.1 | async-start | bytes 4456448 | tf_op jit(solution)/shard_map/all_to_all | solution.py:39
  33.8 0.0 copy-done.3
  33.8 0.4 shard_map.85.own_rows
  34.2 1.9 %collective-permute-start = (bf16[32,64,128]{2,1,0:T(8,128)(2,1)S(1)}, bf16[32,64,128]{2,1,0:T(8,128)(2,1)S(1)}, u32[]{:S(2)}, u32[]{:S(2)}) collective-permute-start(bf16[32,64,128]{2,1,0:T(8,128)(2,1)S(1)} %shard_map.85.own_rows), channel_id=1, source_target_pairs={{0,4},{4,0},{8,12},{12,8},{16,20},{20,16},{24,28},{28,24},{32,36},... | collective-permute-start | bytes 1572872 | tf_op jit(solution)/shard_map/ppermute | solution.py:323
  36.1 0.0 copy-done.10
  36.2 12.3 %all_gather.3.positives = bf16[16,64,128]{2,1,0:T(8,128)(2,1)S(1)} all-gather(bf16[4,64,128]{2,1,0:T(8,128)(2,1)S(1)} %copy-done.10), channel_id=1, replica_groups=mesh['dp'=128,'group'=4] {'group'}, dimensions={0}, use_global_device_ids=true | all-gather | bytes 327680 | tf_op jit(solution)/shard_map/all_gather | solution.py:324
  48.4 0.6 shard_map.86
  49.0 0.0 copy-start.4
  49.0 0.7 copy-done.4
  49.8 0.1 pad_add_fusion.me
  49.8 0.0 collective-permute-done.other_rows
  49.8 15.7 %all-to-all-done.1 = bf16[8,8,136,128]{3,2,1,0:T(8,128)(2,1)S(1)} async-done(((bf16[8,8,136,128]{3,2,1,0:T(8,128)(2,1)}), bf16[8,8,136,128]{3,2,1,0:T(8,128)(2,1)S(1)}, u32[]{:S(2)}, u32[]{:S(2)}) %all-to-all-start.1) | async-done | bytes 2228256 | tf_op jit(solution)/shard_map/all_to_all | solution.py:39
  65.5 4.1 %shard_map.87 = (f32[64,128]{1,0:T(8,128)S(1)}, f32[64,4,128]{2,1,0:T(4,128)S(1)}, s32[8,512]{1,0:T(8,128)S(1)}) custom-call(s32[4]{0:T(128)S(1)} %pad_add_fusion.me, bf16[64,136,128]{2,1,0:T(8,128)(2,1)S(1)} %bitcast.6, bf16[32,64,128]{2,1,0:T(8,128)(2,1)S(1)} %shard_map.85.own_rows, bf16[32,64,128]{2,1,0:T(8,128)(2,1)S(1)} %collective-permute-done.other_rows, ...), custom_call_target="tpu_custom_call" | custom-call | tf_op jit(solution)/shard_map/pallas_call | solution.py:329
  69.6 0.0 copy-start.6
  69.6 0.6 copy-done.6
  70.3 4.6 %all-to-all-start.2 = ((f32[64,4,128]{2,1,0:T(4,128)}), f32[64,4,128]{2,1,0:T(4,128)S(1)}, u32[]{:S(2)}, u32[]{:S(2)}) async-start(f32[64,4,128]{2,1,0:T(4,128)} %copy-done.6), calls=%async_computation.2 | async-start | bytes 262144 | tf_op jit(solution)/shard_map/all_to_all | solution.py:39
  74.9 7.6 %shard_map.88 = (bf16[64,64,128]{2,1,0:T(8,128)(2,1)S(1)}, bf16[64,128,128]{2,1,0:T(8,128)(2,1)S(1)}) custom-call(s32[8,512]{1,0:T(8,128)S(1)} %get-tuple-element.26.codes, bf16[64,136,128]{2,1,0:T(8,128)(2,1)S(1)} %bitcast.7, bf16[32,64,128]{2,1,0:T(8,128)(2,1)S(1)} %shard_map.85.own_rows, bf16[32,64,128]{2,1,0:T(8,128)(2,1)S(1)} %collective-permute-done.other_rows, ...), custom_call_target="tpu_custom_call" | custom-call | tf_op jit(solution)/shard_map/pallas_call | solution.py:347
  82.5 0.0 copy-start
  82.5 1.3 copy-done
  83.8 0.0 copy-start.1
  83.8 1.0 copy-done.1
  84.8 0.0 copy-start.5
  84.8 2.8 %all-to-all-done.2.sums = f32[64,4,128]{2,1,0:T(4,128)S(1)} async-done(((f32[64,4,128]{2,1,0:T(4,128)}), f32[64,4,128]{2,1,0:T(4,128)S(1)}, u32[]{:S(2)}, u32[]{:S(2)}) %all-to-all-start.2) | async-done | bytes 131104 | tf_op jit(solution)/shard_map/all_to_all | solution.py:39
  87.6 4.4 %all-to-all-start.3 = ((bf16[8,8,128,128]{3,2,1,0:T(8,128)(2,1)}), bf16[8,8,128,128]{3,2,1,0:T(8,128)(2,1)}, u32[]{:S(2)}, u32[]{:S(2)}) async-start(bf16[8,8,128,128]{3,2,1,0:T(8,128)(2,1)} %bitcast.9), calls=%async_computation.3 | async-start | bytes 4194304 | tf_op jit(solution)/shard_map/all_to_all | solution.py:39
  91.9 0.0 copy-done.5
  92.0 0.0 copy-start.2
  92.0 1.2 copy-done.2
  93.2 6.1 %shard_map.89 = (f32[32,64,128]{2,1,0:T(8,128)S(1)}, bf16[32,64,128]{2,1,0:T(8,128)(2,1)S(1)}, f32[16,64,128]{2,1,0:T(8,128)S(1)}, f32[128,128]{1,0:T(8,128)S(1)...) custom-call(s32[4]{0:T(128)S(1)} %pad_add_fusion.me, s32[8,512]{1,0:T(8,128)S(1)} %get-tuple-element.26.codes, ...), custom_call_target="tpu_custom_call" | custom-call | tf_op jit(solution)/shard_map/pallas_call | solution.py:355
  99.3 1.9 %collective-permute-start.1 = (bf16[32,64,128]{2,1,0:T(8,128)(2,1)S(1)}, bf16[32,64,128]{2,1,0:T(8,128)(2,1)S(1)}, u32[]{:S(2)}, u32[]{:S(2)}) collective-permute-start(bf16[32,64,128]{2,1,0:T(8,128)(2,1)S(1)} %get-tuple-element.36), channel_id=1, source_target_pairs={{0,4},{4,0},{8,12},{12,8},{16,20},{20,16},{24,28},{28,24},{32,36},... | collective-permute-start | bytes 1572872 | tf_op jit(solution)/shard_map/ppermute | solution.py:382
  101.2 1.9 %collective-permute-done.1.moved = bf16[32,64,128]{2,1,0:T(8,128)(2,1)S(1)} collective-permute-done((bf16[32,64,128]{2,1,0:T(8,128)(2,1)S(1)}, bf16[32,64,128]{2,1,0:T(8,128)(2,1)S(1)}, u32[]{:S(2)}, u32[]{:S(2)}) %collective-permute-start.1) | collective-permute-done | bytes 524320 | tf_op jit(solution)/shard_map/ppermute | solution.py:382
  103.1 0.7 shard_map.90
  103.7 2.4 %collective-permute-start.2 = (bf16[12,64,128]{2,1,0:T(8,128)(2,1)S(1)}, bf16[12,64,128]{2,1,0:T(8,128)(2,1)S(1)}, u32[]{:S(2)}, u32[]{:S(2)}) collective-permute-start(bf16[12,64,128]{2,1,0:T(8,128)(2,1)S(1)} %get-tuple-element.39), channel_id=1, source_target_pairs={{0,1},{1,2},{2,3},{3,0},{4,5},{5,6},{6,7},{7,4},{8,9},{9,10},{10,1... | collective-permute-start | bytes 589832 | tf_op jit(solution)/shard_map/ppermute | solution.py:385
  106.1 4.3 %collective-permute-start.3 = (bf16[12,64,128]{2,1,0:T(8,128)(2,1)S(1)}, bf16[12,64,128]{2,1,0:T(8,128)(2,1)S(1)}, u32[]{:S(2)}, u32[]{:S(2)}) collective-permute-start(bf16[12,64,128]{2,1,0:T(8,128)(2,1)S(1)} %get-tuple-element.40), channel_id=1, source_target_pairs={{0,2},{1,3},{2,0},{3,1},{4,6},{5,7},{6,4},{7,5},{8,10},{9,11},{10,... | collective-permute-start | bytes 589832 | tf_op jit(solution)/shard_map/ppermute | solution.py:385
  110.5 1.9 %collective-permute-start.4 = (bf16[12,64,128]{2,1,0:T(8,128)(2,1)S(1)}, bf16[12,64,128]{2,1,0:T(8,128)(2,1)S(1)}, u32[]{:S(2)}, u32[]{:S(2)}) collective-permute-start(bf16[12,64,128]{2,1,0:T(8,128)(2,1)S(1)} %get-tuple-element.41), channel_id=1, source_target_pairs={{0,3},{1,0},{2,1},{3,2},{4,7},{5,4},{6,5},{7,6},{8,11},{9,8},{10,9... | collective-permute-start | bytes 589832 | tf_op jit(solution)/shard_map/ppermute | solution.py:385
  112.4 1.0 collective-permute-done.2
  113.4 3.2 %collective-permute-done.3 = bf16[12,64,128]{2,1,0:T(8,128)(2,1)S(1)} collective-permute-done((bf16[12,64,128]{2,1,0:T(8,128)(2,1)S(1)}, bf16[12,64,128]{2,1,0:T(8,128)(2,1)S(1)}, u32[]{:S(2)}, u32[]{:S(2)}) %collective-permute-start.3) | collective-permute-done | bytes 196640 | tf_op jit(solution)/shard_map/ppermute | solution.py:385
  116.5 3.9 %collective-permute-done.4 = bf16[12,64,128]{2,1,0:T(8,128)(2,1)S(1)} collective-permute-done((bf16[12,64,128]{2,1,0:T(8,128)(2,1)S(1)}, bf16[12,64,128]{2,1,0:T(8,128)(2,1)S(1)}, u32[]{:S(2)}, u32[]{:S(2)}) %collective-permute-start.4) | collective-permute-done | bytes 196640 | tf_op jit(solution)/shard_map/ppermute | solution.py:385
  120.4 0.1 convert_add_fusion.after
  120.5 1.7 %all-to-all-done.3.arrived = bf16[8,8,128,128]{3,2,1,0:T(8,128)(2,1)} async-done(((bf16[8,8,128,128]{3,2,1,0:T(8,128)(2,1)}), bf16[8,8,128,128]{3,2,1,0:T(8,128)(2,1)}, u32[]{:S(2)}, u32[]{:S(2)}) %all-to-all-start.3) | async-done | bytes 2097184 | tf_op jit(solution)/shard_map/all_to_all | solution.py:39
  122.2 2.3 %shard_map.91 = bf16[8,128,128]{2,1,0:T(8,128)(2,1)} custom-call(bf16[8,8,128,128]{3,2,1,0:T(8,128)(2,1)} %all-to-all-done.3.arrived, f32[12,64,128]{2,1,0:T(8,128)S(1)} %convert_add_fusion.after), custom_call_target="tpu_custom_call" | custom-call | tf_op jit(solution)/shard_map/pallas_call | solution.py:388
  124.5 6.6 %all-to-all-start.4 = ((bf16[8,128,128]{2,1,0:T(8,128)(2,1)}), bf16[8,128,128]{2,1,0:T(8,128)(2,1)S(1)}, u32[]{:S(2)}, u32[]{:S(2)}) async-start(bf16[8,128,128]{2,1,0:T(8,128)(2,1)} %shard_map.91), calls=%async_computation.4 | async-start | bytes 524288 | tf_op jit(solution)/shard_map/all_to_all | solution.py:39
  131.2 0.5 broadcast.9
  131.7 0.7 reduce.5
  132.4 0.1 reshape.19
  132.4 0.6 slice_reduce_fusion
  133.1 0.7 slice.13
  133.8 0.7 slice.12
  134.5 7.2 %all-to-all-done.4.arrived = bf16[8,128,128]{2,1,0:T(8,128)(2,1)S(1)} async-done(((bf16[8,128,128]{2,1,0:T(8,128)(2,1)}), bf16[8,128,128]{2,1,0:T(8,128)(2,1)S(1)}, u32[]{:S(2)}, u32[]{:S(2)}) %all-to-all-start.4) | async-done | bytes 262176 | tf_op jit(solution)/shard_map/all_to_all | solution.py:39
  141.7 1.3 shard_map.92
Async XLA Ops:
  0.6 0.8 copy-start.7
  1.4 0.7 copy-start.8
  2.1 0.7 copy-start.9
  23.3 10.5 %copy-start.3 = (bf16[32,64,128]{2,1,0:T(8,128)(2,1)S(1)}, bf16[32,64,128]{2,1,0:T(8,128)(2,1)}, u32[]{:S(2)}) copy-start(bf16[32,64,128]{2,1,0:T(8,128)(2,1)} %values.1) | copy-start | bytes 1572868
  23.4 12.8 %copy-start.10 = (bf16[4,64,128]{2,1,0:T(8,128)(2,1)S(1)}, bf16[4,64,128]{2,1,0:T(8,128)(2,1)}, u32[]{:S(2)}) copy-start(bf16[4,64,128]{2,1,0:T(8,128)(2,1)} %param.6) | copy-start | bytes 196612
  23.4 42.1 %all-to-all-start.1 = ((bf16[8,8,136,128]{3,2,1,0:T(8,128)(2,1)}), bf16[8,8,136,128]{3,2,1,0:T(8,128)(2,1)S(1)}, u32[]{:S(2)}, u32[]{:S(2)}) async-start(bf16[8,8,136,128]{3,2,1,0:T(8,128)(2,1)} %broadcast_in_dim.2), calls=%async_computation.1 | async-start | bytes 4456448 | tf_op jit(solution)/shard_map/all_to_all | solution.py:39
  34.2 15.7 %collective-permute-start = (bf16[32,64,128]{2,1,0:T(8,128)(2,1)S(1)}, bf16[32,64,128]{2,1,0:T(8,128)(2,1)S(1)}, u32[]{:S(2)}, u32[]{:S(2)}) collective-permute-start(bf16[32,64,128]{2,1,0:T(8,128)(2,1)S(1)} %shard_map.85.own_rows), channel_id=1, source_target_pairs={{0,4},{4,0},{8,12},{12,8},{16,20},{20,16},{24,28},{28,24},{32,36},... | collective-permute-start | bytes 1572872 | tf_op jit(solution)/shard_map/ppermute | solution.py:323
  49.0 0.7 copy-start.4
  69.6 0.7 copy-start.6
  70.3 17.3 %all-to-all-start.2 = ((f32[64,4,128]{2,1,0:T(4,128)}), f32[64,4,128]{2,1,0:T(4,128)S(1)}, u32[]{:S(2)}, u32[]{:S(2)}) async-start(f32[64,4,128]{2,1,0:T(4,128)} %copy-done.6), calls=%async_computation.2 | async-start | bytes 262144 | tf_op jit(solution)/shard_map/all_to_all | solution.py:39
  82.5 1.3 copy-start
  83.8 1.0 copy-start.1
  84.8 7.1 %copy-start.5 = (bf16[16,64,128]{2,1,0:T(8,128)(2,1)S(1)}, bf16[16,64,128]{2,1,0:T(8,128)(2,1)}, u32[]{:S(2)}) copy-start(bf16[16,64,128]{2,1,0:T(8,128)(2,1)} %copy-done.4) | copy-start | bytes 786436
  87.6 34.6 %all-to-all-start.3 = ((bf16[8,8,128,128]{3,2,1,0:T(8,128)(2,1)}), bf16[8,8,128,128]{3,2,1,0:T(8,128)(2,1)}, u32[]{:S(2)}, u32[]{:S(2)}) async-start(bf16[8,8,128,128]{3,2,1,0:T(8,128)(2,1)} %bitcast.9), calls=%async_computation.3 | async-start | bytes 4194304 | tf_op jit(solution)/shard_map/all_to_all | solution.py:39
  92.0 1.2 copy-start.2
  99.3 3.8 %collective-permute-start.1 = (bf16[32,64,128]{2,1,0:T(8,128)(2,1)S(1)}, bf16[32,64,128]{2,1,0:T(8,128)(2,1)S(1)}, u32[]{:S(2)}, u32[]{:S(2)}) collective-permute-start(bf16[32,64,128]{2,1,0:T(8,128)(2,1)S(1)} %get-tuple-element.36), channel_id=1, source_target_pairs={{0,4},{4,0},{8,12},{12,8},{16,20},{20,16},{24,28},{28,24},{32,36},... | collective-permute-start | bytes 1572872 | tf_op jit(solution)/shard_map/ppermute | solution.py:382
  103.7 9.6 %collective-permute-start.2 = (bf16[12,64,128]{2,1,0:T(8,128)(2,1)S(1)}, bf16[12,64,128]{2,1,0:T(8,128)(2,1)S(1)}, u32[]{:S(2)}, u32[]{:S(2)}) collective-permute-start(bf16[12,64,128]{2,1,0:T(8,128)(2,1)S(1)} %get-tuple-element.39), channel_id=1, source_target_pairs={{0,1},{1,2},{2,3},{3,0},{4,5},{5,6},{6,7},{7,4},{8,9},{9,10},{10,1... | collective-permute-start | bytes 589832 | tf_op jit(solution)/shard_map/ppermute | solution.py:385
  106.1 10.4 %collective-permute-start.3 = (bf16[12,64,128]{2,1,0:T(8,128)(2,1)S(1)}, bf16[12,64,128]{2,1,0:T(8,128)(2,1)S(1)}, u32[]{:S(2)}, u32[]{:S(2)}) collective-permute-start(bf16[12,64,128]{2,1,0:T(8,128)(2,1)S(1)} %get-tuple-element.40), channel_id=1, source_target_pairs={{0,2},{1,3},{2,0},{3,1},{4,6},{5,7},{6,4},{7,5},{8,10},{9,11},{10,... | collective-permute-start | bytes 589832 | tf_op jit(solution)/shard_map/ppermute | solution.py:385
  110.5 9.9 %collective-permute-start.4 = (bf16[12,64,128]{2,1,0:T(8,128)(2,1)S(1)}, bf16[12,64,128]{2,1,0:T(8,128)(2,1)S(1)}, u32[]{:S(2)}, u32[]{:S(2)}) collective-permute-start(bf16[12,64,128]{2,1,0:T(8,128)(2,1)S(1)} %get-tuple-element.41), channel_id=1, source_target_pairs={{0,3},{1,0},{2,1},{3,2},{4,7},{5,4},{6,5},{7,6},{8,11},{9,8},{10,9... | collective-permute-start | bytes 589832 | tf_op jit(solution)/shard_map/ppermute | solution.py:385
  124.5 17.1 %all-to-all-start.4 = ((bf16[8,128,128]{2,1,0:T(8,128)(2,1)}), bf16[8,128,128]{2,1,0:T(8,128)(2,1)S(1)}, u32[]{:S(2)}, u32[]{:S(2)}) async-start(bf16[8,128,128]{2,1,0:T(8,128)(2,1)} %shard_map.91), calls=%async_computation.4 | async-start | bytes 524288 | tf_op jit(solution)/shard_map/all_to_all | solution.py:39

commit v7 on v6

--- a/solution.py
+++ b/solution.py
@@ -23,16 +23,43 @@
     return ((z * N_Y + y) * N_C + c) * GROUP + x
 
 
+def chip(far_z, far_y, near_z, near_y, core):
+    return (2 * far_z + near_z + core) % N_Z, (2 * far_y + near_y + core) % N_Y
+
+
+FAR, NEAR = range(4), range(2)
+PAIRS = [(i, j) for i in NEAR for j in NEAR]
+
+
 def along(z_core):
-    z_lines = [[device(z, y, z_core, x) for z in range(N_Z)] for y in range(N_Y) for x in range(GROUP)]
-    y_lines = [[device(z, y, 1 - z_core, x) for y in range(N_Y)] for z in range(N_Z) for x in range(GROUP)]
-    return z_lines + y_lines
+    groups = []
+    for core in range(N_C):
+        for x in range(GROUP):
+            for i, j in PAIRS:
+                for fixed in FAR:
+                    if core == z_core:
+                        chips = [chip(move, fixed, i, j, core) for move in FAR]
+                    else:
+                        chips = [chip(fixed, move, i, j, core) for move in FAR]
+                    groups.append([device(z, y, core, x) for z, y in chips])
+    return groups
+
+
+def neighbours():
+    return [
+        [device(*chip(fz, fy, i, j, core), core, x) for i, j in PAIRS]
+        for core in range(N_C) for x in range(GROUP) for fz in FAR for fy in FAR
+    ]
 
 
 def planes():
-    first = [[device(z, y, 0, x) for z in range(N_Z) for y in range(N_Y)] for x in range(GROUP)]
-    second = [[device(z, y, 1, x) for y in range(N_Y) for z in range(N_Z)] for x in range(GROUP)]
-    return first + second
+    return [
+        [
+            device(*(chip(f, g, i, j, core) if core == 0 else chip(g, f, i, j, core)), core, x)
+            for i, j in PAIRS for f in FAR for g in FAR
+        ]
+        for core in range(N_C) for x in range(GROUP)
+    ]
 
 
 def exchange(blocks, groups):
@@ -111,7 +138,7 @@
         rank = count[lane_of]
         count[lane_of] = rank + 1
         codes = jnp.where((lane == lane_of) & (sub == rank), code.astype(F32), codes)
-    for copy in range(N_Y):
+    for copy in range(4):
         sent[copy, 0:QROWS, :] = tiles.reshape(QROWS, D)
         sent[copy, QROWS:SENT, :] = codes.astype(BF16)
 
@@ -279,11 +306,20 @@
 
 def add_blocks(arrived, after, out, blocks, sems):
     del after
-    pairs = [(arrived.at[:, pl.ds(2 * i, 2)], blocks.at[:, pl.ds(2 * i, 2)]) for i in range(N_Y // 2)]
-    for i, copy in enumerate(fetch(pairs, sems)):
+    parts = [slice(i * out.shape[0] // 4, (i + 1) * out.shape[0] // 4) for i in range(4)]
+    for part, copy in zip(parts, fetch([(arrived.at[:, part], blocks.at[:, part]) for part in parts], sems)):
         copy.wait()
-        part = slice(2 * i, 2 * i + 2)
         out[part] = jnp.sum(blocks[:, part].astype(F32), axis=0).astype(BF16)
+
+
+def add_four(arrived, after):
+    return call(
+        add_blocks,
+        jax.ShapeDtypeStruct(arrived.shape[1:], BF16),
+        [hbm(), anywhere()],
+        vmem(),
+        [pltpu.VMEM(arrived.shape, BF16), pltpu.SemaphoreType.DMA((4,))],
+    )(arrived, after)
 
 
 def collect(weight_inv, me, query_part, arrived, out):
@@ -297,7 +333,9 @@
     struct = jax.ShapeDtypeStruct
     holder = lax.axis_index("dp")
     z, y, core = holder // (N_Y * N_C), (holder // N_C) % N_Y, holder % N_C
-    source = jnp.where(core == 0, z * N_Y + y, y * N_Z + z)
+    z, y = (z - core) % N_Z, (y - core) % N_Y
+    near = (z % 2) * 2 + y % 2
+    source = near * 16 + jnp.where(core == 0, (z // 2) * 4 + y // 2, (y // 2) * 4 + z // 2)
     spot = holder // N_C
     me = jnp.stack([source, lax.axis_index("group"), core * SPOTS + spot, (1 - core) * SPOTS + spot]).astype(I32)
     swap = [(h, h ^ 1) for h in range(N_DP)]
@@ -305,7 +343,7 @@
 
     sent, q_unit = call(
         prepare,
-        (struct((N_Y, SENT, D), BF16), tiles),
+        (struct((4, SENT, D), BF16), tiles),
         [hbm()] * 3,
         (vmem(), vmem()),
         [
@@ -317,7 +355,8 @@
         ],
     )(negative_ids, storage_row, queries)
     asked = exchange(sent, along(1))
-    asked = exchange(jnp.broadcast_to(asked[None], (N_Z, N_Y, SENT, D)), along(0)).reshape(SPOTS, SENT, D)
+    asked = exchange(jnp.broadcast_to(asked[None], (4, 4, SENT, D)), along(0)).reshape(16, SENT, D)
+    asked = exchange(jnp.broadcast_to(asked[None], (4, 16, SENT, D)), neighbours()).reshape(SPOTS, SENT, D)
 
     own_rows = call(normalize, struct((ROWS, PT, D), BF16), [vmem()], vmem())(passage_pool)
     other_rows = lax.ppermute(own_rows, "dp", swap)
@@ -350,7 +389,7 @@
         [smem()] + [vmem()] * 4,
         (vmem(), vmem()),
     )(codes, asked, own_rows, other_rows, factor)
-    arrived = exchange(back.reshape(N_Z, N_Y, QROWS, D), along(0))
+    arrived = exchange(back.reshape(4, 16, QROWS, D), neighbours())
 
     own_grad, other_grad, pos_grad, query_part, losses, weight_inv = call(
         weigh,
@@ -385,14 +424,8 @@
         moved = lax.ppermute(part, "group", [(g, (g + ahead) % GROUP) for g in range(GROUP)])
         total = total + moved.astype(F32)
 
-    arrived = call(
-        add_blocks,
-        struct((N_Y, QROWS, D), BF16),
-        [hbm(), anywhere()],
-        vmem(),
-        [pltpu.VMEM((N_Z, N_Y, QROWS, D), BF16), pltpu.SemaphoreType.DMA((N_Y // 2,))],
-    )(arrived, total)
-    arrived = exchange(arrived, along(1))
+    arrived = exchange(add_four(arrived, kept).reshape(4, 4, QROWS, D), along(0))
+    arrived = exchange(add_four(arrived, total), along(1))
     query_grad = call(
         collect, struct((QD, QT, D), F32), [smem(), smem(), vmem(), vmem()], vmem()
     )(weight_inv, me, query_part, arrived)

time: 144 us -> 149 us (1.035)
  blocking collectives: 29.8 us -> 51.7 us
  waiting for transfers between devices: 37.2 us -> 19.5 us
  starting transfers between devices: 38.5 us -> 36.3 us
  local copies, waits for them, and re-layouts: 11.3 us -> 12.8 us
    all_to_all x1 -> x2, blocking collectives: 17.6 us -> 39.4 us  [exchange(): lax.all_to_all(blocks, EVERY, split_axis=0, concat_axis=0, axis_index_gro...]
    all_to_all x4 -> x5, waiting for transfers between devices: 27.3 us -> 9.84 us  [exchange(): lax.all_to_all(blocks, EVERY, split_axis=0, concat_axis=0, axis_index_gro...]
    all_to_all x4 -> x5, starting transfers between devices: 26.1 us -> 23.7 us  [exchange(): lax.all_to_all(blocks, EVERY, split_axis=0, concat_axis=0, axis_index_gro...]
    unnamed x22 -> x30, local copies, waits for them, and re-layouts: 7.05 us -> 8.39 us
    pallas_call x2 -> x3, Pallas kernels: 3.62 us -> 4.72 us  [the longest x2 3.42 us: add_four(): call(add_blocks, jax.ShapeDtypeStruct(arrived.shape[1:], BF16), [hbm(), a...]
  transfers between devices with their start and end apart: 9 -> 10, of which waited for: 8 -> 7; matrix products, arithmetic and copies ran while one was open for 2% -> 2% of each run, Pallas kernels for 11% -> 10%
where the time goes in v7:
time: 149 us; the launch traced here: 147 us
  blocking collectives  51.7 us (35%)
  starting transfers between devices  36.3 us (24%)
  Pallas kernels  25.4 us (17%)
  waiting for transfers between devices  19.5 us (13%)
  local copies, waits for them, and re-layouts  12.8 us (9%)
    all_to_all x2, blocking collectives, exchange(): lax.all_to_all(blocks, EVERY, split_axis=0, concat_axis=0, axis_index_gro...  39.4 us
    all_to_all x5, starting transfers between devices, exchange(): lax.all_to_all(blocks, EVERY, split_axis=0, concat_axis=0, axis_index_gro...  23.7 us
    all_gather x1, blocking collectives, per_device(): gathered = lax.all_gather(positives, 'group', axis=0, tiled=True)  12.3 us
    all_to_all x5, waiting for transfers between devices, exchange(): lax.all_to_all(blocks, EVERY, split_axis=0, concat_axis=0, axis_index_gro...  9.84 us
    ppermute x3, starting transfers between devices, per_device(): lax.ppermute(part, 'group', [(g, (g + ahead) % GROUP) for g in range(GROU...  8.6 us
    unnamed x30, local copies, waits for them, and re-layouts  8.39 us
    ppermute x3, waiting for transfers between devices, per_device(): lax.ppermute(part, 'group', [(g, (g + ahead) % GROUP) for g in range(GROU...  7.93 us
    pallas_call x1, Pallas kernels, per_device(): call(terms, (struct((SPOTS, PT, QROWS), BF16), struct((SPOTS, QROWS, D),...  7.59 us
  transfers between devices with their start and end apart: 10, of which 7 were waited for; matrix products, arithmetic and copies ran while one was open for 2% of the time, Pallas kernels for 10%

profile of v7, /device:TPU:6, one launch (start us, length us, event | category | flops | bytes accessed | tf_op | source)
XLA Modules:
  0.0 147.5 jit_solution(10620835404898621560)
XLA Ops:
  0.6 0.0 copy-start.7
  0.6 0.7 copy-done.7
  1.4 0.7 copy-done.8
  2.1 0.7 copy-done.9
  2.8 1.3 shard_map.84
  4.1 15.7 %all_to_all.35 = bf16[4,136,128]{2,1,0:T(8,128)(2,1)S(1)} all-to-all(bf16[4,136,128]{2,1,0:T(8,128)(2,1)S(1)} %get-tuple-element.23), channel_id=1, replica_groups={{0,16,32,48},{128,144,160,176},{256,272,288,304},{384,400,416,432},{8,2..., dimensions={0} | all-to-all | bytes 278528 | tf_op jit(solution)/shard_map/all_to_all | solution.py:66
  19.8 0.1 broadcast_in_dim.6
  19.9 23.7 %all_to_all.36 = bf16[4,4,136,128]{3,2,1,0:T(8,128)(2,1)S(1)} all-to-all(bf16[4,4,136,128]{3,2,1,0:T(8,128)(2,1)S(1)} %broadcast_in_dim.6), channel_id=1, replica_groups={{0,128,256,384},{16,144,272,400},{32,160,288,416},{48,176,304,432},{8,1..., dimensions={0} | all-to-all | bytes 1114112 | tf_op jit(solution)/shard_map/all_to_all | solution.py:66
  43.6 1.7 %broadcast_in_dim.15 = bf16[4,16,136,128]{3,2,1,0:T(8,128)(2,1)} broadcast(bf16[16,136,128]{2,1,0:T(8,128)(2,1)S(1)} %bitcast.12), dimensions={1,2,3} | broadcast | bytes 2785280 | tf_op jit(solution)/shard_map/broadcast_in_dim | solution.py:359
  45.3 3.8 %all-to-all-start.2 = ((bf16[4,16,136,128]{3,2,1,0:T(8,128)(2,1)}), bf16[4,16,136,128]{3,2,1,0:T(8,128)(2,1)S(1)}, u32[]{:S(2)}, u32[]{:S(2)}) async-start(bf16[4,16,136,128]{3,2,1,0:T(8,128)(2,1)} %broadcast_in_dim.15), calls=%async_computation.2 | async-start | bytes 4456448 | tf_op jit(solution)/shard_map/all_to_all | solution.py:66
  49.1 0.0 copy-done.3
  49.1 0.4 shard_map.85.own_rows
  49.4 1.9 %collective-permute-start = (bf16[32,64,128]{2,1,0:T(8,128)(2,1)S(1)}, bf16[32,64,128]{2,1,0:T(8,128)(2,1)S(1)}, u32[]{:S(2)}, u32[]{:S(2)}) collective-permute-start(bf16[32,64,128]{2,1,0:T(8,128)(2,1)S(1)} %shard_map.85.own_rows), channel_id=1, source_target_pairs={{0,4},{4,0},{8,12},{12,8},{16,20},{20,16},{24,28},{28,24},{32,36},... | collective-permute-start | bytes 1572872 | tf_op jit(solution)/shard_map/ppermute | solution.py:362
  51.5 0.0 copy-done.14
  51.5 12.3 %all_gather.3.positives = bf16[16,64,128]{2,1,0:T(8,128)(2,1)S(1)} all-gather(bf16[4,64,128]{2,1,0:T(8,128)(2,1)S(1)} %copy-done.14), channel_id=1, replica_groups=mesh['dp'=128,'group'=4] {'group'}, dimensions={0}, use_global_device_ids=true | all-gather | bytes 327680 | tf_op jit(solution)/shard_map/all_gather | solution.py:363
  63.8 0.6 shard_map.86
  64.4 0.0 copy-start.4
  64.4 0.7 copy-done.4
  65.1 0.1 pad_add_fusion.me
  65.2 0.0 collective-permute-done.other_rows
  65.2 0.0 all-to-all-done.2
  65.2 4.1 %shard_map.87 = (f32[64,128]{1,0:T(8,128)S(1)}, f32[64,4,128]{2,1,0:T(4,128)S(1)}, s32[8,512]{1,0:T(8,128)S(1)}) custom-call(s32[4]{0:T(128)S(1)} %pad_add_fusion.me, bf16[64,136,128]{2,1,0:T(8,128)(2,1)S(1)} %bitcast.8, bf16[32,64,128]{2,1,0:T(8,128)(2,1)S(1)} %shard_map.85.own_rows, bf16[32,64,128]{2,1,0:T(8,128)(2,1)S(1)} %collective-permute-done.other_rows, ...), custom_call_target="tpu_custom_call" | custom-call | tf_op jit(solution)/shard_map/pallas_call | solution.py:368
  69.3 0.0 copy-start.6
  69.3 0.6 copy-done.6
  70.0 6.2 %all-to-all-start.3 = ((f32[64,4,128]{2,1,0:T(4,128)}), f32[64,4,128]{2,1,0:T(4,128)S(1)}, u32[]{:S(2)}, u32[]{:S(2)}) async-start(f32[64,4,128]{2,1,0:T(4,128)} %copy-done.6), calls=%async_computation.3 | async-start | bytes 262144 | tf_op jit(solution)/shard_map/all_to_all | solution.py:66
  76.2 7.6 %shard_map.88 = (bf16[64,64,128]{2,1,0:T(8,128)(2,1)S(1)}, bf16[64,128,128]{2,1,0:T(8,128)(2,1)S(1)}) custom-call(s32[8,512]{1,0:T(8,128)S(1)} %get-tuple-element.26.codes, bf16[64,136,128]{2,1,0:T(8,128)(2,1)S(1)} %bitcast.9, bf16[32,64,128]{2,1,0:T(8,128)(2,1)S(1)} %shard_map.85.own_rows, bf16[32,64,128]{2,1,0:T(8,128)(2,1)S(1)} %collective-permute-done.other_rows, ...), custom_call_target="tpu_custom_call" | custom-call | tf_op jit(solution)/shard_map/pallas_call | solution.py:386
  83.8 0.0 copy-start
  83.8 1.3 copy-done
  85.1 1.0 copy-done.1
  86.1 2.8 %all-to-all-done.3.sums = f32[64,4,128]{2,1,0:T(4,128)S(1)} async-done(((f32[64,4,128]{2,1,0:T(4,128)}), f32[64,4,128]{2,1,0:T(4,128)S(1)}, u32[]{:S(2)}, u32[]{:S(2)}) %all-to-all-start.3) | async-done | bytes 131104 | tf_op jit(solution)/shard_map/all_to_all | solution.py:66
  88.9 4.5 %all-to-all-start.4 = ((bf16[4,16,128,128]{3,2,1,0:T(8,128)(2,1)}), bf16[4,16,128,128]{3,2,1,0:T(8,128)(2,1)}, u32[]{:S(2)}, u32[]{:S(2)}) async-start(bf16[4,16,128,128]{3,2,1,0:T(8,128)(2,1)} %bitcast.11), calls=%async_computation.4 | async-start | bytes 4194304 | tf_op jit(solution)/shard_map/all_to_all | solution.py:66
  93.4 0.0 copy-done.5
  93.4 0.0 copy-start.2
  93.4 1.2 copy-done.2
  94.6 6.1 %shard_map.89 = (f32[32,64,128]{2,1,0:T(8,128)S(1)}, bf16[32,64,128]{2,1,0:T(8,128)(2,1)S(1)}, f32[16,64,128]{2,1,0:T(8,128)S(1)}, f32[128,128]{1,0:T(8,128)S(1)...) custom-call(s32[4]{0:T(128)S(1)} %pad_add_fusion.me, s32[8,512]{1,0:T(8,128)S(1)} %get-tuple-element.26.codes, ...), custom_call_target="tpu_custom_call" | custom-call | tf_op jit(solution)/shard_map/pallas_call | solution.py:394
  100.7 2.1 %collective-permute-start.1 = (bf16[32,64,128]{2,1,0:T(8,128)(2,1)S(1)}, bf16[32,64,128]{2,1,0:T(8,128)(2,1)S(1)}, u32[]{:S(2)}, u32[]{:S(2)}) collective-permute-start(bf16[32,64,128]{2,1,0:T(8,128)(2,1)S(1)} %get-tuple-element.36), channel_id=1, source_target_pairs={{0,4},{4,0},{8,12},{12,8},{16,20},{20,16},{24,28},{28,24},{32,36},... | collective-permute-start | bytes 1572872 | tf_op jit(solution)/shard_map/ppermute | solution.py:421
  102.8 1.7 %collective-permute-done.1.moved = bf16[32,64,128]{2,1,0:T(8,128)(2,1)S(1)} collective-permute-done((bf16[32,64,128]{2,1,0:T(8,128)(2,1)S(1)}, bf16[32,64,128]{2,1,0:T(8,128)(2,1)S(1)}, u32[]{:S(2)}, u32[]{:S(2)}) %collective-permute-start.1) | collective-permute-done | bytes 524320 | tf_op jit(solution)/shard_map/ppermute | solution.py:421
  104.5 0.7 shard_map.90
  105.2 0.0 copy-start.10
  105.2 0.7 copy-done.10
  105.9 0.7 copy-done.12
  106.6 1.9 %all-to-all-done.4.arrived = bf16[4,16,128,128]{3,2,1,0:T(8,128)(2,1)} async-done(((bf16[4,16,128,128]{3,2,1,0:T(8,128)(2,1)}), bf16[4,16,128,128]{3,2,1,0:T(8,128)(2,1)}, u32[]{:S(2)}, u32[]{:S(2)}) %all-to-all-start.4) | async-done | bytes 2097184 | tf_op jit(solution)/shard_map/all_to_all | solution.py:66
  108.5 2.5 %shard_map.91 = bf16[16,128,128]{2,1,0:T(8,128)(2,1)} custom-call(bf16[4,16,128,128]{3,2,1,0:T(8,128)(2,1)} %all-to-all-done.4.arrived, f32[12,64,128]{2,1,0:T(8,128)S(1)} %get-tuple-element.38.after), custom_call_target="tpu_custom_call" | custom-call | tf_op jit(solution)/shard_map/pallas_call | solution.py:316
  111.0 4.1 %all-to-all-start.5 = ((bf16[4,4,128,128]{3,2,1,0:T(8,128)(2,1)}), bf16[4,4,128,128]{3,2,1,0:T(8,128)(2,1)S(1)}, u32[]{:S(2)}, u32[]{:S(2)}) async-start(bf16[4,4,128,128]{3,2,1,0:T(8,128)(2,1)} %bitcast.7), calls=%async_computation.5 | async-start | bytes 1048576 | tf_op jit(solution)/shard_map/all_to_all | solution.py:66
  115.1 0.0 copy-done.13
  115.1 2.5 %collective-permute-start.2 = (bf16[12,64,128]{2,1,0:T(8,128)(2,1)S(1)}, bf16[12,64,128]{2,1,0:T(8,128)(2,1)S(1)}, u32[]{:S(2)}, u32[]{:S(2)}) collective-permute-start(bf16[12,64,128]{2,1,0:T(8,128)(2,1)S(1)} %copy-done.13), channel_id=1, source_target_pairs={{0,1},{1,2},{2,3},{3,0},{4,5},{5,6},{6,7},{7,4},{8,9},{9,10},{10,1... | collective-permute-start | bytes 589832 | tf_op jit(solution)/shard_map/ppermute | solution.py:424
  117.6 2.8 %collective-permute-start.3 = (bf16[12,64,128]{2,1,0:T(8,128)(2,1)S(1)}, bf16[12,64,128]{2,1,0:T(8,128)(2,1)S(1)}, u32[]{:S(2)}, u32[]{:S(2)}) collective-permute-start(bf16[12,64,128]{2,1,0:T(8,128)(2,1)S(1)} %get-tuple-element.40), channel_id=1, source_target_pairs={{0,2},{1,3},{2,0},{3,1},{4,6},{5,7},{6,4},{7,5},{8,10},{9,11},{10,... | collective-permute-start | bytes 589832 | tf_op jit(solution)/shard_map/ppermute | solution.py:424
  120.4 0.0 copy-done.11
  120.4 3.3 %collective-permute-start.4 = (bf16[12,64,128]{2,1,0:T(8,128)(2,1)S(1)}, bf16[12,64,128]{2,1,0:T(8,128)(2,1)S(1)}, u32[]{:S(2)}, u32[]{:S(2)}) collective-permute-start(bf16[12,64,128]{2,1,0:T(8,128)(2,1)S(1)} %copy-done.11), channel_id=1, source_target_pairs={{0,3},{1,0},{2,1},{3,2},{4,7},{5,4},{6,5},{7,6},{8,11},{9,8},{10,9... | collective-permute-start | bytes 589832 | tf_op jit(solution)/shard_map/ppermute | solution.py:424
  123.7 1.1 collective-permute-done.2
  124.8 3.5 %collective-permute-done.3 = bf16[12,64,128]{2,1,0:T(8,128)(2,1)S(1)} collective-permute-done((bf16[12,64,128]{2,1,0:T(8,128)(2,1)S(1)}, bf16[12,64,128]{2,1,0:T(8,128)(2,1)S(1)}, u32[]{:S(2)}, u32[]{:S(2)}) %collective-permute-start.3) | collective-permute-done | bytes 196640 | tf_op jit(solution)/shard_map/ppermute | solution.py:424
  128.3 3.4 %collective-permute-done.4 = bf16[12,64,128]{2,1,0:T(8,128)(2,1)S(1)} collective-permute-done((bf16[12,64,128]{2,1,0:T(8,128)(2,1)S(1)}, bf16[12,64,128]{2,1,0:T(8,128)(2,1)S(1)}, u32[]{:S(2)}, u32[]{:S(2)}) %collective-permute-start.4) | collective-permute-done | bytes 196640 | tf_op jit(solution)/shard_map/ppermute | solution.py:424
  131.7 0.1 convert_add_fusion.after
  131.8 0.0 all-to-all-done.5.arrived
  131.8 0.9 shard_map.92
  132.7 5.1 %all-to-all-start.6 = ((bf16[4,128,128]{2,1,0:T(8,128)(2,1)}), bf16[4,128,128]{2,1,0:T(8,128)(2,1)S(1)}, u32[]{:S(2)}, u32[]{:S(2)}) async-start(bf16[4,128,128]{2,1,0:T(8,128)(2,1)} %shard_map.92), calls=%async_computation.6 | async-start | bytes 262144 | tf_op jit(solution)/shard_map/all_to_all | solution.py:66
  137.8 0.5 broadcast.15
  138.4 0.7 reduce.5
  139.0 0.1 reshape.23
  139.1 0.6 slice_reduce_fusion
  139.7 0.7 slice.13
  140.5 0.7 slice.12
  141.1 5.1 %all-to-all-done.6.arrived = bf16[4,128,128]{2,1,0:T(8,128)(2,1)S(1)} async-done(((bf16[4,128,128]{2,1,0:T(8,128)(2,1)}), bf16[4,128,128]{2,1,0:T(8,128)(2,1)S(1)}, u32[]{:S(2)}, u32[]{:S(2)}) %all-to-all-start.6) | async-done | bytes 131104 | tf_op jit(solution)/shard_map/all_to_all | solution.py:66
  146.2 1.3 shard_map.93
  (9 shorter events, 0.0 us)
Async XLA Ops:
  0.6 0.8 copy-start.7
  1.4 0.7 copy-start.8
  2.1 0.7 copy-start.9
  45.3 3.8 %copy-start.3 = (bf16[32,64,128]{2,1,0:T(8,128)(2,1)S(1)}, bf16[32,64,128]{2,1,0:T(8,128)(2,1)}, u32[]{:S(2)}) copy-start(bf16[32,64,128]{2,1,0:T(8,128)(2,1)} %values.1) | copy-start | bytes 1572868
  45.3 6.2 %copy-start.14 = (bf16[4,64,128]{2,1,0:T(8,128)(2,1)S(1)}, bf16[4,64,128]{2,1,0:T(8,128)(2,1)}, u32[]{:S(2)}) copy-start(bf16[4,64,128]{2,1,0:T(8,128)(2,1)} %param.6) | copy-start | bytes 196612
  45.3 19.9 %all-to-all-start.2 = ((bf16[4,16,136,128]{3,2,1,0:T(8,128)(2,1)}), bf16[4,16,136,128]{3,2,1,0:T(8,128)(2,1)S(1)}, u32[]{:S(2)}, u32[]{:S(2)}) async-start(bf16[4,16,136,128]{3,2,1,0:T(8,128)(2,1)} %broadcast_in_dim.15), calls=%async_computation.2 | async-start | bytes 4456448 | tf_op jit(solution)/shard_map/all_to_all | solution.py:66
  49.4 15.8 %collective-permute-start = (bf16[32,64,128]{2,1,0:T(8,128)(2,1)S(1)}, bf16[32,64,128]{2,1,0:T(8,128)(2,1)S(1)}, u32[]{:S(2)}, u32[]{:S(2)}) collective-permute-start(bf16[32,64,128]{2,1,0:T(8,128)(2,1)S(1)} %shard_map.85.own_rows), channel_id=1, source_target_pairs={{0,4},{4,0},{8,12},{12,8},{16,20},{20,16},{24,28},{28,24},{32,36},... | collective-permute-start | bytes 1572872 | tf_op jit(solution)/shard_map/ppermute | solution.py:362
  64.4 0.7 copy-start.4
  69.3 0.7 copy-start.6
  70.0 18.9 %all-to-all-start.3 = ((f32[64,4,128]{2,1,0:T(4,128)}), f32[64,4,128]{2,1,0:T(4,128)S(1)}, u32[]{:S(2)}, u32[]{:S(2)}) async-start(f32[64,4,128]{2,1,0:T(4,128)} %copy-done.6), calls=%async_computation.3 | async-start | bytes 262144 | tf_op jit(solution)/shard_map/all_to_all | solution.py:66
  83.8 1.3 copy-start
  85.1 1.0 copy-start.1
  86.1 7.3 %copy-start.5 = (bf16[16,64,128]{2,1,0:T(8,128)(2,1)S(1)}, bf16[16,64,128]{2,1,0:T(8,128)(2,1)}, u32[]{:S(2)}) copy-start(bf16[16,64,128]{2,1,0:T(8,128)(2,1)} %copy-done.4) | copy-start | bytes 786436
  88.9 19.6 %all-to-all-start.4 = ((bf16[4,16,128,128]{3,2,1,0:T(8,128)(2,1)}), bf16[4,16,128,128]{3,2,1,0:T(8,128)(2,1)}, u32[]{:S(2)}, u32[]{:S(2)}) async-start(bf16[4,16,128,128]{3,2,1,0:T(8,128)(2,1)} %bitcast.11), calls=%async_computation.4 | async-start | bytes 4194304 | tf_op jit(solution)/shard_map/all_to_all | solution.py:66
  93.4 1.2 copy-start.2
  100.7 3.8 %collective-permute-start.1 = (bf16[32,64,128]{2,1,0:T(8,128)(2,1)S(1)}, bf16[32,64,128]{2,1,0:T(8,128)(2,1)S(1)}, u32[]{:S(2)}, u32[]{:S(2)}) collective-permute-start(bf16[32,64,128]{2,1,0:T(8,128)(2,1)S(1)} %get-tuple-element.36), channel_id=1, source_target_pairs={{0,4},{4,0},{8,12},{12,8},{16,20},{20,16},{24,28},{28,24},{32,36},... | collective-permute-start | bytes 1572872 | tf_op jit(solution)/shard_map/ppermute | solution.py:421
  105.2 0.7 copy-start.10
  105.9 0.7 copy-start.12
  108.5 6.6 %copy-start.13 = (bf16[12,64,128]{2,1,0:T(8,128)(2,1)S(1)}, bf16[12,64,128]{2,1,0:T(8,128)(2,1)}, u32[]{:S(2)}) copy-start(bf16[12,64,128]{2,1,0:T(8,128)(2,1)} %copy-done.12) | copy-start | bytes 589828
  108.5 11.9 %copy-start.11 = (bf16[12,64,128]{2,1,0:T(8,128)(2,1)S(1)}, bf16[12,64,128]{2,1,0:T(8,128)(2,1)}, u32[]{:S(2)}) copy-start(bf16[12,64,128]{2,1,0:T(8,128)(2,1)} %copy-done.10) | copy-start | bytes 589828
  111.0 20.8 %all-to-all-start.5 = ((bf16[4,4,128,128]{3,2,1,0:T(8,128)(2,1)}), bf16[4,4,128,128]{3,2,1,0:T(8,128)(2,1)S(1)}, u32[]{:S(2)}, u32[]{:S(2)}) async-start(bf16[4,4,128,128]{3,2,1,0:T(8,128)(2,1)} %bitcast.7), calls=%async_computation.5 | async-start | bytes 1048576 | tf_op jit(solution)/shard_map/all_to_all | solution.py:66
  115.1 9.7 %collective-permute-start.2 = (bf16[12,64,128]{2,1,0:T(8,128)(2,1)S(1)}, bf16[12,64,128]{2,1,0:T(8,128)(2,1)S(1)}, u32[]{:S(2)}, u32[]{:S(2)}) collective-permute-start(bf16[12,64,128]{2,1,0:T(8,128)(2,1)S(1)} %copy-done.13), channel_id=1, source_target_pairs={{0,1},{1,2},{2,3},{3,0},{4,5},{5,6},{6,7},{7,4},{8,9},{9,10},{10,1... | collective-permute-start | bytes 589832 | tf_op jit(solution)/shard_map/ppermute | solution.py:424
  117.6 10.7 %collective-permute-start.3 = (bf16[12,64,128]{2,1,0:T(8,128)(2,1)S(1)}, bf16[12,64,128]{2,1,0:T(8,128)(2,1)S(1)}, u32[]{:S(2)}, u32[]{:S(2)}) collective-permute-start(bf16[12,64,128]{2,1,0:T(8,128)(2,1)S(1)} %get-tuple-element.40), channel_id=1, source_target_pairs={{0,2},{1,3},{2,0},{3,1},{4,6},{5,7},{6,4},{7,5},{8,10},{9,11},{10,... | collective-permute-start | bytes 589832 | tf_op jit(solution)/shard_map/ppermute | solution.py:424
  120.4 11.3 %collective-permute-start.4 = (bf16[12,64,128]{2,1,0:T(8,128)(2,1)S(1)}, bf16[12,64,128]{2,1,0:T(8,128)(2,1)S(1)}, u32[]{:S(2)}, u32[]{:S(2)}) collective-permute-start(bf16[12,64,128]{2,1,0:T(8,128)(2,1)S(1)} %copy-done.11), channel_id=1, source_target_pairs={{0,3},{1,0},{2,1},{3,2},{4,7},{5,4},{6,5},{7,6},{8,11},{9,8},{10,9... | collective-permute-start | bytes 589832 | tf_op jit(solution)/shard_map/ppermute | solution.py:424
  132.7 13.5 %all-to-all-start.6 = ((bf16[4,128,128]{2,1,0:T(8,128)(2,1)}), bf16[4,128,128]{2,1,0:T(8,128)(2,1)S(1)}, u32[]{:S(2)}, u32[]{:S(2)}) async-start(bf16[4,128,128]{2,1,0:T(8,128)(2,1)} %shard_map.92), calls=%async_computation.6 | async-start | bytes 262144 | tf_op jit(solution)/shard_map/all_to_all | solution.py:66

commit v8 on v6

--- a/solution.py
+++ b/solution.py
@@ -13,7 +13,7 @@
 SENT = QROWS + 8
 BATCH = QD * GROUP
 SLOTS = 4
-VMEM = 16 * 1024 * 1024
+VMEM = 6 * 1024 * 1024
 F32, BF16, I32 = jnp.float32, jnp.bfloat16, jnp.int32
 EXACT = lax.Precision.HIGHEST
 EVERY = ("dp", "group")
@@ -88,6 +88,13 @@
     for copy in copies:
         copy.start()
     return copies
+
+
+def position():
+    holder = lax.axis_index("dp")
+    spot, core = holder // N_C, holder % N_C
+    source = jnp.where(core == 0, spot, (spot % N_Y) * N_Z + spot // N_Y)
+    return spot, core, source
 
 
 def prepare(ids_in, storage_in, queries_in, sent, q_unit, ids, storage, queries, sems, count):
@@ -155,11 +162,12 @@
     return jnp.concatenate([jnp.where(block == b, packed, 0.0).astype(BF16) for b in range(SLOTS)], axis=0)
 
 
-def read_codes(me, asked, table, codes, sem):
+def read_codes(asked, table, codes, sem):
+    spot, core, _ = position()
     rows = asked[:, QROWS:SENT, :].reshape(SPOTS * 8, N_DP)
     which = iota((8, N_DP), 0)
-    spot = jnp.where(which == 0, me[2], me[3])
-    pick = ((iota((8, N_DP), 1) == spot) & (which < 2)).astype(F32).astype(BF16)
+    lane = jnp.where(which == 0, core * SPOTS + spot, (1 - core) * SPOTS + spot)
+    pick = ((iota((8, N_DP), 1) == lane) & (which < 2)).astype(F32).astype(BF16)
     table[...] = dot(pick, rows, ((1,), (1,))).astype(I32)
     copy = pltpu.make_async_copy(table, codes, sem)
     copy.start()
@@ -175,8 +183,9 @@
     return jnp.exp(10.0 * packed)
 
 
-def score(me, asked, own_rows, other_rows, pos_weight, factor, sums, table, totals, marks, codes, sem):
-    read_codes(me, asked, table, codes, sem)
+def score(asked, own_rows, other_rows, pos_weight, factor, sums, table, totals, marks, codes, sem):
+    read_codes(asked, table, codes, sem)
+    source_here = position()[2]
     lane = iota((1, QROWS), 1)
 
     def one(source, carry):
@@ -206,7 +215,7 @@
         mine = jnp.where((mark == float(q)) & first, weight, 0.0)
         part = dot(ones, jnp.concatenate([mine, pad], axis=0), ((1,), (1,)), EXACT)[0:1]
         own = jnp.sum(jnp.where(lane == q * QT, pos_weight[...], 0.0), axis=1, keepdims=True)
-        parts.append(part + jnp.where(lane == me[0], own, 0.0))
+        parts.append(part + jnp.where(lane == source_here, own, 0.0))
     sums[...] = jnp.broadcast_to(jnp.concatenate(parts, axis=0)[None], (SPOTS, QD, QROWS))
 
 
@@ -227,7 +236,7 @@
 
 
 def weigh(
-    me, codes, sums, asked, probs, q_in, gathered_in, own_grad, other_grad, pos_grad, query_part, losses, weight_inv,
+    codes, sums, asked, probs, q_in, gathered_in, own_grad, other_grad, pos_grad, query_part, losses, weight_inv,
     other_acc, inverse, q_tiles, gathered, sems,
 ):
     later = fetch([(q_in, q_tiles), (gathered_in, gathered)], sems)
@@ -256,11 +265,11 @@
     q_unit = q_tiles[...].reshape(QROWS, D)
     cands, exp_scores, total, scores = positive_scores(q_unit, gathered)
     lane = iota((1, QROWS), 1)
-    mine = jnp.sum(jnp.where(lane == me[0], weight_sum, 0.0), axis=1, keepdims=True)
+    mine = jnp.sum(jnp.where(lane == position()[2], weight_sum, 0.0), axis=1, keepdims=True)
     own_sum = jnp.zeros((1, QROWS), F32)
     for q in range(QD):
         own_sum = jnp.where(lane // QT == q, mine[q : q + 1], own_sum)
-    own = (iota((BATCH, QROWS), 0) == me[1] * QD + iota((BATCH, QROWS), 1) // QT).astype(F32)
+    own = (iota((BATCH, QROWS), 0) == lax.axis_index("group") * QD + iota((BATCH, QROWS), 1) // QT).astype(F32)
     score_grad = jnp.exp(scores) / own_sum - own
     losses[...] = jnp.log(own_sum) - jnp.sum(scores * own, axis=0, keepdims=True)
     weight_grad = (exp_scores * (score_grad / total)[:, None, :]).astype(BF16).reshape(BATCH * PT, QROWS)
@@ -268,38 +277,31 @@
     pos_grad[...] = dot(weight_grad, q_unit, ((1,), (0,))).reshape(BATCH, PT, D)
 
 
-def split(me, own_grad, moved, pos_grad, kept, off1, off2, off3):
+def split(own_grad, moved, pos_grad, kept, off1, off2, off3):
     share = ROWS // GROUP
     for ahead, out in enumerate((kept, off1, off2, off3)):
-        g = (me[1] + ahead) % GROUP
+        g = (lax.axis_index("group") + ahead) % GROUP
         out[0:QD] = pos_grad[pl.ds(g * QD, QD)].astype(out.dtype)
         rows = pl.ds(g * share, share)
         out[QD:] = (own_grad[rows] + moved[rows].astype(F32)).astype(out.dtype)
 
 
-def add_blocks(arrived, after, out, blocks, sems):
+def add_blocks(arrived, after, out):
     del after
-    pairs = [(arrived.at[:, pl.ds(2 * i, 2)], blocks.at[:, pl.ds(2 * i, 2)]) for i in range(N_Y // 2)]
-    for i, copy in enumerate(fetch(pairs, sems)):
-        copy.wait()
-        part = slice(2 * i, 2 * i + 2)
-        out[part] = jnp.sum(blocks[:, part].astype(F32), axis=0).astype(BF16)
-
-
-def collect(weight_inv, me, query_part, arrived, out):
+    for part in range(N_Y):
+        out[part] = jnp.sum(arrived[:, part].astype(F32), axis=0).astype(BF16)
+
+
+def collect(weight_inv, query_part, arrived, out):
+    source = position()[2]
     total = jnp.sum(arrived[...].astype(F32), axis=0)
     for q in range(QD):
         rows = slice(q * QT, (q + 1) * QT)
-        out[q] = query_part[rows, :] + total[rows] * weight_inv[q, me[0]]
+        out[q] = query_part[rows, :] + total[rows] * weight_inv[q, source]
 
 
 def per_device(queries, positives, passage_pool, negative_ids, storage_row):
     struct = jax.ShapeDtypeStruct
-    holder = lax.axis_index("dp")
-    z, y, core = holder // (N_Y * N_C), (holder // N_C) % N_Y, holder % N_C
-    source = jnp.where(core == 0, z * N_Y + y, y * N_Z + z)
-    spot = holder // N_C
-    me = jnp.stack([source, lax.axis_index("group"), core * SPOTS + spot, (1 - core) * SPOTS + spot]).astype(I32)
     swap = [(h, h ^ 1) for h in range(N_DP)]
     tiles = struct((QD, QT, D), BF16)
 
@@ -333,7 +335,7 @@
             struct((SPOTS, QD, QROWS), F32),
             struct((8, SPOTS * 8), I32),
         ),
-        [smem(), vmem(), vmem(), vmem(), vmem()],
+        [vmem(), vmem(), vmem(), vmem()],
         (vmem(), vmem(), vmem()),
         [
             pltpu.VMEM((SPOTS, QROWS), F32),
@@ -341,7 +343,7 @@
             pltpu.SMEM((8, SPOTS * 8), I32),
             pltpu.SemaphoreType.DMA,
         ],
-    )(me, asked, own_rows, other_rows, pos_weight)
+    )(asked, own_rows, other_rows, pos_weight)
     sums = exchange(sums, planes())
 
     probs, back = call(
@@ -362,7 +364,7 @@
             struct((1, QROWS), F32),
             struct((8, QROWS), F32),
         ),
-        [smem(), smem(), vmem(), vmem(), vmem(), hbm(), hbm()],
+        [smem(), vmem(), vmem(), vmem(), hbm(), hbm()],
         (vmem(),) * 5 + (smem(),),
         [
             pltpu.VMEM((ROWS, PT, D), F32),
@@ -371,31 +373,25 @@
             pltpu.VMEM((BATCH, PT, D), BF16),
             pltpu.SemaphoreType.DMA((3,)),
         ],
-    )(me, codes, sums, asked, probs, q_unit, gathered)
+    )(codes, sums, asked, probs, q_unit, gathered)
 
     block = (QD + ROWS // GROUP, PT, D)
     kept, off1, off2, off3 = call(
         split,
         (struct(block, F32), struct(block, BF16), struct(block, BF16), struct(block, BF16)),
-        [smem(), vmem(), vmem(), vmem()],
+        [vmem(), vmem(), vmem()],
         (vmem(),) * 4,
-    )(me, own_grad, lax.ppermute(other_grad, "dp", swap), pos_grad)
+    )(own_grad, lax.ppermute(other_grad, "dp", swap), pos_grad)
     total = kept
     for ahead, part in ((1, off1), (2, off2), (3, off3)):
         moved = lax.ppermute(part, "group", [(g, (g + ahead) % GROUP) for g in range(GROUP)])
         total = total + moved.astype(F32)
 
-    arrived = call(
-        add_blocks,
-        struct((N_Y, QROWS, D), BF16),
-        [hbm(), anywhere()],
-        vmem(),
-        [pltpu.VMEM((N_Z, N_Y, QROWS, D), BF16), pltpu.SemaphoreType.DMA((N_Y // 2,))],
-    )(arrived, total)
+    arrived = call(add_blocks, struct((N_Y, QROWS, D), BF16), [vmem(), anywhere()], vmem())(arrived, total)
     arrived = exchange(arrived, along(1))
     query_grad = call(
-        collect, struct((QD, QT, D), F32), [smem(), smem(), vmem(), vmem()], vmem()
-    )(weight_inv, me, query_part, arrived)
+        collect, struct((QD, QT, D), F32), [smem(), vmem(), vmem()], vmem()
+    )(weight_inv, query_part, arrived)
     return losses.reshape(QD, QT)[:, 0], query_grad, total[:QD], total[QD:]
 
 

time: 144 us -> 143 us (level)
  transfers between devices with their start and end apart: 9 -> 9, of which waited for: 8 -> 8; matrix products, arithmetic and copies ran while one was open for 2% -> 2% of each run, Pallas kernels for 11% -> 10%
where the time goes in v8:
time: 143 us
  starting transfers between devices  38.5 us (27%)
  waiting for transfers between devices  38.1 us (27%)
  blocking collectives  29.8 us (21%)
  Pallas kernels  23.6 us (17%)
  local copies, waits for them, and re-layouts  11.1 us (8%)
    all_to_all x4, waiting for transfers between devices, exchange(): lax.all_to_all(blocks, EVERY, split_axis=0, concat_axis=0, axis_index_gro...  28.2 us
    all_to_all x4, starting transfers between devices, exchange(): lax.all_to_all(blocks, EVERY, split_axis=0, concat_axis=0, axis_index_gro...  26.1 us
    all_to_all x1, blocking collectives, exchange(): lax.all_to_all(blocks, EVERY, split_axis=0, concat_axis=0, axis_index_gro...  17.6 us
    all_gather x1, blocking collectives, per_device(): gathered = lax.all_gather(positives, 'group', axis=0, tiled=True)  12.3 us
    ppermute x3, starting transfers between devices, per_device(): lax.ppermute(part, 'group', [(g, (g + ahead) % GROUP) for g in range(GROU...  8.64 us
    ppermute x3, waiting for transfers between devices, per_device(): lax.ppermute(part, 'group', [(g, (g + ahead) % GROUP) for g in range(GROU...  8.01 us
    pallas_call x1, Pallas kernels, per_device(): call(terms, (struct((SPOTS, PT, QROWS), BF16), struct((SPOTS, QROWS, D),...  7.59 us
    unnamed x22, local copies, waits for them, and re-layouts  6.78 us
  transfers between devices with their start and end apart: 9, of which 8 were waited for; matrix products, arithmetic and copies ran while one was open for 2% of the time, Pallas kernels for 10%

profile of v8, /device:TPU:6, one launch (start us, length us, event | category | flops | bytes accessed | tf_op | source)
XLA Modules:
  0.0 142.6 jit_solution(8843272138715881795)
XLA Ops:
  0.6 0.0 copy-start.7
  0.6 0.7 copy-done.7
  1.4 0.0 copy-start.8
  1.4 0.7 copy-done.8
  2.1 0.0 copy-start.9
  2.1 0.7 copy-done.9
  2.8 1.3 shard_map.84
  4.1 17.6 %all_to_all.25 = bf16[8,136,128]{2,1,0:T(8,128)(2,1)S(1)} all-to-all(bf16[8,136,128]{2,1,0:T(8,128)(2,1)S(1)} %get-tuple-element.23), channel_id=1, replica_groups={{4,68,132,196,260,324,388,452},{5,69,133,197,261,325,389,453},{6,70,134..., dimensions={0} | all-to-all | bytes 557056 | tf_op jit(solution)/shard_map/all_to_all | solution.py:39
  21.7 1.7 %broadcast_in_dim.2 = bf16[8,8,136,128]{3,2,1,0:T(8,128)(2,1)} broadcast(bf16[8,136,128]{2,1,0:T(8,128)(2,1)S(1)} %all_to_all.25), dimensions={1,2,3} | broadcast | bytes 2506752 | tf_op jit(solution)/shard_map/broadcast_in_dim | solution.py:322
  23.3 0.0 copy-start.3
  23.4 0.0 copy-start.10
  23.4 10.4 %all-to-all-start.1 = ((bf16[8,8,136,128]{3,2,1,0:T(8,128)(2,1)}), bf16[8,8,136,128]{3,2,1,0:T(8,128)(2,1)S(1)}, u32[]{:S(2)}, u32[]{:S(2)}) async-start(bf16[8,8,136,128]{3,2,1,0:T(8,128)(2,1)} %broadcast_in_dim.2), calls=%async_computation.1 | async-start | bytes 4456448 | tf_op jit(solution)/shard_map/all_to_all | solution.py:39
  33.8 0.0 copy-done.3
  33.8 0.4 shard_map.85.own_rows
  34.2 1.9 %collective-permute-start = (bf16[32,64,128]{2,1,0:T(8,128)(2,1)S(1)}, bf16[32,64,128]{2,1,0:T(8,128)(2,1)S(1)}, u32[]{:S(2)}, u32[]{:S(2)}) collective-permute-start(bf16[32,64,128]{2,1,0:T(8,128)(2,1)S(1)} %shard_map.85.own_rows), channel_id=1, source_target_pairs={{0,4},{4,0},{8,12},{12,8},{16,20},{20,16},{24,28},{28,24},{32,36},... | collective-permute-start | bytes 1572872 | tf_op jit(solution)/shard_map/ppermute | solution.py:325
  36.1 0.0 copy-done.10
  36.1 12.3 %all_gather.3.positives = bf16[16,64,128]{2,1,0:T(8,128)(2,1)S(1)} all-gather(bf16[4,64,128]{2,1,0:T(8,128)(2,1)S(1)} %copy-done.10), channel_id=1, replica_groups=mesh['dp'=128,'group'=4] {'group'}, dimensions={0}, use_global_device_ids=true | all-gather | bytes 327680 | tf_op jit(solution)/shard_map/all_gather | solution.py:326
  48.4 0.6 shard_map.86
  49.0 0.0 copy-start.4
  49.0 0.7 copy-done.4
  49.7 0.0 collective-permute-done.other_rows
  49.7 15.8 %all-to-all-done.1 = bf16[8,8,136,128]{3,2,1,0:T(8,128)(2,1)S(1)} async-done(((bf16[8,8,136,128]{3,2,1,0:T(8,128)(2,1)}), bf16[8,8,136,128]{3,2,1,0:T(8,128)(2,1)S(1)}, u32[]{:S(2)}, u32[]{:S(2)}) %all-to-all-start.1) | async-done | bytes 2228256 | tf_op jit(solution)/shard_map/all_to_all | solution.py:39
  65.5 3.6 %shard_map.87 = (f32[64,128]{1,0:T(8,128)S(1)}, f32[64,4,128]{2,1,0:T(4,128)S(1)}, s32[8,512]{1,0:T(8,128)S(1)}) custom-call(bf16[64,136,128]{2,1,0:T(8,128)(2,1)S(1)} %bitcast.2, bf16[32,64,128]{2,1,0:T(8,128)(2,1)S(1)} %shard_map.85.own_rows, bf16[32,64,128]{2,1,0:T(8,128)(2,1)S(1)} %collective-permute-done.other_rows, ...), custom_call_target="tpu_custom_call" | custom-call | tf_op jit(solution)/shard_map/pallas_call | solution.py:331
  69.1 0.0 copy-start.6
  69.1 0.6 copy-done.6
  69.7 4.6 %all-to-all-start.2 = ((f32[64,4,128]{2,1,0:T(4,128)}), f32[64,4,128]{2,1,0:T(4,128)S(1)}, u32[]{:S(2)}, u32[]{:S(2)}) async-start(f32[64,4,128]{2,1,0:T(4,128)} %copy-done.6), calls=%async_computation.2 | async-start | bytes 262144 | tf_op jit(solution)/shard_map/all_to_all | solution.py:39
  74.3 7.6 %shard_map.88 = (bf16[64,64,128]{2,1,0:T(8,128)(2,1)S(1)}, bf16[64,128,128]{2,1,0:T(8,128)(2,1)S(1)}) custom-call(s32[8,512]{1,0:T(8,128)S(1)} %get-tuple-element.26.codes, bf16[64,136,128]{2,1,0:T(8,128)(2,1)S(1)} %bitcast.3, bf16[32,64,128]{2,1,0:T(8,128)(2,1)S(1)} %shard_map.85.own_rows, bf16[32,64,128]{2,1,0:T(8,128)(2,1)S(1)} %collective-permute-done.other_rows, ...), custom_call_target="tpu_custom_call" | custom-call | tf_op jit(solution)/shard_map/pallas_call | solution.py:349
  81.9 0.0 copy-start
  81.9 1.3 copy-done
  83.2 0.0 copy-start.1
  83.3 1.0 copy-done.1
  84.3 2.8 %all-to-all-done.2.sums = f32[64,4,128]{2,1,0:T(4,128)S(1)} async-done(((f32[64,4,128]{2,1,0:T(4,128)}), f32[64,4,128]{2,1,0:T(4,128)S(1)}, u32[]{:S(2)}, u32[]{:S(2)}) %all-to-all-start.2) | async-done | bytes 131104 | tf_op jit(solution)/shard_map/all_to_all | solution.py:39
  87.0 0.0 copy-start.2
  87.0 4.5 %all-to-all-start.3 = ((bf16[8,8,128,128]{3,2,1,0:T(8,128)(2,1)}), bf16[8,8,128,128]{3,2,1,0:T(8,128)(2,1)}, u32[]{:S(2)}, u32[]{:S(2)}) async-start(bf16[8,8,128,128]{3,2,1,0:T(8,128)(2,1)} %bitcast.5), calls=%async_computation.3 | async-start | bytes 4194304 | tf_op jit(solution)/shard_map/all_to_all | solution.py:39
  91.5 0.0 copy-done.2
  91.5 0.0 copy-start.5
  91.6 0.9 copy-done.5
  92.5 6.2 %shard_map.89 = (f32[32,64,128]{2,1,0:T(8,128)S(1)}, bf16[32,64,128]{2,1,0:T(8,128)(2,1)S(1)}, f32[16,64,128]{2,1,0:T(8,128)S(1)}, f32[128,128]{1,0:T(8,128)S(1)...) custom-call(s32[8,512]{1,0:T(8,128)S(1)} %get-tuple-element.26.codes, f32[64,4,128]{2,1,0:T(4,128)S(1)} %all-to-all-done.2.sums, ...), custom_call_target="tpu_custom_call" | custom-call | tf_op jit(solution)/shard_map/pallas_call | solution.py:357
  98.7 1.9 %collective-permute-start.1 = (bf16[32,64,128]{2,1,0:T(8,128)(2,1)S(1)}, bf16[32,64,128]{2,1,0:T(8,128)(2,1)S(1)}, u32[]{:S(2)}, u32[]{:S(2)}) collective-permute-start(bf16[32,64,128]{2,1,0:T(8,128)(2,1)S(1)} %get-tuple-element.36), channel_id=1, source_target_pairs={{0,4},{4,0},{8,12},{12,8},{16,20},{20,16},{24,28},{28,24},{32,36},... | collective-permute-start | bytes 1572872 | tf_op jit(solution)/shard_map/ppermute | solution.py:384
  100.6 1.9 %collective-permute-done.1.moved = bf16[32,64,128]{2,1,0:T(8,128)(2,1)S(1)} collective-permute-done((bf16[32,64,128]{2,1,0:T(8,128)(2,1)S(1)}, bf16[32,64,128]{2,1,0:T(8,128)(2,1)S(1)}, u32[]{:S(2)}, u32[]{:S(2)}) %collective-permute-start.1) | collective-permute-done | bytes 524320 | tf_op jit(solution)/shard_map/ppermute | solution.py:384
  102.5 0.1 shard_map.90
  102.6 2.4 %collective-permute-start.2 = (bf16[12,64,128]{2,1,0:T(8,128)(2,1)S(1)}, bf16[12,64,128]{2,1,0:T(8,128)(2,1)S(1)}, u32[]{:S(2)}, u32[]{:S(2)}) collective-permute-start(bf16[12,64,128]{2,1,0:T(8,128)(2,1)S(1)} %get-tuple-element.39), channel_id=1, source_target_pairs={{0,1},{1,2},{2,3},{3,0},{4,5},{5,6},{6,7},{7,4},{8,9},{9,10},{10,1... | collective-permute-start | bytes 589832 | tf_op jit(solution)/shard_map/ppermute | solution.py:387
  105.0 4.3 %collective-permute-start.3 = (bf16[12,64,128]{2,1,0:T(8,128)(2,1)S(1)}, bf16[12,64,128]{2,1,0:T(8,128)(2,1)S(1)}, u32[]{:S(2)}, u32[]{:S(2)}) collective-permute-start(bf16[12,64,128]{2,1,0:T(8,128)(2,1)S(1)} %get-tuple-element.40), channel_id=1, source_target_pairs={{0,2},{1,3},{2,0},{3,1},{4,6},{5,7},{6,4},{7,5},{8,10},{9,11},{10,... | collective-permute-start | bytes 589832 | tf_op jit(solution)/shard_map/ppermute | solution.py:387
  109.4 1.9 %collective-permute-start.4 = (bf16[12,64,128]{2,1,0:T(8,128)(2,1)S(1)}, bf16[12,64,128]{2,1,0:T(8,128)(2,1)S(1)}, u32[]{:S(2)}, u32[]{:S(2)}) collective-permute-start(bf16[12,64,128]{2,1,0:T(8,128)(2,1)S(1)} %get-tuple-element.41), channel_id=1, source_target_pairs={{0,3},{1,0},{2,1},{3,2},{4,7},{5,4},{6,5},{7,6},{8,11},{9,8},{10,9... | collective-permute-start | bytes 589832 | tf_op jit(solution)/shard_map/ppermute | solution.py:387
  111.3 1.0 collective-permute-done.2
  112.3 3.2 %collective-permute-done.3 = bf16[12,64,128]{2,1,0:T(8,128)(2,1)S(1)} collective-permute-done((bf16[12,64,128]{2,1,0:T(8,128)(2,1)S(1)}, bf16[12,64,128]{2,1,0:T(8,128)(2,1)S(1)}, u32[]{:S(2)}, u32[]{:S(2)}) %collective-permute-start.3) | collective-permute-done | bytes 196640 | tf_op jit(solution)/shard_map/ppermute | solution.py:387
  115.4 3.9 %collective-permute-done.4 = bf16[12,64,128]{2,1,0:T(8,128)(2,1)S(1)} collective-permute-done((bf16[12,64,128]{2,1,0:T(8,128)(2,1)S(1)}, bf16[12,64,128]{2,1,0:T(8,128)(2,1)S(1)}, u32[]{:S(2)}, u32[]{:S(2)}) %collective-permute-start.4) | collective-permute-done | bytes 196640 | tf_op jit(solution)/shard_map/ppermute | solution.py:387
  119.3 0.1 convert_add_fusion.after
  119.4 2.4 %all-to-all-done.3.arrived = bf16[8,8,128,128]{3,2,1,0:T(8,128)(2,1)} async-done(((bf16[8,8,128,128]{3,2,1,0:T(8,128)(2,1)}), bf16[8,8,128,128]{3,2,1,0:T(8,128)(2,1)}, u32[]{:S(2)}, u32[]{:S(2)}) %all-to-all-start.3) | async-done | bytes 2097184 | tf_op jit(solution)/shard_map/all_to_all | solution.py:39
  121.8 2.6 %shard_map.91 = bf16[8,128,128]{2,1,0:T(8,128)(2,1)} custom-call(bf16[8,8,128,128]{3,2,1,0:T(8,128)(2,1)} %all-to-all-done.3.arrived, f32[12,64,128]{2,1,0:T(8,128)S(1)} %convert_add_fusion.after), custom_call_target="tpu_custom_call" | custom-call | tf_op jit(solution)/shard_map/pallas_call | solution.py:390
  124.4 6.5 %all-to-all-start.4 = ((bf16[8,128,128]{2,1,0:T(8,128)(2,1)}), bf16[8,128,128]{2,1,0:T(8,128)(2,1)S(1)}, u32[]{:S(2)}, u32[]{:S(2)}) async-start(bf16[8,128,128]{2,1,0:T(8,128)(2,1)} %shard_map.91), calls=%async_computation.4 | async-start | bytes 524288 | tf_op jit(solution)/shard_map/all_to_all | solution.py:39
  130.9 0.5 broadcast.5
  131.4 0.7 reduce.5
  132.0 0.1 reshape.19
  132.1 0.6 slice_reduce_fusion
  132.8 0.7 slice.13
  133.5 0.7 slice.12
  134.1 7.2 %all-to-all-done.4.arrived = bf16[8,128,128]{2,1,0:T(8,128)(2,1)S(1)} async-done(((bf16[8,128,128]{2,1,0:T(8,128)(2,1)}), bf16[8,128,128]{2,1,0:T(8,128)(2,1)S(1)}, u32[]{:S(2)}, u32[]{:S(2)}) %all-to-all-start.4) | async-done | bytes 262176 | tf_op jit(solution)/shard_map/all_to_all | solution.py:39
  141.4 1.3 shard_map.92
Async XLA Ops:
  0.6 0.8 copy-start.7
  1.4 0.7 copy-start.8
  2.1 0.7 copy-start.9
  23.3 10.5 %copy-start.3 = (bf16[32,64,128]{2,1,0:T(8,128)(2,1)S(1)}, bf16[32,64,128]{2,1,0:T(8,128)(2,1)}, u32[]{:S(2)}) copy-start(bf16[32,64,128]{2,1,0:T(8,128)(2,1)} %values.1) | copy-start | bytes 1572868
  23.4 12.7 %copy-start.10 = (bf16[4,64,128]{2,1,0:T(8,128)(2,1)S(1)}, bf16[4,64,128]{2,1,0:T(8,128)(2,1)}, u32[]{:S(2)}) copy-start(bf16[4,64,128]{2,1,0:T(8,128)(2,1)} %param.6) | copy-start | bytes 196612
  23.4 42.1 %all-to-all-start.1 = ((bf16[8,8,136,128]{3,2,1,0:T(8,128)(2,1)}), bf16[8,8,136,128]{3,2,1,0:T(8,128)(2,1)S(1)}, u32[]{:S(2)}, u32[]{:S(2)}) async-start(bf16[8,8,136,128]{3,2,1,0:T(8,128)(2,1)} %broadcast_in_dim.2), calls=%async_computation.1 | async-start | bytes 4456448 | tf_op jit(solution)/shard_map/all_to_all | solution.py:39
  34.2 15.5 %collective-permute-start = (bf16[32,64,128]{2,1,0:T(8,128)(2,1)S(1)}, bf16[32,64,128]{2,1,0:T(8,128)(2,1)S(1)}, u32[]{:S(2)}, u32[]{:S(2)}) collective-permute-start(bf16[32,64,128]{2,1,0:T(8,128)(2,1)S(1)} %shard_map.85.own_rows), channel_id=1, source_target_pairs={{0,4},{4,0},{8,12},{12,8},{16,20},{20,16},{24,28},{28,24},{32,36},... | collective-permute-start | bytes 1572872 | tf_op jit(solution)/shard_map/ppermute | solution.py:325
  49.0 0.7 copy-start.4
  69.1 0.7 copy-start.6
  69.7 17.3 %all-to-all-start.2 = ((f32[64,4,128]{2,1,0:T(4,128)}), f32[64,4,128]{2,1,0:T(4,128)S(1)}, u32[]{:S(2)}, u32[]{:S(2)}) async-start(f32[64,4,128]{2,1,0:T(4,128)} %copy-done.6), calls=%async_computation.2 | async-start | bytes 262144 | tf_op jit(solution)/shard_map/all_to_all | solution.py:39
  81.9 1.3 copy-start
  83.2 1.0 copy-start.1
  87.0 4.5 %copy-start.2 = (bf16[64,64,128]{2,1,0:T(8,128)(2,1)S(1)}, bf16[64,64,128]{2,1,0:T(8,128)(2,1)}, u32[]{:S(2)}) copy-start(bf16[64,64,128]{2,1,0:T(8,128)(2,1)} %copy-done.1) | copy-start | bytes 3145732
  87.0 34.8 %all-to-all-start.3 = ((bf16[8,8,128,128]{3,2,1,0:T(8,128)(2,1)}), bf16[8,8,128,128]{3,2,1,0:T(8,128)(2,1)}, u32[]{:S(2)}, u32[]{:S(2)}) async-start(bf16[8,8,128,128]{3,2,1,0:T(8,128)(2,1)} %bitcast.5), calls=%async_computation.3 | async-start | bytes 4194304 | tf_op jit(solution)/shard_map/all_to_all | solution.py:39
  91.5 1.0 copy-start.5
  98.7 3.8 %collective-permute-start.1 = (bf16[32,64,128]{2,1,0:T(8,128)(2,1)S(1)}, bf16[32,64,128]{2,1,0:T(8,128)(2,1)S(1)}, u32[]{:S(2)}, u32[]{:S(2)}) collective-permute-start(bf16[32,64,128]{2,1,0:T(8,128)(2,1)S(1)} %get-tuple-element.36), channel_id=1, source_target_pairs={{0,4},{4,0},{8,12},{12,8},{16,20},{20,16},{24,28},{28,24},{32,36},... | collective-permute-start | bytes 1572872 | tf_op jit(solution)/shard_map/ppermute | solution.py:384
  102.6 9.6 %collective-permute-start.2 = (bf16[12,64,128]{2,1,0:T(8,128)(2,1)S(1)}, bf16[12,64,128]{2,1,0:T(8,128)(2,1)S(1)}, u32[]{:S(2)}, u32[]{:S(2)}) collective-permute-start(bf16[12,64,128]{2,1,0:T(8,128)(2,1)S(1)} %get-tuple-element.39), channel_id=1, source_target_pairs={{0,1},{1,2},{2,3},{3,0},{4,5},{5,6},{6,7},{7,4},{8,9},{9,10},{10,1... | collective-permute-start | bytes 589832 | tf_op jit(solution)/shard_map/ppermute | solution.py:387
  105.0 10.4 %collective-permute-start.3 = (bf16[12,64,128]{2,1,0:T(8,128)(2,1)S(1)}, bf16[12,64,128]{2,1,0:T(8,128)(2,1)S(1)}, u32[]{:S(2)}, u32[]{:S(2)}) collective-permute-start(bf16[12,64,128]{2,1,0:T(8,128)(2,1)S(1)} %get-tuple-element.40), channel_id=1, source_target_pairs={{0,2},{1,3},{2,0},{3,1},{4,6},{5,7},{6,4},{7,5},{8,10},{9,11},{10,... | collective-permute-start | bytes 589832 | tf_op jit(solution)/shard_map/ppermute | solution.py:387
  109.4 9.9 %collective-permute-start.4 = (bf16[12,64,128]{2,1,0:T(8,128)(2,1)S(1)}, bf16[12,64,128]{2,1,0:T(8,128)(2,1)S(1)}, u32[]{:S(2)}, u32[]{:S(2)}) collective-permute-start(bf16[12,64,128]{2,1,0:T(8,128)(2,1)S(1)} %get-tuple-element.41), channel_id=1, source_target_pairs={{0,3},{1,0},{2,1},{3,2},{4,7},{5,4},{6,5},{7,6},{8,11},{9,8},{10,9... | collective-permute-start | bytes 589832 | tf_op jit(solution)/shard_map/ppermute | solution.py:387
  124.4 17.0 %all-to-all-start.4 = ((bf16[8,128,128]{2,1,0:T(8,128)(2,1)}), bf16[8,128,128]{2,1,0:T(8,128)(2,1)S(1)}, u32[]{:S(2)}, u32[]{:S(2)}) async-start(bf16[8,128,128]{2,1,0:T(8,128)(2,1)} %shard_map.91), calls=%async_computation.4 | async-start | bytes 524288 | tf_op jit(solution)/shard_map/all_to_all | solution.py:39

commit v9 on v8

--- a/solution.py
+++ b/solution.py
@@ -162,6 +162,11 @@
     return jnp.concatenate([jnp.where(block == b, packed, 0.0).astype(BF16) for b in range(SLOTS)], axis=0)
 
 
+def for_sources(step):
+    for first in range(0, SPOTS, 8):
+        lax.fori_loop(first, first + 8, step, 0, unroll=8)
+
+
 def read_codes(asked, table, codes, sem):
     spot, core, _ = position()
     rows = asked[:, QROWS:SENT, :].reshape(SPOTS * 8, N_DP)
@@ -198,9 +203,7 @@
         marks[pl.ds(source, 1), :] = mark
         return carry
 
-    size = 8
-    for chunk in range(SPOTS // size):
-        lax.fori_loop(chunk * size, (chunk + 1) * size, one, 0, unroll=size)
+    for_sources(one)
 
     total = totals[...]
     mark = marks[...]
@@ -232,7 +235,7 @@
             back[source, q * QT : (q + 1) * QT, :] = total.astype(BF16)
         return carry
 
-    lax.fori_loop(0, SPOTS, one, 0, unroll=8)
+    for_sources(one)
 
 
 def weigh(
@@ -257,7 +260,7 @@
             acc[row] += grads[b * PT : (b + 1) * PT] * weight_inv[q, source]
         return carry
 
-    lax.fori_loop(0, SPOTS, add, 0, unroll=8)
+    for_sources(add)
     other_grad[...] = other_acc[...].astype(BF16)
 
     for copy in later:
@@ -382,16 +385,17 @@
         [vmem(), vmem(), vmem()],
         (vmem(),) * 4,
     )(own_grad, lax.ppermute(other_grad, "dp", swap), pos_grad)
-    total = kept
-    for ahead, part in ((1, off1), (2, off2), (3, off3)):
-        moved = lax.ppermute(part, "group", [(g, (g + ahead) % GROUP) for g in range(GROUP)])
-        total = total + moved.astype(F32)
-
+    moved = [
+        lax.ppermute(part, "group", [(g, (g + ahead) % GROUP) for g in range(GROUP)]).astype(F32)
+        for ahead, part in ((2, off2), (1, off1), (3, off3))
+    ]
+    total = kept + moved[0] + moved[1]
     arrived = call(add_blocks, struct((N_Y, QROWS, D), BF16), [vmem(), anywhere()], vmem())(arrived, total)
     arrived = exchange(arrived, along(1))
     query_grad = call(
         collect, struct((QD, QT, D), F32), [smem(), vmem(), vmem()], vmem()
     )(weight_inv, query_part, arrived)
+    total = total + moved[2]
     return losses.reshape(QD, QT)[:, 0], query_grad, total[:QD], total[QD:]
 
 

time: 143 us -> 141 us (0.986)
  Pallas kernels: 23.6 us -> 19.8 us
  waiting for transfers between devices: 38.1 us -> 41 us
  starting transfers between devices: 38.5 us -> 36.8 us
    all_to_all x4, waiting for transfers between devices: 28.2 us -> 31.6 us  [exchange(): lax.all_to_all(blocks, EVERY, split_axis=0, concat_axis=0, axis_index_gro...]
    pallas_call x1, Pallas kernels: 7.59 us -> 5.13 us  [per_device(): call(terms, (struct((SPOTS, PT, QROWS), BF16), struct((SPOTS, QROWS, D),...]
    all_to_all x4, starting transfers between devices: 26.1 us -> 23.8 us  [exchange(): lax.all_to_all(blocks, EVERY, split_axis=0, concat_axis=0, axis_index_gro...]
  transfers between devices with their start and end apart: 9 -> 9, of which waited for: 8 -> 8; matrix products, arithmetic and copies ran while one was open for 2% -> 2% of each run, Pallas kernels for 10% -> 8%
where the time goes in v9:
time: 141 us; the launch traced here: 140 us
  waiting for transfers between devices  41 us (29%)
  starting transfers between devices  36.8 us (26%)
  blocking collectives  29.8 us (21%)
  Pallas kernels  19.8 us (14%)
  local copies, waits for them, and re-layouts  11.1 us (8%)
    all_to_all x4, waiting for transfers between devices, exchange(): lax.all_to_all(blocks, EVERY, split_axis=0, concat_axis=0, axis_index_gro...  31.6 us
    all_to_all x4, starting transfers between devices, exchange(): lax.all_to_all(blocks, EVERY, split_axis=0, concat_axis=0, axis_index_gro...  23.8 us
    all_to_all x1, blocking collectives, exchange(): lax.all_to_all(blocks, EVERY, split_axis=0, concat_axis=0, axis_index_gro...  17.6 us
    all_gather x1, blocking collectives, per_device(): gathered = lax.all_gather(positives, 'group', axis=0, tiled=True)  12.3 us
    ppermute x3, starting transfers between devices, per_device(): lax.ppermute(part, 'group', [(g, (g + ahead) % GROUP) for g in range(GROU...  9.24 us
    ppermute x3, waiting for transfers between devices, per_device(): lax.ppermute(part, 'group', [(g, (g + ahead) % GROUP) for g in range(GROU...  7.56 us
    unnamed x22, local copies, waits for them, and re-layouts  6.77 us
    pallas_call x1, Pallas kernels, per_device(): call(terms, (struct((SPOTS, PT, QROWS), BF16), struct((SPOTS, QROWS, D),...  5.13 us
  transfers between devices with their start and end apart: 9, of which 8 were waited for; matrix products, arithmetic and copies ran while one was open for 2% of the time, Pallas kernels for 8%

profile of v9, /device:TPU:6, one launch (start us, length us, event | category | flops | bytes accessed | tf_op | source)
XLA Modules:
  0.0 140.1 jit_solution(8419560560336899629)
XLA Ops:
  0.6 0.0 copy-start.7
  0.6 0.7 copy-done.7
  1.4 0.0 copy-start.8
  1.4 0.7 copy-done.8
  2.1 0.0 copy-start.9
  2.1 0.7 copy-done.9
  2.8 1.3 shard_map.84
  4.1 17.6 %all_to_all.25 = bf16[8,136,128]{2,1,0:T(8,128)(2,1)S(1)} all-to-all(bf16[8,136,128]{2,1,0:T(8,128)(2,1)S(1)} %get-tuple-element.23), channel_id=1, replica_groups={{4,68,132,196,260,324,388,452},{5,69,133,197,261,325,389,453},{6,70,134..., dimensions={0} | all-to-all | bytes 557056 | tf_op jit(solution)/shard_map/all_to_all | solution.py:39
  21.7 1.7 %broadcast_in_dim.2 = bf16[8,8,136,128]{3,2,1,0:T(8,128)(2,1)} broadcast(bf16[8,136,128]{2,1,0:T(8,128)(2,1)S(1)} %all_to_all.25), dimensions={1,2,3} | broadcast | bytes 2506752 | tf_op jit(solution)/shard_map/broadcast_in_dim | solution.py:325
  23.3 0.0 copy-start.3
  23.3 0.0 copy-start.10
  23.3 10.4 %all-to-all-start.1 = ((bf16[8,8,136,128]{3,2,1,0:T(8,128)(2,1)}), bf16[8,8,136,128]{3,2,1,0:T(8,128)(2,1)S(1)}, u32[]{:S(2)}, u32[]{:S(2)}) async-start(bf16[8,8,136,128]{3,2,1,0:T(8,128)(2,1)} %broadcast_in_dim.2), calls=%async_computation.1 | async-start | bytes 4456448 | tf_op jit(solution)/shard_map/all_to_all | solution.py:39
  33.8 0.0 copy-done.3
  33.8 0.4 shard_map.85.own_rows
  34.2 1.9 %collective-permute-start = (bf16[32,64,128]{2,1,0:T(8,128)(2,1)S(1)}, bf16[32,64,128]{2,1,0:T(8,128)(2,1)S(1)}, u32[]{:S(2)}, u32[]{:S(2)}) collective-permute-start(bf16[32,64,128]{2,1,0:T(8,128)(2,1)S(1)} %shard_map.85.own_rows), channel_id=1, source_target_pairs={{0,4},{4,0},{8,12},{12,8},{16,20},{20,16},{24,28},{28,24},{32,36},... | collective-permute-start | bytes 1572872 | tf_op jit(solution)/shard_map/ppermute | solution.py:328
  36.1 0.0 copy-done.10
  36.1 12.3 %all_gather.3.positives = bf16[16,64,128]{2,1,0:T(8,128)(2,1)S(1)} all-gather(bf16[4,64,128]{2,1,0:T(8,128)(2,1)S(1)} %copy-done.10), channel_id=1, replica_groups=mesh['dp'=128,'group'=4] {'group'}, dimensions={0}, use_global_device_ids=true | all-gather | bytes 327680 | tf_op jit(solution)/shard_map/all_gather | solution.py:329
  48.4 0.6 shard_map.86
  49.0 0.0 copy-start.4
  49.0 0.7 copy-done.4
  49.7 0.0 collective-permute-done.other_rows
  49.7 15.8 %all-to-all-done.1 = bf16[8,8,136,128]{3,2,1,0:T(8,128)(2,1)S(1)} async-done(((bf16[8,8,136,128]{3,2,1,0:T(8,128)(2,1)}), bf16[8,8,136,128]{3,2,1,0:T(8,128)(2,1)S(1)}, u32[]{:S(2)}, u32[]{:S(2)}) %all-to-all-start.1) | async-done | bytes 2228256 | tf_op jit(solution)/shard_map/all_to_all | solution.py:39
  65.5 3.6 %shard_map.87 = (f32[64,128]{1,0:T(8,128)S(1)}, f32[64,4,128]{2,1,0:T(4,128)S(1)}, s32[8,512]{1,0:T(8,128)S(1)}) custom-call(bf16[64,136,128]{2,1,0:T(8,128)(2,1)S(1)} %bitcast.2, bf16[32,64,128]{2,1,0:T(8,128)(2,1)S(1)} %shard_map.85.own_rows, bf16[32,64,128]{2,1,0:T(8,128)(2,1)S(1)} %collective-permute-done.other_rows, ...), custom_call_target="tpu_custom_call" | custom-call | tf_op jit(solution)/shard_map/pallas_call | solution.py:334
  69.1 0.0 copy-start.6
  69.1 0.6 copy-done.6
  69.7 4.6 %all-to-all-start.2 = ((f32[64,4,128]{2,1,0:T(4,128)}), f32[64,4,128]{2,1,0:T(4,128)S(1)}, u32[]{:S(2)}, u32[]{:S(2)}) async-start(f32[64,4,128]{2,1,0:T(4,128)} %copy-done.6), calls=%async_computation.2 | async-start | bytes 262144 | tf_op jit(solution)/shard_map/all_to_all | solution.py:39
  74.3 5.1 %shard_map.88 = (bf16[64,64,128]{2,1,0:T(8,128)(2,1)S(1)}, bf16[64,128,128]{2,1,0:T(8,128)(2,1)S(1)}) custom-call(s32[8,512]{1,0:T(8,128)S(1)} %get-tuple-element.26.codes, bf16[64,136,128]{2,1,0:T(8,128)(2,1)S(1)} %bitcast.3, bf16[32,64,128]{2,1,0:T(8,128)(2,1)S(1)} %shard_map.85.own_rows, bf16[32,64,128]{2,1,0:T(8,128)(2,1)S(1)} %collective-permute-done.other_rows, ...), custom_call_target="tpu_custom_call" | custom-call | tf_op jit(solution)/shard_map/pallas_call | solution.py:352
  79.5 0.0 copy-start
  79.5 1.3 copy-done
  80.8 0.0 copy-start.1
  80.8 1.0 copy-done.1
  81.8 5.2 %all-to-all-done.2.sums = f32[64,4,128]{2,1,0:T(4,128)S(1)} async-done(((f32[64,4,128]{2,1,0:T(4,128)}), f32[64,4,128]{2,1,0:T(4,128)S(1)}, u32[]{:S(2)}, u32[]{:S(2)}) %all-to-all-start.2) | async-done | bytes 131104 | tf_op jit(solution)/shard_map/all_to_all | solution.py:39
  87.0 0.0 copy-start.2
  87.0 4.7 %all-to-all-start.3 = ((bf16[8,8,128,128]{3,2,1,0:T(8,128)(2,1)}), bf16[8,8,128,128]{3,2,1,0:T(8,128)(2,1)}, u32[]{:S(2)}, u32[]{:S(2)}) async-start(bf16[8,8,128,128]{3,2,1,0:T(8,128)(2,1)} %bitcast.5), calls=%async_computation.3 | async-start | bytes 4194304 | tf_op jit(solution)/shard_map/all_to_all | solution.py:39
  91.7 0.0 copy-done.2
  91.7 0.0 copy-start.5
  91.7 0.9 copy-done.5
  92.7 4.9 %shard_map.89 = (f32[32,64,128]{2,1,0:T(8,128)S(1)}, bf16[32,64,128]{2,1,0:T(8,128)(2,1)S(1)}, f32[16,64,128]{2,1,0:T(8,128)S(1)}, f32[128,128]{1,0:T(8,128)S(1)...) custom-call(s32[8,512]{1,0:T(8,128)S(1)} %get-tuple-element.26.codes, f32[64,4,128]{2,1,0:T(4,128)S(1)} %all-to-all-done.2.sums, ...), custom_call_target="tpu_custom_call" | custom-call | tf_op jit(solution)/shard_map/pallas_call | solution.py:360
  97.6 1.9 %collective-permute-start.1 = (bf16[32,64,128]{2,1,0:T(8,128)(2,1)S(1)}, bf16[32,64,128]{2,1,0:T(8,128)(2,1)S(1)}, u32[]{:S(2)}, u32[]{:S(2)}) collective-permute-start(bf16[32,64,128]{2,1,0:T(8,128)(2,1)S(1)} %get-tuple-element.36), channel_id=1, source_target_pairs={{0,4},{4,0},{8,12},{12,8},{16,20},{20,16},{24,28},{28,24},{32,36},... | collective-permute-start | bytes 1572872 | tf_op jit(solution)/shard_map/ppermute | solution.py:387
  99.5 1.9 %collective-permute-done.1.moved = bf16[32,64,128]{2,1,0:T(8,128)(2,1)S(1)} collective-permute-done((bf16[32,64,128]{2,1,0:T(8,128)(2,1)S(1)}, bf16[32,64,128]{2,1,0:T(8,128)(2,1)S(1)}, u32[]{:S(2)}, u32[]{:S(2)}) %collective-permute-start.1) | collective-permute-done | bytes 524320 | tf_op jit(solution)/shard_map/ppermute | solution.py:387
  101.4 0.1 shard_map.90
  101.5 3.3 %collective-permute-start.2 = (bf16[12,64,128]{2,1,0:T(8,128)(2,1)S(1)}, bf16[12,64,128]{2,1,0:T(8,128)(2,1)S(1)}, u32[]{:S(2)}, u32[]{:S(2)}) collective-permute-start(bf16[12,64,128]{2,1,0:T(8,128)(2,1)S(1)} %get-tuple-element.39), channel_id=1, source_target_pairs={{0,2},{1,3},{2,0},{3,1},{4,6},{5,7},{6,4},{7,5},{8,10},{9,11},{10,... | collective-permute-start | bytes 589832 | tf_op jit(solution)/shard_map/ppermute | solution.py:389
  104.8 4.0 %collective-permute-start.3 = (bf16[12,64,128]{2,1,0:T(8,128)(2,1)S(1)}, bf16[12,64,128]{2,1,0:T(8,128)(2,1)S(1)}, u32[]{:S(2)}, u32[]{:S(2)}) collective-permute-start(bf16[12,64,128]{2,1,0:T(8,128)(2,1)S(1)} %get-tuple-element.40), channel_id=1, source_target_pairs={{0,1},{1,2},{2,3},{3,0},{4,5},{5,6},{6,7},{7,4},{8,9},{9,10},{10,1... | collective-permute-start | bytes 589832 | tf_op jit(solution)/shard_map/ppermute | solution.py:389
  108.8 1.9 %collective-permute-start.4 = (bf16[12,64,128]{2,1,0:T(8,128)(2,1)S(1)}, bf16[12,64,128]{2,1,0:T(8,128)(2,1)S(1)}, u32[]{:S(2)}, u32[]{:S(2)}) collective-permute-start(bf16[12,64,128]{2,1,0:T(8,128)(2,1)S(1)} %get-tuple-element.41), channel_id=1, source_target_pairs={{0,3},{1,0},{2,1},{3,2},{4,7},{5,4},{6,5},{7,6},{8,11},{9,8},{10,9... | collective-permute-start | bytes 589832 | tf_op jit(solution)/shard_map/ppermute | solution.py:389
  110.8 1.1 collective-permute-done.2
  111.8 2.0 %collective-permute-done.3 = bf16[12,64,128]{2,1,0:T(8,128)(2,1)S(1)} collective-permute-done((bf16[12,64,128]{2,1,0:T(8,128)(2,1)S(1)}, bf16[12,64,128]{2,1,0:T(8,128)(2,1)S(1)}, u32[]{:S(2)}, u32[]{:S(2)}) %collective-permute-start.3) | collective-permute-done | bytes 196640 | tf_op jit(solution)/shard_map/ppermute | solution.py:389
  113.9 4.5 %collective-permute-done.4 = bf16[12,64,128]{2,1,0:T(8,128)(2,1)S(1)} collective-permute-done((bf16[12,64,128]{2,1,0:T(8,128)(2,1)S(1)}, bf16[12,64,128]{2,1,0:T(8,128)(2,1)S(1)}, u32[]{:S(2)}, u32[]{:S(2)}) %collective-permute-start.4) | collective-permute-done | bytes 196640 | tf_op jit(solution)/shard_map/ppermute | solution.py:389
  118.3 0.1 convert_add_fusion
  118.4 3.4 %all-to-all-done.3.arrived = bf16[8,8,128,128]{3,2,1,0:T(8,128)(2,1)} async-done(((bf16[8,8,128,128]{3,2,1,0:T(8,128)(2,1)}), bf16[8,8,128,128]{3,2,1,0:T(8,128)(2,1)}, u32[]{:S(2)}, u32[]{:S(2)}) %all-to-all-start.3) | async-done | bytes 2097184 | tf_op jit(solution)/shard_map/all_to_all | solution.py:39
  121.8 2.6 %shard_map.91 = bf16[8,128,128]{2,1,0:T(8,128)(2,1)} custom-call(bf16[8,8,128,128]{3,2,1,0:T(8,128)(2,1)} %all-to-all-done.3.arrived, f32[12,64,128]{2,1,0:T(8,128)S(1)} %get-tuple-element.43.after), custom_call_target="tpu_custom_call" | custom-call | tf_op jit(solution)/shard_map/pallas_call | solution.py:393
  124.3 4.0 %all-to-all-start.4 = ((bf16[8,128,128]{2,1,0:T(8,128)(2,1)}), bf16[8,128,128]{2,1,0:T(8,128)(2,1)S(1)}, u32[]{:S(2)}, u32[]{:S(2)}) async-start(bf16[8,128,128]{2,1,0:T(8,128)(2,1)} %shard_map.91), calls=%async_computation.4 | async-start | bytes 524288 | tf_op jit(solution)/shard_map/all_to_all | solution.py:39
  128.4 0.5 broadcast.5
  128.9 0.7 reduce.5
  129.6 0.1 reshape.19
  129.6 0.6 slice_reduce_fusion
  130.3 0.7 slice.13
  131.0 0.7 slice.12
  131.7 7.2 %all-to-all-done.4.arrived = bf16[8,128,128]{2,1,0:T(8,128)(2,1)S(1)} async-done(((bf16[8,128,128]{2,1,0:T(8,128)(2,1)}), bf16[8,128,128]{2,1,0:T(8,128)(2,1)S(1)}, u32[]{:S(2)}, u32[]{:S(2)}) %all-to-all-start.4) | async-done | bytes 262176 | tf_op jit(solution)/shard_map/all_to_all | solution.py:39
  138.9 1.3 shard_map.92
Async XLA Ops:
  0.6 0.8 copy-start.7
  1.4 0.7 copy-start.8
  2.1 0.7 copy-start.9
  23.3 10.5 %copy-start.3 = (bf16[32,64,128]{2,1,0:T(8,128)(2,1)S(1)}, bf16[32,64,128]{2,1,0:T(8,128)(2,1)}, u32[]{:S(2)}) copy-start(bf16[32,64,128]{2,1,0:T(8,128)(2,1)} %values.1) | copy-start | bytes 1572868
  23.3 12.7 %copy-start.10 = (bf16[4,64,128]{2,1,0:T(8,128)(2,1)S(1)}, bf16[4,64,128]{2,1,0:T(8,128)(2,1)}, u32[]{:S(2)}) copy-start(bf16[4,64,128]{2,1,0:T(8,128)(2,1)} %param.6) | copy-start | bytes 196612
  23.3 42.1 %all-to-all-start.1 = ((bf16[8,8,136,128]{3,2,1,0:T(8,128)(2,1)}), bf16[8,8,136,128]{3,2,1,0:T(8,128)(2,1)S(1)}, u32[]{:S(2)}, u32[]{:S(2)}) async-start(bf16[8,8,136,128]{3,2,1,0:T(8,128)(2,1)} %broadcast_in_dim.2), calls=%async_computation.1 | async-start | bytes 4456448 | tf_op jit(solution)/shard_map/all_to_all | solution.py:39
  34.2 15.5 %collective-permute-start = (bf16[32,64,128]{2,1,0:T(8,128)(2,1)S(1)}, bf16[32,64,128]{2,1,0:T(8,128)(2,1)S(1)}, u32[]{:S(2)}, u32[]{:S(2)}) collective-permute-start(bf16[32,64,128]{2,1,0:T(8,128)(2,1)S(1)} %shard_map.85.own_rows), channel_id=1, source_target_pairs={{0,4},{4,0},{8,12},{12,8},{16,20},{20,16},{24,28},{28,24},{32,36},... | collective-permute-start | bytes 1572872 | tf_op jit(solution)/shard_map/ppermute | solution.py:328
  49.0 0.7 copy-start.4
  69.1 0.7 copy-start.6
  69.7 17.3 %all-to-all-start.2 = ((f32[64,4,128]{2,1,0:T(4,128)}), f32[64,4,128]{2,1,0:T(4,128)S(1)}, u32[]{:S(2)}, u32[]{:S(2)}) async-start(f32[64,4,128]{2,1,0:T(4,128)} %copy-done.6), calls=%async_computation.2 | async-start | bytes 262144 | tf_op jit(solution)/shard_map/all_to_all | solution.py:39
  79.5 1.3 copy-start
  80.8 1.0 copy-start.1
  87.0 4.7 %copy-start.2 = (bf16[64,64,128]{2,1,0:T(8,128)(2,1)S(1)}, bf16[64,64,128]{2,1,0:T(8,128)(2,1)}, u32[]{:S(2)}) copy-start(bf16[64,64,128]{2,1,0:T(8,128)(2,1)} %copy-done.1) | copy-start | bytes 3145732
  87.0 34.8 %all-to-all-start.3 = ((bf16[8,8,128,128]{3,2,1,0:T(8,128)(2,1)}), bf16[8,8,128,128]{3,2,1,0:T(8,128)(2,1)}, u32[]{:S(2)}, u32[]{:S(2)}) async-start(bf16[8,8,128,128]{3,2,1,0:T(8,128)(2,1)} %bitcast.5), calls=%async_computation.3 | async-start | bytes 4194304 | tf_op jit(solution)/shard_map/all_to_all | solution.py:39
  91.7 1.0 copy-start.5
  97.6 3.8 %collective-permute-start.1 = (bf16[32,64,128]{2,1,0:T(8,128)(2,1)S(1)}, bf16[32,64,128]{2,1,0:T(8,128)(2,1)S(1)}, u32[]{:S(2)}, u32[]{:S(2)}) collective-permute-start(bf16[32,64,128]{2,1,0:T(8,128)(2,1)S(1)} %get-tuple-element.36), channel_id=1, source_target_pairs={{0,4},{4,0},{8,12},{12,8},{16,20},{20,16},{24,28},{28,24},{32,36},... | collective-permute-start | bytes 1572872 | tf_op jit(solution)/shard_map/ppermute | solution.py:387
  101.5 10.3 %collective-permute-start.2 = (bf16[12,64,128]{2,1,0:T(8,128)(2,1)S(1)}, bf16[12,64,128]{2,1,0:T(8,128)(2,1)S(1)}, u32[]{:S(2)}, u32[]{:S(2)}) collective-permute-start(bf16[12,64,128]{2,1,0:T(8,128)(2,1)S(1)} %get-tuple-element.39), channel_id=1, source_target_pairs={{0,2},{1,3},{2,0},{3,1},{4,6},{5,7},{6,4},{7,5},{8,10},{9,11},{10,... | collective-permute-start | bytes 589832 | tf_op jit(solution)/shard_map/ppermute | solution.py:389
  104.8 9.0 %collective-permute-start.3 = (bf16[12,64,128]{2,1,0:T(8,128)(2,1)S(1)}, bf16[12,64,128]{2,1,0:T(8,128)(2,1)S(1)}, u32[]{:S(2)}, u32[]{:S(2)}) collective-permute-start(bf16[12,64,128]{2,1,0:T(8,128)(2,1)S(1)} %get-tuple-element.40), channel_id=1, source_target_pairs={{0,1},{1,2},{2,3},{3,0},{4,5},{5,6},{6,7},{7,4},{8,9},{9,10},{10,1... | collective-permute-start | bytes 589832 | tf_op jit(solution)/shard_map/ppermute | solution.py:389
  108.8 9.5 %collective-permute-start.4 = (bf16[12,64,128]{2,1,0:T(8,128)(2,1)S(1)}, bf16[12,64,128]{2,1,0:T(8,128)(2,1)S(1)}, u32[]{:S(2)}, u32[]{:S(2)}) collective-permute-start(bf16[12,64,128]{2,1,0:T(8,128)(2,1)S(1)} %get-tuple-element.41), channel_id=1, source_target_pairs={{0,3},{1,0},{2,1},{3,2},{4,7},{5,4},{6,5},{7,6},{8,11},{9,8},{10,9... | collective-permute-start | bytes 589832 | tf_op jit(solution)/shard_map/ppermute | solution.py:389
  124.3 14.5 %all-to-all-start.4 = ((bf16[8,128,128]{2,1,0:T(8,128)(2,1)}), bf16[8,128,128]{2,1,0:T(8,128)(2,1)S(1)}, u32[]{:S(2)}, u32[]{:S(2)}) async-start(bf16[8,128,128]{2,1,0:T(8,128)(2,1)} %shard_map.91), calls=%async_computation.4 | async-start | bytes 524288 | tf_op jit(solution)/shard_map/all_to_all | solution.py:39

commit v10 on v9

--- a/solution.py
+++ b/solution.py
@@ -10,6 +10,7 @@
 SPOTS = N_Z * N_Y
 QD, QT, PT, D, NEG, ROWS = 4, 32, 64, 128, 7, 32
 QROWS = QD * QT
+PASSAGE_ROWS = 4096 // 128
 SENT = QROWS + 8
 BATCH = QD * GROUP
 SLOTS = 4
@@ -97,8 +98,8 @@
     return spot, core, source
 
 
-def prepare(ids_in, storage_in, queries_in, sent, q_unit, ids, storage, queries, sems, count):
-    pairs = [(storage_in, storage), (ids_in, ids), (queries_in, queries)]
+def prepare(table_in, queries_in, sent, q_unit, table, queries, sems, count):
+    pairs = [(table_in, table), (queries_in, queries)]
     for copy in fetch(pairs, sems):
         copy.wait()
     tiles = unit(queries[...])
@@ -106,7 +107,8 @@
     homes = []
     for q in range(QD):
         for k in range(NEG):
-            home = storage[ids[q, k]]
+            passage = table[PASSAGE_ROWS + q, k]
+            home = table[passage // 128, passage % 128]
             owner = home // ROWS
             lane_of = (owner % N_C) * SPOTS + owner // N_C
             count[lane_of] = 0
@@ -289,8 +291,8 @@
         out[QD:] = (own_grad[rows] + moved[rows].astype(F32)).astype(out.dtype)
 
 
-def add_blocks(arrived, after, out):
-    del after
+def add_blocks(arrived, first, second, out):
+    del first, second
     for part in range(N_Y):
         out[part] = jnp.sum(arrived[:, part].astype(F32), axis=0).astype(BF16)
 
@@ -308,19 +310,19 @@
     swap = [(h, h ^ 1) for h in range(N_DP)]
     tiles = struct((QD, QT, D), BF16)
 
+    table = jnp.concatenate([storage_row.reshape(PASSAGE_ROWS, 128), jnp.pad(negative_ids, ((0, 4), (0, 121)))], axis=0)
     sent, q_unit = call(
         prepare,
         (struct((N_Y, SENT, D), BF16), tiles),
-        [hbm()] * 3,
+        [hbm()] * 2,
         (vmem(), vmem()),
         [
-            pltpu.SMEM(negative_ids.shape, I32),
-            pltpu.SMEM(storage_row.shape, I32),
+            pltpu.SMEM(table.shape, I32),
             pltpu.VMEM((QD, QT, D), BF16),
-            pltpu.SemaphoreType.DMA((3,)),
+            pltpu.SemaphoreType.DMA((2,)),
             pltpu.SMEM((N_DP,), I32),
         ],
-    )(negative_ids, storage_row, queries)
+    )(table, queries)
     asked = exchange(sent, along(1))
     asked = exchange(jnp.broadcast_to(asked[None], (N_Z, N_Y, SENT, D)), along(0)).reshape(SPOTS, SENT, D)
 
@@ -386,16 +388,17 @@
         (vmem(),) * 4,
     )(own_grad, lax.ppermute(other_grad, "dp", swap), pos_grad)
     moved = [
-        lax.ppermute(part, "group", [(g, (g + ahead) % GROUP) for g in range(GROUP)]).astype(F32)
+        lax.ppermute(part, "group", [(g, (g + ahead) % GROUP) for g in range(GROUP)])
         for ahead, part in ((2, off2), (1, off1), (3, off3))
     ]
-    total = kept + moved[0] + moved[1]
-    arrived = call(add_blocks, struct((N_Y, QROWS, D), BF16), [vmem(), anywhere()], vmem())(arrived, total)
+    arrived = call(
+        add_blocks, struct((N_Y, QROWS, D), BF16), [vmem(), anywhere(), anywhere()], vmem()
+    )(arrived, moved[0], moved[1])
     arrived = exchange(arrived, along(1))
     query_grad = call(
         collect, struct((QD, QT, D), F32), [smem(), vmem(), vmem()], vmem()
     )(weight_inv, query_part, arrived)
-    total = total + moved[2]
+    total = kept + moved[0].astype(F32) + moved[1].astype(F32) + moved[2].astype(F32)
     return losses.reshape(QD, QT)[:, 0], query_grad, total[:QD], total[QD:]
 
 

time: 141 us -> 141 us (level)
  local copies, waits for them, and re-layouts: 11.1 us -> 9.65 us
    all_to_all x4, waiting for transfers between devices: 31.6 us -> 29.2 us  [exchange(): lax.all_to_all(blocks, EVERY, split_axis=0, concat_axis=0, axis_index_gro...]
    ppermute x3, waiting for transfers between devices: 7.56 us -> 9.16 us  [per_device(): lax.ppermute(part, 'group', [(g, (g + ahead) % GROUP) for g in range(GROU...]
    unnamed x22 -> x18, local copies, waits for them, and re-layouts: 6.77 us -> 5.36 us
where the time goes in v10:
time: 141 us; the launch traced here: 140 us
  waiting for transfers between devices  40.3 us (29%)
  starting transfers between devices  37.6 us (27%)
  blocking collectives  29.8 us (21%)
  Pallas kernels  20 us (14%)
  local copies, waits for them, and re-layouts  9.65 us (7%)
  other arithmetic  1.49 us (1%)
    all_to_all x4, waiting for transfers between devices, exchange(): lax.all_to_all(blocks, EVERY, split_axis=0, concat_axis=0, axis_index_gro...  29.2 us
    all_to_all x4, starting transfers between devices, exchange(): lax.all_to_all(blocks, EVERY, split_axis=0, concat_axis=0, axis_index_gro...  23.7 us
    all_to_all x1, blocking collectives, exchange(): lax.all_to_all(blocks, EVERY, split_axis=0, concat_axis=0, axis_index_gro...  17.6 us
    all_gather x1, blocking collectives, per_device(): gathered = lax.all_gather(positives, 'group', axis=0, tiled=True)  12.3 us
    ppermute x3, starting transfers between devices, per_device(): lax.ppermute(part, 'group', [(g, (g + ahead) % GROUP) for g in range(GROU...  10 us
    ppermute x3, waiting for transfers between devices, per_device(): lax.ppermute(part, 'group', [(g, (g + ahead) % GROUP) for g in range(GROU...  9.16 us
    unnamed x18, local copies, waits for them, and re-layouts  5.36 us
    pallas_call x1, Pallas kernels, per_device(): call(terms, (struct((SPOTS, PT, QROWS), BF16), struct((SPOTS, QROWS, D),...  5.13 us
  transfers between devices with their start and end apart: 9, of which 8 were waited for; matrix products, arithmetic and copies ran while one was open for 2% of the time, Pallas kernels for 8%

profile of v10, /device:TPU:6, one launch (start us, length us, event | category | flops | bytes accessed | tf_op | source)
XLA Modules:
  0.0 139.7 jit_solution(4158797709207894038)
XLA Ops:
  0.6 0.7 pad_add_fusion.table_in
  1.4 0.0 copy-start.7
  1.4 0.8 copy-done.7
  2.1 1.5 %shard_map.84 = (bf16[8,136,128]{2,1,0:T(8,128)(2,1)S(1)}, bf16[4,32,128]{2,1,0:T(8,128)(2,1)S(1)}) custom-call(s32[40,128]{1,0:T(8,128)S(1)} %pad_add_fusion.table_in, bf16[4,32,128]{2,1,0:T(8,128)(2,1)S(1)} %copy-done.7), custom_call_target="tpu_custom_call" | custom-call | tf_op jit(solution)/shard_map/pallas_call | solution.py:314
  3.7 17.6 %all_to_all.25 = bf16[8,136,128]{2,1,0:T(8,128)(2,1)S(1)} all-to-all(bf16[8,136,128]{2,1,0:T(8,128)(2,1)S(1)} %get-tuple-element.23), channel_id=1, replica_groups={{4,68,132,196,260,324,388,452},{5,69,133,197,261,325,389,453},{6,70,134..., dimensions={0} | all-to-all | bytes 557056 | tf_op jit(solution)/shard_map/all_to_all | solution.py:40
  21.2 1.7 %broadcast_in_dim.2 = bf16[8,8,136,128]{3,2,1,0:T(8,128)(2,1)} broadcast(bf16[8,136,128]{2,1,0:T(8,128)(2,1)S(1)} %all_to_all.25), dimensions={1,2,3} | broadcast | bytes 2506752 | tf_op jit(solution)/shard_map/broadcast_in_dim | solution.py:327
  22.9 0.0 copy-start.3
  22.9 0.0 copy-start.8
  22.9 10.4 %all-to-all-start.1 = ((bf16[8,8,136,128]{3,2,1,0:T(8,128)(2,1)}), bf16[8,8,136,128]{3,2,1,0:T(8,128)(2,1)S(1)}, u32[]{:S(2)}, u32[]{:S(2)}) async-start(bf16[8,8,136,128]{3,2,1,0:T(8,128)(2,1)} %broadcast_in_dim.2), calls=%async_computation.1 | async-start | bytes 4456448 | tf_op jit(solution)/shard_map/all_to_all | solution.py:40
  33.4 0.0 copy-done.3
  33.4 0.4 shard_map.85.own_rows
  33.7 1.9 %collective-permute-start = (bf16[32,64,128]{2,1,0:T(8,128)(2,1)S(1)}, bf16[32,64,128]{2,1,0:T(8,128)(2,1)S(1)}, u32[]{:S(2)}, u32[]{:S(2)}) collective-permute-start(bf16[32,64,128]{2,1,0:T(8,128)(2,1)S(1)} %shard_map.85.own_rows), channel_id=1, source_target_pairs={{0,4},{4,0},{8,12},{12,8},{16,20},{20,16},{24,28},{28,24},{32,36},... | collective-permute-start | bytes 1572872 | tf_op jit(solution)/shard_map/ppermute | solution.py:330
  35.6 0.0 copy-done.8
  35.7 12.3 %all_gather.3.positives = bf16[16,64,128]{2,1,0:T(8,128)(2,1)S(1)} all-gather(bf16[4,64,128]{2,1,0:T(8,128)(2,1)S(1)} %copy-done.8), channel_id=1, replica_groups=mesh['dp'=128,'group'=4] {'group'}, dimensions={0}, use_global_device_ids=true | all-gather | bytes 327680 | tf_op jit(solution)/shard_map/all_gather | solution.py:331
  47.9 0.6 shard_map.86
  48.5 0.0 copy-start.4
  48.5 0.7 copy-done.4
  49.2 0.0 collective-permute-done.other_rows
  49.2 15.8 %all-to-all-done.1 = bf16[8,8,136,128]{3,2,1,0:T(8,128)(2,1)S(1)} async-done(((bf16[8,8,136,128]{3,2,1,0:T(8,128)(2,1)}), bf16[8,8,136,128]{3,2,1,0:T(8,128)(2,1)S(1)}, u32[]{:S(2)}, u32[]{:S(2)}) %all-to-all-start.1) | async-done | bytes 2228256 | tf_op jit(solution)/shard_map/all_to_all | solution.py:40
  65.0 3.6 %shard_map.87 = (f32[64,128]{1,0:T(8,128)S(1)}, f32[64,4,128]{2,1,0:T(4,128)S(1)}, s32[8,512]{1,0:T(8,128)S(1)}) custom-call(bf16[64,136,128]{2,1,0:T(8,128)(2,1)S(1)} %bitcast.3, bf16[32,64,128]{2,1,0:T(8,128)(2,1)S(1)} %shard_map.85.own_rows, bf16[32,64,128]{2,1,0:T(8,128)(2,1)S(1)} %collective-permute-done.other_rows, ...), custom_call_target="tpu_custom_call" | custom-call | tf_op jit(solution)/shard_map/pallas_call | solution.py:336
  68.6 0.0 copy-start.6
  68.6 0.6 copy-done.6
  69.3 4.6 %all-to-all-start.2 = ((f32[64,4,128]{2,1,0:T(4,128)}), f32[64,4,128]{2,1,0:T(4,128)S(1)}, u32[]{:S(2)}, u32[]{:S(2)}) async-start(f32[64,4,128]{2,1,0:T(4,128)} %copy-done.6), calls=%async_computation.2 | async-start | bytes 262144 | tf_op jit(solution)/shard_map/all_to_all | solution.py:40
  73.9 5.1 %shard_map.88 = (bf16[64,64,128]{2,1,0:T(8,128)(2,1)S(1)}, bf16[64,128,128]{2,1,0:T(8,128)(2,1)S(1)}) custom-call(s32[8,512]{1,0:T(8,128)S(1)} %get-tuple-element.26.codes, bf16[64,136,128]{2,1,0:T(8,128)(2,1)S(1)} %bitcast.4, bf16[32,64,128]{2,1,0:T(8,128)(2,1)S(1)} %shard_map.85.own_rows, bf16[32,64,128]{2,1,0:T(8,128)(2,1)S(1)} %collective-permute-done.other_rows, ...), custom_call_target="tpu_custom_call" | custom-call | tf_op jit(solution)/shard_map/pallas_call | solution.py:354
  79.0 0.0 copy-start
  79.0 1.3 copy-done
  80.3 0.0 copy-start.1
  80.3 1.0 copy-done.1
  81.3 5.3 %all-to-all-done.2.sums = f32[64,4,128]{2,1,0:T(4,128)S(1)} async-done(((f32[64,4,128]{2,1,0:T(4,128)}), f32[64,4,128]{2,1,0:T(4,128)S(1)}, u32[]{:S(2)}, u32[]{:S(2)}) %all-to-all-start.2) | async-done | bytes 131104 | tf_op jit(solution)/shard_map/all_to_all | solution.py:40
  86.6 0.0 copy-start.2
  86.6 4.7 %all-to-all-start.3 = ((bf16[8,8,128,128]{3,2,1,0:T(8,128)(2,1)}), bf16[8,8,128,128]{3,2,1,0:T(8,128)(2,1)}, u32[]{:S(2)}, u32[]{:S(2)}) async-start(bf16[8,8,128,128]{3,2,1,0:T(8,128)(2,1)} %bitcast.6), calls=%async_computation.3 | async-start | bytes 4194304 | tf_op jit(solution)/shard_map/all_to_all | solution.py:40
  91.2 0.0 copy-done.2
  91.3 0.0 copy-start.5
  91.3 0.9 copy-done.5
  92.2 4.9 %shard_map.89 = (f32[32,64,128]{2,1,0:T(8,128)S(1)}, bf16[32,64,128]{2,1,0:T(8,128)(2,1)S(1)}, f32[16,64,128]{2,1,0:T(8,128)S(1)}, f32[128,128]{1,0:T(8,128)S(1)...) custom-call(s32[8,512]{1,0:T(8,128)S(1)} %get-tuple-element.26.codes, f32[64,4,128]{2,1,0:T(4,128)S(1)} %all-to-all-done.2.sums, ...), custom_call_target="tpu_custom_call" | custom-call | tf_op jit(solution)/shard_map/pallas_call | solution.py:362
  97.1 1.9 %collective-permute-start.1 = (bf16[32,64,128]{2,1,0:T(8,128)(2,1)S(1)}, bf16[32,64,128]{2,1,0:T(8,128)(2,1)S(1)}, u32[]{:S(2)}, u32[]{:S(2)}) collective-permute-start(bf16[32,64,128]{2,1,0:T(8,128)(2,1)S(1)} %get-tuple-element.36), channel_id=1, source_target_pairs={{0,4},{4,0},{8,12},{12,8},{16,20},{20,16},{24,28},{28,24},{32,36},... | collective-permute-start | bytes 1572872 | tf_op jit(solution)/shard_map/ppermute | solution.py:389
  99.1 1.9 %collective-permute-done.1.moved = bf16[32,64,128]{2,1,0:T(8,128)(2,1)S(1)} collective-permute-done((bf16[32,64,128]{2,1,0:T(8,128)(2,1)S(1)}, bf16[32,64,128]{2,1,0:T(8,128)(2,1)S(1)}, u32[]{:S(2)}, u32[]{:S(2)}) %collective-permute-start.1) | collective-permute-done | bytes 524320 | tf_op jit(solution)/shard_map/ppermute | solution.py:389
  100.9 0.1 shard_map.90
  101.0 3.3 %collective-permute-start.2 = (bf16[12,64,128]{2,1,0:T(8,128)(2,1)S(1)}, bf16[12,64,128]{2,1,0:T(8,128)(2,1)S(1)}, u32[]{:S(2)}, u32[]{:S(2)}) collective-permute-start(bf16[12,64,128]{2,1,0:T(8,128)(2,1)S(1)} %get-tuple-element.38), channel_id=1, source_target_pairs={{0,2},{1,3},{2,0},{3,1},{4,6},{5,7},{6,4},{7,5},{8,10},{9,11},{10,... | collective-permute-start | bytes 589832 | tf_op jit(solution)/shard_map/ppermute | solution.py:391
  104.4 4.0 %collective-permute-start.3 = (bf16[12,64,128]{2,1,0:T(8,128)(2,1)S(1)}, bf16[12,64,128]{2,1,0:T(8,128)(2,1)S(1)}, u32[]{:S(2)}, u32[]{:S(2)}) collective-permute-start(bf16[12,64,128]{2,1,0:T(8,128)(2,1)S(1)} %get-tuple-element.39), channel_id=1, source_target_pairs={{0,1},{1,2},{2,3},{3,0},{4,5},{5,6},{6,7},{7,4},{8,9},{9,10},{10,1... | collective-permute-start | bytes 589832 | tf_op jit(solution)/shard_map/ppermute | solution.py:391
  108.4 3.0 %collective-permute-done.2.first = bf16[12,64,128]{2,1,0:T(8,128)(2,1)S(1)} collective-permute-done((bf16[12,64,128]{2,1,0:T(8,128)(2,1)S(1)}, bf16[12,64,128]{2,1,0:T(8,128)(2,1)S(1)}, u32[]{:S(2)}, u32[]{:S(2)}) %collective-permute-start.2) | collective-permute-done | bytes 196640 | tf_op jit(solution)/shard_map/ppermute | solution.py:391
  111.4 2.0 %collective-permute-done.3.second = bf16[12,64,128]{2,1,0:T(8,128)(2,1)S(1)} collective-permute-done((bf16[12,64,128]{2,1,0:T(8,128)(2,1)S(1)}, bf16[12,64,128]{2,1,0:T(8,128)(2,1)S(1)}, u32[]{:S(2)}, u32[]{:S(2)}) %collective-permute-start.3) | collective-permute-done | bytes 196640 | tf_op jit(solution)/shard_map/ppermute | solution.py:391
  113.4 7.9 %all-to-all-done.3.arrived = bf16[8,8,128,128]{3,2,1,0:T(8,128)(2,1)} async-done(((bf16[8,8,128,128]{3,2,1,0:T(8,128)(2,1)}), bf16[8,8,128,128]{3,2,1,0:T(8,128)(2,1)}, u32[]{:S(2)}, u32[]{:S(2)}) %all-to-all-start.3) | async-done | bytes 2097184 | tf_op jit(solution)/shard_map/all_to_all | solution.py:40
  121.3 2.6 %shard_map.91 = bf16[8,128,128]{2,1,0:T(8,128)(2,1)} custom-call(bf16[8,8,128,128]{3,2,1,0:T(8,128)(2,1)} %all-to-all-done.3.arrived, bf16[12,64,128]{2,1,0:T(8,128)(2,1)S(1)} %collective-permute-done.2.first, bf16[12,64,128]{2,1,0:T(8,128)(2,1)S(1)} %collective-permute-done.3.second), custom_call_target="tpu_custom_call" | custom-call | tf_op jit(solution)/shard_map/pallas_call | solution.py:394
  123.9 4.0 %all-to-all-start.4 = ((bf16[8,128,128]{2,1,0:T(8,128)(2,1)}), bf16[8,128,128]{2,1,0:T(8,128)(2,1)S(1)}, u32[]{:S(2)}, u32[]{:S(2)}) async-start(bf16[8,128,128]{2,1,0:T(8,128)(2,1)} %shard_map.91), calls=%async_computation.4 | async-start | bytes 524288 | tf_op jit(solution)/shard_map/all_to_all | solution.py:40
  127.9 2.7 %collective-permute-start.4 = (bf16[12,64,128]{2,1,0:T(8,128)(2,1)S(1)}, bf16[12,64,128]{2,1,0:T(8,128)(2,1)S(1)}, u32[]{:S(2)}, u32[]{:S(2)}) collective-permute-start(bf16[12,64,128]{2,1,0:T(8,128)(2,1)S(1)} %get-tuple-element.41), channel_id=1, source_target_pairs={{0,3},{1,0},{2,1},{3,2},{4,7},{5,4},{6,5},{7,6},{8,11},{9,8},{10,9... | collective-permute-start | bytes 589832 | tf_op jit(solution)/shard_map/ppermute | solution.py:391
  130.7 0.5 broadcast.7
  131.2 0.7 reduce.5
  131.8 0.1 reshape.23
  131.9 0.6 slice_reduce_fusion
  132.6 4.1 %collective-permute-done.4 = bf16[12,64,128]{2,1,0:T(8,128)(2,1)S(1)} collective-permute-done((bf16[12,64,128]{2,1,0:T(8,128)(2,1)S(1)}, bf16[12,64,128]{2,1,0:T(8,128)(2,1)S(1)}, u32[]{:S(2)}, u32[]{:S(2)}) %collective-permute-start.4) | collective-permute-done | bytes 196640 | tf_op jit(solution)/shard_map/ppermute | solution.py:391
  136.7 0.1 convert_add_fusion
  136.8 0.7 slice.13
  137.5 0.7 slice.12
  138.2 0.2 all-to-all-done.4.arrived
  138.4 1.3 shard_map.92
Async XLA Ops:
  1.4 0.8 copy-start.7
  22.9 10.5 %copy-start.3 = (bf16[32,64,128]{2,1,0:T(8,128)(2,1)S(1)}, bf16[32,64,128]{2,1,0:T(8,128)(2,1)}, u32[]{:S(2)}) copy-start(bf16[32,64,128]{2,1,0:T(8,128)(2,1)} %values.1) | copy-start | bytes 1572868
  22.9 12.7 %copy-start.8 = (bf16[4,64,128]{2,1,0:T(8,128)(2,1)S(1)}, bf16[4,64,128]{2,1,0:T(8,128)(2,1)}, u32[]{:S(2)}) copy-start(bf16[4,64,128]{2,1,0:T(8,128)(2,1)} %param.6) | copy-start | bytes 196612
  22.9 42.1 %all-to-all-start.1 = ((bf16[8,8,136,128]{3,2,1,0:T(8,128)(2,1)}), bf16[8,8,136,128]{3,2,1,0:T(8,128)(2,1)S(1)}, u32[]{:S(2)}, u32[]{:S(2)}) async-start(bf16[8,8,136,128]{3,2,1,0:T(8,128)(2,1)} %broadcast_in_dim.2), calls=%async_computation.1 | async-start | bytes 4456448 | tf_op jit(solution)/shard_map/all_to_all | solution.py:40
  33.7 15.5 %collective-permute-start = (bf16[32,64,128]{2,1,0:T(8,128)(2,1)S(1)}, bf16[32,64,128]{2,1,0:T(8,128)(2,1)S(1)}, u32[]{:S(2)}, u32[]{:S(2)}) collective-permute-start(bf16[32,64,128]{2,1,0:T(8,128)(2,1)S(1)} %shard_map.85.own_rows), channel_id=1, source_target_pairs={{0,4},{4,0},{8,12},{12,8},{16,20},{20,16},{24,28},{28,24},{32,36},... | collective-permute-start | bytes 1572872 | tf_op jit(solution)/shard_map/ppermute | solution.py:330
  48.5 0.7 copy-start.4
  68.6 0.7 copy-start.6
  69.3 17.3 %all-to-all-start.2 = ((f32[64,4,128]{2,1,0:T(4,128)}), f32[64,4,128]{2,1,0:T(4,128)S(1)}, u32[]{:S(2)}, u32[]{:S(2)}) async-start(f32[64,4,128]{2,1,0:T(4,128)} %copy-done.6), calls=%async_computation.2 | async-start | bytes 262144 | tf_op jit(solution)/shard_map/all_to_all | solution.py:40
  79.0 1.3 copy-start
  80.3 1.0 copy-start.1
  86.6 4.7 %copy-start.2 = (bf16[64,64,128]{2,1,0:T(8,128)(2,1)S(1)}, bf16[64,64,128]{2,1,0:T(8,128)(2,1)}, u32[]{:S(2)}) copy-start(bf16[64,64,128]{2,1,0:T(8,128)(2,1)} %copy-done.1) | copy-start | bytes 3145732
  86.6 34.8 %all-to-all-start.3 = ((bf16[8,8,128,128]{3,2,1,0:T(8,128)(2,1)}), bf16[8,8,128,128]{3,2,1,0:T(8,128)(2,1)}, u32[]{:S(2)}, u32[]{:S(2)}) async-start(bf16[8,8,128,128]{3,2,1,0:T(8,128)(2,1)} %bitcast.6), calls=%async_computation.3 | async-start | bytes 4194304 | tf_op jit(solution)/shard_map/all_to_all | solution.py:40
  91.3 1.0 copy-start.5
  97.1 3.8 %collective-permute-start.1 = (bf16[32,64,128]{2,1,0:T(8,128)(2,1)S(1)}, bf16[32,64,128]{2,1,0:T(8,128)(2,1)S(1)}, u32[]{:S(2)}, u32[]{:S(2)}) collective-permute-start(bf16[32,64,128]{2,1,0:T(8,128)(2,1)S(1)} %get-tuple-element.36), channel_id=1, source_target_pairs={{0,4},{4,0},{8,12},{12,8},{16,20},{20,16},{24,28},{28,24},{32,36},... | collective-permute-start | bytes 1572872 | tf_op jit(solution)/shard_map/ppermute | solution.py:389
  101.0 10.3 %collective-permute-start.2 = (bf16[12,64,128]{2,1,0:T(8,128)(2,1)S(1)}, bf16[12,64,128]{2,1,0:T(8,128)(2,1)S(1)}, u32[]{:S(2)}, u32[]{:S(2)}) collective-permute-start(bf16[12,64,128]{2,1,0:T(8,128)(2,1)S(1)} %get-tuple-element.38), channel_id=1, source_target_pairs={{0,2},{1,3},{2,0},{3,1},{4,6},{5,7},{6,4},{7,5},{8,10},{9,11},{10,... | collective-permute-start | bytes 589832 | tf_op jit(solution)/shard_map/ppermute | solution.py:391
  104.4 9.0 %collective-permute-start.3 = (bf16[12,64,128]{2,1,0:T(8,128)(2,1)S(1)}, bf16[12,64,128]{2,1,0:T(8,128)(2,1)S(1)}, u32[]{:S(2)}, u32[]{:S(2)}) collective-permute-start(bf16[12,64,128]{2,1,0:T(8,128)(2,1)S(1)} %get-tuple-element.39), channel_id=1, source_target_pairs={{0,1},{1,2},{2,3},{3,0},{4,5},{5,6},{6,7},{7,4},{8,9},{9,10},{10,1... | collective-permute-start | bytes 589832 | tf_op jit(solution)/shard_map/ppermute | solution.py:391
  123.9 14.5 %all-to-all-start.4 = ((bf16[8,128,128]{2,1,0:T(8,128)(2,1)}), bf16[8,128,128]{2,1,0:T(8,128)(2,1)S(1)}, u32[]{:S(2)}, u32[]{:S(2)}) async-start(bf16[8,128,128]{2,1,0:T(8,128)(2,1)} %shard_map.91), calls=%async_computation.4 | async-start | bytes 524288 | tf_op jit(solution)/shard_map/all_to_all | solution.py:40
  127.9 8.8 %collective-permute-start.4 = (bf16[12,64,128]{2,1,0:T(8,128)(2,1)S(1)}, bf16[12,64,128]{2,1,0:T(8,128)(2,1)S(1)}, u32[]{:S(2)}, u32[]{:S(2)}) collective-permute-start(bf16[12,64,128]{2,1,0:T(8,128)(2,1)S(1)} %get-tuple-element.41), channel_id=1, source_target_pairs={{0,3},{1,0},{2,1},{3,2},{4,7},{5,4},{6,5},{7,6},{8,11},{9,8},{10,9... | collective-permute-start | bytes 589832 | tf_op jit(solution)/shard_map/ppermute | solution.py:391

commit v11 on v10

--- a/solution.py
+++ b/solution.py
@@ -18,6 +18,7 @@
 F32, BF16, I32 = jnp.float32, jnp.bfloat16, jnp.int32
 EXACT = lax.Precision.HIGHEST
 EVERY = ("dp", "group")
+DOWN = range(N_Z - 1, -1, -1)
 
 
 def device(z, y, c, x):
@@ -25,14 +26,14 @@
 
 
 def along(z_core):
-    z_lines = [[device(z, y, z_core, x) for z in range(N_Z)] for y in range(N_Y) for x in range(GROUP)]
+    z_lines = [[device(z, y, z_core, x) for z in DOWN] for y in range(N_Y) for x in range(GROUP)]
     y_lines = [[device(z, y, 1 - z_core, x) for y in range(N_Y)] for z in range(N_Z) for x in range(GROUP)]
     return z_lines + y_lines
 
 
 def planes():
-    first = [[device(z, y, 0, x) for z in range(N_Z) for y in range(N_Y)] for x in range(GROUP)]
-    second = [[device(z, y, 1, x) for y in range(N_Y) for z in range(N_Z)] for x in range(GROUP)]
+    first = [[device(z, y, 0, x) for z in DOWN for y in range(N_Y)] for x in range(GROUP)]
+    second = [[device(z, y, 1, x) for y in range(N_Y) for z in DOWN] for x in range(GROUP)]
     return first + second
 
 
@@ -94,7 +95,8 @@
 def position():
     holder = lax.axis_index("dp")
     spot, core = holder // N_C, holder % N_C
-    source = jnp.where(core == 0, spot, (spot % N_Y) * N_Z + spot // N_Y)
+    z, y = N_Z - 1 - spot // N_Y, spot % N_Y
+    source = jnp.where(core == 0, z * N_Y + y, y * N_Z + z)
     return spot, core, source
 
 
@@ -276,7 +278,9 @@
         own_sum = jnp.where(lane // QT == q, mine[q : q + 1], own_sum)
     own = (iota((BATCH, QROWS), 0) == lax.axis_index("group") * QD + iota((BATCH, QROWS), 1) // QT).astype(F32)
     score_grad = jnp.exp(scores) / own_sum - own
-    losses[...] = jnp.log(own_sum) - jnp.sum(scores * own, axis=0, keepdims=True)
+    loss = jnp.log(own_sum) - jnp.sum(scores * own, axis=0, keepdims=True)
+    for q in range(QD):
+        losses[q] = jnp.sum(jnp.where(lane == q * QT, loss, 0.0))
     weight_grad = (exp_scores * (score_grad / total)[:, None, :]).astype(BF16).reshape(BATCH * PT, QROWS)
     query_part[...] = dot(weight_grad, cands, ((0,), (0,)))
     pos_grad[...] = dot(weight_grad, q_unit, ((1,), (0,))).reshape(BATCH, PT, D)
@@ -291,8 +295,8 @@
         out[QD:] = (own_grad[rows] + moved[rows].astype(F32)).astype(out.dtype)
 
 
-def add_blocks(arrived, first, second, out):
-    del first, second
+def add_blocks(arrived, first, second, third, out):
+    del first, second, third
     for part in range(N_Y):
         out[part] = jnp.sum(arrived[:, part].astype(F32), axis=0).astype(BF16)
 
@@ -366,11 +370,11 @@
             struct((ROWS, PT, D), BF16),
             struct((BATCH, PT, D), F32),
             struct((QROWS, D), F32),
-            struct((1, QROWS), F32),
+            struct((QD,), F32),
             struct((8, QROWS), F32),
         ),
         [smem(), vmem(), vmem(), vmem(), hbm(), hbm()],
-        (vmem(),) * 5 + (smem(),),
+        (vmem(),) * 4 + (smem(),) * 2,
         [
             pltpu.VMEM((ROWS, PT, D), F32),
             pltpu.VMEM((8, QROWS), F32),
@@ -392,14 +396,14 @@
         for ahead, part in ((2, off2), (1, off1), (3, off3))
     ]
     arrived = call(
-        add_blocks, struct((N_Y, QROWS, D), BF16), [vmem(), anywhere(), anywhere()], vmem()
-    )(arrived, moved[0], moved[1])
+        add_blocks, struct((N_Y, QROWS, D), BF16), [vmem(), anywhere(), anywhere(), anywhere()], vmem()
+    )(arrived, *moved)
     arrived = exchange(arrived, along(1))
     query_grad = call(
         collect, struct((QD, QT, D), F32), [smem(), vmem(), vmem()], vmem()
     )(weight_inv, query_part, arrived)
     total = kept + moved[0].astype(F32) + moved[1].astype(F32) + moved[2].astype(F32)
-    return losses.reshape(QD, QT)[:, 0], query_grad, total[:QD], total[QD:]
+    return losses, query_grad, total[:QD], total[QD:]
 
 
 def solution(mesh):

time: 141 us -> 139 us (0.986)
  starting transfers between devices: 37.6 us -> 46.7 us
  waiting for transfers between devices: 40.3 us -> 31.5 us
    all_to_all x4, starting transfers between devices: 23.7 us -> 33.6 us  [exchange(): lax.all_to_all(blocks, EVERY, split_axis=0, concat_axis=0, axis_index_gro...]
    all_to_all x4, waiting for transfers between devices: 29.2 us -> 22.1 us  [exchange(): lax.all_to_all(blocks, EVERY, split_axis=0, concat_axis=0, axis_index_gro...]
    ppermute x3, waiting for transfers between devices: 9.16 us -> 7.56 us  [per_device(): lax.ppermute(part, 'group', [(g, (g + ahead) % GROUP) for g in range(GROU...]
  transfers between devices with their start and end apart: 9 -> 9, of which waited for: 8 -> 7; matrix products, arithmetic and copies ran while one was open for 2% -> 1% of each run, Pallas kernels for 8% -> 8%
where the time goes in v11:
time: 139 us; the launch traced here: 138 us
  starting transfers between devices  46.7 us (34%)
  waiting for transfers between devices  31.5 us (23%)
  blocking collectives  29.8 us (21%)
  Pallas kernels  20.4 us (15%)
  local copies, waits for them, and re-layouts  8.42 us (6%)
    all_to_all x4, starting transfers between devices, exchange(): lax.all_to_all(blocks, EVERY, split_axis=0, concat_axis=0, axis_index_gro...  33.6 us
    all_to_all x4, waiting for transfers between devices, exchange(): lax.all_to_all(blocks, EVERY, split_axis=0, concat_axis=0, axis_index_gro...  22.1 us
    all_to_all x1, blocking collectives, exchange(): lax.all_to_all(blocks, EVERY, split_axis=0, concat_axis=0, axis_index_gro...  17.6 us
    all_gather x1, blocking collectives, per_device(): gathered = lax.all_gather(positives, 'group', axis=0, tiled=True)  12.3 us
    ppermute x3, starting transfers between devices, per_device(): lax.ppermute(part, 'group', [(g, (g + ahead) % GROUP) for g in range(GROU...  9.23 us
    ppermute x3, waiting for transfers between devices, per_device(): lax.ppermute(part, 'group', [(g, (g + ahead) % GROUP) for g in range(GROU...  7.56 us
    unnamed x18, local copies, waits for them, and re-layouts  5.36 us
    pallas_call x1, Pallas kernels, per_device(): call(weigh, (struct((ROWS, PT, D), F32), struct((ROWS, PT, D), BF16), str...  5.3 us
  transfers between devices with their start and end apart: 9, of which 7 were waited for; matrix products, arithmetic and copies ran while one was open for 1% of the time, Pallas kernels for 8%

profile of v11, /device:TPU:6, one launch (start us, length us, event | category | flops | bytes accessed | tf_op | source)
XLA Modules:
  0.0 138.5 jit_solution(12860151302703200133)
XLA Ops:
  0.6 0.7 pad_add_fusion.table_in
  1.4 0.0 copy-start.7
  1.4 0.8 copy-done.7
  2.1 1.5 %shard_map.84 = (bf16[8,136,128]{2,1,0:T(8,128)(2,1)S(1)}, bf16[4,32,128]{2,1,0:T(8,128)(2,1)S(1)}) custom-call(s32[40,128]{1,0:T(8,128)S(1)} %pad_add_fusion.table_in, bf16[4,32,128]{2,1,0:T(8,128)(2,1)S(1)} %copy-done.7), custom_call_target="tpu_custom_call" | custom-call | tf_op jit(solution)/shard_map/pallas_call | solution.py:318
  3.7 17.6 %all_to_all.25 = bf16[8,136,128]{2,1,0:T(8,128)(2,1)S(1)} all-to-all(bf16[8,136,128]{2,1,0:T(8,128)(2,1)S(1)} %get-tuple-element.23), channel_id=1, replica_groups={{452,388,324,260,196,132,68,4},{453,389,325,261,197,133,69,5},{454,390,..., dimensions={0} | all-to-all | bytes 557056 | tf_op jit(solution)/shard_map/all_to_all | solution.py:41
  21.2 1.7 %broadcast_in_dim.2 = bf16[8,8,136,128]{3,2,1,0:T(8,128)(2,1)} broadcast(bf16[8,136,128]{2,1,0:T(8,128)(2,1)S(1)} %all_to_all.25), dimensions={1,2,3} | broadcast | bytes 2506752 | tf_op jit(solution)/shard_map/broadcast_in_dim | solution.py:331
  22.9 0.0 copy-start.3
  22.9 0.0 copy-start.8
  22.9 12.7 %all-to-all-start.1 = ((bf16[8,8,136,128]{3,2,1,0:T(8,128)(2,1)}), bf16[8,8,136,128]{3,2,1,0:T(8,128)(2,1)S(1)}, u32[]{:S(2)}, u32[]{:S(2)}) async-start(bf16[8,8,136,128]{3,2,1,0:T(8,128)(2,1)} %broadcast_in_dim.2), calls=%async_computation.1 | async-start | bytes 4456448 | tf_op jit(solution)/shard_map/all_to_all | solution.py:41
  35.6 0.0 copy-done.3
  35.6 0.4 shard_map.85.own_rows
  36.0 1.9 %collective-permute-start = (bf16[32,64,128]{2,1,0:T(8,128)(2,1)S(1)}, bf16[32,64,128]{2,1,0:T(8,128)(2,1)S(1)}, u32[]{:S(2)}, u32[]{:S(2)}) collective-permute-start(bf16[32,64,128]{2,1,0:T(8,128)(2,1)S(1)} %shard_map.85.own_rows), channel_id=1, source_target_pairs={{0,4},{4,0},{8,12},{12,8},{16,20},{20,16},{24,28},{28,24},{32,36},... | collective-permute-start | bytes 1572872 | tf_op jit(solution)/shard_map/ppermute | solution.py:334
  37.9 0.0 copy-done.8
  37.9 12.3 %all_gather.3.positives = bf16[16,64,128]{2,1,0:T(8,128)(2,1)S(1)} all-gather(bf16[4,64,128]{2,1,0:T(8,128)(2,1)S(1)} %copy-done.8), channel_id=1, replica_groups=mesh['dp'=128,'group'=4] {'group'}, dimensions={0}, use_global_device_ids=true | all-gather | bytes 327680 | tf_op jit(solution)/shard_map/all_gather | solution.py:335
  50.2 0.6 shard_map.86
  50.8 0.0 copy-start.4
  50.8 0.7 copy-done.4
  51.5 0.0 collective-permute-done.other_rows
  51.5 10.4 %all-to-all-done.1 = bf16[8,8,136,128]{3,2,1,0:T(8,128)(2,1)S(1)} async-done(((bf16[8,8,136,128]{3,2,1,0:T(8,128)(2,1)}), bf16[8,8,136,128]{3,2,1,0:T(8,128)(2,1)S(1)}, u32[]{:S(2)}, u32[]{:S(2)}) %all-to-all-start.1) | async-done | bytes 2228256 | tf_op jit(solution)/shard_map/all_to_all | solution.py:41
  61.9 3.6 %shard_map.87 = (f32[64,128]{1,0:T(8,128)S(1)}, f32[64,4,128]{2,1,0:T(4,128)S(1)}, s32[8,512]{1,0:T(8,128)S(1)}) custom-call(bf16[64,136,128]{2,1,0:T(8,128)(2,1)S(1)} %bitcast.3, bf16[32,64,128]{2,1,0:T(8,128)(2,1)S(1)} %shard_map.85.own_rows, bf16[32,64,128]{2,1,0:T(8,128)(2,1)S(1)} %collective-permute-done.other_rows, ...), custom_call_target="tpu_custom_call" | custom-call | tf_op jit(solution)/shard_map/pallas_call | solution.py:340
  65.5 0.0 copy-start.6
  65.5 0.6 copy-done.6
  66.1 9.8 %all-to-all-start.2 = ((f32[64,4,128]{2,1,0:T(4,128)}), f32[64,4,128]{2,1,0:T(4,128)S(1)}, u32[]{:S(2)}, u32[]{:S(2)}) async-start(f32[64,4,128]{2,1,0:T(4,128)} %copy-done.6), calls=%async_computation.2 | async-start | bytes 262144 | tf_op jit(solution)/shard_map/all_to_all | solution.py:41
  75.9 5.1 %shard_map.88 = (bf16[64,64,128]{2,1,0:T(8,128)(2,1)S(1)}, bf16[64,128,128]{2,1,0:T(8,128)(2,1)S(1)}) custom-call(s32[8,512]{1,0:T(8,128)S(1)} %get-tuple-element.26.codes, bf16[64,136,128]{2,1,0:T(8,128)(2,1)S(1)} %bitcast.4, bf16[32,64,128]{2,1,0:T(8,128)(2,1)S(1)} %shard_map.85.own_rows, bf16[32,64,128]{2,1,0:T(8,128)(2,1)S(1)} %collective-permute-done.other_rows, ...), custom_call_target="tpu_custom_call" | custom-call | tf_op jit(solution)/shard_map/pallas_call | solution.py:358
  81.0 0.0 copy-start
  81.0 1.3 copy-done
  82.3 0.0 copy-start.1
  82.3 1.0 copy-done.1
  83.3 2.7 %all-to-all-done.2.sums = f32[64,4,128]{2,1,0:T(4,128)S(1)} async-done(((f32[64,4,128]{2,1,0:T(4,128)}), f32[64,4,128]{2,1,0:T(4,128)S(1)}, u32[]{:S(2)}, u32[]{:S(2)}) %all-to-all-start.2) | async-done | bytes 131104 | tf_op jit(solution)/shard_map/all_to_all | solution.py:41
  86.1 0.0 copy-start.2
  86.1 7.1 %all-to-all-start.3 = ((bf16[8,8,128,128]{3,2,1,0:T(8,128)(2,1)}), bf16[8,8,128,128]{3,2,1,0:T(8,128)(2,1)}, u32[]{:S(2)}, u32[]{:S(2)}) async-start(bf16[8,8,128,128]{3,2,1,0:T(8,128)(2,1)} %bitcast.6), calls=%async_computation.3 | async-start | bytes 4194304 | tf_op jit(solution)/shard_map/all_to_all | solution.py:41
  93.2 0.0 copy-done.2
  93.2 0.0 copy-start.5
  93.2 0.9 copy-done.5
  94.1 5.3 %shard_map.89 = (f32[32,64,128]{2,1,0:T(8,128)S(1)}, bf16[32,64,128]{2,1,0:T(8,128)(2,1)S(1)}, f32[16,64,128]{2,1,0:T(8,128)S(1)}, f32[128,128]{1,0:T(8,128)S(1)}, f32[4]{0:T(128)}, /*index=5*/f32[8,128]{1,0:T(8,128)S(1)}) custom-call(s32[8,512]{1,0:T(8,128)S(1)} %get-tuple-element.26.codes, f32[64,4,128]{2,1,0:T(4,128)S(1)} %all-to-all-done.2.sums, ...), custom_call_target="tpu_custom_call" | custom-call | tf_op jit(solution)/shard_map/pallas_call | solution.py:366
  99.4 1.9 %collective-permute-start.1 = (bf16[32,64,128]{2,1,0:T(8,128)(2,1)S(1)}, bf16[32,64,128]{2,1,0:T(8,128)(2,1)S(1)}, u32[]{:S(2)}, u32[]{:S(2)}) collective-permute-start(bf16[32,64,128]{2,1,0:T(8,128)(2,1)S(1)} %get-tuple-element.36), channel_id=1, source_target_pairs={{0,4},{4,0},{8,12},{12,8},{16,20},{20,16},{24,28},{28,24},{32,36},... | collective-permute-start | bytes 1572872 | tf_op jit(solution)/shard_map/ppermute | solution.py:393
  101.4 1.9 %collective-permute-done.1.moved = bf16[32,64,128]{2,1,0:T(8,128)(2,1)S(1)} collective-permute-done((bf16[32,64,128]{2,1,0:T(8,128)(2,1)S(1)}, bf16[32,64,128]{2,1,0:T(8,128)(2,1)S(1)}, u32[]{:S(2)}, u32[]{:S(2)}) %collective-permute-start.1) | collective-permute-done | bytes 524320 | tf_op jit(solution)/shard_map/ppermute | solution.py:393
  103.2 0.1 shard_map.90
  103.4 3.3 %collective-permute-start.2 = (bf16[12,64,128]{2,1,0:T(8,128)(2,1)S(1)}, bf16[12,64,128]{2,1,0:T(8,128)(2,1)S(1)}, u32[]{:S(2)}, u32[]{:S(2)}) collective-permute-start(bf16[12,64,128]{2,1,0:T(8,128)(2,1)S(1)} %get-tuple-element.38), channel_id=1, source_target_pairs={{0,2},{1,3},{2,0},{3,1},{4,6},{5,7},{6,4},{7,5},{8,10},{9,11},{10,... | collective-permute-start | bytes 589832 | tf_op jit(solution)/shard_map/ppermute | solution.py:395
  106.7 4.0 %collective-permute-start.3 = (bf16[12,64,128]{2,1,0:T(8,128)(2,1)S(1)}, bf16[12,64,128]{2,1,0:T(8,128)(2,1)S(1)}, u32[]{:S(2)}, u32[]{:S(2)}) collective-permute-start(bf16[12,64,128]{2,1,0:T(8,128)(2,1)S(1)} %get-tuple-element.39), channel_id=1, source_target_pairs={{0,1},{1,2},{2,3},{3,0},{4,5},{5,6},{6,7},{7,4},{8,9},{9,10},{10,1... | collective-permute-start | bytes 589832 | tf_op jit(solution)/shard_map/ppermute | solution.py:395
  110.7 1.9 %collective-permute-start.4 = (bf16[12,64,128]{2,1,0:T(8,128)(2,1)S(1)}, bf16[12,64,128]{2,1,0:T(8,128)(2,1)S(1)}, u32[]{:S(2)}, u32[]{:S(2)}) collective-permute-start(bf16[12,64,128]{2,1,0:T(8,128)(2,1)S(1)} %get-tuple-element.40), channel_id=1, source_target_pairs={{0,3},{1,0},{2,1},{3,2},{4,7},{5,4},{6,5},{7,6},{8,11},{9,8},{10,9... | collective-permute-start | bytes 589832 | tf_op jit(solution)/shard_map/ppermute | solution.py:395
  112.6 1.1 collective-permute-done.2.first
  113.7 2.0 %collective-permute-done.3.second = bf16[12,64,128]{2,1,0:T(8,128)(2,1)S(1)} collective-permute-done((bf16[12,64,128]{2,1,0:T(8,128)(2,1)S(1)}, bf16[12,64,128]{2,1,0:T(8,128)(2,1)S(1)}, u32[]{:S(2)}, u32[]{:S(2)}) %collective-permute-start.3) | collective-permute-done | bytes 196640 | tf_op jit(solution)/shard_map/ppermute | solution.py:395
  115.7 4.5 %collective-permute-done.4.third = bf16[12,64,128]{2,1,0:T(8,128)(2,1)S(1)} collective-permute-done((bf16[12,64,128]{2,1,0:T(8,128)(2,1)S(1)}, bf16[12,64,128]{2,1,0:T(8,128)(2,1)S(1)}, u32[]{:S(2)}, u32[]{:S(2)}) %collective-permute-start.4) | collective-permute-done | bytes 196640 | tf_op jit(solution)/shard_map/ppermute | solution.py:395
  120.2 0.0 all-to-all-done.3.arrived
  120.2 2.5 %shard_map.91 = bf16[8,128,128]{2,1,0:T(8,128)(2,1)} custom-call(bf16[8,8,128,128]{3,2,1,0:T(8,128)(2,1)} %all-to-all-done.3.arrived, bf16[12,64,128]{2,1,0:T(8,128)(2,1)S(1)} %collective-permute-done.2.first, bf16[12,64,128]{2,1,0:T(8,128)(2,1)S(1)} %collective-permute-done.3.second, bf16[12,64,128]{2,1,0:T(8,128)(2,1)S(1)} %collective-permute-done.4.third), custom_call_target="tpu_custom_call" | custom-call | tf_op jit(solution)/shard_map/pallas_call | solution.py:398
  122.7 4.0 %all-to-all-start.4 = ((bf16[8,128,128]{2,1,0:T(8,128)(2,1)}), bf16[8,128,128]{2,1,0:T(8,128)(2,1)S(1)}, u32[]{:S(2)}, u32[]{:S(2)}) async-start(bf16[8,128,128]{2,1,0:T(8,128)(2,1)} %shard_map.91), calls=%async_computation.4 | async-start | bytes 524288 | tf_op jit(solution)/shard_map/all_to_all | solution.py:41
  126.7 0.1 convert_add_fusion
  126.8 0.7 slice.8
  127.5 0.7 slice.9
  128.2 9.0 %all-to-all-done.4.arrived = bf16[8,128,128]{2,1,0:T(8,128)(2,1)S(1)} async-done(((bf16[8,128,128]{2,1,0:T(8,128)(2,1)}), bf16[8,128,128]{2,1,0:T(8,128)(2,1)S(1)}, u32[]{:S(2)}, u32[]{:S(2)}) %all-to-all-start.4) | async-done | bytes 262176 | tf_op jit(solution)/shard_map/all_to_all | solution.py:41
  137.2 1.3 shard_map.92
Async XLA Ops:
  1.4 0.8 copy-start.7
  22.9 12.7 %copy-start.3 = (bf16[32,64,128]{2,1,0:T(8,128)(2,1)S(1)}, bf16[32,64,128]{2,1,0:T(8,128)(2,1)}, u32[]{:S(2)}) copy-start(bf16[32,64,128]{2,1,0:T(8,128)(2,1)} %values.1) | copy-start | bytes 1572868
  22.9 15.0 %copy-start.8 = (bf16[4,64,128]{2,1,0:T(8,128)(2,1)S(1)}, bf16[4,64,128]{2,1,0:T(8,128)(2,1)}, u32[]{:S(2)}) copy-start(bf16[4,64,128]{2,1,0:T(8,128)(2,1)} %param.6) | copy-start | bytes 196612
  22.9 39.0 %all-to-all-start.1 = ((bf16[8,8,136,128]{3,2,1,0:T(8,128)(2,1)}), bf16[8,8,136,128]{3,2,1,0:T(8,128)(2,1)S(1)}, u32[]{:S(2)}, u32[]{:S(2)}) async-start(bf16[8,8,136,128]{3,2,1,0:T(8,128)(2,1)} %broadcast_in_dim.2), calls=%async_computation.1 | async-start | bytes 4456448 | tf_op jit(solution)/shard_map/all_to_all | solution.py:41
  36.0 15.5 %collective-permute-start = (bf16[32,64,128]{2,1,0:T(8,128)(2,1)S(1)}, bf16[32,64,128]{2,1,0:T(8,128)(2,1)S(1)}, u32[]{:S(2)}, u32[]{:S(2)}) collective-permute-start(bf16[32,64,128]{2,1,0:T(8,128)(2,1)S(1)} %shard_map.85.own_rows), channel_id=1, source_target_pairs={{0,4},{4,0},{8,12},{12,8},{16,20},{20,16},{24,28},{28,24},{32,36},... | collective-permute-start | bytes 1572872 | tf_op jit(solution)/shard_map/ppermute | solution.py:334
  50.8 0.7 copy-start.4
  65.5 0.7 copy-start.6
  66.1 19.9 %all-to-all-start.2 = ((f32[64,4,128]{2,1,0:T(4,128)}), f32[64,4,128]{2,1,0:T(4,128)S(1)}, u32[]{:S(2)}, u32[]{:S(2)}) async-start(f32[64,4,128]{2,1,0:T(4,128)} %copy-done.6), calls=%async_computation.2 | async-start | bytes 262144 | tf_op jit(solution)/shard_map/all_to_all | solution.py:41
  81.0 1.3 copy-start
  82.3 1.0 copy-start.1
  86.1 7.1 %copy-start.2 = (bf16[64,64,128]{2,1,0:T(8,128)(2,1)S(1)}, bf16[64,64,128]{2,1,0:T(8,128)(2,1)}, u32[]{:S(2)}) copy-start(bf16[64,64,128]{2,1,0:T(8,128)(2,1)} %copy-done.1) | copy-start | bytes 3145732
  86.1 34.1 %all-to-all-start.3 = ((bf16[8,8,128,128]{3,2,1,0:T(8,128)(2,1)}), bf16[8,8,128,128]{3,2,1,0:T(8,128)(2,1)}, u32[]{:S(2)}, u32[]{:S(2)}) async-start(bf16[8,8,128,128]{3,2,1,0:T(8,128)(2,1)} %bitcast.6), calls=%async_computation.3 | async-start | bytes 4194304 | tf_op jit(solution)/shard_map/all_to_all | solution.py:41
  93.2 1.0 copy-start.5
  99.4 3.8 %collective-permute-start.1 = (bf16[32,64,128]{2,1,0:T(8,128)(2,1)S(1)}, bf16[32,64,128]{2,1,0:T(8,128)(2,1)S(1)}, u32[]{:S(2)}, u32[]{:S(2)}) collective-permute-start(bf16[32,64,128]{2,1,0:T(8,128)(2,1)S(1)} %get-tuple-element.36), channel_id=1, source_target_pairs={{0,4},{4,0},{8,12},{12,8},{16,20},{20,16},{24,28},{28,24},{32,36},... | collective-permute-start | bytes 1572872 | tf_op jit(solution)/shard_map/ppermute | solution.py:393
  103.4 10.3 %collective-permute-start.2 = (bf16[12,64,128]{2,1,0:T(8,128)(2,1)S(1)}, bf16[12,64,128]{2,1,0:T(8,128)(2,1)S(1)}, u32[]{:S(2)}, u32[]{:S(2)}) collective-permute-start(bf16[12,64,128]{2,1,0:T(8,128)(2,1)S(1)} %get-tuple-element.38), channel_id=1, source_target_pairs={{0,2},{1,3},{2,0},{3,1},{4,6},{5,7},{6,4},{7,5},{8,10},{9,11},{10,... | collective-permute-start | bytes 589832 | tf_op jit(solution)/shard_map/ppermute | solution.py:395
  106.7 9.0 %collective-permute-start.3 = (bf16[12,64,128]{2,1,0:T(8,128)(2,1)S(1)}, bf16[12,64,128]{2,1,0:T(8,128)(2,1)S(1)}, u32[]{:S(2)}, u32[]{:S(2)}) collective-permute-start(bf16[12,64,128]{2,1,0:T(8,128)(2,1)S(1)} %get-tuple-element.39), channel_id=1, source_target_pairs={{0,1},{1,2},{2,3},{3,0},{4,5},{5,6},{6,7},{7,4},{8,9},{9,10},{10,1... | collective-permute-start | bytes 589832 | tf_op jit(solution)/shard_map/ppermute | solution.py:395
  110.7 9.5 %collective-permute-start.4 = (bf16[12,64,128]{2,1,0:T(8,128)(2,1)S(1)}, bf16[12,64,128]{2,1,0:T(8,128)(2,1)S(1)}, u32[]{:S(2)}, u32[]{:S(2)}) collective-permute-start(bf16[12,64,128]{2,1,0:T(8,128)(2,1)S(1)} %get-tuple-element.40), channel_id=1, source_target_pairs={{0,3},{1,0},{2,1},{3,2},{4,7},{5,4},{6,5},{7,6},{8,11},{9,8},{10,9... | collective-permute-start | bytes 589832 | tf_op jit(solution)/shard_map/ppermute | solution.py:395
  122.7 14.5 %all-to-all-start.4 = ((bf16[8,128,128]{2,1,0:T(8,128)(2,1)}), bf16[8,128,128]{2,1,0:T(8,128)(2,1)S(1)}, u32[]{:S(2)}, u32[]{:S(2)}) async-start(bf16[8,128,128]{2,1,0:T(8,128)(2,1)} %shard_map.91), calls=%async_computation.4 | async-start | bytes 524288 | tf_op jit(solution)/shard_map/all_to_all | solution.py:41

commit v12 on v11

--- a/solution.py
+++ b/solution.py
@@ -242,16 +242,18 @@
     for_sources(one)
 
 
-def weigh(
-    codes, sums, asked, probs, q_in, gathered_in, own_grad, other_grad, pos_grad, query_part, losses, weight_inv,
-    other_acc, inverse, q_tiles, gathered, sems,
-):
-    later = fetch([(q_in, q_tiles), (gathered_in, gathered)], sems)
+def weigh(codes, sums, asked, probs, own_grad, other_grad, own_sum, weight_inv, other_acc, inverse, sem):
     weight_sum = jnp.sum(sums[...], axis=0)
     inverse[...] = jnp.zeros_like(inverse)
     inverse[0:QD] = 1.0 / weight_sum
-    copy = pltpu.make_async_copy(inverse, weight_inv, sems.at[2])
+    copy = pltpu.make_async_copy(inverse, weight_inv, sem)
     copy.start()
+    lane = iota((1, QROWS), 1)
+    mine = jnp.sum(jnp.where(lane == position()[2], weight_sum, 0.0), axis=1, keepdims=True)
+    spread_sum = jnp.zeros((1, QROWS), F32)
+    for q in range(QD):
+        spread_sum = jnp.where(lane // QT == q, mine[q : q + 1], spread_sum)
+    own_sum[...] = spread_sum
     own_grad[...] = jnp.zeros_like(own_grad)
     other_acc[...] = jnp.zeros_like(other_acc)
     copy.wait()
@@ -267,18 +269,14 @@
     for_sources(add)
     other_grad[...] = other_acc[...].astype(BF16)
 
-    for copy in later:
-        copy.wait()
+
+def weigh_positives(own_sum, q_tiles, gathered, pos_grad, query_part, losses):
     q_unit = q_tiles[...].reshape(QROWS, D)
     cands, exp_scores, total, scores = positive_scores(q_unit, gathered)
     lane = iota((1, QROWS), 1)
-    mine = jnp.sum(jnp.where(lane == position()[2], weight_sum, 0.0), axis=1, keepdims=True)
-    own_sum = jnp.zeros((1, QROWS), F32)
-    for q in range(QD):
-        own_sum = jnp.where(lane // QT == q, mine[q : q + 1], own_sum)
     own = (iota((BATCH, QROWS), 0) == lax.axis_index("group") * QD + iota((BATCH, QROWS), 1) // QT).astype(F32)
-    score_grad = jnp.exp(scores) / own_sum - own
-    loss = jnp.log(own_sum) - jnp.sum(scores * own, axis=0, keepdims=True)
+    score_grad = jnp.exp(scores) / own_sum[...] - own
+    loss = jnp.log(own_sum[...]) - jnp.sum(scores * own, axis=0, keepdims=True)
     for q in range(QD):
         losses[q] = jnp.sum(jnp.where(lane == q * QT, loss, 0.0))
     weight_grad = (exp_scores * (score_grad / total)[:, None, :]).astype(BF16).reshape(BATCH * PT, QROWS)
@@ -295,8 +293,8 @@
         out[QD:] = (own_grad[rows] + moved[rows].astype(F32)).astype(out.dtype)
 
 
-def add_blocks(arrived, first, second, third, out):
-    del first, second, third
+def add_blocks(arrived, first, second, out):
+    del first, second
     for part in range(N_Y):
         out[part] = jnp.sum(arrived[:, part].astype(F32), axis=0).astype(BF16)
 
@@ -363,26 +361,24 @@
     )(codes, asked, own_rows, other_rows, factor)
     arrived = exchange(back.reshape(N_Z, N_Y, QROWS, D), along(0))
 
-    own_grad, other_grad, pos_grad, query_part, losses, weight_inv = call(
+    own_grad, other_grad, own_sum, weight_inv = call(
         weigh,
         (
             struct((ROWS, PT, D), F32),
             struct((ROWS, PT, D), BF16),
-            struct((BATCH, PT, D), F32),
-            struct((QROWS, D), F32),
-            struct((QD,), F32),
+            struct((1, QROWS), F32),
             struct((8, QROWS), F32),
         ),
-        [smem(), vmem(), vmem(), vmem(), hbm(), hbm()],
-        (vmem(),) * 4 + (smem(),) * 2,
-        [
-            pltpu.VMEM((ROWS, PT, D), F32),
-            pltpu.VMEM((8, QROWS), F32),
-            pltpu.VMEM((QD, QT, D), BF16),
-            pltpu.VMEM((BATCH, PT, D), BF16),
-            pltpu.SemaphoreType.DMA((3,)),
-        ],
-    )(codes, sums, asked, probs, q_unit, gathered)
+        [smem(), vmem(), vmem(), vmem()],
+        (vmem(), vmem(), vmem(), smem()),
+        [pltpu.VMEM((ROWS, PT, D), F32), pltpu.VMEM((8, QROWS), F32), pltpu.SemaphoreType.DMA],
+    )(codes, sums, asked, probs)
+    pos_grad, query_part, losses = call(
+        weigh_positives,
+        (struct((BATCH, PT, D), F32), struct((QROWS, D), F32), struct((QD,), F32)),
+        [vmem()] * 3,
+        (vmem(), vmem(), smem()),
+    )(own_sum, q_unit, gathered)
 
     block = (QD + ROWS // GROUP, PT, D)
     kept, off1, off2, off3 = call(
@@ -396,8 +392,8 @@
         for ahead, part in ((2, off2), (1, off1), (3, off3))
     ]
     arrived = call(
-        add_blocks, struct((N_Y, QROWS, D), BF16), [vmem(), anywhere(), anywhere(), anywhere()], vmem()
-    )(arrived, *moved)
+        add_blocks, struct((N_Y, QROWS, D), BF16), [vmem(), anywhere(), anywhere()], vmem()
+    )(arrived, moved[0], moved[1])
     arrived = exchange(arrived, along(1))
     query_grad = call(
         collect, struct((QD, QT, D), F32), [smem(), vmem(), vmem()], vmem()

time: 139 us -> 138 us (level)
  waiting for transfers between devices: 31.5 us -> 29.8 us
    all_to_all x4, waiting for transfers between devices: 22.1 us -> 17.4 us  [exchange(): lax.all_to_all(blocks, EVERY, split_axis=0, concat_axis=0, axis_index_gro...]
    ppermute x3, waiting for transfers between devices: 7.56 us -> 11.8 us  [per_device(): lax.ppermute(part, 'group', [(g, (g + ahead) % GROUP) for g in range(GROU...]
  transfers between devices with their start and end apart: 9 -> 9, of which waited for: 7 -> 7; matrix products, arithmetic and copies ran while one was open for 1% -> 1% of each run, Pallas kernels for 8% -> 9%
where the time goes in v12:
time: 138 us; the launch traced here: 137 us
  starting transfers between devices  47.5 us (34%)
  blocking collectives  29.8 us (22%)
  waiting for transfers between devices  29.8 us (22%)
  Pallas kernels  20.9 us (15%)
  local copies, waits for them, and re-layouts  7.5 us (5%)
    all_to_all x4, starting transfers between devices, exchange(): lax.all_to_all(blocks, EVERY, split_axis=0, concat_axis=0, axis_index_gro...  33.7 us
    all_to_all x1, blocking collectives, exchange(): lax.all_to_all(blocks, EVERY, split_axis=0, concat_axis=0, axis_index_gro...  17.6 us
    all_to_all x4, waiting for transfers between devices, exchange(): lax.all_to_all(blocks, EVERY, split_axis=0, concat_axis=0, axis_index_gro...  17.4 us
    all_gather x1, blocking collectives, per_device(): gathered = lax.all_gather(positives, 'group', axis=0, tiled=True)  12.3 us
    ppermute x3, waiting for transfers between devices, per_device(): lax.ppermute(part, 'group', [(g, (g + ahead) % GROUP) for g in range(GROU...  11.8 us
    ppermute x3, starting transfers between devices, per_device(): lax.ppermute(part, 'group', [(g, (g + ahead) % GROUP) for g in range(GROU...  10 us
    pallas_call x1, Pallas kernels, per_device(): call(terms, (struct((SPOTS, PT, QROWS), BF16), struct((SPOTS, QROWS, D),...  5.13 us
    pallas_call x1, Pallas kernels, per_device(): call(weigh, (struct((ROWS, PT, D), F32), struct((ROWS, PT, D), BF16), str...  4.51 us
  transfers between devices with their start and end apart: 9, of which 7 were waited for; matrix products, arithmetic and copies ran while one was open for 1% of the time, Pallas kernels for 9%

profile of v12, /device:TPU:6, one launch (start us, length us, event | category | flops | bytes accessed | tf_op | source)
XLA Modules:
  0.0 137.1 jit_solution(15433861511642014043)
XLA Ops:
  0.6 0.7 pad_add_fusion.table_in
  1.4 0.0 copy-start.7
  1.4 0.8 copy-done.7
  2.1 1.5 %shard_map.84 = (bf16[8,136,128]{2,1,0:T(8,128)(2,1)S(1)}, bf16[4,32,128]{2,1,0:T(8,128)(2,1)S(1)}) custom-call(s32[40,128]{1,0:T(8,128)S(1)} %pad_add_fusion.table_in, bf16[4,32,128]{2,1,0:T(8,128)(2,1)S(1)} %copy-done.7), custom_call_target="tpu_custom_call" | custom-call | tf_op jit(solution)/shard_map/pallas_call | solution.py:316
  3.7 17.6 %all_to_all.25 = bf16[8,136,128]{2,1,0:T(8,128)(2,1)S(1)} all-to-all(bf16[8,136,128]{2,1,0:T(8,128)(2,1)S(1)} %get-tuple-element.24), channel_id=1, replica_groups={{452,388,324,260,196,132,68,4},{453,389,325,261,197,133,69,5},{454,390,..., dimensions={0} | all-to-all | bytes 557056 | tf_op jit(solution)/shard_map/all_to_all | solution.py:41
  21.2 1.7 %broadcast_in_dim.2 = bf16[8,8,136,128]{3,2,1,0:T(8,128)(2,1)} broadcast(bf16[8,136,128]{2,1,0:T(8,128)(2,1)S(1)} %all_to_all.25), dimensions={1,2,3} | broadcast | bytes 2506752 | tf_op jit(solution)/shard_map/broadcast_in_dim | solution.py:329
  22.9 0.0 copy-start.3
  22.9 0.0 copy-start.8
  22.9 12.7 %all-to-all-start.1 = ((bf16[8,8,136,128]{3,2,1,0:T(8,128)(2,1)}), bf16[8,8,136,128]{3,2,1,0:T(8,128)(2,1)S(1)}, u32[]{:S(2)}, u32[]{:S(2)}) async-start(bf16[8,8,136,128]{3,2,1,0:T(8,128)(2,1)} %broadcast_in_dim.2), calls=%async_computation.1 | async-start | bytes 4456448 | tf_op jit(solution)/shard_map/all_to_all | solution.py:41
  35.6 0.0 copy-done.3
  35.6 0.4 shard_map.85.own_rows
  36.0 1.9 %collective-permute-start = (bf16[32,64,128]{2,1,0:T(8,128)(2,1)S(1)}, bf16[32,64,128]{2,1,0:T(8,128)(2,1)S(1)}, u32[]{:S(2)}, u32[]{:S(2)}) collective-permute-start(bf16[32,64,128]{2,1,0:T(8,128)(2,1)S(1)} %shard_map.85.own_rows), channel_id=1, source_target_pairs={{0,4},{4,0},{8,12},{12,8},{16,20},{20,16},{24,28},{28,24},{32,36},... | collective-permute-start | bytes 1572872 | tf_op jit(solution)/shard_map/ppermute | solution.py:332
  37.9 0.0 copy-done.8
  37.9 12.3 %all_gather.3.positives = bf16[16,64,128]{2,1,0:T(8,128)(2,1)S(1)} all-gather(bf16[4,64,128]{2,1,0:T(8,128)(2,1)S(1)} %copy-done.8), channel_id=1, replica_groups=mesh['dp'=128,'group'=4] {'group'}, dimensions={0}, use_global_device_ids=true | all-gather | bytes 327680 | tf_op jit(solution)/shard_map/all_gather | solution.py:333
  50.2 0.6 shard_map.86
  50.8 0.0 copy-start.4
  50.8 0.7 copy-done.4
  51.5 0.0 collective-permute-done.other_rows
  51.5 10.4 %all-to-all-done.1 = bf16[8,8,136,128]{3,2,1,0:T(8,128)(2,1)S(1)} async-done(((bf16[8,8,136,128]{3,2,1,0:T(8,128)(2,1)}), bf16[8,8,136,128]{3,2,1,0:T(8,128)(2,1)S(1)}, u32[]{:S(2)}, u32[]{:S(2)}) %all-to-all-start.1) | async-done | bytes 2228256 | tf_op jit(solution)/shard_map/all_to_all | solution.py:41
  61.9 3.6 %shard_map.87 = (f32[64,128]{1,0:T(8,128)S(1)}, f32[64,4,128]{2,1,0:T(4,128)S(1)}, s32[8,512]{1,0:T(8,128)S(1)}) custom-call(bf16[64,136,128]{2,1,0:T(8,128)(2,1)S(1)} %bitcast.3, bf16[32,64,128]{2,1,0:T(8,128)(2,1)S(1)} %shard_map.85.own_rows, bf16[32,64,128]{2,1,0:T(8,128)(2,1)S(1)} %collective-permute-done.other_rows, ...), custom_call_target="tpu_custom_call" | custom-call | tf_op jit(solution)/shard_map/pallas_call | solution.py:338
  65.5 0.0 copy-start.6
  65.5 0.6 copy-done.6
  66.1 9.8 %all-to-all-start.2 = ((f32[64,4,128]{2,1,0:T(4,128)}), f32[64,4,128]{2,1,0:T(4,128)S(1)}, u32[]{:S(2)}, u32[]{:S(2)}) async-start(f32[64,4,128]{2,1,0:T(4,128)} %copy-done.6), calls=%async_computation.2 | async-start | bytes 262144 | tf_op jit(solution)/shard_map/all_to_all | solution.py:41
  75.9 5.1 %shard_map.88 = (bf16[64,64,128]{2,1,0:T(8,128)(2,1)S(1)}, bf16[64,128,128]{2,1,0:T(8,128)(2,1)S(1)}) custom-call(s32[8,512]{1,0:T(8,128)S(1)} %get-tuple-element.27.codes, bf16[64,136,128]{2,1,0:T(8,128)(2,1)S(1)} %bitcast.4, bf16[32,64,128]{2,1,0:T(8,128)(2,1)S(1)} %shard_map.85.own_rows, bf16[32,64,128]{2,1,0:T(8,128)(2,1)S(1)} %collective-permute-done.other_rows, ...), custom_call_target="tpu_custom_call" | custom-call | tf_op jit(solution)/shard_map/pallas_call | solution.py:356
  81.0 0.0 copy-start
  81.0 1.3 copy-done
  82.3 0.0 copy-start.1
  82.3 1.0 copy-done.1
  83.4 2.7 %all-to-all-done.2.sums = f32[64,4,128]{2,1,0:T(4,128)S(1)} async-done(((f32[64,4,128]{2,1,0:T(4,128)}), f32[64,4,128]{2,1,0:T(4,128)S(1)}, u32[]{:S(2)}, u32[]{:S(2)}) %all-to-all-start.2) | async-done | bytes 131104 | tf_op jit(solution)/shard_map/all_to_all | solution.py:41
  86.0 0.0 copy-start.2
  86.1 7.1 %all-to-all-start.3 = ((bf16[8,8,128,128]{3,2,1,0:T(8,128)(2,1)}), bf16[8,8,128,128]{3,2,1,0:T(8,128)(2,1)}, u32[]{:S(2)}, u32[]{:S(2)}) async-start(bf16[8,8,128,128]{3,2,1,0:T(8,128)(2,1)} %bitcast.6), calls=%async_computation.3 | async-start | bytes 4194304 | tf_op jit(solution)/shard_map/all_to_all | solution.py:41
  93.2 0.0 copy-start.5
  93.2 0.0 copy-done.2
  93.2 4.5 %shard_map.89 = (f32[32,64,128]{2,1,0:T(8,128)S(1)}, bf16[32,64,128]{2,1,0:T(8,128)(2,1)S(1)}, f32[1,128]{1,0:T(1,128)S(1)}, f32[8,128]{1,0:T(8,128)S(1)}) custom-call(s32[8,512]{1,0:T(8,128)S(1)} %get-tuple-element.27.codes, f32[64,4,128]{2,1,0:T(4,128)S(1)} %all-to-all-done.2.sums, bf16[64,136,128]{2,1,0:T(8,128)(2,1)S(1)} %bitcast.5, ...), custom_call_target="tpu_custom_call" | custom-call | tf_op jit(solution)/shard_map/pallas_call | solution.py:364
  97.7 1.9 %collective-permute-start.1 = (bf16[32,64,128]{2,1,0:T(8,128)(2,1)S(1)}, bf16[32,64,128]{2,1,0:T(8,128)(2,1)S(1)}, u32[]{:S(2)}, u32[]{:S(2)}) collective-permute-start(bf16[32,64,128]{2,1,0:T(8,128)(2,1)S(1)} %get-tuple-element.38), channel_id=1, source_target_pairs={{0,4},{4,0},{8,12},{12,8},{16,20},{20,16},{24,28},{28,24},{32,36},... | collective-permute-start | bytes 1572872 | tf_op jit(solution)/shard_map/ppermute | solution.py:389
  99.6 0.0 copy-done.5
  99.6 1.2 shard_map.90
  100.9 0.6 collective-permute-done.1.moved
  101.5 0.1 shard_map.91
  101.6 3.3 %collective-permute-start.2 = (bf16[12,64,128]{2,1,0:T(8,128)(2,1)S(1)}, bf16[12,64,128]{2,1,0:T(8,128)(2,1)S(1)}, u32[]{:S(2)}, u32[]{:S(2)}) collective-permute-start(bf16[12,64,128]{2,1,0:T(8,128)(2,1)S(1)} %get-tuple-element.40), channel_id=1, source_target_pairs={{0,2},{1,3},{2,0},{3,1},{4,6},{5,7},{6,4},{7,5},{8,10},{9,11},{10,... | collective-permute-start | bytes 589832 | tf_op jit(solution)/shard_map/ppermute | solution.py:391
  104.9 4.0 %collective-permute-start.3 = (bf16[12,64,128]{2,1,0:T(8,128)(2,1)S(1)}, bf16[12,64,128]{2,1,0:T(8,128)(2,1)S(1)}, u32[]{:S(2)}, u32[]{:S(2)}) collective-permute-start(bf16[12,64,128]{2,1,0:T(8,128)(2,1)S(1)} %get-tuple-element.41), channel_id=1, source_target_pairs={{0,1},{1,2},{2,3},{3,0},{4,5},{5,6},{6,7},{7,4},{8,9},{9,10},{10,1... | collective-permute-start | bytes 589832 | tf_op jit(solution)/shard_map/ppermute | solution.py:391
  109.0 3.0 %collective-permute-done.2.first = bf16[12,64,128]{2,1,0:T(8,128)(2,1)S(1)} collective-permute-done((bf16[12,64,128]{2,1,0:T(8,128)(2,1)S(1)}, bf16[12,64,128]{2,1,0:T(8,128)(2,1)S(1)}, u32[]{:S(2)}, u32[]{:S(2)}) %collective-permute-start.2) | collective-permute-done | bytes 196640 | tf_op jit(solution)/shard_map/ppermute | solution.py:391
  112.0 2.0 %collective-permute-done.3.second = bf16[12,64,128]{2,1,0:T(8,128)(2,1)S(1)} collective-permute-done((bf16[12,64,128]{2,1,0:T(8,128)(2,1)S(1)}, bf16[12,64,128]{2,1,0:T(8,128)(2,1)S(1)}, u32[]{:S(2)}, u32[]{:S(2)}) %collective-permute-start.3) | collective-permute-done | bytes 196640 | tf_op jit(solution)/shard_map/ppermute | solution.py:391
  114.0 4.3 %all-to-all-done.3.arrived = bf16[8,8,128,128]{3,2,1,0:T(8,128)(2,1)} async-done(((bf16[8,8,128,128]{3,2,1,0:T(8,128)(2,1)}), bf16[8,8,128,128]{3,2,1,0:T(8,128)(2,1)}, u32[]{:S(2)}, u32[]{:S(2)}) %all-to-all-start.3) | async-done | bytes 2097184 | tf_op jit(solution)/shard_map/all_to_all | solution.py:41
  118.3 2.6 %shard_map.92 = bf16[8,128,128]{2,1,0:T(8,128)(2,1)} custom-call(bf16[8,8,128,128]{3,2,1,0:T(8,128)(2,1)} %all-to-all-done.3.arrived, bf16[12,64,128]{2,1,0:T(8,128)(2,1)S(1)} %collective-permute-done.2.first, bf16[12,64,128]{2,1,0:T(8,128)(2,1)S(1)} %collective-permute-done.3.second), custom_call_target="tpu_custom_call" | custom-call | tf_op jit(solution)/shard_map/pallas_call | solution.py:394
  120.8 4.0 %all-to-all-start.4 = ((bf16[8,128,128]{2,1,0:T(8,128)(2,1)}), bf16[8,128,128]{2,1,0:T(8,128)(2,1)S(1)}, u32[]{:S(2)}, u32[]{:S(2)}) async-start(bf16[8,128,128]{2,1,0:T(8,128)(2,1)} %shard_map.92), calls=%async_computation.4 | async-start | bytes 524288 | tf_op jit(solution)/shard_map/all_to_all | solution.py:41
  124.9 2.7 %collective-permute-start.4 = (bf16[12,64,128]{2,1,0:T(8,128)(2,1)S(1)}, bf16[12,64,128]{2,1,0:T(8,128)(2,1)S(1)}, u32[]{:S(2)}, u32[]{:S(2)}) collective-permute-start(bf16[12,64,128]{2,1,0:T(8,128)(2,1)S(1)} %get-tuple-element.43), channel_id=1, source_target_pairs={{0,3},{1,0},{2,1},{3,2},{4,7},{5,4},{6,5},{7,6},{8,11},{9,8},{10,9... | collective-permute-start | bytes 589832 | tf_op jit(solution)/shard_map/ppermute | solution.py:391
  127.6 6.8 %collective-permute-done.4 = bf16[12,64,128]{2,1,0:T(8,128)(2,1)S(1)} collective-permute-done((bf16[12,64,128]{2,1,0:T(8,128)(2,1)S(1)}, bf16[12,64,128]{2,1,0:T(8,128)(2,1)S(1)}, u32[]{:S(2)}, u32[]{:S(2)}) %collective-permute-start.4) | collective-permute-done | bytes 196640 | tf_op jit(solution)/shard_map/ppermute | solution.py:391
  134.4 0.1 convert_add_fusion
  134.5 0.7 slice.8
  135.1 0.7 slice.9
  135.8 0.0 all-to-all-done.4.arrived
  135.9 1.3 shard_map.93
Async XLA Ops:
  1.4 0.8 copy-start.7
  22.9 12.7 %copy-start.3 = (bf16[32,64,128]{2,1,0:T(8,128)(2,1)S(1)}, bf16[32,64,128]{2,1,0:T(8,128)(2,1)}, u32[]{:S(2)}) copy-start(bf16[32,64,128]{2,1,0:T(8,128)(2,1)} %values.1) | copy-start | bytes 1572868
  22.9 15.0 %copy-start.8 = (bf16[4,64,128]{2,1,0:T(8,128)(2,1)S(1)}, bf16[4,64,128]{2,1,0:T(8,128)(2,1)}, u32[]{:S(2)}) copy-start(bf16[4,64,128]{2,1,0:T(8,128)(2,1)} %param.6) | copy-start | bytes 196612
  22.9 39.0 %all-to-all-start.1 = ((bf16[8,8,136,128]{3,2,1,0:T(8,128)(2,1)}), bf16[8,8,136,128]{3,2,1,0:T(8,128)(2,1)S(1)}, u32[]{:S(2)}, u32[]{:S(2)}) async-start(bf16[8,8,136,128]{3,2,1,0:T(8,128)(2,1)} %broadcast_in_dim.2), calls=%async_computation.1 | async-start | bytes 4456448 | tf_op jit(solution)/shard_map/all_to_all | solution.py:41
  36.0 15.5 %collective-permute-start = (bf16[32,64,128]{2,1,0:T(8,128)(2,1)S(1)}, bf16[32,64,128]{2,1,0:T(8,128)(2,1)S(1)}, u32[]{:S(2)}, u32[]{:S(2)}) collective-permute-start(bf16[32,64,128]{2,1,0:T(8,128)(2,1)S(1)} %shard_map.85.own_rows), channel_id=1, source_target_pairs={{0,4},{4,0},{8,12},{12,8},{16,20},{20,16},{24,28},{28,24},{32,36},... | collective-permute-start | bytes 1572872 | tf_op jit(solution)/shard_map/ppermute | solution.py:332
  50.8 0.7 copy-start.4
  65.5 0.7 copy-start.6
  66.1 19.9 %all-to-all-start.2 = ((f32[64,4,128]{2,1,0:T(4,128)}), f32[64,4,128]{2,1,0:T(4,128)S(1)}, u32[]{:S(2)}, u32[]{:S(2)}) async-start(f32[64,4,128]{2,1,0:T(4,128)} %copy-done.6), calls=%async_computation.2 | async-start | bytes 262144 | tf_op jit(solution)/shard_map/all_to_all | solution.py:41
  81.0 1.3 copy-start
  82.3 1.0 copy-start.1
  86.0 7.1 %copy-start.2 = (bf16[64,64,128]{2,1,0:T(8,128)(2,1)S(1)}, bf16[64,64,128]{2,1,0:T(8,128)(2,1)}, u32[]{:S(2)}) copy-start(bf16[64,64,128]{2,1,0:T(8,128)(2,1)} %copy-done.1) | copy-start | bytes 3145732
  86.1 32.2 %all-to-all-start.3 = ((bf16[8,8,128,128]{3,2,1,0:T(8,128)(2,1)}), bf16[8,8,128,128]{3,2,1,0:T(8,128)(2,1)}, u32[]{:S(2)}, u32[]{:S(2)}) async-start(bf16[8,8,128,128]{3,2,1,0:T(8,128)(2,1)} %bitcast.6), calls=%async_computation.3 | async-start | bytes 4194304 | tf_op jit(solution)/shard_map/all_to_all | solution.py:41
  93.2 6.5 %copy-start.5 = (bf16[16,64,128]{2,1,0:T(8,128)(2,1)S(1)}, bf16[16,64,128]{2,1,0:T(8,128)(2,1)}, u32[]{:S(2)}) copy-start(bf16[16,64,128]{2,1,0:T(8,128)(2,1)} %copy-done.4) | copy-start | bytes 786436
  97.7 3.8 %collective-permute-start.1 = (bf16[32,64,128]{2,1,0:T(8,128)(2,1)S(1)}, bf16[32,64,128]{2,1,0:T(8,128)(2,1)S(1)}, u32[]{:S(2)}, u32[]{:S(2)}) collective-permute-start(bf16[32,64,128]{2,1,0:T(8,128)(2,1)S(1)} %get-tuple-element.38), channel_id=1, source_target_pairs={{0,4},{4,0},{8,12},{12,8},{16,20},{20,16},{24,28},{28,24},{32,36},... | collective-permute-start | bytes 1572872 | tf_op jit(solution)/shard_map/ppermute | solution.py:389
  101.6 10.3 %collective-permute-start.2 = (bf16[12,64,128]{2,1,0:T(8,128)(2,1)S(1)}, bf16[12,64,128]{2,1,0:T(8,128)(2,1)S(1)}, u32[]{:S(2)}, u32[]{:S(2)}) collective-permute-start(bf16[12,64,128]{2,1,0:T(8,128)(2,1)S(1)} %get-tuple-element.40), channel_id=1, source_target_pairs={{0,2},{1,3},{2,0},{3,1},{4,6},{5,7},{6,4},{7,5},{8,10},{9,11},{10,... | collective-permute-start | bytes 589832 | tf_op jit(solution)/shard_map/ppermute | solution.py:391
  104.9 9.0 %collective-permute-start.3 = (bf16[12,64,128]{2,1,0:T(8,128)(2,1)S(1)}, bf16[12,64,128]{2,1,0:T(8,128)(2,1)S(1)}, u32[]{:S(2)}, u32[]{:S(2)}) collective-permute-start(bf16[12,64,128]{2,1,0:T(8,128)(2,1)S(1)} %get-tuple-element.41), channel_id=1, source_target_pairs={{0,1},{1,2},{2,3},{3,0},{4,5},{5,6},{6,7},{7,4},{8,9},{9,10},{10,1... | collective-permute-start | bytes 589832 | tf_op jit(solution)/shard_map/ppermute | solution.py:391
  120.8 15.0 %all-to-all-start.4 = ((bf16[8,128,128]{2,1,0:T(8,128)(2,1)}), bf16[8,128,128]{2,1,0:T(8,128)(2,1)S(1)}, u32[]{:S(2)}, u32[]{:S(2)}) async-start(bf16[8,128,128]{2,1,0:T(8,128)(2,1)} %shard_map.92), calls=%async_computation.4 | async-start | bytes 524288 | tf_op jit(solution)/shard_map/all_to_all | solution.py:41
  124.9 9.5 %collective-permute-start.4 = (bf16[12,64,128]{2,1,0:T(8,128)(2,1)S(1)}, bf16[12,64,128]{2,1,0:T(8,128)(2,1)S(1)}, u32[]{:S(2)}, u32[]{:S(2)}) collective-permute-start(bf16[12,64,128]{2,1,0:T(8,128)(2,1)S(1)} %get-tuple-element.43), channel_id=1, source_target_pairs={{0,3},{1,0},{2,1},{3,2},{4,7},{5,4},{6,5},{7,6},{8,11},{9,8},{10,9... | collective-permute-start | bytes 589832 | tf_op jit(solution)/shard_map/ppermute | solution.py:391

commit v13 on v12

--- a/solution.py
+++ b/solution.py
@@ -18,7 +18,7 @@
 F32, BF16, I32 = jnp.float32, jnp.bfloat16, jnp.int32
 EXACT = lax.Precision.HIGHEST
 EVERY = ("dp", "group")
-DOWN = range(N_Z - 1, -1, -1)
+DOWN = range(7, -1, -1)
 
 
 def device(z, y, c, x):
@@ -27,13 +27,13 @@
 
 def along(z_core):
     z_lines = [[device(z, y, z_core, x) for z in DOWN] for y in range(N_Y) for x in range(GROUP)]
-    y_lines = [[device(z, y, 1 - z_core, x) for y in range(N_Y)] for z in range(N_Z) for x in range(GROUP)]
+    y_lines = [[device(z, y, 1 - z_core, x) for y in DOWN] for z in range(N_Z) for x in range(GROUP)]
     return z_lines + y_lines
 
 
 def planes():
-    first = [[device(z, y, 0, x) for z in DOWN for y in range(N_Y)] for x in range(GROUP)]
-    second = [[device(z, y, 1, x) for y in range(N_Y) for z in DOWN] for x in range(GROUP)]
+    first = [[device(z, y, 0, x) for z in DOWN for y in DOWN] for x in range(GROUP)]
+    second = [[device(z, y, 1, x) for y in DOWN for z in DOWN] for x in range(GROUP)]
     return first + second
 
 
@@ -95,7 +95,7 @@
 def position():
     holder = lax.axis_index("dp")
     spot, core = holder // N_C, holder % N_C
-    z, y = N_Z - 1 - spot // N_Y, spot % N_Y
+    z, y = N_Z - 1 - spot // N_Y, N_Y - 1 - spot % N_Y
     source = jnp.where(core == 0, z * N_Y + y, y * N_Z + z)
     return spot, core, source
 
@@ -293,10 +293,11 @@
         out[QD:] = (own_grad[rows] + moved[rows].astype(F32)).astype(out.dtype)
 
 
-def add_blocks(arrived, first, second, out):
+def add_blocks(arrived, first, second, out, blocks, sems):
     del first, second
-    for part in range(N_Y):
-        out[part] = jnp.sum(arrived[:, part].astype(F32), axis=0).astype(BF16)
+    for part, copy in enumerate(fetch([(arrived.at[:, part], blocks.at[:, part]) for part in range(N_Y)], sems)):
+        copy.wait()
+        out[part] = jnp.sum(blocks[:, part].astype(F32), axis=0).astype(BF16)
 
 
 def collect(weight_inv, query_part, arrived, out):
@@ -392,7 +393,11 @@
         for ahead, part in ((2, off2), (1, off1), (3, off3))
     ]
     arrived = call(
-        add_blocks, struct((N_Y, QROWS, D), BF16), [vmem(), anywhere(), anywhere()], vmem()
+        add_blocks,
+        struct((N_Y, QROWS, D), BF16),
+        [hbm(), anywhere(), anywhere()],
+        vmem(),
+        [pltpu.VMEM((N_Z, N_Y, QROWS, D), BF16), pltpu.SemaphoreType.DMA((N_Y,))],
     )(arrived, moved[0], moved[1])
     arrived = exchange(arrived, along(1))
     query_grad = call(

time: 138 us -> 138 us (level)
  starting transfers between devices: 47.5 us -> 52.5 us
  waiting for transfers between devices: 29.8 us -> 27 us
  blocking collectives: 29.8 us -> 27.6 us
    all_to_all x4, starting transfers between devices: 33.7 us -> 38.6 us  [exchange(): lax.all_to_all(blocks, EVERY, split_axis=0, concat_axis=0, axis_index_gro...]
    all_to_all x1, blocking collectives: 17.6 us -> 15.3 us  [exchange(): lax.all_to_all(blocks, EVERY, split_axis=0, concat_axis=0, axis_index_gro...]
    all_to_all x4, waiting for transfers between devices: 17.4 us -> 15.3 us  [exchange(): lax.all_to_all(blocks, EVERY, split_axis=0, concat_axis=0, axis_index_gro...]
where the time goes in v13:
time: 138 us; the launch traced here: 137 us
  starting transfers between devices  52.5 us (38%)
  blocking collectives  27.6 us (20%)
  waiting for transfers between devices  27 us (20%)
  Pallas kernels  20.6 us (15%)
  local copies, waits for them, and re-layouts  7.5 us (5%)
    all_to_all x4, starting transfers between devices, exchange(): lax.all_to_all(blocks, EVERY, split_axis=0, concat_axis=0, axis_index_gro...  38.6 us
    all_to_all x1, blocking collectives, exchange(): lax.all_to_all(blocks, EVERY, split_axis=0, concat_axis=0, axis_index_gro...  15.3 us
    all_to_all x4, waiting for transfers between devices, exchange(): lax.all_to_all(blocks, EVERY, split_axis=0, concat_axis=0, axis_index_gro...  15.3 us
    all_gather x1, blocking collectives, per_device(): gathered = lax.all_gather(positives, 'group', axis=0, tiled=True)  12.3 us
    ppermute x3, waiting for transfers between devices, per_device(): lax.ppermute(part, 'group', [(g, (g + ahead) % GROUP) for g in range(GROU...  11.1 us
    ppermute x3, starting transfers between devices, per_device(): lax.ppermute(part, 'group', [(g, (g + ahead) % GROUP) for g in range(GROU...  10 us
    pallas_call x1, Pallas kernels, per_device(): call(terms, (struct((SPOTS, PT, QROWS), BF16), struct((SPOTS, QROWS, D),...  5.12 us
    pallas_call x1, Pallas kernels, per_device(): call(weigh, (struct((ROWS, PT, D), F32), struct((ROWS, PT, D), BF16), str...  4.46 us
  transfers between devices with their start and end apart: 9, of which 7 were waited for; matrix products, arithmetic and copies ran while one was open for 1% of the time, Pallas kernels for 9%

profile of v13, /device:TPU:6, one launch (start us, length us, event | category | flops | bytes accessed | tf_op | source)
XLA Modules:
  0.0 136.7 jit_solution(14967131293889806154)
XLA Ops:
  0.6 0.7 pad_add_fusion.table_in
  1.4 0.0 copy-start.7
  1.4 0.8 copy-done.7
  2.1 1.5 %shard_map.84 = (bf16[8,136,128]{2,1,0:T(8,128)(2,1)S(1)}, bf16[4,32,128]{2,1,0:T(8,128)(2,1)S(1)}) custom-call(s32[40,128]{1,0:T(8,128)S(1)} %pad_add_fusion.table_in, bf16[4,32,128]{2,1,0:T(8,128)(2,1)S(1)} %copy-done.7), custom_call_target="tpu_custom_call" | custom-call | tf_op jit(solution)/shard_map/pallas_call | solution.py:317
  3.7 15.3 %all_to_all.25 = bf16[8,136,128]{2,1,0:T(8,128)(2,1)S(1)} all-to-all(bf16[8,136,128]{2,1,0:T(8,128)(2,1)S(1)} %get-tuple-element.24), channel_id=1, replica_groups={{452,388,324,260,196,132,68,4},{453,389,325,261,197,133,69,5},{454,390,..., dimensions={0} | all-to-all | bytes 557056 | tf_op jit(solution)/shard_map/all_to_all | solution.py:41
  19.0 1.7 %broadcast_in_dim.2 = bf16[8,8,136,128]{3,2,1,0:T(8,128)(2,1)} broadcast(bf16[8,136,128]{2,1,0:T(8,128)(2,1)S(1)} %all_to_all.25), dimensions={1,2,3} | broadcast | bytes 2506752 | tf_op jit(solution)/shard_map/broadcast_in_dim | solution.py:330
  20.7 0.0 copy-start.3
  20.7 0.0 copy-start.8
  20.7 12.7 %all-to-all-start.1 = ((bf16[8,8,136,128]{3,2,1,0:T(8,128)(2,1)}), bf16[8,8,136,128]{3,2,1,0:T(8,128)(2,1)S(1)}, u32[]{:S(2)}, u32[]{:S(2)}) async-start(bf16[8,8,136,128]{3,2,1,0:T(8,128)(2,1)} %broadcast_in_dim.2), calls=%async_computation.1 | async-start | bytes 4456448 | tf_op jit(solution)/shard_map/all_to_all | solution.py:41
  33.4 0.0 copy-done.3
  33.4 0.4 shard_map.85.own_rows
  33.8 1.9 %collective-permute-start = (bf16[32,64,128]{2,1,0:T(8,128)(2,1)S(1)}, bf16[32,64,128]{2,1,0:T(8,128)(2,1)S(1)}, u32[]{:S(2)}, u32[]{:S(2)}) collective-permute-start(bf16[32,64,128]{2,1,0:T(8,128)(2,1)S(1)} %shard_map.85.own_rows), channel_id=1, source_target_pairs={{0,4},{4,0},{8,12},{12,8},{16,20},{20,16},{24,28},{28,24},{32,36},... | collective-permute-start | bytes 1572872 | tf_op jit(solution)/shard_map/ppermute | solution.py:333
  35.7 0.0 copy-done.8
  35.7 12.3 %all_gather.3.positives = bf16[16,64,128]{2,1,0:T(8,128)(2,1)S(1)} all-gather(bf16[4,64,128]{2,1,0:T(8,128)(2,1)S(1)} %copy-done.8), channel_id=1, replica_groups=mesh['dp'=128,'group'=4] {'group'}, dimensions={0}, use_global_device_ids=true | all-gather | bytes 327680 | tf_op jit(solution)/shard_map/all_gather | solution.py:334
  47.9 0.6 shard_map.86
  48.6 0.0 copy-start.4
  48.6 0.7 copy-done.4
  49.3 0.0 collective-permute-done.other_rows
  49.3 10.4 %all-to-all-done.1 = bf16[8,8,136,128]{3,2,1,0:T(8,128)(2,1)S(1)} async-done(((bf16[8,8,136,128]{3,2,1,0:T(8,128)(2,1)}), bf16[8,8,136,128]{3,2,1,0:T(8,128)(2,1)S(1)}, u32[]{:S(2)}, u32[]{:S(2)}) %all-to-all-start.1) | async-done | bytes 2228256 | tf_op jit(solution)/shard_map/all_to_all | solution.py:41
  59.7 3.6 %shard_map.87 = (f32[64,128]{1,0:T(8,128)S(1)}, f32[64,4,128]{2,1,0:T(4,128)S(1)}, s32[8,512]{1,0:T(8,128)S(1)}) custom-call(bf16[64,136,128]{2,1,0:T(8,128)(2,1)S(1)} %bitcast.3, bf16[32,64,128]{2,1,0:T(8,128)(2,1)S(1)} %shard_map.85.own_rows, bf16[32,64,128]{2,1,0:T(8,128)(2,1)S(1)} %collective-permute-done.other_rows, ...), custom_call_target="tpu_custom_call" | custom-call | tf_op jit(solution)/shard_map/pallas_call | solution.py:339
  63.2 0.0 copy-start.6
  63.2 0.6 copy-done.6
  63.9 12.0 %all-to-all-start.2 = ((f32[64,4,128]{2,1,0:T(4,128)}), f32[64,4,128]{2,1,0:T(4,128)S(1)}, u32[]{:S(2)}, u32[]{:S(2)}) async-start(f32[64,4,128]{2,1,0:T(4,128)} %copy-done.6), calls=%async_computation.2 | async-start | bytes 262144 | tf_op jit(solution)/shard_map/all_to_all | solution.py:41
  75.9 5.1 %shard_map.88 = (bf16[64,64,128]{2,1,0:T(8,128)(2,1)S(1)}, bf16[64,128,128]{2,1,0:T(8,128)(2,1)S(1)}) custom-call(s32[8,512]{1,0:T(8,128)S(1)} %get-tuple-element.27.codes, bf16[64,136,128]{2,1,0:T(8,128)(2,1)S(1)} %bitcast.4, bf16[32,64,128]{2,1,0:T(8,128)(2,1)S(1)} %shard_map.85.own_rows, bf16[32,64,128]{2,1,0:T(8,128)(2,1)S(1)} %collective-permute-done.other_rows, ...), custom_call_target="tpu_custom_call" | custom-call | tf_op jit(solution)/shard_map/pallas_call | solution.py:357
  81.1 0.0 copy-start
  81.1 1.3 copy-done
  82.4 0.0 copy-start.1
  82.4 1.0 copy-done.1
  83.4 0.5 all-to-all-done.2.sums
  83.9 0.0 copy-start.2
  83.9 6.7 %all-to-all-start.3 = ((bf16[8,8,128,128]{3,2,1,0:T(8,128)(2,1)}), bf16[8,8,128,128]{3,2,1,0:T(8,128)(2,1)}, u32[]{:S(2)}, u32[]{:S(2)}) async-start(bf16[8,8,128,128]{3,2,1,0:T(8,128)(2,1)} %bitcast.6), calls=%async_computation.3 | async-start | bytes 4194304 | tf_op jit(solution)/shard_map/all_to_all | solution.py:41
  90.6 0.0 copy-start.5
  90.6 0.0 copy-done.2
  90.6 4.5 %shard_map.89 = (f32[32,64,128]{2,1,0:T(8,128)S(1)}, bf16[32,64,128]{2,1,0:T(8,128)(2,1)S(1)}, f32[1,128]{1,0:T(1,128)S(1)}, f32[8,128]{1,0:T(8,128)S(1)}) custom-call(s32[8,512]{1,0:T(8,128)S(1)} %get-tuple-element.27.codes, f32[64,4,128]{2,1,0:T(4,128)S(1)} %all-to-all-done.2.sums, bf16[64,136,128]{2,1,0:T(8,128)(2,1)S(1)} %bitcast.5, ...), custom_call_target="tpu_custom_call" | custom-call | tf_op jit(solution)/shard_map/pallas_call | solution.py:365
  95.1 1.9 %collective-permute-start.1 = (bf16[32,64,128]{2,1,0:T(8,128)(2,1)S(1)}, bf16[32,64,128]{2,1,0:T(8,128)(2,1)S(1)}, u32[]{:S(2)}, u32[]{:S(2)}) collective-permute-start(bf16[32,64,128]{2,1,0:T(8,128)(2,1)S(1)} %get-tuple-element.38), channel_id=1, source_target_pairs={{0,4},{4,0},{8,12},{12,8},{16,20},{20,16},{24,28},{28,24},{32,36},... | collective-permute-start | bytes 1572872 | tf_op jit(solution)/shard_map/ppermute | solution.py:390
  97.0 0.0 copy-done.5
  97.0 1.3 shard_map.90
  98.3 0.6 collective-permute-done.1.moved
  98.9 0.1 shard_map.91
  99.0 3.3 %collective-permute-start.2 = (bf16[12,64,128]{2,1,0:T(8,128)(2,1)S(1)}, bf16[12,64,128]{2,1,0:T(8,128)(2,1)S(1)}, u32[]{:S(2)}, u32[]{:S(2)}) collective-permute-start(bf16[12,64,128]{2,1,0:T(8,128)(2,1)S(1)} %get-tuple-element.40), channel_id=1, source_target_pairs={{0,2},{1,3},{2,0},{3,1},{4,6},{5,7},{6,4},{7,5},{8,10},{9,11},{10,... | collective-permute-start | bytes 589832 | tf_op jit(solution)/shard_map/ppermute | solution.py:392
  102.3 4.0 %collective-permute-start.3 = (bf16[12,64,128]{2,1,0:T(8,128)(2,1)S(1)}, bf16[12,64,128]{2,1,0:T(8,128)(2,1)S(1)}, u32[]{:S(2)}, u32[]{:S(2)}) collective-permute-start(bf16[12,64,128]{2,1,0:T(8,128)(2,1)S(1)} %get-tuple-element.41), channel_id=1, source_target_pairs={{0,1},{1,2},{2,3},{3,0},{4,5},{5,6},{6,7},{7,4},{8,9},{9,10},{10,1... | collective-permute-start | bytes 589832 | tf_op jit(solution)/shard_map/ppermute | solution.py:392
  106.3 3.0 %collective-permute-done.2.first = bf16[12,64,128]{2,1,0:T(8,128)(2,1)S(1)} collective-permute-done((bf16[12,64,128]{2,1,0:T(8,128)(2,1)S(1)}, bf16[12,64,128]{2,1,0:T(8,128)(2,1)S(1)}, u32[]{:S(2)}, u32[]{:S(2)}) %collective-permute-start.2) | collective-permute-done | bytes 196640 | tf_op jit(solution)/shard_map/ppermute | solution.py:392
  109.3 2.0 %collective-permute-done.3.second = bf16[12,64,128]{2,1,0:T(8,128)(2,1)S(1)} collective-permute-done((bf16[12,64,128]{2,1,0:T(8,128)(2,1)S(1)}, bf16[12,64,128]{2,1,0:T(8,128)(2,1)S(1)}, u32[]{:S(2)}, u32[]{:S(2)}) %collective-permute-start.3) | collective-permute-done | bytes 196640 | tf_op jit(solution)/shard_map/ppermute | solution.py:392
  111.3 4.4 %all-to-all-done.3.arrived = bf16[8,8,128,128]{3,2,1,0:T(8,128)(2,1)} async-done(((bf16[8,8,128,128]{3,2,1,0:T(8,128)(2,1)}), bf16[8,8,128,128]{3,2,1,0:T(8,128)(2,1)}, u32[]{:S(2)}, u32[]{:S(2)}) %all-to-all-start.3) | async-done | bytes 2097184 | tf_op jit(solution)/shard_map/all_to_all | solution.py:41
  115.7 2.3 %shard_map.92 = bf16[8,128,128]{2,1,0:T(8,128)(2,1)} custom-call(bf16[8,8,128,128]{3,2,1,0:T(8,128)(2,1)} %all-to-all-done.3.arrived, bf16[12,64,128]{2,1,0:T(8,128)(2,1)S(1)} %collective-permute-done.2.first, bf16[12,64,128]{2,1,0:T(8,128)(2,1)S(1)} %collective-permute-done.3.second), custom_call_target="tpu_custom_call" | custom-call | tf_op jit(solution)/shard_map/pallas_call | solution.py:395
  118.1 7.2 %all-to-all-start.4 = ((bf16[8,128,128]{2,1,0:T(8,128)(2,1)}), bf16[8,128,128]{2,1,0:T(8,128)(2,1)S(1)}, u32[]{:S(2)}, u32[]{:S(2)}) async-start(bf16[8,128,128]{2,1,0:T(8,128)(2,1)} %shard_map.92), calls=%async_computation.4 | async-start | bytes 524288 | tf_op jit(solution)/shard_map/all_to_all | solution.py:41
  125.2 2.7 %collective-permute-start.4 = (bf16[12,64,128]{2,1,0:T(8,128)(2,1)S(1)}, bf16[12,64,128]{2,1,0:T(8,128)(2,1)S(1)}, u32[]{:S(2)}, u32[]{:S(2)}) collective-permute-start(bf16[12,64,128]{2,1,0:T(8,128)(2,1)S(1)} %get-tuple-element.43), channel_id=1, source_target_pairs={{0,3},{1,0},{2,1},{3,2},{4,7},{5,4},{6,5},{7,6},{8,11},{9,8},{10,9... | collective-permute-start | bytes 589832 | tf_op jit(solution)/shard_map/ppermute | solution.py:392
  127.9 6.0 %collective-permute-done.4 = bf16[12,64,128]{2,1,0:T(8,128)(2,1)S(1)} collective-permute-done((bf16[12,64,128]{2,1,0:T(8,128)(2,1)S(1)}, bf16[12,64,128]{2,1,0:T(8,128)(2,1)S(1)}, u32[]{:S(2)}, u32[]{:S(2)}) %collective-permute-start.4) | collective-permute-done | bytes 196640 | tf_op jit(solution)/shard_map/ppermute | solution.py:392
  134.0 0.1 convert_add_fusion
  134.1 0.7 slice.8
  134.7 0.7 slice.9
  135.4 0.0 all-to-all-done.4.arrived
  135.5 1.3 shard_map.93
Async XLA Ops:
  1.4 0.8 copy-start.7
  20.7 12.7 %copy-start.3 = (bf16[32,64,128]{2,1,0:T(8,128)(2,1)S(1)}, bf16[32,64,128]{2,1,0:T(8,128)(2,1)}, u32[]{:S(2)}) copy-start(bf16[32,64,128]{2,1,0:T(8,128)(2,1)} %values.1) | copy-start | bytes 1572868
  20.7 15.0 %copy-start.8 = (bf16[4,64,128]{2,1,0:T(8,128)(2,1)S(1)}, bf16[4,64,128]{2,1,0:T(8,128)(2,1)}, u32[]{:S(2)}) copy-start(bf16[4,64,128]{2,1,0:T(8,128)(2,1)} %param.6) | copy-start | bytes 196612
  20.7 39.0 %all-to-all-start.1 = ((bf16[8,8,136,128]{3,2,1,0:T(8,128)(2,1)}), bf16[8,8,136,128]{3,2,1,0:T(8,128)(2,1)S(1)}, u32[]{:S(2)}, u32[]{:S(2)}) async-start(bf16[8,8,136,128]{3,2,1,0:T(8,128)(2,1)} %broadcast_in_dim.2), calls=%async_computation.1 | async-start | bytes 4456448 | tf_op jit(solution)/shard_map/all_to_all | solution.py:41
  33.8 15.5 %collective-permute-start = (bf16[32,64,128]{2,1,0:T(8,128)(2,1)S(1)}, bf16[32,64,128]{2,1,0:T(8,128)(2,1)S(1)}, u32[]{:S(2)}, u32[]{:S(2)}) collective-permute-start(bf16[32,64,128]{2,1,0:T(8,128)(2,1)S(1)} %shard_map.85.own_rows), channel_id=1, source_target_pairs={{0,4},{4,0},{8,12},{12,8},{16,20},{20,16},{24,28},{28,24},{32,36},... | collective-permute-start | bytes 1572872 | tf_op jit(solution)/shard_map/ppermute | solution.py:333
  48.6 0.7 copy-start.4
  63.2 0.7 copy-start.6
  63.9 20.0 %all-to-all-start.2 = ((f32[64,4,128]{2,1,0:T(4,128)}), f32[64,4,128]{2,1,0:T(4,128)S(1)}, u32[]{:S(2)}, u32[]{:S(2)}) async-start(f32[64,4,128]{2,1,0:T(4,128)} %copy-done.6), calls=%async_computation.2 | async-start | bytes 262144 | tf_op jit(solution)/shard_map/all_to_all | solution.py:41
  81.1 1.3 copy-start
  82.4 1.0 copy-start.1
  83.9 6.7 %copy-start.2 = (bf16[64,64,128]{2,1,0:T(8,128)(2,1)S(1)}, bf16[64,64,128]{2,1,0:T(8,128)(2,1)}, u32[]{:S(2)}) copy-start(bf16[64,64,128]{2,1,0:T(8,128)(2,1)} %copy-done.1) | copy-start | bytes 3145732
  83.9 31.8 %all-to-all-start.3 = ((bf16[8,8,128,128]{3,2,1,0:T(8,128)(2,1)}), bf16[8,8,128,128]{3,2,1,0:T(8,128)(2,1)}, u32[]{:S(2)}, u32[]{:S(2)}) async-start(bf16[8,8,128,128]{3,2,1,0:T(8,128)(2,1)} %bitcast.6), calls=%async_computation.3 | async-start | bytes 4194304 | tf_op jit(solution)/shard_map/all_to_all | solution.py:41
  90.6 6.4 %copy-start.5 = (bf16[16,64,128]{2,1,0:T(8,128)(2,1)S(1)}, bf16[16,64,128]{2,1,0:T(8,128)(2,1)}, u32[]{:S(2)}) copy-start(bf16[16,64,128]{2,1,0:T(8,128)(2,1)} %copy-done.4) | copy-start | bytes 786436
  95.1 3.8 %collective-permute-start.1 = (bf16[32,64,128]{2,1,0:T(8,128)(2,1)S(1)}, bf16[32,64,128]{2,1,0:T(8,128)(2,1)S(1)}, u32[]{:S(2)}, u32[]{:S(2)}) collective-permute-start(bf16[32,64,128]{2,1,0:T(8,128)(2,1)S(1)} %get-tuple-element.38), channel_id=1, source_target_pairs={{0,4},{4,0},{8,12},{12,8},{16,20},{20,16},{24,28},{28,24},{32,36},... | collective-permute-start | bytes 1572872 | tf_op jit(solution)/shard_map/ppermute | solution.py:390
  99.0 10.3 %collective-permute-start.2 = (bf16[12,64,128]{2,1,0:T(8,128)(2,1)S(1)}, bf16[12,64,128]{2,1,0:T(8,128)(2,1)S(1)}, u32[]{:S(2)}, u32[]{:S(2)}) collective-permute-start(bf16[12,64,128]{2,1,0:T(8,128)(2,1)S(1)} %get-tuple-element.40), channel_id=1, source_target_pairs={{0,2},{1,3},{2,0},{3,1},{4,6},{5,7},{6,4},{7,5},{8,10},{9,11},{10,... | collective-permute-start | bytes 589832 | tf_op jit(solution)/shard_map/ppermute | solution.py:392
  102.3 9.0 %collective-permute-start.3 = (bf16[12,64,128]{2,1,0:T(8,128)(2,1)S(1)}, bf16[12,64,128]{2,1,0:T(8,128)(2,1)S(1)}, u32[]{:S(2)}, u32[]{:S(2)}) collective-permute-start(bf16[12,64,128]{2,1,0:T(8,128)(2,1)S(1)} %get-tuple-element.41), channel_id=1, source_target_pairs={{0,1},{1,2},{2,3},{3,0},{4,5},{5,6},{6,7},{7,4},{8,9},{9,10},{10,1... | collective-permute-start | bytes 589832 | tf_op jit(solution)/shard_map/ppermute | solution.py:392
  118.1 17.4 %all-to-all-start.4 = ((bf16[8,128,128]{2,1,0:T(8,128)(2,1)}), bf16[8,128,128]{2,1,0:T(8,128)(2,1)S(1)}, u32[]{:S(2)}, u32[]{:S(2)}) async-start(bf16[8,128,128]{2,1,0:T(8,128)(2,1)} %shard_map.92), calls=%async_computation.4 | async-start | bytes 524288 | tf_op jit(solution)/shard_map/all_to_all | solution.py:41
  125.2 8.8 %collective-permute-start.4 = (bf16[12,64,128]{2,1,0:T(8,128)(2,1)S(1)}, bf16[12,64,128]{2,1,0:T(8,128)(2,1)S(1)}, u32[]{:S(2)}, u32[]{:S(2)}) collective-permute-start(bf16[12,64,128]{2,1,0:T(8,128)(2,1)S(1)} %get-tuple-element.43), channel_id=1, source_target_pairs={{0,3},{1,0},{2,1},{3,2},{4,7},{5,4},{6,5},{7,6},{8,11},{9,8},{10,9... | collective-permute-start | bytes 589832 | tf_op jit(solution)/shard_map/ppermute | solution.py:392

commit v14 on v13

--- a/solution.py
+++ b/solution.py
@@ -293,8 +293,8 @@
         out[QD:] = (own_grad[rows] + moved[rows].astype(F32)).astype(out.dtype)
 
 
-def add_blocks(arrived, first, second, out, blocks, sems):
-    del first, second
+def add_blocks(arrived, first, second, third, out, blocks, sems):
+    del first, second, third
     for part, copy in enumerate(fetch([(arrived.at[:, part], blocks.at[:, part]) for part in range(N_Y)], sems)):
         copy.wait()
         out[part] = jnp.sum(blocks[:, part].astype(F32), axis=0).astype(BF16)
@@ -395,10 +395,10 @@
     arrived = call(
         add_blocks,
         struct((N_Y, QROWS, D), BF16),
-        [hbm(), anywhere(), anywhere()],
+        [hbm()] + [anywhere()] * 3,
         vmem(),
         [pltpu.VMEM((N_Z, N_Y, QROWS, D), BF16), pltpu.SemaphoreType.DMA((N_Y,))],
-    )(arrived, moved[0], moved[1])
+    )(arrived, *moved)
     arrived = exchange(arrived, along(1))
     query_grad = call(
         collect, struct((QD, QT, D), F32), [smem(), vmem(), vmem()], vmem()

time: 138 us -> 135 us (0.978)
  waiting for transfers between devices: 27 us -> 24 us
    ppermute x3, waiting for transfers between devices: 11.1 us -> 7.56 us  [per_device(): lax.ppermute(part, 'group', [(g, (g + ahead) % GROUP) for g in range(GROU...]
where the time goes in v14:
time: 135 us; the launch traced here: 133 us
  starting transfers between devices  51.7 us (38%)
  blocking collectives  27.6 us (20%)
  waiting for transfers between devices  24 us (18%)
  Pallas kernels  20.6 us (15%)
  local copies, waits for them, and re-layouts  7.5 us (6%)
    all_to_all x4, starting transfers between devices, exchange(): lax.all_to_all(blocks, EVERY, split_axis=0, concat_axis=0, axis_index_gro...  38.6 us
    all_to_all x4, waiting for transfers between devices, exchange(): lax.all_to_all(blocks, EVERY, split_axis=0, concat_axis=0, axis_index_gro...  15.8 us
    all_to_all x1, blocking collectives, exchange(): lax.all_to_all(blocks, EVERY, split_axis=0, concat_axis=0, axis_index_gro...  15.3 us
    all_gather x1, blocking collectives, per_device(): gathered = lax.all_gather(positives, 'group', axis=0, tiled=True)  12.3 us
    ppermute x3, starting transfers between devices, per_device(): lax.ppermute(part, 'group', [(g, (g + ahead) % GROUP) for g in range(GROU...  9.24 us
    ppermute x3, waiting for transfers between devices, per_device(): lax.ppermute(part, 'group', [(g, (g + ahead) % GROUP) for g in range(GROU...  7.56 us
    pallas_call x1, Pallas kernels, per_device(): call(terms, (struct((SPOTS, PT, QROWS), BF16), struct((SPOTS, QROWS, D),...  5.13 us
    pallas_call x1, Pallas kernels, per_device(): call(weigh, (struct((ROWS, PT, D), F32), struct((ROWS, PT, D), BF16), str...  4.5 us
  transfers between devices with their start and end apart: 9, of which 7 were waited for; matrix products, arithmetic and copies ran while one was open for 1% of the time, Pallas kernels for 9%

profile of v14, /device:TPU:6, one launch (start us, length us, event | category | flops | bytes accessed | tf_op | source)
XLA Modules:
  0.0 133.0 jit_solution(16555103415014842662)
XLA Ops:
  0.6 0.7 pad_add_fusion.table_in
  1.4 0.0 copy-start.7
  1.4 0.8 copy-done.7
  2.1 1.5 %shard_map.84 = (bf16[8,136,128]{2,1,0:T(8,128)(2,1)S(1)}, bf16[4,32,128]{2,1,0:T(8,128)(2,1)S(1)}) custom-call(s32[40,128]{1,0:T(8,128)S(1)} %pad_add_fusion.table_in, bf16[4,32,128]{2,1,0:T(8,128)(2,1)S(1)} %copy-done.7), custom_call_target="tpu_custom_call" | custom-call | tf_op jit(solution)/shard_map/pallas_call | solution.py:317
  3.7 15.3 %all_to_all.25 = bf16[8,136,128]{2,1,0:T(8,128)(2,1)S(1)} all-to-all(bf16[8,136,128]{2,1,0:T(8,128)(2,1)S(1)} %get-tuple-element.24), channel_id=1, replica_groups={{452,388,324,260,196,132,68,4},{453,389,325,261,197,133,69,5},{454,390,..., dimensions={0} | all-to-all | bytes 557056 | tf_op jit(solution)/shard_map/all_to_all | solution.py:41
  19.0 1.7 %broadcast_in_dim.2 = bf16[8,8,136,128]{3,2,1,0:T(8,128)(2,1)} broadcast(bf16[8,136,128]{2,1,0:T(8,128)(2,1)S(1)} %all_to_all.25), dimensions={1,2,3} | broadcast | bytes 2506752 | tf_op jit(solution)/shard_map/broadcast_in_dim | solution.py:330
  20.7 0.0 copy-start.3
  20.7 0.0 copy-start.8
  20.7 12.7 %all-to-all-start.1 = ((bf16[8,8,136,128]{3,2,1,0:T(8,128)(2,1)}), bf16[8,8,136,128]{3,2,1,0:T(8,128)(2,1)S(1)}, u32[]{:S(2)}, u32[]{:S(2)}) async-start(bf16[8,8,136,128]{3,2,1,0:T(8,128)(2,1)} %broadcast_in_dim.2), calls=%async_computation.1 | async-start | bytes 4456448 | tf_op jit(solution)/shard_map/all_to_all | solution.py:41
  33.4 0.0 copy-done.3
  33.4 0.4 shard_map.85.own_rows
  33.8 1.9 %collective-permute-start = (bf16[32,64,128]{2,1,0:T(8,128)(2,1)S(1)}, bf16[32,64,128]{2,1,0:T(8,128)(2,1)S(1)}, u32[]{:S(2)}, u32[]{:S(2)}) collective-permute-start(bf16[32,64,128]{2,1,0:T(8,128)(2,1)S(1)} %shard_map.85.own_rows), channel_id=1, source_target_pairs={{0,4},{4,0},{8,12},{12,8},{16,20},{20,16},{24,28},{28,24},{32,36},... | collective-permute-start | bytes 1572872 | tf_op jit(solution)/shard_map/ppermute | solution.py:333
  35.7 0.0 copy-done.8
  35.7 12.3 %all_gather.3.positives = bf16[16,64,128]{2,1,0:T(8,128)(2,1)S(1)} all-gather(bf16[4,64,128]{2,1,0:T(8,128)(2,1)S(1)} %copy-done.8), channel_id=1, replica_groups=mesh['dp'=128,'group'=4] {'group'}, dimensions={0}, use_global_device_ids=true | all-gather | bytes 327680 | tf_op jit(solution)/shard_map/all_gather | solution.py:334
  47.9 0.6 shard_map.86
  48.6 0.0 copy-start.4
  48.6 0.7 copy-done.4
  49.3 0.0 collective-permute-done.other_rows
  49.3 10.4 %all-to-all-done.1 = bf16[8,8,136,128]{3,2,1,0:T(8,128)(2,1)S(1)} async-done(((bf16[8,8,136,128]{3,2,1,0:T(8,128)(2,1)}), bf16[8,8,136,128]{3,2,1,0:T(8,128)(2,1)S(1)}, u32[]{:S(2)}, u32[]{:S(2)}) %all-to-all-start.1) | async-done | bytes 2228256 | tf_op jit(solution)/shard_map/all_to_all | solution.py:41
  59.7 3.6 %shard_map.87 = (f32[64,128]{1,0:T(8,128)S(1)}, f32[64,4,128]{2,1,0:T(4,128)S(1)}, s32[8,512]{1,0:T(8,128)S(1)}) custom-call(bf16[64,136,128]{2,1,0:T(8,128)(2,1)S(1)} %bitcast.3, bf16[32,64,128]{2,1,0:T(8,128)(2,1)S(1)} %shard_map.85.own_rows, bf16[32,64,128]{2,1,0:T(8,128)(2,1)S(1)} %collective-permute-done.other_rows, ...), custom_call_target="tpu_custom_call" | custom-call | tf_op jit(solution)/shard_map/pallas_call | solution.py:339
  63.2 0.0 copy-start.6
  63.2 0.6 copy-done.6
  63.9 12.0 %all-to-all-start.2 = ((f32[64,4,128]{2,1,0:T(4,128)}), f32[64,4,128]{2,1,0:T(4,128)S(1)}, u32[]{:S(2)}, u32[]{:S(2)}) async-start(f32[64,4,128]{2,1,0:T(4,128)} %copy-done.6), calls=%async_computation.2 | async-start | bytes 262144 | tf_op jit(solution)/shard_map/all_to_all | solution.py:41
  75.9 5.1 %shard_map.88 = (bf16[64,64,128]{2,1,0:T(8,128)(2,1)S(1)}, bf16[64,128,128]{2,1,0:T(8,128)(2,1)S(1)}) custom-call(s32[8,512]{1,0:T(8,128)S(1)} %get-tuple-element.27.codes, bf16[64,136,128]{2,1,0:T(8,128)(2,1)S(1)} %bitcast.4, bf16[32,64,128]{2,1,0:T(8,128)(2,1)S(1)} %shard_map.85.own_rows, bf16[32,64,128]{2,1,0:T(8,128)(2,1)S(1)} %collective-permute-done.other_rows, ...), custom_call_target="tpu_custom_call" | custom-call | tf_op jit(solution)/shard_map/pallas_call | solution.py:357
  81.1 0.0 copy-start
  81.1 1.3 copy-done
  82.4 0.0 copy-start.1
  82.4 1.0 copy-done.1
  83.4 0.5 all-to-all-done.2.sums
  83.9 0.0 copy-start.2
  83.9 6.7 %all-to-all-start.3 = ((bf16[8,8,128,128]{3,2,1,0:T(8,128)(2,1)}), bf16[8,8,128,128]{3,2,1,0:T(8,128)(2,1)}, u32[]{:S(2)}, u32[]{:S(2)}) async-start(bf16[8,8,128,128]{3,2,1,0:T(8,128)(2,1)} %bitcast.6), calls=%async_computation.3 | async-start | bytes 4194304 | tf_op jit(solution)/shard_map/all_to_all | solution.py:41
  90.6 0.0 copy-start.5
  90.6 0.0 copy-done.2
  90.6 4.5 %shard_map.89 = (f32[32,64,128]{2,1,0:T(8,128)S(1)}, bf16[32,64,128]{2,1,0:T(8,128)(2,1)S(1)}, f32[1,128]{1,0:T(1,128)S(1)}, f32[8,128]{1,0:T(8,128)S(1)}) custom-call(s32[8,512]{1,0:T(8,128)S(1)} %get-tuple-element.27.codes, f32[64,4,128]{2,1,0:T(4,128)S(1)} %all-to-all-done.2.sums, bf16[64,136,128]{2,1,0:T(8,128)(2,1)S(1)} %bitcast.5, ...), custom_call_target="tpu_custom_call" | custom-call | tf_op jit(solution)/shard_map/pallas_call | solution.py:365
  95.1 1.9 %collective-permute-start.1 = (bf16[32,64,128]{2,1,0:T(8,128)(2,1)S(1)}, bf16[32,64,128]{2,1,0:T(8,128)(2,1)S(1)}, u32[]{:S(2)}, u32[]{:S(2)}) collective-permute-start(bf16[32,64,128]{2,1,0:T(8,128)(2,1)S(1)} %get-tuple-element.38), channel_id=1, source_target_pairs={{0,4},{4,0},{8,12},{12,8},{16,20},{20,16},{24,28},{28,24},{32,36},... | collective-permute-start | bytes 1572872 | tf_op jit(solution)/shard_map/ppermute | solution.py:390
  97.0 0.0 copy-done.5
  97.0 1.3 shard_map.90
  98.3 0.6 collective-permute-done.1.moved
  98.9 0.1 shard_map.91
  99.0 3.3 %collective-permute-start.2 = (bf16[12,64,128]{2,1,0:T(8,128)(2,1)S(1)}, bf16[12,64,128]{2,1,0:T(8,128)(2,1)S(1)}, u32[]{:S(2)}, u32[]{:S(2)}) collective-permute-start(bf16[12,64,128]{2,1,0:T(8,128)(2,1)S(1)} %get-tuple-element.40), channel_id=1, source_target_pairs={{0,2},{1,3},{2,0},{3,1},{4,6},{5,7},{6,4},{7,5},{8,10},{9,11},{10,... | collective-permute-start | bytes 589832 | tf_op jit(solution)/shard_map/ppermute | solution.py:392
  102.3 4.0 %collective-permute-start.3 = (bf16[12,64,128]{2,1,0:T(8,128)(2,1)S(1)}, bf16[12,64,128]{2,1,0:T(8,128)(2,1)S(1)}, u32[]{:S(2)}, u32[]{:S(2)}) collective-permute-start(bf16[12,64,128]{2,1,0:T(8,128)(2,1)S(1)} %get-tuple-element.41), channel_id=1, source_target_pairs={{0,1},{1,2},{2,3},{3,0},{4,5},{5,6},{6,7},{7,4},{8,9},{9,10},{10,1... | collective-permute-start | bytes 589832 | tf_op jit(solution)/shard_map/ppermute | solution.py:392
  106.4 1.9 %collective-permute-start.4 = (bf16[12,64,128]{2,1,0:T(8,128)(2,1)S(1)}, bf16[12,64,128]{2,1,0:T(8,128)(2,1)S(1)}, u32[]{:S(2)}, u32[]{:S(2)}) collective-permute-start(bf16[12,64,128]{2,1,0:T(8,128)(2,1)S(1)} %get-tuple-element.42), channel_id=1, source_target_pairs={{0,3},{1,0},{2,1},{3,2},{4,7},{5,4},{6,5},{7,6},{8,11},{9,8},{10,9... | collective-permute-start | bytes 589832 | tf_op jit(solution)/shard_map/ppermute | solution.py:392
  108.3 1.1 collective-permute-done.2.first
  109.4 2.0 %collective-permute-done.3.second = bf16[12,64,128]{2,1,0:T(8,128)(2,1)S(1)} collective-permute-done((bf16[12,64,128]{2,1,0:T(8,128)(2,1)S(1)}, bf16[12,64,128]{2,1,0:T(8,128)(2,1)S(1)}, u32[]{:S(2)}, u32[]{:S(2)}) %collective-permute-start.3) | collective-permute-done | bytes 196640 | tf_op jit(solution)/shard_map/ppermute | solution.py:392
  111.4 4.5 %collective-permute-done.4.third = bf16[12,64,128]{2,1,0:T(8,128)(2,1)S(1)} collective-permute-done((bf16[12,64,128]{2,1,0:T(8,128)(2,1)S(1)}, bf16[12,64,128]{2,1,0:T(8,128)(2,1)S(1)}, u32[]{:S(2)}, u32[]{:S(2)}) %collective-permute-start.4) | collective-permute-done | bytes 196640 | tf_op jit(solution)/shard_map/ppermute | solution.py:392
  115.8 0.0 all-to-all-done.3.arrived
  115.8 2.3 %shard_map.92 = bf16[8,128,128]{2,1,0:T(8,128)(2,1)} custom-call(bf16[8,8,128,128]{3,2,1,0:T(8,128)(2,1)} %all-to-all-done.3.arrived, bf16[12,64,128]{2,1,0:T(8,128)(2,1)S(1)} %collective-permute-done.2.first, bf16[12,64,128]{2,1,0:T(8,128)(2,1)S(1)} %collective-permute-done.3.second, bf16[12,64,128]{2,1,0:T(8,128)(2,1)S(1)} %collective-permute-done.4.third), custom_call_target="tpu_custom_call" | custom-call | tf_op jit(solution)/shard_map/pallas_call | solution.py:395
  118.2 7.2 %all-to-all-start.4 = ((bf16[8,128,128]{2,1,0:T(8,128)(2,1)}), bf16[8,128,128]{2,1,0:T(8,128)(2,1)S(1)}, u32[]{:S(2)}, u32[]{:S(2)}) async-start(bf16[8,128,128]{2,1,0:T(8,128)(2,1)} %shard_map.92), calls=%async_computation.4 | async-start | bytes 524288 | tf_op jit(solution)/shard_map/all_to_all | solution.py:41
  125.4 0.1 convert_add_fusion
  125.4 0.7 slice.8
  126.1 0.7 slice.9
  126.8 4.9 %all-to-all-done.4.arrived = bf16[8,128,128]{2,1,0:T(8,128)(2,1)S(1)} async-done(((bf16[8,128,128]{2,1,0:T(8,128)(2,1)}), bf16[8,128,128]{2,1,0:T(8,128)(2,1)S(1)}, u32[]{:S(2)}, u32[]{:S(2)}) %all-to-all-start.4) | async-done | bytes 262176 | tf_op jit(solution)/shard_map/all_to_all | solution.py:41
  131.8 1.3 shard_map.93
Async XLA Ops:
  1.4 0.8 copy-start.7
  20.7 12.7 %copy-start.3 = (bf16[32,64,128]{2,1,0:T(8,128)(2,1)S(1)}, bf16[32,64,128]{2,1,0:T(8,128)(2,1)}, u32[]{:S(2)}) copy-start(bf16[32,64,128]{2,1,0:T(8,128)(2,1)} %values.1) | copy-start | bytes 1572868
  20.7 15.0 %copy-start.8 = (bf16[4,64,128]{2,1,0:T(8,128)(2,1)S(1)}, bf16[4,64,128]{2,1,0:T(8,128)(2,1)}, u32[]{:S(2)}) copy-start(bf16[4,64,128]{2,1,0:T(8,128)(2,1)} %param.6) | copy-start | bytes 196612
  20.7 39.0 %all-to-all-start.1 = ((bf16[8,8,136,128]{3,2,1,0:T(8,128)(2,1)}), bf16[8,8,136,128]{3,2,1,0:T(8,128)(2,1)S(1)}, u32[]{:S(2)}, u32[]{:S(2)}) async-start(bf16[8,8,136,128]{3,2,1,0:T(8,128)(2,1)} %broadcast_in_dim.2), calls=%async_computation.1 | async-start | bytes 4456448 | tf_op jit(solution)/shard_map/all_to_all | solution.py:41
  33.8 15.5 %collective-permute-start = (bf16[32,64,128]{2,1,0:T(8,128)(2,1)S(1)}, bf16[32,64,128]{2,1,0:T(8,128)(2,1)S(1)}, u32[]{:S(2)}, u32[]{:S(2)}) collective-permute-start(bf16[32,64,128]{2,1,0:T(8,128)(2,1)S(1)} %shard_map.85.own_rows), channel_id=1, source_target_pairs={{0,4},{4,0},{8,12},{12,8},{16,20},{20,16},{24,28},{28,24},{32,36},... | collective-permute-start | bytes 1572872 | tf_op jit(solution)/shard_map/ppermute | solution.py:333
  48.6 0.7 copy-start.4
  63.2 0.7 copy-start.6
  63.9 20.0 %all-to-all-start.2 = ((f32[64,4,128]{2,1,0:T(4,128)}), f32[64,4,128]{2,1,0:T(4,128)S(1)}, u32[]{:S(2)}, u32[]{:S(2)}) async-start(f32[64,4,128]{2,1,0:T(4,128)} %copy-done.6), calls=%async_computation.2 | async-start | bytes 262144 | tf_op jit(solution)/shard_map/all_to_all | solution.py:41
  81.1 1.3 copy-start
  82.4 1.0 copy-start.1
  83.9 6.7 %copy-start.2 = (bf16[64,64,128]{2,1,0:T(8,128)(2,1)S(1)}, bf16[64,64,128]{2,1,0:T(8,128)(2,1)}, u32[]{:S(2)}) copy-start(bf16[64,64,128]{2,1,0:T(8,128)(2,1)} %copy-done.1) | copy-start | bytes 3145732
  83.9 31.9 %all-to-all-start.3 = ((bf16[8,8,128,128]{3,2,1,0:T(8,128)(2,1)}), bf16[8,8,128,128]{3,2,1,0:T(8,128)(2,1)}, u32[]{:S(2)}, u32[]{:S(2)}) async-start(bf16[8,8,128,128]{3,2,1,0:T(8,128)(2,1)} %bitcast.6), calls=%async_computation.3 | async-start | bytes 4194304 | tf_op jit(solution)/shard_map/all_to_all | solution.py:41
  90.6 6.5 %copy-start.5 = (bf16[16,64,128]{2,1,0:T(8,128)(2,1)S(1)}, bf16[16,64,128]{2,1,0:T(8,128)(2,1)}, u32[]{:S(2)}) copy-start(bf16[16,64,128]{2,1,0:T(8,128)(2,1)} %copy-done.4) | copy-start | bytes 786436
  95.1 3.8 %collective-permute-start.1 = (bf16[32,64,128]{2,1,0:T(8,128)(2,1)S(1)}, bf16[32,64,128]{2,1,0:T(8,128)(2,1)S(1)}, u32[]{:S(2)}, u32[]{:S(2)}) collective-permute-start(bf16[32,64,128]{2,1,0:T(8,128)(2,1)S(1)} %get-tuple-element.38), channel_id=1, source_target_pairs={{0,4},{4,0},{8,12},{12,8},{16,20},{20,16},{24,28},{28,24},{32,36},... | collective-permute-start | bytes 1572872 | tf_op jit(solution)/shard_map/ppermute | solution.py:390
  99.0 10.3 %collective-permute-start.2 = (bf16[12,64,128]{2,1,0:T(8,128)(2,1)S(1)}, bf16[12,64,128]{2,1,0:T(8,128)(2,1)S(1)}, u32[]{:S(2)}, u32[]{:S(2)}) collective-permute-start(bf16[12,64,128]{2,1,0:T(8,128)(2,1)S(1)} %get-tuple-element.40), channel_id=1, source_target_pairs={{0,2},{1,3},{2,0},{3,1},{4,6},{5,7},{6,4},{7,5},{8,10},{9,11},{10,... | collective-permute-start | bytes 589832 | tf_op jit(solution)/shard_map/ppermute | solution.py:392
  102.3 9.0 %collective-permute-start.3 = (bf16[12,64,128]{2,1,0:T(8,128)(2,1)S(1)}, bf16[12,64,128]{2,1,0:T(8,128)(2,1)S(1)}, u32[]{:S(2)}, u32[]{:S(2)}) collective-permute-start(bf16[12,64,128]{2,1,0:T(8,128)(2,1)S(1)} %get-tuple-element.41), channel_id=1, source_target_pairs={{0,1},{1,2},{2,3},{3,0},{4,5},{5,6},{6,7},{7,4},{8,9},{9,10},{10,1... | collective-permute-start | bytes 589832 | tf_op jit(solution)/shard_map/ppermute | solution.py:392
  106.4 9.5 %collective-permute-start.4 = (bf16[12,64,128]{2,1,0:T(8,128)(2,1)S(1)}, bf16[12,64,128]{2,1,0:T(8,128)(2,1)S(1)}, u32[]{:S(2)}, u32[]{:S(2)}) collective-permute-start(bf16[12,64,128]{2,1,0:T(8,128)(2,1)S(1)} %get-tuple-element.42), channel_id=1, source_target_pairs={{0,3},{1,0},{2,1},{3,2},{4,7},{5,4},{6,5},{7,6},{8,11},{9,8},{10,9... | collective-permute-start | bytes 589832 | tf_op jit(solution)/shard_map/ppermute | solution.py:392
  118.2 13.6 %all-to-all-start.4 = ((bf16[8,128,128]{2,1,0:T(8,128)(2,1)}), bf16[8,128,128]{2,1,0:T(8,128)(2,1)S(1)}, u32[]{:S(2)}, u32[]{:S(2)}) async-start(bf16[8,128,128]{2,1,0:T(8,128)(2,1)} %shard_map.92), calls=%async_computation.4 | async-start | bytes 524288 | tf_op jit(solution)/shard_map/all_to_all | solution.py:41

commit v15 on v14

--- a/solution.py
+++ b/solution.py
@@ -177,7 +177,7 @@
     which = iota((8, N_DP), 0)
     lane = jnp.where(which == 0, core * SPOTS + spot, (1 - core) * SPOTS + spot)
     pick = ((iota((8, N_DP), 1) == lane) & (which < 2)).astype(F32).astype(BF16)
-    table[...] = dot(pick, rows, ((1,), (1,))).astype(I32)
+    table[...] = dot(pick, rows, ((1,), (1,)))[0:2].astype(I32)
     copy = pltpu.make_async_copy(table, codes, sem)
     copy.start()
     copy.wait()
@@ -242,7 +242,7 @@
     for_sources(one)
 
 
-def weigh(codes, sums, asked, probs, own_grad, other_grad, own_sum, weight_inv, other_acc, inverse, sem):
+def weigh(codes, sums, asked, probs, own_grad, other_grad, own_sum, other_acc, inverse, weight_inv, sem):
     weight_sum = jnp.sum(sums[...], axis=0)
     inverse[...] = jnp.zeros_like(inverse)
     inverse[0:QD] = 1.0 / weight_sum
@@ -270,7 +270,7 @@
     other_grad[...] = other_acc[...].astype(BF16)
 
 
-def weigh_positives(own_sum, q_tiles, gathered, pos_grad, query_part, losses):
+def weigh_positives(own_sum, q_tiles, gathered, pos_grad, query_part, scale, losses):
     q_unit = q_tiles[...].reshape(QROWS, D)
     cands, exp_scores, total, scores = positive_scores(q_unit, gathered)
     lane = iota((1, QROWS), 1)
@@ -281,6 +281,7 @@
         losses[q] = jnp.sum(jnp.where(lane == q * QT, loss, 0.0))
     weight_grad = (exp_scores * (score_grad / total)[:, None, :]).astype(BF16).reshape(BATCH * PT, QROWS)
     query_part[...] = dot(weight_grad, cands, ((0,), (0,)))
+    scale[...] = jnp.transpose(jnp.broadcast_to(1.0 / own_sum[...], (QROWS, D)))
     pos_grad[...] = dot(weight_grad, q_unit, ((1,), (0,))).reshape(BATCH, PT, D)
 
 
@@ -300,12 +301,9 @@
         out[part] = jnp.sum(blocks[:, part].astype(F32), axis=0).astype(BF16)
 
 
-def collect(weight_inv, query_part, arrived, out):
-    source = position()[2]
+def collect(scale, query_part, arrived, out):
     total = jnp.sum(arrived[...].astype(F32), axis=0)
-    for q in range(QD):
-        rows = slice(q * QT, (q + 1) * QT)
-        out[q] = query_part[rows, :] + total[rows] * weight_inv[q, source]
+    out[...] = (query_part[...] + total * scale[...]).reshape(QD, QT, D)
 
 
 def per_device(queries, positives, passage_pool, negative_ids, storage_row):
@@ -341,14 +339,14 @@
         (
             struct((SPOTS, QROWS), F32),
             struct((SPOTS, QD, QROWS), F32),
-            struct((8, SPOTS * 8), I32),
+            struct((2, SPOTS * 8), I32),
         ),
         [vmem(), vmem(), vmem(), vmem()],
         (vmem(), vmem(), vmem()),
         [
             pltpu.VMEM((SPOTS, QROWS), F32),
             pltpu.VMEM((SPOTS, QROWS), F32),
-            pltpu.SMEM((8, SPOTS * 8), I32),
+            pltpu.SMEM((2, SPOTS * 8), I32),
             pltpu.SemaphoreType.DMA,
         ],
     )(asked, own_rows, other_rows, pos_weight)
@@ -362,23 +360,27 @@
     )(codes, asked, own_rows, other_rows, factor)
     arrived = exchange(back.reshape(N_Z, N_Y, QROWS, D), along(0))
 
-    own_grad, other_grad, own_sum, weight_inv = call(
+    own_grad, other_grad, own_sum = call(
         weigh,
         (
             struct((ROWS, PT, D), F32),
             struct((ROWS, PT, D), BF16),
             struct((1, QROWS), F32),
-            struct((8, QROWS), F32),
         ),
         [smem(), vmem(), vmem(), vmem()],
+        (vmem(), vmem(), vmem()),
+        [
+            pltpu.VMEM((ROWS, PT, D), F32),
+            pltpu.VMEM((8, QROWS), F32),
+            pltpu.SMEM((8, QROWS), F32),
+            pltpu.SemaphoreType.DMA,
+        ],
+    )(codes, sums, asked, probs)
+    pos_grad, query_part, scale, losses = call(
+        weigh_positives,
+        (struct((BATCH, PT, D), F32), struct((QROWS, D), F32), struct((QROWS, D), F32), struct((QD,), F32)),
+        [vmem()] * 3,
         (vmem(), vmem(), vmem(), smem()),
-        [pltpu.VMEM((ROWS, PT, D), F32), pltpu.VMEM((8, QROWS), F32), pltpu.SemaphoreType.DMA],
-    )(codes, sums, asked, probs)
-    pos_grad, query_part, losses = call(
-        weigh_positives,
-        (struct((BATCH, PT, D), F32), struct((QROWS, D), F32), struct((QD,), F32)),
-        [vmem()] * 3,
-        (vmem(), vmem(), smem()),
     )(own_sum, q_unit, gathered)
 
     block = (QD + ROWS // GROUP, PT, D)
@@ -401,8 +403,8 @@
     )(arrived, *moved)
     arrived = exchange(arrived, along(1))
     query_grad = call(
-        collect, struct((QD, QT, D), F32), [smem(), vmem(), vmem()], vmem()
-    )(weight_inv, query_part, arrived)
+        collect, struct((QD, QT, D), F32), [vmem()] * 3, vmem()
+    )(scale, query_part, arrived)
     total = kept + moved[0].astype(F32) + moved[1].astype(F32) + moved[2].astype(F32)
     return losses, query_grad, total[:QD], total[QD:]
 

time: 135 us -> 134 us (level)
  Pallas kernels: 20.6 us -> 18.9 us
  transfers between devices with their start and end apart: 9 -> 9, of which waited for: 7 -> 8; matrix products, arithmetic and copies ran while one was open for 1% -> 1% of each run, Pallas kernels for 9% -> 8%
where the time goes in v15:
time: 134 us; the launch traced here: 132 us
  starting transfers between devices  51.5 us (38%)
  blocking collectives  27.6 us (21%)
  waiting for transfers between devices  24.8 us (19%)
  Pallas kernels  18.9 us (14%)
  local copies, waits for them, and re-layouts  7.5 us (6%)
    all_to_all x4, starting transfers between devices, exchange(): lax.all_to_all(blocks, EVERY, split_axis=0, concat_axis=0, axis_index_gro...  38.4 us
    all_to_all x4, waiting for transfers between devices, exchange(): lax.all_to_all(blocks, EVERY, split_axis=0, concat_axis=0, axis_index_gro...  16.6 us
    all_to_all x1, blocking collectives, exchange(): lax.all_to_all(blocks, EVERY, split_axis=0, concat_axis=0, axis_index_gro...  15.3 us
    all_gather x1, blocking collectives, per_device(): gathered = lax.all_gather(positives, 'group', axis=0, tiled=True)  12.3 us
    ppermute x3, starting transfers between devices, per_device(): lax.ppermute(part, 'group', [(g, (g + ahead) % GROUP) for g in range(GROU...  9.24 us
    ppermute x3, waiting for transfers between devices, per_device(): lax.ppermute(part, 'group', [(g, (g + ahead) % GROUP) for g in range(GROU...  7.56 us
    pallas_call x1, Pallas kernels, per_device(): call(terms, (struct((SPOTS, PT, QROWS), BF16), struct((SPOTS, QROWS, D),...  4.92 us
    unnamed x18, local copies, waits for them, and re-layouts  4.45 us
  transfers between devices with their start and end apart: 9, of which 8 were waited for; matrix products, arithmetic and copies ran while one was open for 1% of the time, Pallas kernels for 8%

profile of v15, /device:TPU:6, one launch (start us, length us, event | category | flops | bytes accessed | tf_op | source)
XLA Modules:
  0.0 131.9 jit_solution(1991101046317131000)
XLA Ops:
  0.6 0.7 pad_add_fusion.table_in
  1.4 0.0 copy-start.7
  1.4 0.8 copy-done.7
  2.1 1.5 %shard_map.84 = (bf16[8,136,128]{2,1,0:T(8,128)(2,1)S(1)}, bf16[4,32,128]{2,1,0:T(8,128)(2,1)S(1)}) custom-call(s32[40,128]{1,0:T(8,128)S(1)} %pad_add_fusion.table_in, bf16[4,32,128]{2,1,0:T(8,128)(2,1)S(1)} %copy-done.7), custom_call_target="tpu_custom_call" | custom-call | tf_op jit(solution)/shard_map/pallas_call | solution.py:315
  3.7 15.3 %all_to_all.25 = bf16[8,136,128]{2,1,0:T(8,128)(2,1)S(1)} all-to-all(bf16[8,136,128]{2,1,0:T(8,128)(2,1)S(1)} %get-tuple-element.24), channel_id=1, replica_groups={{452,388,324,260,196,132,68,4},{453,389,325,261,197,133,69,5},{454,390,..., dimensions={0} | all-to-all | bytes 557056 | tf_op jit(solution)/shard_map/all_to_all | solution.py:41
  19.0 1.7 %broadcast_in_dim.2 = bf16[8,8,136,128]{3,2,1,0:T(8,128)(2,1)} broadcast(bf16[8,136,128]{2,1,0:T(8,128)(2,1)S(1)} %all_to_all.25), dimensions={1,2,3} | broadcast | bytes 2506752 | tf_op jit(solution)/shard_map/broadcast_in_dim | solution.py:328
  20.7 0.0 copy-start.3
  20.7 0.0 copy-start.8
  20.7 12.7 %all-to-all-start.1 = ((bf16[8,8,136,128]{3,2,1,0:T(8,128)(2,1)}), bf16[8,8,136,128]{3,2,1,0:T(8,128)(2,1)S(1)}, u32[]{:S(2)}, u32[]{:S(2)}) async-start(bf16[8,8,136,128]{3,2,1,0:T(8,128)(2,1)} %broadcast_in_dim.2), calls=%async_computation.1 | async-start | bytes 4456448 | tf_op jit(solution)/shard_map/all_to_all | solution.py:41
  33.4 0.0 copy-done.3
  33.4 0.4 shard_map.85.own_rows
  33.8 1.9 %collective-permute-start = (bf16[32,64,128]{2,1,0:T(8,128)(2,1)S(1)}, bf16[32,64,128]{2,1,0:T(8,128)(2,1)S(1)}, u32[]{:S(2)}, u32[]{:S(2)}) collective-permute-start(bf16[32,64,128]{2,1,0:T(8,128)(2,1)S(1)} %shard_map.85.own_rows), channel_id=1, source_target_pairs={{0,4},{4,0},{8,12},{12,8},{16,20},{20,16},{24,28},{28,24},{32,36},... | collective-permute-start | bytes 1572872 | tf_op jit(solution)/shard_map/ppermute | solution.py:331
  35.7 0.0 copy-done.8
  35.7 12.3 %all_gather.3.positives = bf16[16,64,128]{2,1,0:T(8,128)(2,1)S(1)} all-gather(bf16[4,64,128]{2,1,0:T(8,128)(2,1)S(1)} %copy-done.8), channel_id=1, replica_groups=mesh['dp'=128,'group'=4] {'group'}, dimensions={0}, use_global_device_ids=true | all-gather | bytes 327680 | tf_op jit(solution)/shard_map/all_gather | solution.py:332
  47.9 0.6 shard_map.86
  48.6 0.0 copy-start.4
  48.6 0.7 copy-done.4
  49.3 0.0 collective-permute-done.other_rows
  49.3 10.4 %all-to-all-done.1 = bf16[8,8,136,128]{3,2,1,0:T(8,128)(2,1)S(1)} async-done(((bf16[8,8,136,128]{3,2,1,0:T(8,128)(2,1)}), bf16[8,8,136,128]{3,2,1,0:T(8,128)(2,1)S(1)}, u32[]{:S(2)}, u32[]{:S(2)}) %all-to-all-start.1) | async-done | bytes 2228256 | tf_op jit(solution)/shard_map/all_to_all | solution.py:41
  59.7 3.4 %shard_map.87 = (f32[64,128]{1,0:T(8,128)S(1)}, f32[64,4,128]{2,1,0:T(4,128)S(1)}, s32[2,512]{1,0:T(2,128)S(1)}) custom-call(bf16[64,136,128]{2,1,0:T(8,128)(2,1)S(1)} %bitcast.3, bf16[32,64,128]{2,1,0:T(8,128)(2,1)S(1)} %shard_map.85.own_rows, bf16[32,64,128]{2,1,0:T(8,128)(2,1)S(1)} %collective-permute-done.other_rows, ...), custom_call_target="tpu_custom_call" | custom-call | tf_op jit(solution)/shard_map/pallas_call | solution.py:337
  63.0 0.0 copy-start.6
  63.0 0.6 copy-done.6
  63.7 12.0 %all-to-all-start.2 = ((f32[64,4,128]{2,1,0:T(4,128)}), f32[64,4,128]{2,1,0:T(4,128)S(1)}, u32[]{:S(2)}, u32[]{:S(2)}) async-start(f32[64,4,128]{2,1,0:T(4,128)} %copy-done.6), calls=%async_computation.2 | async-start | bytes 262144 | tf_op jit(solution)/shard_map/all_to_all | solution.py:41
  75.7 4.9 %shard_map.88 = (bf16[64,64,128]{2,1,0:T(8,128)(2,1)S(1)}, bf16[64,128,128]{2,1,0:T(8,128)(2,1)S(1)}) custom-call(s32[2,512]{1,0:T(2,128)S(1)} %get-tuple-element.27.codes, bf16[64,136,128]{2,1,0:T(8,128)(2,1)S(1)} %bitcast.4, bf16[32,64,128]{2,1,0:T(8,128)(2,1)S(1)} %shard_map.85.own_rows, bf16[32,64,128]{2,1,0:T(8,128)(2,1)S(1)} %collective-permute-done.other_rows, ...), custom_call_target="tpu_custom_call" | custom-call | tf_op jit(solution)/shard_map/pallas_call | solution.py:355
  80.7 0.0 copy-start
  80.7 1.3 copy-done
  82.0 0.0 copy-start.1
  82.0 1.0 copy-done.1
  83.0 0.7 all-to-all-done.2.sums
  83.7 0.0 copy-start.2
  83.7 6.6 %all-to-all-start.3 = ((bf16[8,8,128,128]{3,2,1,0:T(8,128)(2,1)}), bf16[8,8,128,128]{3,2,1,0:T(8,128)(2,1)}, u32[]{:S(2)}, u32[]{:S(2)}) async-start(bf16[8,8,128,128]{3,2,1,0:T(8,128)(2,1)} %bitcast.6), calls=%async_computation.3 | async-start | bytes 4194304 | tf_op jit(solution)/shard_map/all_to_all | solution.py:41
  90.3 0.0 copy-start.5
  90.3 0.0 copy-done.2
  90.3 3.7 %shard_map.89 = (f32[32,64,128]{2,1,0:T(8,128)S(1)}, bf16[32,64,128]{2,1,0:T(8,128)(2,1)S(1)}, f32[1,128]{1,0:T(1,128)S(1)}) custom-call(s32[2,512]{1,0:T(2,128)S(1)} %get-tuple-element.27.codes, f32[64,4,128]{2,1,0:T(4,128)S(1)} %all-to-all-done.2.sums, bf16[64,136,128]{2,1,0:T(8,128)(2,1)S(1)} %bitcast.5, bf16[64,64,128]{2,1,0:T(8,128)(2,1)S(1)} %copy-done.2), custom_call_target="tpu_custom_call" | custom-call | tf_op jit(solution)/shard_map/pallas_call | solution.py:363
  94.0 1.9 %collective-permute-start.1 = (bf16[32,64,128]{2,1,0:T(8,128)(2,1)S(1)}, bf16[32,64,128]{2,1,0:T(8,128)(2,1)S(1)}, u32[]{:S(2)}, u32[]{:S(2)}) collective-permute-start(bf16[32,64,128]{2,1,0:T(8,128)(2,1)S(1)} %get-tuple-element.38), channel_id=1, source_target_pairs={{0,4},{4,0},{8,12},{12,8},{16,20},{20,16},{24,28},{28,24},{32,36},... | collective-permute-start | bytes 1572872 | tf_op jit(solution)/shard_map/ppermute | solution.py:392
  96.0 0.0 copy-done.5
  96.0 1.3 shard_map.90
  97.2 0.6 collective-permute-done.1.moved
  97.8 0.1 shard_map.91
  97.9 3.3 %collective-permute-start.2 = (bf16[12,64,128]{2,1,0:T(8,128)(2,1)S(1)}, bf16[12,64,128]{2,1,0:T(8,128)(2,1)S(1)}, u32[]{:S(2)}, u32[]{:S(2)}) collective-permute-start(bf16[12,64,128]{2,1,0:T(8,128)(2,1)S(1)} %get-tuple-element.40), channel_id=1, source_target_pairs={{0,2},{1,3},{2,0},{3,1},{4,6},{5,7},{6,4},{7,5},{8,10},{9,11},{10,... | collective-permute-start | bytes 589832 | tf_op jit(solution)/shard_map/ppermute | solution.py:394
  101.3 4.0 %collective-permute-start.3 = (bf16[12,64,128]{2,1,0:T(8,128)(2,1)S(1)}, bf16[12,64,128]{2,1,0:T(8,128)(2,1)S(1)}, u32[]{:S(2)}, u32[]{:S(2)}) collective-permute-start(bf16[12,64,128]{2,1,0:T(8,128)(2,1)S(1)} %get-tuple-element.41), channel_id=1, source_target_pairs={{0,1},{1,2},{2,3},{3,0},{4,5},{5,6},{6,7},{7,4},{8,9},{9,10},{10,1... | collective-permute-start | bytes 589832 | tf_op jit(solution)/shard_map/ppermute | solution.py:394
  105.3 1.9 %collective-permute-start.4 = (bf16[12,64,128]{2,1,0:T(8,128)(2,1)S(1)}, bf16[12,64,128]{2,1,0:T(8,128)(2,1)S(1)}, u32[]{:S(2)}, u32[]{:S(2)}) collective-permute-start(bf16[12,64,128]{2,1,0:T(8,128)(2,1)S(1)} %get-tuple-element.42), channel_id=1, source_target_pairs={{0,3},{1,0},{2,1},{3,2},{4,7},{5,4},{6,5},{7,6},{8,11},{9,8},{10,9... | collective-permute-start | bytes 589832 | tf_op jit(solution)/shard_map/ppermute | solution.py:394
  107.2 1.1 collective-permute-done.2.first
  108.3 2.0 %collective-permute-done.3.second = bf16[12,64,128]{2,1,0:T(8,128)(2,1)S(1)} collective-permute-done((bf16[12,64,128]{2,1,0:T(8,128)(2,1)S(1)}, bf16[12,64,128]{2,1,0:T(8,128)(2,1)S(1)}, u32[]{:S(2)}, u32[]{:S(2)}) %collective-permute-start.3) | collective-permute-done | bytes 196640 | tf_op jit(solution)/shard_map/ppermute | solution.py:394
  110.3 4.5 %collective-permute-done.4.third = bf16[12,64,128]{2,1,0:T(8,128)(2,1)S(1)} collective-permute-done((bf16[12,64,128]{2,1,0:T(8,128)(2,1)S(1)}, bf16[12,64,128]{2,1,0:T(8,128)(2,1)S(1)}, u32[]{:S(2)}, u32[]{:S(2)}) %collective-permute-start.4) | collective-permute-done | bytes 196640 | tf_op jit(solution)/shard_map/ppermute | solution.py:394
  114.8 0.6 all-to-all-done.3.arrived
  115.4 2.3 %shard_map.92 = bf16[8,128,128]{2,1,0:T(8,128)(2,1)} custom-call(bf16[8,8,128,128]{3,2,1,0:T(8,128)(2,1)} %all-to-all-done.3.arrived, bf16[12,64,128]{2,1,0:T(8,128)(2,1)S(1)} %collective-permute-done.2.first, bf16[12,64,128]{2,1,0:T(8,128)(2,1)S(1)} %collective-permute-done.3.second, bf16[12,64,128]{2,1,0:T(8,128)(2,1)S(1)} %collective-permute-done.4.third), custom_call_target="tpu_custom_call" | custom-call | tf_op jit(solution)/shard_map/pallas_call | solution.py:397
  117.7 7.1 %all-to-all-start.4 = ((bf16[8,128,128]{2,1,0:T(8,128)(2,1)}), bf16[8,128,128]{2,1,0:T(8,128)(2,1)S(1)}, u32[]{:S(2)}, u32[]{:S(2)}) async-start(bf16[8,128,128]{2,1,0:T(8,128)(2,1)} %shard_map.92), calls=%async_computation.4 | async-start | bytes 524288 | tf_op jit(solution)/shard_map/all_to_all | solution.py:41
  124.8 0.1 convert_add_fusion
  124.9 0.7 slice.8
  125.6 0.7 slice.9
  126.3 4.9 %all-to-all-done.4.arrived = bf16[8,128,128]{2,1,0:T(8,128)(2,1)S(1)} async-done(((bf16[8,128,128]{2,1,0:T(8,128)(2,1)}), bf16[8,128,128]{2,1,0:T(8,128)(2,1)S(1)}, u32[]{:S(2)}, u32[]{:S(2)}) %all-to-all-start.4) | async-done | bytes 262176 | tf_op jit(solution)/shard_map/all_to_all | solution.py:41
  131.2 0.7 shard_map.93
Async XLA Ops:
  1.4 0.8 copy-start.7
  20.7 12.7 %copy-start.3 = (bf16[32,64,128]{2,1,0:T(8,128)(2,1)S(1)}, bf16[32,64,128]{2,1,0:T(8,128)(2,1)}, u32[]{:S(2)}) copy-start(bf16[32,64,128]{2,1,0:T(8,128)(2,1)} %values.1) | copy-start | bytes 1572868
  20.7 15.0 %copy-start.8 = (bf16[4,64,128]{2,1,0:T(8,128)(2,1)S(1)}, bf16[4,64,128]{2,1,0:T(8,128)(2,1)}, u32[]{:S(2)}) copy-start(bf16[4,64,128]{2,1,0:T(8,128)(2,1)} %param.6) | copy-start | bytes 196612
  20.7 39.0 %all-to-all-start.1 = ((bf16[8,8,136,128]{3,2,1,0:T(8,128)(2,1)}), bf16[8,8,136,128]{3,2,1,0:T(8,128)(2,1)S(1)}, u32[]{:S(2)}, u32[]{:S(2)}) async-start(bf16[8,8,136,128]{3,2,1,0:T(8,128)(2,1)} %broadcast_in_dim.2), calls=%async_computation.1 | async-start | bytes 4456448 | tf_op jit(solution)/shard_map/all_to_all | solution.py:41
  33.8 15.5 %collective-permute-start = (bf16[32,64,128]{2,1,0:T(8,128)(2,1)S(1)}, bf16[32,64,128]{2,1,0:T(8,128)(2,1)S(1)}, u32[]{:S(2)}, u32[]{:S(2)}) collective-permute-start(bf16[32,64,128]{2,1,0:T(8,128)(2,1)S(1)} %shard_map.85.own_rows), channel_id=1, source_target_pairs={{0,4},{4,0},{8,12},{12,8},{16,20},{20,16},{24,28},{28,24},{32,36},... | collective-permute-start | bytes 1572872 | tf_op jit(solution)/shard_map/ppermute | solution.py:331
  48.6 0.7 copy-start.4
  63.0 0.7 copy-start.6
  63.7 20.0 %all-to-all-start.2 = ((f32[64,4,128]{2,1,0:T(4,128)}), f32[64,4,128]{2,1,0:T(4,128)S(1)}, u32[]{:S(2)}, u32[]{:S(2)}) async-start(f32[64,4,128]{2,1,0:T(4,128)} %copy-done.6), calls=%async_computation.2 | async-start | bytes 262144 | tf_op jit(solution)/shard_map/all_to_all | solution.py:41
  80.7 1.3 copy-start
  82.0 1.0 copy-start.1
  83.7 6.6 %copy-start.2 = (bf16[64,64,128]{2,1,0:T(8,128)(2,1)S(1)}, bf16[64,64,128]{2,1,0:T(8,128)(2,1)}, u32[]{:S(2)}) copy-start(bf16[64,64,128]{2,1,0:T(8,128)(2,1)} %copy-done.1) | copy-start | bytes 3145732
  83.7 31.6 %all-to-all-start.3 = ((bf16[8,8,128,128]{3,2,1,0:T(8,128)(2,1)}), bf16[8,8,128,128]{3,2,1,0:T(8,128)(2,1)}, u32[]{:S(2)}, u32[]{:S(2)}) async-start(bf16[8,8,128,128]{3,2,1,0:T(8,128)(2,1)} %bitcast.6), calls=%async_computation.3 | async-start | bytes 4194304 | tf_op jit(solution)/shard_map/all_to_all | solution.py:41
  90.3 5.7 %copy-start.5 = (bf16[16,64,128]{2,1,0:T(8,128)(2,1)S(1)}, bf16[16,64,128]{2,1,0:T(8,128)(2,1)}, u32[]{:S(2)}) copy-start(bf16[16,64,128]{2,1,0:T(8,128)(2,1)} %copy-done.4) | copy-start | bytes 786436
  94.0 3.8 %collective-permute-start.1 = (bf16[32,64,128]{2,1,0:T(8,128)(2,1)S(1)}, bf16[32,64,128]{2,1,0:T(8,128)(2,1)S(1)}, u32[]{:S(2)}, u32[]{:S(2)}) collective-permute-start(bf16[32,64,128]{2,1,0:T(8,128)(2,1)S(1)} %get-tuple-element.38), channel_id=1, source_target_pairs={{0,4},{4,0},{8,12},{12,8},{16,20},{20,16},{24,28},{28,24},{32,36},... | collective-permute-start | bytes 1572872 | tf_op jit(solution)/shard_map/ppermute | solution.py:392
  97.9 10.3 %collective-permute-start.2 = (bf16[12,64,128]{2,1,0:T(8,128)(2,1)S(1)}, bf16[12,64,128]{2,1,0:T(8,128)(2,1)S(1)}, u32[]{:S(2)}, u32[]{:S(2)}) collective-permute-start(bf16[12,64,128]{2,1,0:T(8,128)(2,1)S(1)} %get-tuple-element.40), channel_id=1, source_target_pairs={{0,2},{1,3},{2,0},{3,1},{4,6},{5,7},{6,4},{7,5},{8,10},{9,11},{10,... | collective-permute-start | bytes 589832 | tf_op jit(solution)/shard_map/ppermute | solution.py:394
  101.3 9.0 %collective-permute-start.3 = (bf16[12,64,128]{2,1,0:T(8,128)(2,1)S(1)}, bf16[12,64,128]{2,1,0:T(8,128)(2,1)S(1)}, u32[]{:S(2)}, u32[]{:S(2)}) collective-permute-start(bf16[12,64,128]{2,1,0:T(8,128)(2,1)S(1)} %get-tuple-element.41), channel_id=1, source_target_pairs={{0,1},{1,2},{2,3},{3,0},{4,5},{5,6},{6,7},{7,4},{8,9},{9,10},{10,1... | collective-permute-start | bytes 589832 | tf_op jit(solution)/shard_map/ppermute | solution.py:394
  105.3 9.5 %collective-permute-start.4 = (bf16[12,64,128]{2,1,0:T(8,128)(2,1)S(1)}, bf16[12,64,128]{2,1,0:T(8,128)(2,1)S(1)}, u32[]{:S(2)}, u32[]{:S(2)}) collective-permute-start(bf16[12,64,128]{2,1,0:T(8,128)(2,1)S(1)} %get-tuple-element.42), channel_id=1, source_target_pairs={{0,3},{1,0},{2,1},{3,2},{4,7},{5,4},{6,5},{7,6},{8,11},{9,8},{10,9... | collective-permute-start | bytes 589832 | tf_op jit(solution)/shard_map/ppermute | solution.py:394
  117.7 13.5 %all-to-all-start.4 = ((bf16[8,128,128]{2,1,0:T(8,128)(2,1)}), bf16[8,128,128]{2,1,0:T(8,128)(2,1)S(1)}, u32[]{:S(2)}, u32[]{:S(2)}) async-start(bf16[8,128,128]{2,1,0:T(8,128)(2,1)} %shard_map.92), calls=%async_computation.4 | async-start | bytes 524288 | tf_op jit(solution)/shard_map/all_to_all | solution.py:41
